TPU v7x, 32 devices: a whole 2x2x4 slice. The times are simulated.
32 devices in a mesh: tile: 4 (over y, x), cuts: 8 (over z, core).
Axes of the slice: x: 2, y: 2, z: 4, core: 2. Of those that a mesh axis runs over, the one named last changes fastest.
Arguments:
- density: bfloat16 [128, 512, 1024], P('cuts', 'tile'), may hold values from -8 to 8
- valid: int32 [512, 1024], P('tile'), may hold values from 0 to 1, as said below
- row_taps: bfloat16 [4, 128, 17], P(None, 'cuts'), may hold values from -1.5 to 1.5
- col_taps: bfloat16 [4, 128, 17], P(None, 'cuts'), may hold values from -1.5 to 1.5
- amp_matrix: bfloat16 [128, 128], replicated, may hold values from -0.5 to 0.5
- like_matrix: bfloat16 [128, 128], replicated, may hold values from -0.5 to 0.5
Outputs:
- amplitude: bfloat16 [128, 524288], P(None, ('tile', 'cuts'))
- likelihood: bfloat16 [128, 524288], P(None, ('tile', 'cuts'))
Inputs may be any that keep to these rules, and one draw needn't show every extreme that they name: Every pixel row holds at least one valid pixel; the share of valid pixels rises from about 0.3 in the first row to about 0.9 in the last.
All inputs are finite; a program needn't handle non-finite values.
Results may differ from a plain program's by a relative error of at most 0.0082.
Values may be sent and summed in bfloat16 or wider, within the bound.
No kernel may reach another device: no remote copies, remote signals or barrier semaphores. Data moves between devices by JAX's collectives and lax.ppermute only.
A program may use at most 128 MiB of HBM per device.

v0:
```python
import jax
import jax.numpy as jnp
from jax import lax
from jax.sharding import PartitionSpec as P

REACH = 8
CBLK = 256


def extended(shard, sides, width):
    for axis, dim in sides:
        size, length = (lax.axis_size(axis), shard.shape[dim])
        up = [(i, (i + 1) % size) for i in range(size - 1)]
        down = [(j, i) for i, j in up]
        last = lax.slice_in_dim(shard, length - width, length, axis=dim)
        initial = lax.slice_in_dim(shard, 0, width, axis=dim)
        before = lax.ppermute(last, axis, up)
        after = lax.ppermute(initial, axis, down)
        shard = jnp.concatenate([before, shard, after], axis=dim)
    return shard


def band_matrix(taps, out_count, in_count):
    offset = lax.broadcasted_iota(jnp.int32, (out_count, in_count), 1) - lax.broadcasted_iota(
        jnp.int32, (out_count, in_count), 0
    )
    positions = lax.broadcasted_iota(jnp.int32, (1, 1, 2 * REACH + 1), 2)
    choose = (offset[:, :, None] == positions).astype(jnp.bfloat16)
    return jnp.einsum("ijt,kst->ksij", choose, taps, preferred_element_type=jnp.float32).astype(
        jnp.bfloat16
    )


def filter_field(padded, row_taps, col_taps):
    tall = padded.shape[1]
    col_count = padded.shape[2]
    row_band = band_matrix(row_taps, tall - 2 * REACH, tall)
    rowed = jnp.einsum(
        "ksij,sjc->ksic", row_band, padded, preferred_element_type=jnp.float32
    ).astype(jnp.bfloat16)
    widened = jnp.pad(rowed, ((0, 0), (0, 0), (0, 0), (REACH, REACH)))
    col_band = band_matrix(col_taps, CBLK, CBLK + 2 * REACH)
    pieces = []
    for begin in range(0, col_count, CBLK):
        segment = widened[:, :, :, begin : begin + CBLK + 2 * REACH]
        pieces.append(
            jnp.einsum("ksrj,ksij->sri", segment, col_band, preferred_element_type=jnp.float32)
        )
    return jnp.concatenate(pieces, axis=2).astype(jnp.bfloat16)


def project_pencil(pencil, amp_matrix, like_matrix):
    amp_float = jnp.dot(amp_matrix.T, pencil, preferred_element_type=jnp.float32)
    like_float = amp_float * jnp.dot(like_matrix.T, pencil, preferred_element_type=jnp.float32)
    return (amp_float.astype(jnp.bfloat16), like_float.astype(jnp.bfloat16))


def global_background(local_sums, local_count):
    totals, counted = lax.psum((local_sums, local_count), "tile")
    return totals / counted


def per_device(density, valid, row_taps, col_taps, amp_matrix, like_matrix):
    slice_count, row_count, col_count = density.shape
    mask_float = valid.astype(jnp.float32)
    local_sums = jnp.sum(density.astype(jnp.float32) * mask_float[None], axis=(1, 2))
    local_count = jnp.sum(mask_float)
    background = global_background(local_sums, local_count)
    masked_field = (
        mask_float[None] * (density.astype(jnp.float32) - background[:, None, None])
    ).astype(jnp.bfloat16)
    padded = extended(masked_field, (("tile", 1),), REACH)
    filtered = filter_field(padded, row_taps, col_taps)
    peers = lax.axis_size("cuts")
    share = row_count * col_count // peers
    split_flat = filtered.reshape(slice_count, peers, share)
    pencil = lax.all_to_all(split_flat, "cuts", split_axis=1, concat_axis=0, tiled=True).reshape(
        slice_count * peers, share
    )
    amplitude, likelihood = project_pencil(pencil, amp_matrix, like_matrix)
    return (amplitude, likelihood)


def solution(mesh):
    return jax.shard_map(
        per_device,
        mesh=mesh,
        in_specs=(
            P("cuts", "tile", None),
            P("tile", None),
            P(None, "cuts", None),
            P(None, "cuts", None),
            P(),
            P(),
        ),
        out_specs=(P(None, ("tile", "cuts")), P(None, ("tile", "cuts"))),
        check_vma=False,
    )
```

profile of v0, /device:TPU:4, one launch (start us, length us, event | category | flops | bytes accessed | tf_op | source)
XLA Modules:
  0.0 246.7 jit_solution(17683638198846642615)
XLA Ops:
  1.7 3.2 %fusion.2 = f32[16]{0:T(128)S(1)} fusion(bf16[16,128,1024]{2,1,0:T(8,128)(2,1)} %param.6, f32[128,1024]{1,0:T(8,128)S(1)} %convert_element_type.49), kind=kLoop, calls=%fused_computation.9 | loop fusion | flops 6291440 | bytes 4718656 | tf_op jit(solution)/shard_map/reduce_sum | solution.py:66
  5.0 1.8 convert_reduce_fusion
  6.8 9.6 %all-reduce.1 = (f32[16]{0:T(128)S(1)}, f32[]{:T(128)}) all-reduce(f32[16]{0:T(128)S(1)} %fusion.2, f32[]{:T(128)} %convert_reduce_fusion), channel_id=1, replica_groups=mesh['tile'=4,'cuts'=8] {'tile'}, use_global_device_ids=true, to_apply=%region_1.0 | all-reduce | flops 17 | bytes 136 | tf_op jit(solution)/shard_map/psum | solution.py:59
  17.0 3.5 %fusion.4 = bf16[16,128,1024]{2,1,0:T(8,128)(2,1)S(1)} fusion(bf16[16,128,1024]{2,1,0:T(8,128)(2,1)} %param.6, f32[16]{0:T(128)S(1)} %broadcast_divide_fusion, f32[128,1024]{1,0:T(8,128)S(1)} %convert_element_type.49), kind=kLoop, calls=%fused_computation.11 | loop fusion | flops 8388608 | bytes 8912960 | tf_op jit(solution)/shard_map/convert_element_type | solution.py:71
  20.6 2.0 copy-done.2
  22.6 2.4 collective-permute-start
  25.0 4.6 %collective-permute-start.1 = (bf16[16,8,1024]{2,1,0:T(8,128)(2,1)S(1)}, bf16[16,8,1024]{2,1,0:T(8,128)(2,1)S(1)}, u32[]{:S(2)}, u32[]{:S(2)}) collective-permute-start(bf16[16,8,1024]{2,1,0:T(8,128)(2,1)S(1)} %get-tuple-element.11), channel_id=1, source_target_pairs={{8,0},{16,8},{24,16},{9,1},{17,9},{25,17},{10,2},{18,10},{26,18},{... | collective-permute-start | bytes 786440 | tf_op jit(solution)/shard_map/ppermute | solution.py:18
  29.9 1.5 copy.30
  31.4 5.9 %convert_bitcast_fusion.1 = bf16[4,16,256,272]{2,1,0,3:T(8,128)(2,1)} fusion(s32[256,272]{0,1:T(8,128)S(1)} %iota_subtract_fusion, bf16[4,16,17]{2,1,0:T(8,128)(2,1)S(1)} %copy-done.4), kind=kOutput, calls=%fused_computation.8 | convolution fusion | flops 157159424 | bytes 9193600 | tf_op jit(solution)/shard_map/ijt,kst->ksij/dot_general | solution.py:29
  37.3 3.2 %convert_bitcast_fusion.3 = bf16[4,16,128,144]{3,1,0,2:T(8,128)(2,1)} fusion(pred[128,144,17,1]{1,2,3,0:T(8,128)(4,1)S(1)} %copy.30, bf16[4,16,17]{2,1,0:T(8,128)(2,1)S(1)} %copy-done.5), kind=kOutput, calls=%fused_computation.32 | convolution fusion | flops 41287680 | bytes 2674816 | tf_op jit(solution)/shard_map/ijt,kst->ksij/dot_general | solution.py:29
  40.5 19.1 %convert_bitcast_fusion = bf16[4,16,128,1024]{2,3,0,1:T(8,128)(2,1)} fusion(bf16[16,8,1024]{2,1,0:T(8,128)(2,1)S(1)} %collective-permute-done.1, bf16[16,128,1024]{2,1,0:T(8,128)(2,1)} %copy-done.2, bf16[16,8,1024]{2,1,0:T(8,128)(2,1)S(1)} %collective-permute-done, bf16[4,16,128,144]{3,1,0,2:T(8,128)(2,1)} %convert_bitcast_fusion.3), kind=kOutput, calls=%fused_computation.3 | convolution fusion | flops 2438463488 | bytes 23855104 | tf_op jit(solution)/shard_map/ksij,sjc->ksic/dot_general | solution.py:38
  59.7 15.3 %bitcast_convert_fusion.2 = bf16[16,128,256]{2,1,0:T(8,128)(2,1)S(1)} fusion(bf16[4,16,256,272]{2,1,0,3:T(8,128)(2,1)} %convert_bitcast_fusion.1, bf16[4,16,128,1024]{2,3,0,1:T(8,128)(2,1)} %convert_bitcast_fusion), kind=kOutput, calls=%fused_computation.36 | convolution fusion | flops 1141374976 | bytes 14417920 | tf_op jit(solution)/shard_map/ksrj,ksij->sri/dot_general | solution.py:47
  75.0 12.9 %bitcast_convert_fusion.1 = bf16[16,128,256]{2,1,0:T(8,128)(2,1)S(1)} fusion(bf16[4,16,256,272]{2,1,0,3:T(8,128)(2,1)S(1)} %copy-done.1, bf16[4,16,128,1024]{2,3,0,1:T(8,128)(2,1)} %convert_bitcast_fusion), kind=kOutput, calls=%fused_computation.35 | convolution fusion | flops 1141374976 | bytes 14417920 | tf_op jit(solution)/shard_map/ksrj,ksij->sri/dot_general | solution.py:47
  87.9 12.9 %bitcast_convert_fusion = bf16[16,128,256]{2,1,0:T(8,128)(2,1)S(1)} fusion(bf16[4,16,256,272]{2,1,0,3:T(8,128)(2,1)S(1)} %copy-done.1, bf16[4,16,128,1024]{2,3,0,1:T(8,128)(2,1)} %convert_bitcast_fusion), kind=kOutput, calls=%fused_computation.34 | convolution fusion | flops 1141374976 | bytes 26738688 | tf_op jit(solution)/shard_map/ksrj,ksij->sri/dot_general | solution.py:47
  100.8 13.1 %bitcast_convert_fusion.3 = bf16[16,128,256]{2,1,0:T(8,128)(2,1)S(1)} fusion(bf16[4,16,256,272]{2,1,0,3:T(8,128)(2,1)S(1)} %copy-done.1, bf16[4,16,128,1024]{2,3,0,1:T(8,128)(2,1)} %convert_bitcast_fusion), kind=kOutput, calls=%fused_computation.37 | convolution fusion | flops 1141374976 | bytes 26738688 | tf_op jit(solution)/shard_map/ksrj,ksij->sri/dot_general | solution.py:47
  113.9 2.3 pad_maximum_fusion
  116.2 7.4 %convert_element_type.58 = bf16[16,8,16384]{2,1,0:T(8,128)(2,1)} reshape(bf16[16,128,1024]{2,1,0:T(8,128)(2,1)} %pad_maximum_fusion) | data formatting | bytes 8388608 | tf_op jit(solution)/shard_map/convert_element_type | solution.py:49
  123.6 4.5 %copy.27 = bf16[16,8,16384]{2,0,1:T(8,128)(2,1)S(1)} copy(bf16[16,8,16384]{2,1,0:T(8,128)(2,1)} %convert_element_type.58) | data formatting | bytes 8388608 | tf_op jit(solution)/shard_map/convert_element_type | solution.py:49
  128.1 98.9 %all_to_all.15 = bf16[16,8,16384]{2,0,1:T(8,128)(2,1)S(1)} all-to-all(bf16[16,8,16384]{2,0,1:T(8,128)(2,1)S(1)} %copy.27), channel_id=1, replica_groups=mesh['tile'=4,'cuts'=8] {'cuts'}, dimensions={1} | all-to-all | bytes 8388608 | tf_op jit(solution)/shard_map/all_to_all | solution.py:77
  227.0 1.3 fusion.42
  228.3 2.2 convert_bitcast_fusion.2
  230.6 3.3 %fusion.1 = bf16[128,16384]{0,1:T(8,128)(2,1)} fusion(f32[16384,128]{1,0:T(8,128)S(1)} %fusion.42, bf16[128,16384]{1,0:T(8,128)(2,1)S(1)} %bitcast.51, bf16[128,128]{1,0:T(8,128)(2,1)S(1)} %copy-done.3), kind=kOutput, calls=%fused_computation.2 | convolution fusion | flops 541065216 | bytes 16809984 | tf_op jit(solution)/shard_map/dot_general | solution.py:54
  233.8 6.4 %copy.28 = bf16[128,16384]{1,0:T(8,128)(2,1)} copy(bf16[128,16384]{0,1:T(8,128)(2,1)} %convert_bitcast_fusion.2) | data formatting | bytes 8388608
  240.2 6.4 %copy.29 = bf16[128,16384]{1,0:T(8,128)(2,1)} copy(bf16[128,16384]{0,1:T(8,128)(2,1)} %fusion.1) | data formatting | bytes 8388608
  (19 shorter events, 2.0 us)
Async XLA Ops:
  0.6 226.4 %copy-start = (bf16[128,128]{1,0:T(8,128)(2,1)S(1)}, bf16[128,128]{1,0:T(8,128)(2,1)}, u32[]{:S(2)}) copy-start(bf16[128,128]{1,0:T(8,128)(2,1)} %param.10) | copy-start | bytes 98308
  1.7 29.6 %copy-start.4 = (bf16[4,16,17]{2,1,0:T(8,128)(2,1)S(1)}, bf16[4,16,17]{2,1,0:T(8,128)(2,1)}, u32[]{:S(2)}) copy-start(bf16[4,16,17]{2,1,0:T(8,128)(2,1)} %param.9) | copy-start | bytes 6532
  17.0 20.3 %copy-start.5 = (bf16[4,16,17]{2,1,0:T(8,128)(2,1)S(1)}, bf16[4,16,17]{2,1,0:T(8,128)(2,1)}, u32[]{:S(2)}) copy-start(bf16[4,16,17]{2,1,0:T(8,128)(2,1)} %param.8) | copy-start | bytes 6532
  20.5 2.0 copy-start.2
  22.6 17.9 %collective-permute-start = (bf16[16,8,1024]{2,1,0:T(8,128)(2,1)S(1)}, bf16[16,8,1024]{2,1,0:T(8,128)(2,1)S(1)}, u32[]{:S(2)}, u32[]{:S(2)}) collective-permute-start(bf16[16,8,1024]{2,1,0:T(8,128)(2,1)S(1)} %get-tuple-element.10), channel_id=1, source_target_pairs={{0,8},{8,16},{16,24},{1,9},{9,17},{17,25},{2,10},{10,18},{18,26},{... | collective-permute-start | bytes 786440 | tf_op jit(solution)/shard_map/ppermute | solution.py:17
  25.0 15.5 %collective-permute-start.1 = (bf16[16,8,1024]{2,1,0:T(8,128)(2,1)S(1)}, bf16[16,8,1024]{2,1,0:T(8,128)(2,1)S(1)}, u32[]{:S(2)}, u32[]{:S(2)}) collective-permute-start(bf16[16,8,1024]{2,1,0:T(8,128)(2,1)S(1)} %get-tuple-element.11), channel_id=1, source_target_pairs={{8,0},{16,8},{24,16},{9,1},{17,9},{25,17},{10,2},{18,10},{26,18},{... | collective-permute-start | bytes 786440 | tf_op jit(solution)/shard_map/ppermute | solution.py:18
  59.7 15.3 %copy-start.1 = (bf16[4,16,256,272]{2,1,0,3:T(8,128)(2,1)S(1)}, bf16[4,16,256,272]{2,1,0,3:T(8,128)(2,1)}, u32[]{:S(2)}) copy-start(bf16[4,16,256,272]{2,1,0,3:T(8,128)(2,1)} %convert_bitcast_fusion.1) | copy-start | bytes 26738692
  228.3 2.3 copy-start.3
where the time goes:
time: 250 us; the launch traced here: 247 us
  blocking collectives  108 us (43%)
  matrix products  87 us (35%)
  local copies, waits for them, and re-layouts  28.2 us (11%)
  other arithmetic  15 us (6%)
  starting transfers between devices  7.03 us (3%)
    all_to_all x1, blocking collectives, per_device(): lax.all_to_all(split_flat, 'cuts', split_axis=1, concat_axis=0, tiled=True)  98.9 us
    dot_general x4, matrix products, filter_field(): jnp.einsum('ksrj,ksij->sri', segment, col_band, preferred_element_type=jn...  54.2 us
    dot_general x1, matrix products, filter_field(): jnp.einsum('ksij,sjc->ksic', row_band, padded, preferred_element_type=jnp...  19.1 us
    unnamed x14, local copies, waits for them, and re-layouts  14.8 us
    convert_element_type x2, local copies, waits for them, and re-layouts, filter_field(): return jnp.concatenate(pieces, axis=2).astype(jnp.bfloat16)  11.9 us
    psum x1, blocking collectives, global_background(): totals, counted = lax.psum((local_sums, local_count), 'tile')  9.56 us
    dot_general x2, matrix products, band_matrix(): jnp.einsum('ijt,kst->ksij', choose, taps, preferred_element_type=jnp.floa...  9.15 us
  transfers between devices with their start and end apart: 2, of which 0 were waited for; matrix products, arithmetic and copies ran while one was open for 4% of the time, Pallas kernels for 0%

commit v1 on v0

v1 whole, which is shorter than its diff:
```python
import functools

import jax
import jax.numpy as jnp
from jax import lax
from jax.experimental import pallas as pl
from jax.experimental.pallas import tpu as pltpu
from jax.sharding import PartitionSpec as P

REACH = 8
TAPS = 2 * REACH + 1
LANES = 128
GROUP = 8
VMEM_BYTES = 48 * 1024 * 1024
HALO = 2 * REACH


def params():
    return pltpu.CompilerParams(vmem_limit_bytes=VMEM_BYTES)


def cost(flops, moved):
    return pl.CostEstimate(flops=int(flops), bytes_accessed=int(moved), transcendentals=0)


def matrices_kernel(row_taps, col_taps, col_out, row_out):
    terms, slices, _ = row_taps.shape
    wide = 2 * LANES
    window = LANES + HALO
    tap = lax.broadcasted_iota(jnp.int32, (TAPS, wide), 0)
    lane = lax.broadcasted_iota(jnp.int32, (TAPS, wide), 1)
    flip = (lax.rem(tap + lane, wide) == 0).astype(jnp.bfloat16)
    for k in range(terms):
        base = jnp.dot(col_taps[k], flip, preferred_element_type=jnp.float32)
        for s in range(slices):
            rows = jnp.broadcast_to(base[s : s + 1], (window, wide))
            band = pltpu.roll(rows, 0, 1, stride=1, stride_axis=0)
            col_out[s, :window, k * LANES : (k + 1) * LANES] = band[:, :LANES].astype(jnp.bfloat16)
    for s in range(slices):
        col_out[s, window:, :] = jnp.zeros((wide - window, terms * LANES), jnp.bfloat16)
    high = LANES // terms
    block = high - HALO
    tap = lax.broadcasted_iota(jnp.int32, (TAPS, LANES), 0)
    lane = lax.broadcasted_iota(jnp.int32, (TAPS, LANES), 1)
    base = jnp.zeros((slices, LANES), jnp.float32)
    for k in range(terms):
        place = (lane == tap + k * high).astype(jnp.bfloat16)
        base = base + jnp.dot(row_taps[k], place, preferred_element_type=jnp.float32)
    sub = lax.broadcasted_iota(jnp.int32, (GROUP, LANES), 0)
    for g in range(slices // GROUP):
        own = base[g * GROUP : (g + 1) * GROUP]
        for pair in range(block // 2):
            shifted = [pltpu.roll(own, 2 * pair + h, 1) for h in range(2)]
            for s in range(GROUP):
                both = jnp.concatenate([jnp.where(sub == s, x, 0.0) for x in shifted], axis=0)
                row_out[
                    g, pair * 2 * GROUP : (pair + 1) * 2 * GROUP, s * LANES : (s + 1) * LANES
                ] = both.astype(jnp.bfloat16)


def filter_matrices(row_taps, col_taps):
    terms, slices, _ = row_taps.shape
    block = LANES // terms - HALO
    return pl.pallas_call(
        matrices_kernel,
        name="matrices",
        out_shape=(
            jax.ShapeDtypeStruct((slices, 2 * LANES, terms * LANES), jnp.bfloat16),
            jax.ShapeDtypeStruct((slices // GROUP, block * GROUP, GROUP * LANES), jnp.bfloat16),
        ),
        compiler_params=params(),
        cost_estimate=cost(1e6, 5e6),
    )(row_taps, col_taps)


def sums_kernel(density, valid, out):
    slices, rows, cols = density.shape

    @pl.when(pl.program_id(0) == 0)
    def _():
        out[...] = jnp.zeros_like(out)

    mask = valid[...] != 0
    for s in range(slices + 1):
        if s < slices:
            x = jnp.where(mask, density[s].astype(jnp.float32), 0.0)
        else:
            x = jnp.where(mask, 1.0, 0.0)
        x = x.reshape(rows // 8, 8, cols).sum(axis=0)
        x = sum(x[:, c : c + LANES] for c in range(0, cols, LANES))
        out[s : s + 1, :] += jnp.sum(x, axis=0, keepdims=True)


def masked_sums(density, valid):
    slices, rows, cols = density.shape
    step = 32
    return pl.pallas_call(
        sums_kernel,
        name="sums",
        grid=(rows // step,),
        in_specs=[
            pl.BlockSpec((slices, step, cols), lambda i: (0, i, 0)),
            pl.BlockSpec((step, cols), lambda i: (i, 0)),
        ],
        out_specs=pl.BlockSpec((slices + 8, LANES), lambda i: (0, 0)),
        out_shape=jax.ShapeDtypeStruct((slices + 8, LANES), jnp.float32),
        compiler_params=params(),
        cost_estimate=cost(2 * density.size, 2 * density.size),
    )(density, valid)


def filter_kernel(pieces, ids, *refs):
    (before, now, after, mask_before, mask_now, mask_after, above, below, col, row), refs = refs[:10], refs[10:]
    sums, refs = refs[:4], refs[4:]
    outs, (tall,) = refs[:-1], refs[-1:]
    slices, block, cols = now.shape
    terms = col.shape[2] // LANES
    step = pl.program_id(0)
    blocks = pl.num_programs(0)
    me = ids[step]
    first = me == 0
    last = me == ids[blocks]
    total = sums[0][...] + sums[1][...] + sums[2][...] + sums[3][...]
    total = jnp.sum(total, axis=1, keepdims=True)
    mean = total[:slices] / total[slices : slices + 1]
    halo = block + HALO
    f32 = jnp.float32
    top = jnp.where(first, above[slices].astype(f32), mask_before[REACH:, :].astype(f32))
    bottom = jnp.where(last, below[slices].astype(f32), mask_after[:REACH, :].astype(f32))
    mask = jnp.concatenate([top, mask_now[...].astype(f32), bottom], axis=0)
    parts = []
    for g in range(slices // GROUP):
        for j in range(GROUP):
            s = g * GROUP + j
            top = jnp.where(first, above[s].astype(f32), before[s].astype(f32)[REACH:])
            bottom = jnp.where(last, below[s].astype(f32), after[s].astype(f32)[:REACH])
            x = jnp.concatenate([top, now[s].astype(f32), bottom], axis=0)
            x = mask * (x - mean[s : s + 1, :])
            x = jnp.concatenate([x, jnp.zeros((halo, LANES), f32)], axis=1)
            x = pltpu.roll(x, REACH, 1).astype(jnp.bfloat16)
            x = jnp.concatenate([x[:, c : c + 2 * LANES] for c in range(0, cols, LANES)], axis=0)
            y = jnp.dot(x, col[s], preferred_element_type=f32).astype(jnp.bfloat16)
            for c in range(cols // LANES):
                for k in range(terms):
                    tall[(j * terms + k) * halo : (j * terms + k + 1) * halo, c * LANES : (c + 1) * LANES] = y[
                        c * halo : (c + 1) * halo, k * LANES : (k + 1) * LANES
                    ]
        z = jnp.dot(row[g], tall[...], preferred_element_type=f32)
        parts.append(z.reshape(block, GROUP, cols))
    field = jnp.concatenate(parts, axis=1).astype(jnp.bfloat16)
    count = len(pieces)
    for b in range(len(outs) // count):

        @pl.when(step == b)
        def _():
            for p, (start, stop) in enumerate(pieces):
                outs[b * count + p][...] = field[start:stop]


def filter_blocks(ids, pieces, density, valid, above, below, col, row, sums):
    slices, rows, cols = density.shape
    block = row.shape[1] // GROUP
    last = rows // block - 1
    count = ids.shape[0]
    terms = col.shape[2] // LANES

    def rows_at(shift):
        return lambda i, at: (0, jnp.clip(at[i] + shift, 0, last), 0)

    def mask_at(shift):
        return lambda i, at: (jnp.clip(at[i] + shift, 0, last), 0)

    def whole(x):
        return pl.BlockSpec(x.shape, lambda i, at: (0,) * x.ndim, pipeline_mode=pl.Buffered(1))

    shapes = [(stop - start, slices, cols) for start, stop in pieces] * count
    out = pl.pallas_call(
        functools.partial(filter_kernel, pieces),
        name="filter",
        grid_spec=pltpu.PrefetchScalarGridSpec(
            num_scalar_prefetch=1,
            grid=(count,),
            in_specs=[pl.BlockSpec((slices, block, cols), rows_at(d)) for d in (-1, 0, 1)]
            + [pl.BlockSpec((block, cols), mask_at(d)) for d in (-1, 0, 1)]
            + [whole(x) for x in (above, below, col, row, *sums)],
            out_specs=[pl.BlockSpec(shape, lambda i, at: (0, 0, 0)) for shape in shapes],
            scratch_shapes=[pltpu.VMEM((GROUP * terms * (block + HALO), cols), jnp.bfloat16)],
        ),
        out_shape=[jax.ShapeDtypeStruct(shape, jnp.bfloat16) for shape in shapes],
        compiler_params=params(),
        cost_estimate=cost(count * 2 * slices * 805e6 / 16, count * 3e6),
    )(jnp.concatenate([ids, jnp.full((1,), last, ids.dtype)]), *([density] * 3), *([valid] * 3), above, below, col, row, *sums)
    n = len(pieces)
    return [out[b * n : (b + 1) * n] for b in range(count)]


def project_kernel(count, weights, *refs):
    parts, (amp_out, like_out) = refs[:count], refs[-2:]
    zbins = weights.shape[0] // 2
    pencil = jnp.concatenate([x[0] for x in parts], axis=0)
    both = jnp.dot(weights[...], pencil, preferred_element_type=jnp.float32)
    amp = both[:zbins]
    amp_out[...] = amp.astype(jnp.bfloat16)
    like_out[...] = (amp * both[zbins:]).astype(jnp.bfloat16)


def project(weights, parts, start, total, earlier):
    rows, slices, cols = parts[0].shape
    zbins = weights.shape[0] // 2
    count = len(parts)
    shape = jax.ShapeDtypeStruct((zbins, total * cols), jnp.bfloat16)
    return pl.pallas_call(
        functools.partial(project_kernel, count),
        name="project",
        grid=(rows,),
        in_specs=[pl.BlockSpec(weights.shape, lambda i: (0, 0))]
        + [pl.BlockSpec((1, slices, cols), lambda i: (i, 0, 0))] * count
        + [pl.BlockSpec(memory_space=pl.ANY)] * len(earlier),
        out_specs=[pl.BlockSpec((zbins, cols), lambda i: (0, i + start))] * 2,
        out_shape=[shape, shape],
        input_output_aliases={1 + count + i: i for i in range(len(earlier))},
        compiler_params=params(),
        cost_estimate=cost(4 * zbins * rows * cols * slices * count, 2 * rows * cols * (slices * count + 2 * zbins)),
    )(weights, *parts, *earlier)


def fast(density, valid, row_taps, col_taps, amp_matrix, like_matrix):
    slices, rows, cols = density.shape
    peers = lax.axis_size("cuts")
    tiles = lax.axis_size("tile")
    block = rows // peers
    me = lax.axis_index("cuts")
    mask = valid.astype(jnp.bfloat16)[None]
    first = jnp.concatenate([density[:, :REACH], mask[:, :REACH]], axis=0)
    last = jnp.concatenate([density[:, rows - REACH :], mask[:, rows - REACH :]], axis=0)
    above = lax.ppermute(last, "tile", [(i, i + 1) for i in range(tiles - 1)])
    below = lax.ppermute(first, "tile", [(i + 1, i) for i in range(tiles - 1)])
    own = masked_sums(density, valid)
    sums = [own] + [lax.ppermute(own, "tile", [(i, i ^ k) for i in range(tiles)]) for k in range(1, tiles)]
    col, row = filter_matrices(row_taps, col_taps)

    half = block // 2
    pieces = ((0, half), (half, block))
    early = [4]
    late = [6, 5, 7, 2, 3, 1, 0]
    filtered = {}
    for ks in (early, late):
        ids = jnp.stack([me ^ k for k in ks]).astype(jnp.int32)
        for k, got in zip(ks, filter_blocks(ids, pieces, density, valid, above, below, col, row, sums)):
            filtered[k] = got
    order = [(4, 0), (6, 0), (2, 0), (5, 0), (3, 0), (7, 0), (1, 0), (2, 1), (4, 1), (3, 1), (6, 1), (1, 1), (5, 1), (7, 1)]
    arrived = {(0, p): filtered[0][p] for p in range(len(pieces))}
    for k, p in order:
        arrived[k, p] = lax.ppermute(filtered[k][p], "cuts", [(i, i ^ k) for i in range(peers)])
    weights = jnp.concatenate([amp_matrix, like_matrix], axis=1).T.reshape(-1, peers, slices)
    weights = weights[:, me ^ jnp.arange(peers)].reshape(-1, peers * slices)
    result = []
    for p, (start, _) in enumerate(pieces):
        result = project(weights, [arrived[k, p] for k in range(peers)], start, block, result)
    return tuple(result)


def extended(shard, sides, width):
    for axis, dim in sides:
        size, length = (lax.axis_size(axis), shard.shape[dim])
        up = [(i, (i + 1) % size) for i in range(size - 1)]
        down = [(j, i) for i, j in up]
        last = lax.slice_in_dim(shard, length - width, length, axis=dim)
        initial = lax.slice_in_dim(shard, 0, width, axis=dim)
        before = lax.ppermute(last, axis, up)
        after = lax.ppermute(initial, axis, down)
        shard = jnp.concatenate([before, shard, after], axis=dim)
    return shard


def band_matrix(taps, out_count, in_count):
    offset = lax.broadcasted_iota(jnp.int32, (out_count, in_count), 1) - lax.broadcasted_iota(
        jnp.int32, (out_count, in_count), 0
    )
    positions = lax.broadcasted_iota(jnp.int32, (1, 1, TAPS), 2)
    choose = (offset[:, :, None] == positions).astype(jnp.bfloat16)
    return jnp.einsum("ijt,kst->ksij", choose, taps, preferred_element_type=jnp.float32).astype(jnp.bfloat16)


def filter_field(padded, row_taps, col_taps):
    tall = padded.shape[1]
    cols = padded.shape[2]
    width = 2 * LANES
    row_band = band_matrix(row_taps, tall - HALO, tall)
    rowed = jnp.einsum("ksij,sjc->ksic", row_band, padded, preferred_element_type=jnp.float32).astype(jnp.bfloat16)
    widened = jnp.pad(rowed, ((0, 0), (0, 0), (0, 0), (REACH, REACH)))
    col_band = band_matrix(col_taps, width, width + HALO)
    pieces = []
    for begin in range(0, cols, width):
        segment = widened[:, :, :, begin : begin + width + HALO]
        pieces.append(jnp.einsum("ksrj,ksij->sri", segment, col_band, preferred_element_type=jnp.float32))
    return jnp.concatenate(pieces, axis=2).astype(jnp.bfloat16)


def general(density, valid, row_taps, col_taps, amp_matrix, like_matrix):
    slices, rows, cols = density.shape
    mask = valid.astype(jnp.float32)
    field = density.astype(jnp.float32)
    sums, count = lax.psum((jnp.sum(field * mask[None], axis=(1, 2)), jnp.sum(mask)), "tile")
    masked = (mask[None] * (field - (sums / count)[:, None, None])).astype(jnp.bfloat16)
    filtered = filter_field(extended(masked, (("tile", 1),), REACH), row_taps, col_taps)
    peers = lax.axis_size("cuts")
    share = rows * cols // peers
    pencil = lax.all_to_all(
        filtered.reshape(slices, peers, share), "cuts", split_axis=1, concat_axis=0, tiled=True
    ).reshape(slices * peers, share)
    amp = jnp.dot(amp_matrix.T, pencil, preferred_element_type=jnp.float32)
    like = amp * jnp.dot(like_matrix.T, pencil, preferred_element_type=jnp.float32)
    return amp.astype(jnp.bfloat16), like.astype(jnp.bfloat16)


def per_device(density, valid, row_taps, col_taps, amp_matrix, like_matrix):
    slices, rows, cols = density.shape
    terms = row_taps.shape[0]
    peers = lax.axis_size("cuts")
    fits = (
        peers == 8
        and lax.axis_size("tile") == 4
        and slices == 2 * GROUP
        and terms == 4
        and rows == peers * (LANES // terms - HALO)
        and cols % (2 * LANES) == 0
    )
    run = fast if fits else general
    return run(density, valid, row_taps, col_taps, amp_matrix, like_matrix)


def solution(mesh):
    return jax.shard_map(
        per_device,
        mesh=mesh,
        in_specs=(
            P("cuts", "tile", None),
            P("tile", None),
            P(None, "cuts", None),
            P(None, "cuts", None),
            P(),
            P(),
        ),
        out_specs=(P(None, ("tile", "cuts")), P(None, ("tile", "cuts"))),
        check_vma=False,
    )
```

time: 250 us -> 132 us (0.53)
  the two profiles are of different devices: /device:TPU:4 before, /device:TPU:21 now
where the time goes in v1:
time: 132 us; the launch traced here: 131 us
  waiting for transfers between devices  56.2 us (43%)
  Pallas kernels  40.4 us (31%)
  starting transfers between devices  23.7 us (18%)
  local copies, waits for them, and re-layouts  8.72 us (7%)
    ppermute x14, waiting for transfers between devices, fast(): lax.ppermute(filtered[k][p], 'cuts', [(i, i ^ k) for i in range(peers)])  56.2 us
    pallas_call x2, Pallas kernels, filter_blocks(): pl.pallas_call(functools.partial(filter_kernel, pieces), name='filter', g...  26.8 us
    ppermute x14, starting transfers between devices, fast(): lax.ppermute(filtered[k][p], 'cuts', [(i, i ^ k) for i in range(peers)])  14.8 us
    pallas_call x2, Pallas kernels, project(): pl.pallas_call(functools.partial(project_kernel, count), name='project',...  10.6 us
    unnamed x20, local copies, waits for them, and re-layouts  6.91 us
    ppermute x1, starting transfers between devices, fast(): above = lax.ppermute(last, 'tile', [(i, i + 1) for i in range(tiles - 1)])  3.12 us
    ppermute x1, starting transfers between devices, fast(): below = lax.ppermute(first, 'tile', [(i + 1, i) for i in range(tiles - 1)])  3.06 us
    ppermute x3, starting transfers between devices, fast(): lax.ppermute(own, 'tile', [(i, i ^ k) for i in range(tiles)])  2.71 us
  transfers between devices with their start and end apart: 19, of which 7 were waited for; matrix products, arithmetic and copies ran while one was open for 1% of the time, Pallas kernels for 22%

profile of v1, /device:TPU:21, one launch (start us, length us, event | category | flops | bytes accessed | tf_op | source)
XLA Modules:
  0.0 131.2 jit_solution(16046231380345727563)
XLA Ops:
  2.9 3.1 %collective-permute-start = (bf16[17,8,1024]{2,1,0:T(8,128)(2,1)S(1)}, bf16[17,8,1024]{2,1,0:T(8,128)(2,1)S(1)}, u32[]{:S(2)}, u32[]{:S(2)}) collective-permute-start(bf16[17,8,1024]{2,1,0:T(8,128)(2,1)S(1)} %pad_maximum_fusion), channel_id=1, source_target_pairs={{0,8},{8,16},{16,24},{1,9},{9,17},{17,25},{2,10},{10,18},{18,26},{... | collective-permute-start | bytes 835592 | tf_op jit(solution)/shard_map/ppermute | solution.py:236
  6.1 3.1 %collective-permute-start.1 = (bf16[17,8,1024]{2,1,0:T(8,128)(2,1)S(1)}, bf16[17,8,1024]{2,1,0:T(8,128)(2,1)S(1)}, u32[]{:S(2)}, u32[]{:S(2)}) collective-permute-start(bf16[17,8,1024]{2,1,0:T(8,128)(2,1)S(1)} %pad_maximum_fusion.1), channel_id=1, source_target_pairs={{8,0},{16,8},{24,16},{9,1},{17,9},{25,17},{10,2},{18,10},{26,18},{... | collective-permute-start | bytes 835592 | tf_op jit(solution)/shard_map/ppermute | solution.py:237
  9.2 2.2 %copy-done = bf16[16,128,1024]{2,1,0:T(8,128)(2,1)S(1)} copy-done((bf16[16,128,1024]{2,1,0:T(8,128)(2,1)S(1)}, bf16[16,128,1024]{2,1,0:T(8,128)(2,1)}, u32[]{:S(2)}) %copy-start) | copy-done | bytes 4194328
  12.4 1.5 %sums.1.refs_10_ = f32[24,128]{1,0:T(8,128)S(1)} custom-call(bf16[16,128,1024]{2,1,0:T(8,128)(2,1)S(1)} %copy-done, s32[128,1024]{1,0:T(8,128)S(1)} %copy-done.1), custom_call_target="tpu_custom_call" | custom-call | flops 4194304 | bytes 4194304 | tf_op jit(solution)/shard_map/sums/pallas_call | solution.py:97
  14.2 1.2 collective-permute-start.3
  16.8 1.5 %matrices.1 = (bf16[16,256,512]{2,1,0:T(8,128)(2,1)S(1)}, bf16[2,128,1024]{2,1,0:T(8,128)(2,1)S(1)}) custom-call(bf16[4,16,17]{2,1,0:T(8,128)(2,1)S(1)} %copy-done.6, bf16[4,16,17]{2,1,0:T(8,128)(2,1)S(1)} %copy-done.7), custom_call_target="tpu_custom_call" | custom-call | flops 1000000 | bytes 5000000 | tf_op jit(solution)/shard_map/matrices/pallas_call | solution.py:64
  18.3 2.0 %copy-done.3 = bf16[16,256,512]{2,1,0:T(8,128)(2,1)} copy-done((bf16[16,256,512]{2,1,0:T(8,128)(2,1)}, bf16[16,256,512]{2,1,0:T(8,128)(2,1)S(1)}, u32[]{:S(2)}) %copy-start.3) | copy-done | bytes 4194328
  20.3 5.5 %filter.3 = (bf16[8,16,1024]{2,1,0:T(8,128)(2,1)S(1)}, bf16[8,16,1024]{2,1,0:T(8,128)(2,1)S(1)}) custom-call(s32[2]{0:T(128)S(1)} %pad_add_fusion.ids, bf16[16,128,1024]{2,1,0:T(8,128)(2,1)} %refs_2_.3, bf16[16,128,1024]{2,1,0:T(8,128)(2,1)} %refs_2_.3, bf16[16,128,1024]{2,1,0:T(8,128)(2,1)} %refs_2_.3, s32[128,1024]{1,0:T(8,128)S(1)} %copy-done.2, ...), custom_call_target="tpu_custom_call" | custom-call | flops 1610000000 | bytes 3000000 | tf_op jit(solution)/shard_map/filter/pallas_call | solution.py:177
  26.0 2.3 %collective-permute-start.15 = (bf16[8,16,1024]{2,1,0:T(8,128)(2,1)S(1)}, bf16[8,16,1024]{2,1,0:T(8,128)(2,1)S(1)}, u32[]{:S(2)}, u32[]{:S(2)}) collective-permute-start(bf16[8,16,1024]{2,1,0:T(8,128)(2,1)S(1)} %get-tuple-element.36), channel_id=1, source_target_pairs={{0,4},{1,5},{2,6},{3,7},{4,0},{5,1},{6,2},{7,3},{8,12},{9,13},{10,... | collective-permute-start | bytes 786440 | tf_op jit(solution)/shard_map/ppermute | solution.py:254
  28.3 21.3 %filter.2 = (bf16[8,16,1024]{2,1,0:T(8,128)(2,1)S(1)}, bf16[8,16,1024]{2,1,0:T(8,128)(2,1)}, bf16[8,16,1024]{2,1,0:T(8,128)(2,1)S(1)}, bf16[8,16,1024]{2,1,0:T(8...) custom-call(s32[8]{0:T(128)S(1)} %concatenate.16.ids, ...), custom_call_target="tpu_custom_call" | custom-call | flops 11269999616 | bytes 21000000 | tf_op jit(solution)/shard_map/filter/pallas_call | solution.py:177
  49.6 2.6 %collective-permute-start.5 = (bf16[8,16,1024]{2,1,0:T(8,128)(2,1)S(1)}, bf16[8,16,1024]{2,1,0:T(8,128)(2,1)S(1)}, u32[]{:S(2)}, u32[]{:S(2)}) collective-permute-start(bf16[8,16,1024]{2,1,0:T(8,128)(2,1)S(1)} %get-tuple-element.25), channel_id=1, source_target_pairs={{0,1},{1,0},{2,3},{3,2},{4,5},{5,4},{6,7},{7,6},{8,9},{9,8},{10,11... | collective-permute-start | bytes 786440 | tf_op jit(solution)/shard_map/ppermute | solution.py:254
  52.3 1.3 collective-permute-start.13
  54.4 2.1 %collective-permute-start.17 = (bf16[8,16,1024]{2,1,0:T(8,128)(2,1)S(1)}, bf16[8,16,1024]{2,1,0:T(8,128)(2,1)S(1)}, u32[]{:S(2)}, u32[]{:S(2)}) collective-permute-start(bf16[8,16,1024]{2,1,0:T(8,128)(2,1)S(1)} %get-tuple-element.38), channel_id=1, source_target_pairs={{0,6},{1,7},{2,4},{3,5},{4,2},{5,3},{6,0},{7,1},{8,14},{9,15},{10,... | collective-permute-start | bytes 786440 | tf_op jit(solution)/shard_map/ppermute | solution.py:254
  57.2 7.1 %collective-permute-done.13.refs_2_ = bf16[8,16,1024]{2,1,0:T(8,128)(2,1)S(1)} collective-permute-done((bf16[8,16,1024]{2,1,0:T(8,128)(2,1)S(1)}, bf16[8,16,1024]{2,1,0:T(8,128)(2,1)S(1)}, u32[]{:S(2)}, u32[]{:S(2)}) %collective-permute-start.13) | collective-permute-done | bytes 262176 | tf_op jit(solution)/shard_map/ppermute | solution.py:254
  64.4 2.2 %collective-permute-start.6 = (bf16[8,16,1024]{2,1,0:T(8,128)(2,1)}, bf16[8,16,1024]{2,1,0:T(8,128)(2,1)S(1)}, u32[]{:S(2)}, u32[]{:S(2)}) collective-permute-start(bf16[8,16,1024]{2,1,0:T(8,128)(2,1)} %get-tuple-element.26), channel_id=1, source_target_pairs={{0,2},{1,3},{2,0},{3,1},{4,6},{5,7},{6,4},{7,5},{8,10},{9,11},{10,... | collective-permute-start | bytes 786440 | tf_op jit(solution)/shard_map/ppermute | solution.py:254
  66.6 3.4 %collective-permute-done.14.refs_3_ = bf16[8,16,1024]{2,1,0:T(8,128)(2,1)S(1)} collective-permute-done((bf16[8,16,1024]{2,1,0:T(8,128)(2,1)S(1)}, bf16[8,16,1024]{2,1,0:T(8,128)(2,1)S(1)}, u32[]{:S(2)}, u32[]{:S(2)}) %collective-permute-start.14) | collective-permute-done | bytes 262176 | tf_op jit(solution)/shard_map/ppermute | solution.py:254
  70.0 2.6 %collective-permute-start.7 = (bf16[8,16,1024]{2,1,0:T(8,128)(2,1)}, bf16[8,16,1024]{2,1,0:T(8,128)(2,1)S(1)}, u32[]{:S(2)}, u32[]{:S(2)}) collective-permute-start(bf16[8,16,1024]{2,1,0:T(8,128)(2,1)} %get-tuple-element.27), channel_id=1, source_target_pairs={{0,3},{1,2},{2,1},{3,0},{4,7},{5,6},{6,5},{7,4},{8,11},{9,10},{10,... | collective-permute-start | bytes 786440 | tf_op jit(solution)/shard_map/ppermute | solution.py:254
  72.6 12.3 %collective-permute-done.17.refs_6_ = bf16[8,16,1024]{2,1,0:T(8,128)(2,1)S(1)} collective-permute-done((bf16[8,16,1024]{2,1,0:T(8,128)(2,1)S(1)}, bf16[8,16,1024]{2,1,0:T(8,128)(2,1)S(1)}, u32[]{:S(2)}, u32[]{:S(2)}) %collective-permute-start.17) | collective-permute-done | bytes 262176 | tf_op jit(solution)/shard_map/ppermute | solution.py:254
  84.9 7.5 %collective-permute-done.18.refs_7_ = bf16[8,16,1024]{2,1,0:T(8,128)(2,1)S(1)} collective-permute-done((bf16[8,16,1024]{2,1,0:T(8,128)(2,1)S(1)}, bf16[8,16,1024]{2,1,0:T(8,128)(2,1)S(1)}, u32[]{:S(2)}, u32[]{:S(2)}) %collective-permute-start.18) | collective-permute-done | bytes 262176 | tf_op jit(solution)/shard_map/ppermute | solution.py:254
  94.8 4.4 %project.2 = (bf16[128,16384]{1,0:T(8,128)(2,1)}, bf16[128,16384]{1,0:T(8,128)(2,1)}) custom-call(bf16[256,128]{1,0:T(8,128)(2,1)S(1)} %copy.11.weights, bf16[8,16,1024]{2,1,0:T(8,128)(2,1)S(1)} %get-tuple-element.32.refs_0_, bf16[8,16,1024]{2,1,0:T(8,128)(2,1)S(1)} %collective-permute-done.12.refs_1_, ...), custom_call_target="tpu_custom_call" | custom-call | flops 536870912 | bytes 6291456 | tf_op jit(solution)/shard_map/project/pallas_call | solution.py:212
  99.3 1.5 %collective-permute-done.9.refs_5_ = bf16[8,16,1024]{2,1,0:T(8,128)(2,1)} collective-permute-done((bf16[8,16,1024]{2,1,0:T(8,128)(2,1)}, bf16[8,16,1024]{2,1,0:T(8,128)(2,1)}, u32[]{:S(2)}, u32[]{:S(2)}) %collective-permute-start.9) | collective-permute-done | bytes 262176 | tf_op jit(solution)/shard_map/ppermute | solution.py:254
  100.7 18.0 %collective-permute-done.10.refs_6_ = bf16[8,16,1024]{2,1,0:T(8,128)(2,1)} collective-permute-done((bf16[8,16,1024]{2,1,0:T(8,128)(2,1)}, bf16[8,16,1024]{2,1,0:T(8,128)(2,1)}, u32[]{:S(2)}, u32[]{:S(2)}) %collective-permute-start.10) | collective-permute-done | bytes 262176 | tf_op jit(solution)/shard_map/ppermute | solution.py:254
  118.8 6.3 %collective-permute-done.11.refs_7_ = bf16[8,16,1024]{2,1,0:T(8,128)(2,1)} collective-permute-done((bf16[8,16,1024]{2,1,0:T(8,128)(2,1)}, bf16[8,16,1024]{2,1,0:T(8,128)(2,1)}, u32[]{:S(2)}, u32[]{:S(2)}) %collective-permute-start.11) | collective-permute-done | bytes 262176 | tf_op jit(solution)/shard_map/ppermute | solution.py:254
  125.0 6.2 %project.3 = (bf16[128,16384]{1,0:T(8,128)(2,1)}, bf16[128,16384]{1,0:T(8,128)(2,1)}) custom-call(bf16[256,128]{1,0:T(8,128)(2,1)S(1)} %copy.11.weights, bf16[8,16,1024]{2,1,0:T(8,128)(2,1)S(1)} %get-tuple-element.24.refs_0_, bf16[8,16,1024]{2,1,0:T(8,128)(2,1)S(1)} %collective-permute-done.5.refs_1_, ...), custom_call_target="tpu_custom_call", output_to_operand_aliasing={{0}: (9, {}), {1}: (10, {})} | custom-call | flops 536870912 | bytes 6291456 | tf_op jit(solution)/shard_map/project/pallas_call | solution.py:212
  (52 shorter events, 9.0 us)
Async XLA Ops:
  0.6 19.7 %copy-start.2 = (s32[128,1024]{1,0:T(8,128)S(1)}, s32[128,1024]{1,0:T(8,128)}, u32[]{:S(2)}) copy-start(s32[128,1024]{1,0:T(8,128)} %refs_5_.3) | copy-start | bytes 1572868
  0.6 16.1 %copy-start.7 = (bf16[4,16,17]{2,1,0:T(8,128)(2,1)S(1)}, bf16[4,16,17]{2,1,0:T(8,128)(2,1)}, u32[]{:S(2)}) copy-start(bf16[4,16,17]{2,1,0:T(8,128)(2,1)} %col_taps.1) | copy-start | bytes 6532
  0.7 16.1 %copy-start.6 = (bf16[4,16,17]{2,1,0:T(8,128)(2,1)S(1)}, bf16[4,16,17]{2,1,0:T(8,128)(2,1)}, u32[]{:S(2)}) copy-start(bf16[4,16,17]{2,1,0:T(8,128)(2,1)} %row_taps.1) | copy-start | bytes 6532
  2.9 17.4 %collective-permute-start = (bf16[17,8,1024]{2,1,0:T(8,128)(2,1)S(1)}, bf16[17,8,1024]{2,1,0:T(8,128)(2,1)S(1)}, u32[]{:S(2)}, u32[]{:S(2)}) collective-permute-start(bf16[17,8,1024]{2,1,0:T(8,128)(2,1)S(1)} %pad_maximum_fusion), channel_id=1, source_target_pairs={{0,8},{8,16},{16,24},{1,9},{9,17},{17,25},{2,10},{10,18},{18,26},{... | collective-permute-start | bytes 835592 | tf_op jit(solution)/shard_map/ppermute | solution.py:236
  6.1 14.2 %collective-permute-start.1 = (bf16[17,8,1024]{2,1,0:T(8,128)(2,1)S(1)}, bf16[17,8,1024]{2,1,0:T(8,128)(2,1)S(1)}, u32[]{:S(2)}, u32[]{:S(2)}) collective-permute-start(bf16[17,8,1024]{2,1,0:T(8,128)(2,1)S(1)} %pad_maximum_fusion.1), channel_id=1, source_target_pairs={{8,0},{16,8},{24,16},{9,1},{17,9},{25,17},{10,2},{18,10},{26,18},{... | collective-permute-start | bytes 835592 | tf_op jit(solution)/shard_map/ppermute | solution.py:237
  13.9 6.4 %collective-permute-start.4 = (f32[24,128]{1,0:T(8,128)S(1)}, f32[24,128]{1,0:T(8,128)S(1)}, u32[]{:S(2)}, u32[]{:S(2)}) collective-permute-start(f32[24,128]{1,0:T(8,128)S(1)} %sums.1.refs_10_), channel_id=1, source_target_pairs={{0,24},{8,16},{16,8},{24,0},{1,25},{9,17},{17,9},{25,1},{2,26},{10... | collective-permute-start | bytes 36872 | tf_op jit(solution)/shard_map/ppermute | solution.py:239
  14.2 6.1 %collective-permute-start.3 = (f32[24,128]{1,0:T(8,128)S(1)}, f32[24,128]{1,0:T(8,128)S(1)}, u32[]{:S(2)}, u32[]{:S(2)}) collective-permute-start(f32[24,128]{1,0:T(8,128)S(1)} %sums.1.refs_10_), channel_id=1, source_target_pairs={{0,16},{8,24},{16,0},{24,8},{1,17},{9,25},{17,1},{25,9},{2,18},{10... | collective-permute-start | bytes 36872 | tf_op jit(solution)/shard_map/ppermute | solution.py:239
  15.5 4.8 %collective-permute-start.2 = (f32[24,128]{1,0:T(8,128)S(1)}, f32[24,128]{1,0:T(8,128)S(1)}, u32[]{:S(2)}, u32[]{:S(2)}) collective-permute-start(f32[24,128]{1,0:T(8,128)S(1)} %sums.1.refs_10_), channel_id=1, source_target_pairs={{0,8},{8,0},{16,24},{24,16},{1,9},{9,1},{17,25},{25,17},{2,10},{10... | collective-permute-start | bytes 36872 | tf_op jit(solution)/shard_map/ppermute | solution.py:239
  25.9 27.7 %collective-permute-start.8 = (bf16[8,16,1024]{2,1,0:T(8,128)(2,1)S(1)}, bf16[8,16,1024]{2,1,0:T(8,128)(2,1)S(1)}, u32[]{:S(2)}, u32[]{:S(2)}) collective-permute-start(bf16[8,16,1024]{2,1,0:T(8,128)(2,1)S(1)} %get-tuple-element.28), channel_id=1, source_target_pairs={{0,4},{1,5},{2,6},{3,7},{4,0},{5,1},{6,2},{7,3},{8,12},{9,13},{10,... | collective-permute-start | bytes 786440 | tf_op jit(solution)/shard_map/ppermute | solution.py:254
  26.0 67.1 %copy-start.8 = (bf16[128,128]{1,0:T(8,128)(2,1)S(1)}, bf16[128,128]{1,0:T(8,128)(2,1)}, u32[]{:S(2)}) copy-start(bf16[128,128]{1,0:T(8,128)(2,1)} %param.11) | copy-start | bytes 98308
  26.0 67.2 %copy-start.9 = (bf16[128,128]{1,0:T(8,128)(2,1)S(1)}, bf16[128,128]{1,0:T(8,128)(2,1)}, u32[]{:S(2)}) copy-start(bf16[128,128]{1,0:T(8,128)(2,1)} %param.10) | copy-start | bytes 98308
  26.0 28.4 %collective-permute-start.15 = (bf16[8,16,1024]{2,1,0:T(8,128)(2,1)S(1)}, bf16[8,16,1024]{2,1,0:T(8,128)(2,1)S(1)}, u32[]{:S(2)}, u32[]{:S(2)}) collective-permute-start(bf16[8,16,1024]{2,1,0:T(8,128)(2,1)S(1)} %get-tuple-element.36), channel_id=1, source_target_pairs={{0,4},{1,5},{2,6},{3,7},{4,0},{5,1},{6,2},{7,3},{8,12},{9,13},{10,... | collective-permute-start | bytes 786440 | tf_op jit(solution)/shard_map/ppermute | solution.py:254
  49.6 4.8 %collective-permute-start.5 = (bf16[8,16,1024]{2,1,0:T(8,128)(2,1)S(1)}, bf16[8,16,1024]{2,1,0:T(8,128)(2,1)S(1)}, u32[]{:S(2)}, u32[]{:S(2)}) collective-permute-start(bf16[8,16,1024]{2,1,0:T(8,128)(2,1)S(1)} %get-tuple-element.25), channel_id=1, source_target_pairs={{0,1},{1,0},{2,3},{3,2},{4,5},{5,4},{6,7},{7,6},{8,9},{9,8},{10,11... | collective-permute-start | bytes 786440 | tf_op jit(solution)/shard_map/ppermute | solution.py:254
  52.2 4.3 %collective-permute-start.12 = (bf16[8,16,1024]{2,1,0:T(8,128)(2,1)S(1)}, bf16[8,16,1024]{2,1,0:T(8,128)(2,1)S(1)}, u32[]{:S(2)}, u32[]{:S(2)}) collective-permute-start(bf16[8,16,1024]{2,1,0:T(8,128)(2,1)S(1)} %get-tuple-element.33), channel_id=1, source_target_pairs={{0,1},{1,0},{2,3},{3,2},{4,5},{5,4},{6,7},{7,6},{8,9},{9,8},{10,11... | collective-permute-start | bytes 786440 | tf_op jit(solution)/shard_map/ppermute | solution.py:254
  52.3 12.1 %collective-permute-start.13 = (bf16[8,16,1024]{2,1,0:T(8,128)(2,1)S(1)}, bf16[8,16,1024]{2,1,0:T(8,128)(2,1)S(1)}, u32[]{:S(2)}, u32[]{:S(2)}) collective-permute-start(bf16[8,16,1024]{2,1,0:T(8,128)(2,1)S(1)} %get-tuple-element.34), channel_id=1, source_target_pairs={{0,2},{1,3},{2,0},{3,1},{4,6},{5,7},{6,4},{7,5},{8,10},{9,11},{10,... | collective-permute-start | bytes 786440 | tf_op jit(solution)/shard_map/ppermute | solution.py:254
  53.6 16.4 %collective-permute-start.14 = (bf16[8,16,1024]{2,1,0:T(8,128)(2,1)S(1)}, bf16[8,16,1024]{2,1,0:T(8,128)(2,1)S(1)}, u32[]{:S(2)}, u32[]{:S(2)}) collective-permute-start(bf16[8,16,1024]{2,1,0:T(8,128)(2,1)S(1)} %get-tuple-element.35), channel_id=1, source_target_pairs={{0,3},{1,2},{2,1},{3,0},{4,7},{5,6},{6,5},{7,4},{8,11},{9,10},{10,... | collective-permute-start | bytes 786440 | tf_op jit(solution)/shard_map/ppermute | solution.py:254
  54.4 18.2 %collective-permute-start.16 = (bf16[8,16,1024]{2,1,0:T(8,128)(2,1)S(1)}, bf16[8,16,1024]{2,1,0:T(8,128)(2,1)S(1)}, u32[]{:S(2)}, u32[]{:S(2)}) collective-permute-start(bf16[8,16,1024]{2,1,0:T(8,128)(2,1)S(1)} %get-tuple-element.37), channel_id=1, source_target_pairs={{0,5},{1,4},{2,7},{3,6},{4,1},{5,0},{6,3},{7,2},{8,13},{9,12},{10,... | collective-permute-start | bytes 786440 | tf_op jit(solution)/shard_map/ppermute | solution.py:254
  54.4 30.5 %collective-permute-start.17 = (bf16[8,16,1024]{2,1,0:T(8,128)(2,1)S(1)}, bf16[8,16,1024]{2,1,0:T(8,128)(2,1)S(1)}, u32[]{:S(2)}, u32[]{:S(2)}) collective-permute-start(bf16[8,16,1024]{2,1,0:T(8,128)(2,1)S(1)} %get-tuple-element.38), channel_id=1, source_target_pairs={{0,6},{1,7},{2,4},{3,5},{4,2},{5,3},{6,0},{7,1},{8,14},{9,15},{10,... | collective-permute-start | bytes 786440 | tf_op jit(solution)/shard_map/ppermute | solution.py:254
  56.5 35.9 %collective-permute-start.18 = (bf16[8,16,1024]{2,1,0:T(8,128)(2,1)S(1)}, bf16[8,16,1024]{2,1,0:T(8,128)(2,1)S(1)}, u32[]{:S(2)}, u32[]{:S(2)}) collective-permute-start(bf16[8,16,1024]{2,1,0:T(8,128)(2,1)S(1)} %get-tuple-element.39), channel_id=1, source_target_pairs={{0,7},{1,6},{2,5},{3,4},{4,3},{5,2},{6,1},{7,0},{8,15},{9,14},{10,... | collective-permute-start | bytes 786440 | tf_op jit(solution)/shard_map/ppermute | solution.py:254
  64.4 34.9 %collective-permute-start.6 = (bf16[8,16,1024]{2,1,0:T(8,128)(2,1)}, bf16[8,16,1024]{2,1,0:T(8,128)(2,1)S(1)}, u32[]{:S(2)}, u32[]{:S(2)}) collective-permute-start(bf16[8,16,1024]{2,1,0:T(8,128)(2,1)} %get-tuple-element.26), channel_id=1, source_target_pairs={{0,2},{1,3},{2,0},{3,1},{4,6},{5,7},{6,4},{7,5},{8,10},{9,11},{10,... | collective-permute-start | bytes 786440 | tf_op jit(solution)/shard_map/ppermute | solution.py:254
  70.0 29.3 %collective-permute-start.7 = (bf16[8,16,1024]{2,1,0:T(8,128)(2,1)}, bf16[8,16,1024]{2,1,0:T(8,128)(2,1)S(1)}, u32[]{:S(2)}, u32[]{:S(2)}) collective-permute-start(bf16[8,16,1024]{2,1,0:T(8,128)(2,1)} %get-tuple-element.27), channel_id=1, source_target_pairs={{0,3},{1,2},{2,1},{3,0},{4,7},{5,6},{6,5},{7,4},{8,11},{9,10},{10,... | collective-permute-start | bytes 786440 | tf_op jit(solution)/shard_map/ppermute | solution.py:254
  72.6 28.1 %collective-permute-start.9 = (bf16[8,16,1024]{2,1,0:T(8,128)(2,1)}, bf16[8,16,1024]{2,1,0:T(8,128)(2,1)}, u32[]{:S(2)}, u32[]{:S(2)}) collective-permute-start(bf16[8,16,1024]{2,1,0:T(8,128)(2,1)} %get-tuple-element.29), channel_id=1, source_target_pairs={{0,5},{1,4},{2,7},{3,6},{4,1},{5,0},{6,3},{7,2},{8,13},{9,12},{10,... | collective-permute-start | bytes 786440 | tf_op jit(solution)/shard_map/ppermute | solution.py:254
  84.9 33.8 %collective-permute-start.10 = (bf16[8,16,1024]{2,1,0:T(8,128)(2,1)}, bf16[8,16,1024]{2,1,0:T(8,128)(2,1)}, u32[]{:S(2)}, u32[]{:S(2)}) collective-permute-start(bf16[8,16,1024]{2,1,0:T(8,128)(2,1)} %get-tuple-element.30), channel_id=1, source_target_pairs={{0,6},{1,7},{2,4},{3,5},{4,2},{5,3},{6,0},{7,1},{8,14},{9,15},{10,... | collective-permute-start | bytes 786440 | tf_op jit(solution)/shard_map/ppermute | solution.py:254
  93.1 31.9 %collective-permute-start.11 = (bf16[8,16,1024]{2,1,0:T(8,128)(2,1)}, bf16[8,16,1024]{2,1,0:T(8,128)(2,1)}, u32[]{:S(2)}, u32[]{:S(2)}) collective-permute-start(bf16[8,16,1024]{2,1,0:T(8,128)(2,1)} %get-tuple-element.31), channel_id=1, source_target_pairs={{0,7},{1,6},{2,5},{3,4},{4,3},{5,2},{6,1},{7,0},{8,15},{9,14},{10,... | collective-permute-start | bytes 786440 | tf_op jit(solution)/shard_map/ppermute | solution.py:254
  (5 other events, 6.9 us)

commit v2 on v1

v2 whole, which is shorter than its diff:
```python
import functools

import jax
import jax.numpy as jnp
from jax import lax
from jax.experimental import pallas as pl
from jax.experimental.pallas import tpu as pltpu
from jax.sharding import PartitionSpec as P

REACH = 8
TAPS = 2 * REACH + 1
LANES = 128
GROUP = 8
VMEM_BYTES = 48 * 1024 * 1024
HALO = 2 * REACH


def params():
    return pltpu.CompilerParams(vmem_limit_bytes=VMEM_BYTES)


def cost(flops, moved):
    return pl.CostEstimate(flops=int(flops), bytes_accessed=int(moved), transcendentals=0)


def build_matrices(row_taps, col_taps, col_out, row_out):
    terms, slices, _ = row_taps.shape
    wide = 2 * LANES
    window = LANES + HALO
    tap = lax.broadcasted_iota(jnp.int32, (TAPS, wide), 0)
    lane = lax.broadcasted_iota(jnp.int32, (TAPS, wide), 1)
    flip = (lax.rem(tap + lane, wide) == 0).astype(jnp.bfloat16)
    for k in range(terms):
        base = jnp.dot(col_taps[k], flip, preferred_element_type=jnp.float32)
        for s in range(slices):
            rows = jnp.broadcast_to(base[s : s + 1], (window, wide))
            band = pltpu.roll(rows, 0, 1, stride=1, stride_axis=0)
            col_out[s, :window, k * LANES : (k + 1) * LANES] = band[:, :LANES].astype(jnp.bfloat16)
    for s in range(slices):
        col_out[s, window:, :] = jnp.zeros((wide - window, terms * LANES), jnp.bfloat16)
    high = LANES // terms
    tap = lax.broadcasted_iota(jnp.int32, (TAPS, LANES), 0)
    lane = lax.broadcasted_iota(jnp.int32, (TAPS, LANES), 1)
    base = jnp.zeros((slices, LANES), jnp.float32)
    for k in range(terms):
        place = (lane == tap + k * high).astype(jnp.bfloat16)
        base = base + jnp.dot(row_taps[k], place, preferred_element_type=jnp.float32)
    sub = lax.broadcasted_iota(jnp.int32, (GROUP, LANES), 0)
    for g in range(slices // GROUP):
        own = base[g * GROUP : (g + 1) * GROUP]
        for pair in range(row_out.shape[1] // (2 * GROUP)):
            shifted = [pltpu.roll(own, 2 * pair + h, 1) for h in range(2)]
            for s in range(GROUP):
                both = jnp.concatenate([jnp.where(sub == s, x, 0.0) for x in shifted], axis=0)
                row_out[
                    g, pair * 2 * GROUP : (pair + 1) * 2 * GROUP, s * LANES : (s + 1) * LANES
                ] = both.astype(jnp.bfloat16)


def matrix_shapes(terms, slices, rows):
    return (slices, 2 * LANES, terms * LANES), (slices // GROUP, rows * GROUP, GROUP * LANES)


def matrices_kernel(row_taps, col_taps, after, col_out, row_out):
    build_matrices(row_taps, col_taps, col_out, row_out)


def filter_matrices(row_taps, col_taps, after):
    terms, slices, _ = row_taps.shape
    shapes = matrix_shapes(terms, slices, LANES // terms - HALO)
    vmem = pl.BlockSpec(memory_space=pltpu.VMEM)
    return pl.pallas_call(
        matrices_kernel,
        name="matrices",
        in_specs=[vmem, vmem, pl.BlockSpec(memory_space=pl.ANY)],
        out_shape=[jax.ShapeDtypeStruct(shape, jnp.bfloat16) for shape in shapes],
        compiler_params=params(),
        cost_estimate=cost(1e6, 5e6),
    )(row_taps, col_taps, after)


def convolve(field, col, row, tall, rows):
    slices, _, wide = col.shape
    terms = wide // LANES
    high, cols = LANES // terms, tall.shape[1]
    parts = []
    for g in range(slices // GROUP):
        for j in range(GROUP):
            s = g * GROUP + j
            x = jnp.concatenate([field(s), jnp.zeros((high, LANES), jnp.float32)], axis=1)
            x = pltpu.roll(x, REACH, 1).astype(jnp.bfloat16)
            x = jnp.concatenate([x[:, c : c + 2 * LANES] for c in range(0, cols, LANES)], axis=0)
            y = jnp.dot(x, col[s], preferred_element_type=jnp.float32).astype(jnp.bfloat16)
            for c in range(cols // LANES):
                for k in range(terms):
                    tall[(j * terms + k) * high : (j * terms + k + 1) * high, c * LANES : (c + 1) * LANES] = y[
                        c * high : (c + 1) * high, k * LANES : (k + 1) * LANES
                    ]
        z = jnp.dot(row[g, : rows * GROUP], tall[...], preferred_element_type=jnp.float32)
        parts.append(z.reshape(rows, GROUP, cols))
    return jnp.concatenate(parts, axis=1)


def inner_rows(first, second, last):
    both = jnp.concatenate([first.astype(jnp.float32), second.astype(jnp.float32)], axis=0)
    rows = both.shape[0] - REACH
    chosen = jnp.where(last, both[REACH:], both[:rows])
    return jnp.concatenate([chosen, jnp.zeros((REACH, both.shape[1]), jnp.float32)], axis=0)


def early_kernel(ids, one, two, mask_one, mask_two, row_taps, col_taps, after, out, centre, col, row, tall):
    slices = one.shape[0]
    build_matrices(row_taps, col_taps, col, row)
    last = ids[0] == ids[1]
    mask = inner_rows(mask_one[...], mask_two[...], last)

    def folded(x):
        x = x.reshape(x.shape[0] // 8, 8, x.shape[1]).sum(axis=0)
        x = sum(x[:, c : c + LANES] for c in range(0, x.shape[1], LANES))
        return jnp.sum(x, axis=0, keepdims=True)

    sums = jnp.concatenate([folded(mask * inner_rows(one[s], two[s], last)) for s in range(slices)], axis=0)
    mean = jnp.sum(sums, axis=1, keepdims=True) / jnp.sum(folded(mask), axis=1, keepdims=True)
    centre[...] = jnp.broadcast_to(mean, centre.shape)
    field = convolve(
        lambda s: mask * (inner_rows(one[s], two[s], last) - mean[s : s + 1]), col, row, tall, out.shape[0]
    )
    out[...] = field.astype(jnp.bfloat16)


def mend_kernel(ids, mask_one, mask_two, row_taps, col_taps, piece, delta, after, out, col, row, tall):
    build_matrices(row_taps, col_taps, col, row)
    last = ids[0] == ids[1]
    mask = inner_rows(mask_one[...], mask_two[...], last)
    field = convolve(lambda s: mask, col, row, tall, out.shape[0])
    shift = jnp.broadcast_to(delta[:, :1], field.shape[1:])
    out[...] = (piece[...].astype(jnp.float32) + shift[None] * field).astype(jnp.bfloat16)


def early_call(kernel, name, ids, density, valid, row_taps, col_taps, extra, after, out_shape):
    terms, slices, _ = row_taps.shape
    cols = valid.shape[1]
    block = LANES // terms - HALO
    last = valid.shape[0] // block - 1

    def at(shift):
        return lambda i, ids: jnp.minimum(ids[0], last - 1) + shift

    def whole(x):
        return pl.BlockSpec(x.shape, lambda i, ids: (0,) * x.ndim)

    cubes = [] if density is None else [density] * 2
    shapes = matrix_shapes(terms, slices, REACH)
    return pl.pallas_call(
        kernel,
        name=name,
        grid_spec=pltpu.PrefetchScalarGridSpec(
            num_scalar_prefetch=1,
            grid=(1,),
            in_specs=[
                pl.BlockSpec((slices, block, cols), lambda i, ids, f=at(d): (0, f(i, ids), 0)) for d in range(len(cubes))
            ]
            + [pl.BlockSpec((block, cols), lambda i, ids, f=at(d): (f(i, ids), 0)) for d in (0, 1)]
            + [whole(x) for x in (row_taps, col_taps, *extra)]
            + [pl.BlockSpec(memory_space=pl.ANY)],
            out_specs=[whole(x) for x in out_shape],
            scratch_shapes=[pltpu.VMEM(shape, jnp.bfloat16) for shape in shapes]
            + [pltpu.VMEM((GROUP * LANES, cols), jnp.bfloat16)],
        ),
        out_shape=out_shape,
        compiler_params=params(),
        cost_estimate=cost(3e9, 3e6),
    )(jnp.stack([ids, jnp.full_like(ids, last)]).astype(jnp.int32), *cubes, valid, valid, row_taps, col_taps, *extra, after)


def sums_kernel(density, valid, after, out, first, last):
    slices, rows, cols = density.shape
    step = pl.program_id(0)

    @pl.when(step == 0)
    def _():
        out[...] = jnp.zeros_like(out)
        first[:slices] = density[:, :REACH]
        first[slices] = valid[:REACH].astype(jnp.bfloat16)

    @pl.when(step == pl.num_programs(0) - 1)
    def _():
        last[:slices] = density[:, rows - REACH :]
        last[slices] = valid[rows - REACH :].astype(jnp.bfloat16)

    mask = valid[...] != 0
    for s in range(slices + 1):
        if s < slices:
            x = jnp.where(mask, density[s].astype(jnp.float32), 0.0)
        else:
            x = jnp.where(mask, 1.0, 0.0)
        x = x.reshape(rows // 8, 8, cols).sum(axis=0)
        x = sum(x[:, c : c + LANES] for c in range(0, cols, LANES))
        out[s : s + 1, :] += jnp.sum(x, axis=0, keepdims=True)


def masked_sums(density, valid, after):
    slices, rows, cols = density.shape
    step = 32
    edge = jax.ShapeDtypeStruct((slices + 1, REACH, cols), jnp.bfloat16)
    return pl.pallas_call(
        sums_kernel,
        name="sums",
        grid=(rows // step,),
        in_specs=[
            pl.BlockSpec((slices, step, cols), lambda i: (0, i, 0)),
            pl.BlockSpec((step, cols), lambda i: (i, 0)),
            pl.BlockSpec(memory_space=pl.ANY),
        ],
        out_specs=[pl.BlockSpec((slices + 8, LANES), lambda i: (0, 0))]
        + [pl.BlockSpec(edge.shape, lambda i: (0, 0, 0))] * 2,
        out_shape=[jax.ShapeDtypeStruct((slices + 8, LANES), jnp.float32), edge, edge],
        compiler_params=params(),
        cost_estimate=cost(2 * density.size, 2 * density.size),
    )(density, valid, after)


def mean_kernel(*refs):
    sums, centres, out, shifts = refs[:4], refs[4:6], refs[6], refs[7:]
    slices = out.shape[0]
    total = sums[0][...] + sums[1][...] + sums[2][...] + sums[3][...]
    total = jnp.sum(total, axis=1, keepdims=True)
    mean = jnp.broadcast_to(total[:slices] / total[slices : slices + 1], out.shape)
    out[...] = mean
    for centre, shift in zip(centres, shifts):
        shift[...] = centre[...] - mean


def means(sums, centres):
    shape = jax.ShapeDtypeStruct(centres[0].shape, jnp.float32)
    return pl.pallas_call(
        mean_kernel, name="means", out_shape=[shape] * 3, compiler_params=params(), cost_estimate=cost(1e4, 1e5)
    )(*sums, *centres)


def filter_kernel(pieces, ids, before, now, after, mask_before, mask_now, mask_after, *refs):
    (above, below, col, row, mean), outs, (tall, done) = refs[:5], refs[6:-2], refs[-2:]
    slices, block, cols = now.shape
    step = pl.program_id(0)
    first = ids[step] == 0
    last = ids[step] == ids[pl.num_programs(0)]
    f32 = jnp.float32
    top = jnp.where(first, above[slices].astype(f32), mask_before[REACH:, :].astype(f32))
    bottom = jnp.where(last, below[slices].astype(f32), mask_after[:REACH, :].astype(f32))
    mask = jnp.concatenate([top, mask_now[...].astype(f32), bottom], axis=0)

    def field(s):
        top = jnp.where(first, above[s].astype(f32), before[s].astype(f32)[REACH:])
        bottom = jnp.where(last, below[s].astype(f32), after[s].astype(f32)[:REACH])
        x = jnp.concatenate([top, now[s].astype(f32), bottom], axis=0)
        return mask * (x - mean[s : s + 1, :1])

    done[...] = convolve(field, col, row, tall, block).astype(jnp.bfloat16)
    at = 0
    for b, wanted in enumerate(pieces):

        @pl.when(step == b)
        def _():
            for p, (inner, start, stop) in enumerate(wanted):
                here = jnp.where(last != (inner == 1), block - REACH, 0) + start
                outs[at + p][...] = done[pl.ds(here, stop - start)]

        at += len(wanted)


def filter_blocks(ids, pieces, density, valid, above, below, col, row, mean, after):
    slices, rows, cols = density.shape
    block = row.shape[1] // GROUP
    last = rows // block - 1
    count = ids.shape[0]

    def rows_at(shift):
        return lambda i, at: (0, jnp.clip(at[i] + shift, 0, last), 0)

    def mask_at(shift):
        return lambda i, at: (jnp.clip(at[i] + shift, 0, last), 0)

    def whole(x):
        return pl.BlockSpec(x.shape, lambda i, at: (0,) * x.ndim, pipeline_mode=pl.Buffered(1))

    shapes = [(stop - start, slices, cols) for wanted in pieces for _, start, stop in wanted]
    out = pl.pallas_call(
        functools.partial(filter_kernel, pieces),
        name="filter",
        grid_spec=pltpu.PrefetchScalarGridSpec(
            num_scalar_prefetch=1,
            grid=(count,),
            in_specs=[pl.BlockSpec((slices, block, cols), rows_at(d)) for d in (-1, 0, 1)]
            + [pl.BlockSpec((block, cols), mask_at(d)) for d in (-1, 0, 1)]
            + [whole(x) for x in (above, below, col, row, mean)]
            + [pl.BlockSpec(memory_space=pl.ANY)],
            out_specs=[pl.BlockSpec(shape, lambda i, at: (0, 0, 0)) for shape in shapes],
            scratch_shapes=[
                pltpu.VMEM((GROUP * LANES, cols), jnp.bfloat16),
                pltpu.VMEM((block, slices, cols), jnp.bfloat16),
            ],
        ),
        out_shape=[jax.ShapeDtypeStruct(shape, jnp.bfloat16) for shape in shapes],
        compiler_params=params(),
        cost_estimate=cost(count * 2 * 805e6, count * 3e6),
    )(
        jnp.concatenate([ids, jnp.full((1,), last, ids.dtype)]),
        *([density] * 3),
        *([valid] * 3),
        above,
        below,
        col,
        row,
        mean,
        after,
    )
    out = list(out)
    return [[out.pop(0) for _ in wanted] for wanted in pieces]


def project_kernel(count, place, weights, *refs):
    parts, (amp_out, like_out) = refs[:count], refs[-2:]
    zbins = weights.shape[0] // 2
    pencil = jnp.concatenate([x[0] for x in parts], axis=0)
    both = jnp.dot(weights[...], pencil, preferred_element_type=jnp.float32)
    amp = both[:zbins]
    amp_out[...] = amp.astype(jnp.bfloat16)
    like_out[...] = (amp * both[zbins:]).astype(jnp.bfloat16)


def project(place, weights, parts, total, earlier):
    rows, slices, cols = parts[0].shape
    zbins = weights.shape[0] // 2
    count = len(parts)
    shape = jax.ShapeDtypeStruct((zbins, total * cols), jnp.bfloat16)
    return pl.pallas_call(
        functools.partial(project_kernel, count),
        name="project",
        grid_spec=pltpu.PrefetchScalarGridSpec(
            num_scalar_prefetch=1,
            grid=(rows,),
            in_specs=[pl.BlockSpec(weights.shape, lambda i, at: (0, 0))]
            + [pl.BlockSpec((1, slices, cols), lambda i, at: (i, 0, 0))] * count
            + [pl.BlockSpec(memory_space=pl.ANY)] * len(earlier),
            out_specs=[pl.BlockSpec((zbins, cols), lambda i, at: (0, i + at[0]))] * 2,
        ),
        out_shape=[shape, shape],
        input_output_aliases={2 + count + i: i for i in range(len(earlier))},
        compiler_params=params(),
        cost_estimate=cost(4 * zbins * rows * cols * slices * count, 2 * rows * cols * (slices * count + 2 * zbins)),
    )(place.reshape(1), weights, *parts, *earlier)


EARLY = (4, 6)
PIECES = ((1, 0, REACH), (0, 0, 5), (0, 5, REACH))


def fast(density, valid, row_taps, col_taps, amp_matrix, like_matrix):
    slices, rows, cols = density.shape
    terms = row_taps.shape[0]
    peers = lax.axis_size("cuts")
    tiles = lax.axis_size("tile")
    block = rows // peers
    me = lax.axis_index("cuts").astype(jnp.int32)

    def swap(x, k):
        return lax.ppermute(x, "cuts", [(i, i ^ k) for i in range(peers)])

    piece = jax.ShapeDtypeStruct((REACH, slices, cols), jnp.bfloat16)
    centre = jax.ShapeDtypeStruct((slices, LANES), jnp.float32)
    early, centres, after = [], [], row_taps
    for k in EARLY:
        made, about = early_call(
            early_kernel, "early", me ^ k, density, valid, row_taps, col_taps, (), after, [piece, centre]
        )
        early.append(made)
        centres.append(about)
        after = made
    own, first, last = masked_sums(density, valid, after)
    sums = [own] + [lax.ppermute(own, "tile", [(i, i ^ k) for i in range(tiles)]) for k in range(1, tiles)]
    above = lax.ppermute(last, "tile", [(i, i + 1) for i in range(tiles - 1)])
    below = lax.ppermute(first, "tile", [(i + 1, i) for i in range(tiles - 1)])
    col, row = filter_matrices(row_taps, col_taps, own)
    mean, *shifts = means(sums, centres)

    filtered = {}
    after = mean
    for ks in ((5,), (7, 4, 6, 2, 3, 1, 0)):
        ids = jnp.stack([me ^ k for k in ks])
        pieces = [PIECES[1:] if k in EARLY else PIECES for k in ks]
        got = filter_blocks(ids, pieces, density, valid, above, below, col, row, mean, after)
        after = got[0][0]
        for k, made in zip(ks, got):
            for p, x in zip(range(len(PIECES) - len(made), len(PIECES)), made):
                filtered[k, p] = x
    taps = jnp.stack([row_taps, col_taps])
    arrived = {}
    for k, made, shift in zip(EARLY, early, shifts):
        got_taps, got_shift, got = swap(taps, k), swap(shift, k), swap(made, k)
        (arrived[k, 0],) = early_call(
            mend_kernel, "mend", me, None, valid, got_taps[0], got_taps[1], (got, got_shift), after, [piece]
        )
    for p in range(len(PIECES)):
        for k in (5, 7, 4, 6, 2, 3, 1):
            if (k, p) not in arrived:
                arrived[k, p] = swap(filtered[k, p], k)
        arrived[0, p] = filtered[0, p]
    weights = jnp.concatenate([amp_matrix, like_matrix], axis=1).T.reshape(-1, peers, slices)
    weights = weights[:, me ^ jnp.arange(peers)].reshape(-1, peers * slices)
    result = []
    for p, (inner, start, _) in enumerate(PIECES):
        place = jnp.where((me == peers - 1) != (inner == 1), block - REACH, 0) + start
        result = project(place, weights, [arrived[k, p] for k in range(peers)], block, result)
    return tuple(result)


def extended(shard, sides, width):
    for axis, dim in sides:
        size, length = (lax.axis_size(axis), shard.shape[dim])
        up = [(i, (i + 1) % size) for i in range(size - 1)]
        down = [(j, i) for i, j in up]
        last = lax.slice_in_dim(shard, length - width, length, axis=dim)
        initial = lax.slice_in_dim(shard, 0, width, axis=dim)
        before = lax.ppermute(last, axis, up)
        after = lax.ppermute(initial, axis, down)
        shard = jnp.concatenate([before, shard, after], axis=dim)
    return shard


def band_matrix(taps, out_count, in_count):
    offset = lax.broadcasted_iota(jnp.int32, (out_count, in_count), 1) - lax.broadcasted_iota(
        jnp.int32, (out_count, in_count), 0
    )
    positions = lax.broadcasted_iota(jnp.int32, (1, 1, TAPS), 2)
    choose = (offset[:, :, None] == positions).astype(jnp.bfloat16)
    return jnp.einsum("ijt,kst->ksij", choose, taps, preferred_element_type=jnp.float32).astype(jnp.bfloat16)


def filter_field(padded, row_taps, col_taps):
    tall = padded.shape[1]
    cols = padded.shape[2]
    width = 2 * LANES
    row_band = band_matrix(row_taps, tall - HALO, tall)
    rowed = jnp.einsum("ksij,sjc->ksic", row_band, padded, preferred_element_type=jnp.float32).astype(jnp.bfloat16)
    widened = jnp.pad(rowed, ((0, 0), (0, 0), (0, 0), (REACH, REACH)))
    col_band = band_matrix(col_taps, width, width + HALO)
    pieces = []
    for begin in range(0, cols, width):
        segment = widened[:, :, :, begin : begin + width + HALO]
        pieces.append(jnp.einsum("ksrj,ksij->sri", segment, col_band, preferred_element_type=jnp.float32))
    return jnp.concatenate(pieces, axis=2).astype(jnp.bfloat16)


def general(density, valid, row_taps, col_taps, amp_matrix, like_matrix):
    slices, rows, cols = density.shape
    mask = valid.astype(jnp.float32)
    field = density.astype(jnp.float32)
    sums, count = lax.psum((jnp.sum(field * mask[None], axis=(1, 2)), jnp.sum(mask)), "tile")
    masked = (mask[None] * (field - (sums / count)[:, None, None])).astype(jnp.bfloat16)
    filtered = filter_field(extended(masked, (("tile", 1),), REACH), row_taps, col_taps)
    peers = lax.axis_size("cuts")
    share = rows * cols // peers
    pencil = lax.all_to_all(
        filtered.reshape(slices, peers, share), "cuts", split_axis=1, concat_axis=0, tiled=True
    ).reshape(slices * peers, share)
    amp = jnp.dot(amp_matrix.T, pencil, preferred_element_type=jnp.float32)
    like = amp * jnp.dot(like_matrix.T, pencil, preferred_element_type=jnp.float32)
    return amp.astype(jnp.bfloat16), like.astype(jnp.bfloat16)


def per_device(density, valid, row_taps, col_taps, amp_matrix, like_matrix):
    slices, rows, cols = density.shape
    terms = row_taps.shape[0]
    peers = lax.axis_size("cuts")
    fits = (
        peers == 8
        and lax.axis_size("tile") == 4
        and slices == 2 * GROUP
        and terms == 4
        and rows == peers * (LANES // terms - HALO)
        and cols % (2 * LANES) == 0
    )
    run = fast if fits else general
    return run(density, valid, row_taps, col_taps, amp_matrix, like_matrix)


def solution(mesh):
    return jax.shard_map(
        per_device,
        mesh=mesh,
        in_specs=(
            P("cuts", "tile", None),
            P("tile", None),
            P(None, "cuts", None),
            P(None, "cuts", None),
            P(),
            P(),
        ),
        out_specs=(P(None, ("tile", "cuts")), P(None, ("tile", "cuts"))),
        check_vma=False,
    )
```

time: 132 us -> 163 us (1.23)
  the two profiles are of different devices: /device:TPU:21 before, /device:TPU:0 now
where the time goes in v2:
time: 163 us; the launch traced here: 161 us
  starting transfers between devices  60.3 us (37%)
  Pallas kernels  52.6 us (32%)
  waiting for transfers between devices  39.5 us (24%)
  local copies, waits for them, and re-layouts  7.45 us (5%)
    ppermute x25, starting transfers between devices, swap(): return lax.ppermute(x, 'cuts', [(i, i ^ k) for i in range(peers)])  50.6 us
    ppermute x25, waiting for transfers between devices, swap(): return lax.ppermute(x, 'cuts', [(i, i ^ k) for i in range(peers)])  39 us
    pallas_call x2, Pallas kernels, filter_blocks(): pl.pallas_call(functools.partial(filter_kernel, pieces), name='filter', g...  25.7 us
    pallas_call x4, Pallas kernels, early_call(): pl.pallas_call(kernel, name=name, grid_spec=pltpu.PrefetchScalarGridSpec(...  14 us
    pallas_call x3, Pallas kernels, project(): pl.pallas_call(functools.partial(project_kernel, count), name='project',...  9.78 us
    unnamed x22, local copies, waits for them, and re-layouts  6.7 us
    ppermute x3, starting transfers between devices, fast(): lax.ppermute(own, 'tile', [(i, i ^ k) for i in range(tiles)])  4.54 us
    ppermute x1, starting transfers between devices, fast(): above = lax.ppermute(last, 'tile', [(i, i + 1) for i in range(tiles - 1)])  3.86 us
  transfers between devices with their start and end apart: 30, of which 7 were waited for; matrix products, arithmetic and copies ran while one was open for 1% of the time, Pallas kernels for 26%

profile of v2, /device:TPU:0, one launch (start us, length us, event | category | flops | bytes accessed | tf_op | source)
XLA Modules:
  0.0 161.0 jit_solution(4984224213592220864)
XLA Ops:
  0.7 2.2 %copy-done = bf16[16,128,1024]{2,1,0:T(8,128)(2,1)S(1)} copy-done((bf16[16,128,1024]{2,1,0:T(8,128)(2,1)S(1)}, bf16[16,128,1024]{2,1,0:T(8,128)(2,1)}, u32[]{:S(2)}) %copy-start) | copy-done | bytes 4194328
  5.4 3.8 %early.2 = (bf16[8,16,1024]{2,1,0:T(8,128)(2,1)S(1)}, f32[16,128]{1,0:T(8,128)S(1)}) custom-call(s32[2]{0:T(128)S(1)} %get-tuple-element.82.ids, bf16[16,128,1024]{2,1,0:T(8,128)(2,1)S(1)} %copy-done, bf16[16,128,1024]{2,1,0:T(8,128)(2,1)S(1)} %copy-done, s32[128,1024]{1,0:T(8,128)S(1)} %copy-done.2, s32[128,1024]{1,0:T(8,128)S(1)} %copy-done.2, ...), custom_call_target="tpu_custom_call" | custom-call | flops 3000000000 | bytes 3000000 | tf_op jit(solution)/shard_map/early/pallas_call | solution.py:154
  9.3 3.8 %early.3 = (bf16[8,16,1024]{2,1,0:T(8,128)(2,1)S(1)}, f32[16,128]{1,0:T(8,128)S(1)}) custom-call(s32[2]{0:T(128)S(1)} %get-tuple-element.83.ids, bf16[16,128,1024]{2,1,0:T(8,128)(2,1)S(1)} %copy-done.1, bf16[16,128,1024]{2,1,0:T(8,128)(2,1)S(1)} %copy-done.1, s32[128,1024]{1,0:T(8,128)S(1)} %copy-done.3, s32[128,1024]{1,0:T(8,128)S(1)} %copy-done.3, ...), custom_call_target="tpu_custom_call" | custom-call | flops 3000000000 | bytes 3000000 | tf_op jit(solution)/shard_map/early/pallas_call | solution.py:154
  14.7 3.0 %collective-permute-start.2 = (f32[24,128]{1,0:T(8,128)S(1)}, f32[24,128]{1,0:T(8,128)S(1)}, u32[]{:S(2)}, u32[]{:S(2)}) collective-permute-start(f32[24,128]{1,0:T(8,128)S(1)} %get-tuple-element.44.after.refs_0_), channel_id=1, source_target_pairs={{0,8},{8,0},{16,24},{24,16},{1,9},{9,1},{17,25},{25,17},{2,10},{10... | collective-permute-start | bytes 36872 | tf_op jit(solution)/shard_map/ppermute | solution.py:380
  19.3 3.9 %collective-permute-start = (bf16[17,8,1024]{2,1,0:T(8,128)(2,1)S(1)}, bf16[17,8,1024]{2,1,0:T(8,128)(2,1)S(1)}, u32[]{:S(2)}, u32[]{:S(2)}) collective-permute-start(bf16[17,8,1024]{2,1,0:T(8,128)(2,1)S(1)} %get-tuple-element.42), channel_id=1, source_target_pairs={{0,8},{8,16},{16,24},{1,9},{9,17},{17,25},{2,10},{10,18},{18,26},{... | collective-permute-start | bytes 835592 | tf_op jit(solution)/shard_map/ppermute | solution.py:381
  28.9 3.6 %collective-permute-start.27 = (bf16[8,16,1024]{2,1,0:T(8,128)(2,1)S(1)}, bf16[8,16,1024]{2,1,0:T(8,128)(2,1)S(1)}, u32[]{:S(2)}, u32[]{:S(2)}) collective-permute-start(bf16[8,16,1024]{2,1,0:T(8,128)(2,1)S(1)} %get-tuple-element.41.after), channel_id=1, source_target_pairs={{0,6},{1,7},{2,4},{3,5},{4,2},{5,3},{6,0},{7,1},{8,14},{9,15},{10,... | collective-permute-start | bytes 786440 | tf_op jit(solution)/shard_map/ppermute | solution.py:367
  36.1 3.6 %collective-permute-start.28 = (f32[16,128]{1,0:T(8,128)S(1)}, f32[16,128]{1,0:T(8,128)S(1)}, u32[]{:S(2)}, u32[]{:S(2)}) collective-permute-start(f32[16,128]{1,0:T(8,128)S(1)} %get-tuple-element.73), channel_id=1, source_target_pairs={{0,6},{1,7},{2,4},{3,5},{4,2},{5,3},{6,0},{7,1},{8,14},{9,15},{10,... | collective-permute-start | bytes 24584 | tf_op jit(solution)/shard_map/ppermute | solution.py:367
  39.7 5.5 %filter.2 = (bf16[8,16,1024]{2,1,0:T(8,128)(2,1)S(1)}, bf16[5,16,1024]{2,1,0:T(8,128)(2,1)S(1)}, bf16[3,16,1024]{2,1,0:T(8,128)(2,1)S(1)}) custom-call(s32[2]{0:T(128)S(1)} %pad_add_fusion.1.ids, bf16[16,128,1024]{2,1,0:T(8,128)(2,1)} %after.5, bf16[16,128,1024]{2,1,0:T(8,128)(2,1)} %after.5, bf16[16,128,1024]{2,1,0:T(8,128)(2,1)} %after.5, ...), custom_call_target="tpu_custom_call" | custom-call | flops 1610000000 | bytes 3000000 | tf_op jit(solution)/shard_map/filter/pallas_call | solution.py:287
  45.2 12.9 %collective-permute-start.24 = (f32[16,128]{1,0:T(8,128)S(1)}, f32[16,128]{1,0:T(8,128)S(1)}, u32[]{:S(2)}, u32[]{:S(2)}) collective-permute-start(f32[16,128]{1,0:T(8,128)S(1)} %get-tuple-element.71), channel_id=1, source_target_pairs={{0,4},{1,5},{2,6},{3,7},{4,0},{5,1},{6,2},{7,3},{8,12},{9,13},{10,... | collective-permute-start | bytes 24584 | tf_op jit(solution)/shard_map/ppermute | solution.py:367
  58.1 20.1 %filter.3 = (bf16[8,16,1024]{2,1,0:T(8,128)(2,1)S(1)}, bf16[5,16,1024]{2,1,0:T(8,128)(2,1)S(1)}, bf16[3,16,1024]{2,1,0:T(8,128)(2,1)S(1)}, bf16[5,16,1024]{2,1,0...) custom-call(s32[8]{0:T(128)S(1)} %concatenate.10.ids, ...), custom_call_target="tpu_custom_call" | custom-call | flops 11269999616 | bytes 21000000 | tf_op jit(solution)/shard_map/filter/pallas_call | solution.py:287
  79.9 2.2 %collective-permute-start.11 = (bf16[3,16,1024]{2,1,0:T(8,128)(2,1)S(1)}, bf16[3,16,1024]{2,1,0:T(8,128)(2,1)S(1)}, u32[]{:S(2)}, u32[]{:S(2)}) collective-permute-start(bf16[3,16,1024]{2,1,0:T(8,128)(2,1)S(1)} %get-tuple-element.58), channel_id=1, source_target_pairs={{0,7},{1,6},{2,5},{3,4},{4,3},{5,2},{6,1},{7,0},{8,15},{9,14},{10,... | collective-permute-start | bytes 294920 | tf_op jit(solution)/shard_map/ppermute | solution.py:367
  82.2 4.9 %collective-permute-done.10.refs_6_ = bf16[3,16,1024]{2,1,0:T(8,128)(2,1)S(1)} collective-permute-done((bf16[3,16,1024]{2,1,0:T(8,128)(2,1)S(1)}, bf16[3,16,1024]{2,1,0:T(8,128)(2,1)S(1)}, u32[]{:S(2)}, u32[]{:S(2)}) %collective-permute-start.10) | collective-permute-done | bytes 98336 | tf_op jit(solution)/shard_map/ppermute | solution.py:367
  89.1 3.5 %collective-permute-start.17 = (bf16[5,16,1024]{2,1,0:T(8,128)(2,1)S(1)}, bf16[5,16,1024]{2,1,0:T(8,128)(2,1)S(1)}, u32[]{:S(2)}, u32[]{:S(2)}) collective-permute-start(bf16[5,16,1024]{2,1,0:T(8,128)(2,1)S(1)} %get-tuple-element.65), channel_id=1, source_target_pairs={{0,6},{1,7},{2,4},{3,5},{4,2},{5,3},{6,0},{7,1},{8,14},{9,15},{10,... | collective-permute-start | bytes 491528 | tf_op jit(solution)/shard_map/ppermute | solution.py:367
  95.4 19.6 %collective-permute-done.15.refs_4_ = bf16[5,16,1024]{2,1,0:T(8,128)(2,1)S(1)} collective-permute-done((bf16[5,16,1024]{2,1,0:T(8,128)(2,1)S(1)}, bf16[5,16,1024]{2,1,0:T(8,128)(2,1)S(1)}, u32[]{:S(2)}, u32[]{:S(2)}) %collective-permute-start.15) | collective-permute-done | bytes 163872 | tf_op jit(solution)/shard_map/ppermute | solution.py:367
  115.0 4.1 %collective-permute-start.20 = (bf16[8,16,1024]{2,1,0:T(8,128)(2,1)S(1)}, bf16[8,16,1024]{2,1,0:T(8,128)(2,1)S(1)}, u32[]{:S(2)}, u32[]{:S(2)}) collective-permute-start(bf16[8,16,1024]{2,1,0:T(8,128)(2,1)S(1)} %get-tuple-element.69), channel_id=1, source_target_pairs={{0,2},{1,3},{2,0},{3,1},{4,6},{5,7},{6,4},{7,5},{8,10},{9,11},{10,... | collective-permute-start | bytes 786440 | tf_op jit(solution)/shard_map/ppermute | solution.py:367
  119.1 2.9 %collective-permute-start.21 = (bf16[8,16,1024]{2,1,0:T(8,128)(2,1)S(1)}, bf16[8,16,1024]{2,1,0:T(8,128)(2,1)S(1)}, u32[]{:S(2)}, u32[]{:S(2)}) collective-permute-start(bf16[8,16,1024]{2,1,0:T(8,128)(2,1)S(1)} %get-tuple-element.70), channel_id=1, source_target_pairs={{0,3},{1,2},{2,1},{3,0},{4,7},{5,6},{6,5},{7,4},{8,11},{9,10},{10,... | collective-permute-start | bytes 786440 | tf_op jit(solution)/shard_map/ppermute | solution.py:367
  124.1 3.1 %collective-permute-start.29 = (bf16[8,16,1024]{2,1,0:T(8,128)(2,1)S(1)}, bf16[8,16,1024]{2,1,0:T(8,128)(2,1)S(1)}, u32[]{:S(2)}, u32[]{:S(2)}) collective-permute-start(bf16[8,16,1024]{2,1,0:T(8,128)(2,1)S(1)} %get-tuple-element.72.after), channel_id=1, source_target_pairs={{0,7},{1,6},{2,5},{3,4},{4,3},{5,2},{6,1},{7,0},{8,15},{9,14},{10,... | collective-permute-start | bytes 786440 | tf_op jit(solution)/shard_map/ppermute | solution.py:367
  127.1 3.1 %mend.3.refs_6_ = bf16[8,16,1024]{2,1,0:T(8,128)(2,1)S(1)} custom-call(s32[2]{0:T(128)S(1)} %pad_add_fusion.ids, s32[128,1024]{1,0:T(8,128)S(1)} %copy-done.3, s32[128,1024]{1,0:T(8,128)S(1)} %copy-done.3, bf16[4,16,17]{2,1,0:T(8,128)(2,1)S(1)} %get-tuple-element.79.row_taps, bf16[4,16,17]{2,1,0:T(8,128)(2,1)S(1)} %get-tuple-element.78.col_taps, ...), custom_call_target="tpu_custom_call" | custom-call | flops 3000000000 | bytes 3000000 | tf_op jit(solution)/shard_map/mend/pallas_call | solution.py:154
  130.4 10.6 %collective-permute-done.20.refs_2_ = bf16[8,16,1024]{2,1,0:T(8,128)(2,1)S(1)} collective-permute-done((bf16[8,16,1024]{2,1,0:T(8,128)(2,1)S(1)}, bf16[8,16,1024]{2,1,0:T(8,128)(2,1)S(1)}, u32[]{:S(2)}, u32[]{:S(2)}) %collective-permute-start.20) | collective-permute-done | bytes 262176 | tf_op jit(solution)/shard_map/ppermute | solution.py:367
  142.3 5.1 %collective-permute-start.8 = (bf16[3,16,1024]{2,1,0:T(8,128)(2,1)S(1)}, bf16[3,16,1024]{2,1,0:T(8,128)(2,1)S(1)}, u32[]{:S(2)}, u32[]{:S(2)}) collective-permute-start(bf16[3,16,1024]{2,1,0:T(8,128)(2,1)S(1)} %get-tuple-element.55), channel_id=1, source_target_pairs={{0,4},{1,5},{2,6},{3,7},{4,0},{5,1},{6,2},{7,3},{8,12},{9,13},{10,... | collective-permute-start | bytes 294920 | tf_op jit(solution)/shard_map/ppermute | solution.py:367
  148.0 3.1 %mend.2.refs_4_ = bf16[8,16,1024]{2,1,0:T(8,128)(2,1)S(1)} custom-call(s32[2]{0:T(128)S(1)} %pad_add_fusion.ids, s32[128,1024]{1,0:T(8,128)S(1)} %copy-done.3, s32[128,1024]{1,0:T(8,128)S(1)} %copy-done.3, bf16[4,16,17]{2,1,0:T(8,128)(2,1)S(1)} %get-tuple-element.81.row_taps, bf16[4,16,17]{2,1,0:T(8,128)(2,1)S(1)} %get-tuple-element.80.col_taps, ...), custom_call_target="tpu_custom_call" | custom-call | flops 3000000000 | bytes 3000000 | tf_op jit(solution)/shard_map/mend/pallas_call | solution.py:154
  151.2 4.5 %project.3 = (bf16[128,16384]{1,0:T(8,128)(2,1)}, bf16[128,16384]{1,0:T(8,128)(2,1)}) custom-call(s32[1]{0:T(128)} %bitcast.15.place, bf16[256,128]{1,0:T(8,128)(2,1)S(1)} %copy.14.weights, bf16[8,16,1024]{2,1,0:T(8,128)(2,1)S(1)} %get-tuple-element.67.refs_0_, bf16[8,16,1024]{2,1,0:T(8,128)(2,1)S(1)} %collective-permute-done.19.refs_1_, ...), custom_call_target="tpu_custom_call" | custom-call | flops 536870912 | bytes 6291456 | tf_op jit(solution)/shard_map/project/pallas_call | solution.py:336
  155.7 3.1 %project.4 = (bf16[128,16384]{1,0:T(8,128)(2,1)}, bf16[128,16384]{1,0:T(8,128)(2,1)}) custom-call(s32[1]{0:T(128)} %bitcast.14.place, bf16[256,128]{1,0:T(8,128)(2,1)S(1)} %copy.14.weights, bf16[5,16,1024]{2,1,0:T(8,128)(2,1)S(1)} %get-tuple-element.59.refs_0_, ...), custom_call_target="tpu_custom_call", output_to_operand_aliasing={{0}: (10, {}), {1}: (11, {})} | custom-call | flops 335544320 | bytes 3932160 | tf_op jit(solution)/shard_map/project/pallas_call | solution.py:336
  158.8 2.1 %project.5 = (bf16[128,16384]{1,0:T(8,128)(2,1)}, bf16[128,16384]{1,0:T(8,128)(2,1)}) custom-call(s32[1]{0:T(128)} %bitcast.place, bf16[256,128]{1,0:T(8,128)(2,1)S(1)} %copy.14.weights, bf16[3,16,1024]{2,1,0:T(8,128)(2,1)S(1)} %get-tuple-element.51.refs_0_, ...), custom_call_target="tpu_custom_call", output_to_operand_aliasing={{0}: (10, {}), {1}: (11, {})} | custom-call | flops 201326592 | bytes 2359296 | tf_op jit(solution)/shard_map/project/pallas_call | solution.py:336
  (82 shorter events, 25.6 us)
Async XLA Ops:
  14.7 14.2 %collective-permute-start.2 = (f32[24,128]{1,0:T(8,128)S(1)}, f32[24,128]{1,0:T(8,128)S(1)}, u32[]{:S(2)}, u32[]{:S(2)}) collective-permute-start(f32[24,128]{1,0:T(8,128)S(1)} %get-tuple-element.44.after.refs_0_), channel_id=1, source_target_pairs={{0,8},{8,0},{16,24},{24,16},{1,9},{9,1},{17,25},{25,17},{2,10},{10... | collective-permute-start | bytes 36872 | tf_op jit(solution)/shard_map/ppermute | solution.py:380
  17.7 14.8 %collective-permute-start.3 = (f32[24,128]{1,0:T(8,128)S(1)}, f32[24,128]{1,0:T(8,128)S(1)}, u32[]{:S(2)}, u32[]{:S(2)}) collective-permute-start(f32[24,128]{1,0:T(8,128)S(1)} %get-tuple-element.44.after.refs_0_), channel_id=1, source_target_pairs={{0,16},{8,24},{16,0},{24,8},{1,17},{9,25},{17,1},{25,9},{2,18},{10... | collective-permute-start | bytes 36872 | tf_op jit(solution)/shard_map/ppermute | solution.py:380
  19.2 13.3 %collective-permute-start.4 = (f32[24,128]{1,0:T(8,128)S(1)}, f32[24,128]{1,0:T(8,128)S(1)}, u32[]{:S(2)}, u32[]{:S(2)}) collective-permute-start(f32[24,128]{1,0:T(8,128)S(1)} %get-tuple-element.44.after.refs_0_), channel_id=1, source_target_pairs={{0,24},{8,16},{16,8},{24,0},{1,25},{9,17},{17,9},{25,1},{2,26},{10... | collective-permute-start | bytes 36872 | tf_op jit(solution)/shard_map/ppermute | solution.py:380
  19.3 15.3 %collective-permute-start = (bf16[17,8,1024]{2,1,0:T(8,128)(2,1)S(1)}, bf16[17,8,1024]{2,1,0:T(8,128)(2,1)S(1)}, u32[]{:S(2)}, u32[]{:S(2)}) collective-permute-start(bf16[17,8,1024]{2,1,0:T(8,128)(2,1)S(1)} %get-tuple-element.42), channel_id=1, source_target_pairs={{0,8},{8,16},{16,24},{1,9},{9,17},{17,25},{2,10},{10,18},{18,26},{... | collective-permute-start | bytes 835592 | tf_op jit(solution)/shard_map/ppermute | solution.py:381
  28.9 50.9 %collective-permute-start.27 = (bf16[8,16,1024]{2,1,0:T(8,128)(2,1)S(1)}, bf16[8,16,1024]{2,1,0:T(8,128)(2,1)S(1)}, u32[]{:S(2)}, u32[]{:S(2)}) collective-permute-start(bf16[8,16,1024]{2,1,0:T(8,128)(2,1)S(1)} %get-tuple-element.41.after), channel_id=1, source_target_pairs={{0,6},{1,7},{2,4},{3,5},{4,2},{5,3},{6,0},{7,1},{8,14},{9,15},{10,... | collective-permute-start | bytes 786440 | tf_op jit(solution)/shard_map/ppermute | solution.py:367
  32.5 49.5 %collective-permute-start.23 = (bf16[8,16,1024]{2,1,0:T(8,128)(2,1)S(1)}, bf16[8,16,1024]{2,1,0:T(8,128)(2,1)S(1)}, u32[]{:S(2)}, u32[]{:S(2)}) collective-permute-start(bf16[8,16,1024]{2,1,0:T(8,128)(2,1)S(1)} %get-tuple-element.40.after), channel_id=1, source_target_pairs={{0,4},{1,5},{2,6},{3,7},{4,0},{5,1},{6,2},{7,3},{8,12},{9,13},{10,... | collective-permute-start | bytes 786440 | tf_op jit(solution)/shard_map/ppermute | solution.py:367
  34.5 43.7 %collective-permute-start.22 = (bf16[2,4,16,17]{3,2,1,0:T(8,128)(2,1)S(1)}, bf16[2,4,16,17]{3,2,1,0:T(8,128)(2,1)S(1)}, u32[]{:S(2)}, u32[]{:S(2)}) collective-permute-start(bf16[2,4,16,17]{3,2,1,0:T(8,128)(2,1)S(1)} %pad_maximum_fusion.1), channel_id=1, source_target_pairs={{0,4},{1,5},{2,6},{3,7},{4,0},{5,1},{6,2},{7,3},{8,12},{9,13},{10,... | collective-permute-start | bytes 13064 | tf_op jit(solution)/shard_map/ppermute | solution.py:367
  36.1 42.2 %collective-permute-start.28 = (f32[16,128]{1,0:T(8,128)S(1)}, f32[16,128]{1,0:T(8,128)S(1)}, u32[]{:S(2)}, u32[]{:S(2)}) collective-permute-start(f32[16,128]{1,0:T(8,128)S(1)} %get-tuple-element.73), channel_id=1, source_target_pairs={{0,6},{1,7},{2,4},{3,5},{4,2},{5,3},{6,0},{7,1},{8,14},{9,15},{10,... | collective-permute-start | bytes 24584 | tf_op jit(solution)/shard_map/ppermute | solution.py:367
  45.2 33.2 %collective-permute-start.24 = (f32[16,128]{1,0:T(8,128)S(1)}, f32[16,128]{1,0:T(8,128)S(1)}, u32[]{:S(2)}, u32[]{:S(2)}) collective-permute-start(f32[16,128]{1,0:T(8,128)S(1)} %get-tuple-element.71), channel_id=1, source_target_pairs={{0,4},{1,5},{2,6},{3,7},{4,0},{5,1},{6,2},{7,3},{8,12},{9,13},{10,... | collective-permute-start | bytes 24584 | tf_op jit(solution)/shard_map/ppermute | solution.py:367
  78.2 14.4 %collective-permute-start.12 = (bf16[5,16,1024]{2,1,0:T(8,128)(2,1)S(1)}, bf16[5,16,1024]{2,1,0:T(8,128)(2,1)S(1)}, u32[]{:S(2)}, u32[]{:S(2)}) collective-permute-start(bf16[5,16,1024]{2,1,0:T(8,128)(2,1)S(1)} %get-tuple-element.60), channel_id=1, source_target_pairs={{0,1},{1,0},{2,3},{3,2},{4,5},{5,4},{6,7},{7,6},{8,9},{9,8},{10,11... | collective-permute-start | bytes 491528 | tf_op jit(solution)/shard_map/ppermute | solution.py:367
  78.3 14.3 %collective-permute-start.13 = (bf16[5,16,1024]{2,1,0:T(8,128)(2,1)S(1)}, bf16[5,16,1024]{2,1,0:T(8,128)(2,1)S(1)}, u32[]{:S(2)}, u32[]{:S(2)}) collective-permute-start(bf16[5,16,1024]{2,1,0:T(8,128)(2,1)S(1)} %get-tuple-element.61), channel_id=1, source_target_pairs={{0,2},{1,3},{2,0},{3,1},{4,6},{5,7},{6,4},{7,5},{8,10},{9,11},{10,... | collective-permute-start | bytes 491528 | tf_op jit(solution)/shard_map/ppermute | solution.py:367
  87.1 27.9 %collective-permute-start.15 = (bf16[5,16,1024]{2,1,0:T(8,128)(2,1)S(1)}, bf16[5,16,1024]{2,1,0:T(8,128)(2,1)S(1)}, u32[]{:S(2)}, u32[]{:S(2)}) collective-permute-start(bf16[5,16,1024]{2,1,0:T(8,128)(2,1)S(1)} %get-tuple-element.63), channel_id=1, source_target_pairs={{0,4},{1,5},{2,6},{3,7},{4,0},{5,1},{6,2},{7,3},{8,12},{9,13},{10,... | collective-permute-start | bytes 491528 | tf_op jit(solution)/shard_map/ppermute | solution.py:367
  89.1 25.9 %collective-permute-start.17 = (bf16[5,16,1024]{2,1,0:T(8,128)(2,1)S(1)}, bf16[5,16,1024]{2,1,0:T(8,128)(2,1)S(1)}, u32[]{:S(2)}, u32[]{:S(2)}) collective-permute-start(bf16[5,16,1024]{2,1,0:T(8,128)(2,1)S(1)} %get-tuple-element.65), channel_id=1, source_target_pairs={{0,6},{1,7},{2,4},{3,5},{4,2},{5,3},{6,0},{7,1},{8,14},{9,15},{10,... | collective-permute-start | bytes 491528 | tf_op jit(solution)/shard_map/ppermute | solution.py:367
  92.6 26.4 %collective-permute-start.18 = (bf16[5,16,1024]{2,1,0:T(8,128)(2,1)S(1)}, bf16[5,16,1024]{2,1,0:T(8,128)(2,1)S(1)}, u32[]{:S(2)}, u32[]{:S(2)}) collective-permute-start(bf16[5,16,1024]{2,1,0:T(8,128)(2,1)S(1)} %get-tuple-element.66), channel_id=1, source_target_pairs={{0,7},{1,6},{2,5},{3,4},{4,3},{5,2},{6,1},{7,0},{8,15},{9,14},{10,... | collective-permute-start | bytes 491528 | tf_op jit(solution)/shard_map/ppermute | solution.py:367
  92.7 31.4 %collective-permute-start.16 = (bf16[5,16,1024]{2,1,0:T(8,128)(2,1)S(1)}, bf16[5,16,1024]{2,1,0:T(8,128)(2,1)S(1)}, u32[]{:S(2)}, u32[]{:S(2)}) collective-permute-start(bf16[5,16,1024]{2,1,0:T(8,128)(2,1)S(1)} %get-tuple-element.64), channel_id=1, source_target_pairs={{0,5},{1,4},{2,7},{3,6},{4,1},{5,0},{6,3},{7,2},{8,13},{9,12},{10,... | collective-permute-start | bytes 491528 | tf_op jit(solution)/shard_map/ppermute | solution.py:367
  93.8 53.6 %collective-permute-start.25 = (bf16[8,16,1024]{2,1,0:T(8,128)(2,1)S(1)}, bf16[8,16,1024]{2,1,0:T(8,128)(2,1)S(1)}, u32[]{:S(2)}, u32[]{:S(2)}) collective-permute-start(bf16[8,16,1024]{2,1,0:T(8,128)(2,1)S(1)} %get-tuple-element.50.refs_5_), channel_id=1, source_target_pairs={{0,5},{1,4},{2,7},{3,6},{4,1},{5,0},{6,3},{7,2},{8,13},{9,12},{10,... | collective-permute-start | bytes 786440 | tf_op jit(solution)/shard_map/ppermute | solution.py:367
  115.0 15.3 %collective-permute-start.19 = (bf16[8,16,1024]{2,1,0:T(8,128)(2,1)S(1)}, bf16[8,16,1024]{2,1,0:T(8,128)(2,1)S(1)}, u32[]{:S(2)}, u32[]{:S(2)}) collective-permute-start(bf16[8,16,1024]{2,1,0:T(8,128)(2,1)S(1)} %get-tuple-element.68), channel_id=1, source_target_pairs={{0,1},{1,0},{2,3},{3,2},{4,5},{5,4},{6,7},{7,6},{8,9},{9,8},{10,11... | collective-permute-start | bytes 786440 | tf_op jit(solution)/shard_map/ppermute | solution.py:367
  115.0 26.0 %collective-permute-start.20 = (bf16[8,16,1024]{2,1,0:T(8,128)(2,1)S(1)}, bf16[8,16,1024]{2,1,0:T(8,128)(2,1)S(1)}, u32[]{:S(2)}, u32[]{:S(2)}) collective-permute-start(bf16[8,16,1024]{2,1,0:T(8,128)(2,1)S(1)} %get-tuple-element.69), channel_id=1, source_target_pairs={{0,2},{1,3},{2,0},{3,1},{4,6},{5,7},{6,4},{7,5},{8,10},{9,11},{10,... | collective-permute-start | bytes 786440 | tf_op jit(solution)/shard_map/ppermute | solution.py:367
  119.1 23.3 %collective-permute-start.21 = (bf16[8,16,1024]{2,1,0:T(8,128)(2,1)S(1)}, bf16[8,16,1024]{2,1,0:T(8,128)(2,1)S(1)}, u32[]{:S(2)}, u32[]{:S(2)}) collective-permute-start(bf16[8,16,1024]{2,1,0:T(8,128)(2,1)S(1)} %get-tuple-element.70), channel_id=1, source_target_pairs={{0,3},{1,2},{2,1},{3,0},{4,7},{5,6},{6,5},{7,4},{8,11},{9,10},{10,... | collective-permute-start | bytes 786440 | tf_op jit(solution)/shard_map/ppermute | solution.py:367
  124.1 18.3 %collective-permute-start.29 = (bf16[8,16,1024]{2,1,0:T(8,128)(2,1)S(1)}, bf16[8,16,1024]{2,1,0:T(8,128)(2,1)S(1)}, u32[]{:S(2)}, u32[]{:S(2)}) collective-permute-start(bf16[8,16,1024]{2,1,0:T(8,128)(2,1)S(1)} %get-tuple-element.72.after), channel_id=1, source_target_pairs={{0,7},{1,6},{2,5},{3,4},{4,3},{5,2},{6,1},{7,0},{8,15},{9,14},{10,... | collective-permute-start | bytes 786440 | tf_op jit(solution)/shard_map/ppermute | solution.py:367
  130.3 28.5 %collective-permute-start.5 = (bf16[3,16,1024]{2,1,0:T(8,128)(2,1)S(1)}, bf16[3,16,1024]{2,1,0:T(8,128)(2,1)S(1)}, u32[]{:S(2)}, u32[]{:S(2)}) collective-permute-start(bf16[3,16,1024]{2,1,0:T(8,128)(2,1)S(1)} %get-tuple-element.52), channel_id=1, source_target_pairs={{0,1},{1,0},{2,3},{3,2},{4,5},{5,4},{6,7},{7,6},{8,9},{9,8},{10,11... | collective-permute-start | bytes 294920 | tf_op jit(solution)/shard_map/ppermute | solution.py:367
  141.0 17.9 %collective-permute-start.6 = (bf16[3,16,1024]{2,1,0:T(8,128)(2,1)S(1)}, bf16[3,16,1024]{2,1,0:T(8,128)(2,1)S(1)}, u32[]{:S(2)}, u32[]{:S(2)}) collective-permute-start(bf16[3,16,1024]{2,1,0:T(8,128)(2,1)S(1)} %get-tuple-element.53), channel_id=1, source_target_pairs={{0,2},{1,3},{2,0},{3,1},{4,6},{5,7},{6,4},{7,5},{8,10},{9,11},{10,... | collective-permute-start | bytes 294920 | tf_op jit(solution)/shard_map/ppermute | solution.py:367
  142.3 16.5 %collective-permute-start.7 = (bf16[3,16,1024]{2,1,0:T(8,128)(2,1)S(1)}, bf16[3,16,1024]{2,1,0:T(8,128)(2,1)S(1)}, u32[]{:S(2)}, u32[]{:S(2)}) collective-permute-start(bf16[3,16,1024]{2,1,0:T(8,128)(2,1)S(1)} %get-tuple-element.54), channel_id=1, source_target_pairs={{0,3},{1,2},{2,1},{3,0},{4,7},{5,6},{6,5},{7,4},{8,11},{9,10},{10,... | collective-permute-start | bytes 294920 | tf_op jit(solution)/shard_map/ppermute | solution.py:367
  142.3 16.5 %collective-permute-start.8 = (bf16[3,16,1024]{2,1,0:T(8,128)(2,1)S(1)}, bf16[3,16,1024]{2,1,0:T(8,128)(2,1)S(1)}, u32[]{:S(2)}, u32[]{:S(2)}) collective-permute-start(bf16[3,16,1024]{2,1,0:T(8,128)(2,1)S(1)} %get-tuple-element.55), channel_id=1, source_target_pairs={{0,4},{1,5},{2,6},{3,7},{4,0},{5,1},{6,2},{7,3},{8,12},{9,13},{10,... | collective-permute-start | bytes 294920 | tf_op jit(solution)/shard_map/ppermute | solution.py:367
  (17 other events, 111.7 us)

commit v3 on v2

--- a/solution.py
+++ b/solution.py
@@ -11,12 +11,12 @@
 TAPS = 2 * REACH + 1
 LANES = 128
 GROUP = 8
-VMEM_BYTES = 48 * 1024 * 1024
+MIB = 1024 * 1024
 HALO = 2 * REACH
 
 
-def params():
-    return pltpu.CompilerParams(vmem_limit_bytes=VMEM_BYTES)
+def params(mib=40):
+    return pltpu.CompilerParams(vmem_limit_bytes=mib * MIB)
 
 
 def cost(flops, moved):
@@ -24,7 +24,7 @@
 
 
 def build_matrices(row_taps, col_taps, col_out, row_out):
-    terms, slices, _ = row_taps.shape
+    terms, slices = len(row_taps), row_taps[0].shape[0]
     wide = 2 * LANES
     window = LANES + HALO
     tap = lax.broadcasted_iota(jnp.int32, (TAPS, wide), 0)
@@ -57,12 +57,16 @@
                 ] = both.astype(jnp.bfloat16)
 
 
+def listed(taps):
+    return [taps[k] for k in range(taps.shape[0])]
+
+
 def matrix_shapes(terms, slices, rows):
     return (slices, 2 * LANES, terms * LANES), (slices // GROUP, rows * GROUP, GROUP * LANES)
 
 
 def matrices_kernel(row_taps, col_taps, after, col_out, row_out):
-    build_matrices(row_taps, col_taps, col_out, row_out)
+    build_matrices(listed(row_taps), listed(col_taps), col_out, row_out)
 
 
 def filter_matrices(row_taps, col_taps, after):
@@ -75,7 +79,7 @@
         in_specs=[vmem, vmem, pl.BlockSpec(memory_space=pl.ANY)],
         out_shape=[jax.ShapeDtypeStruct(shape, jnp.bfloat16) for shape in shapes],
         compiler_params=params(),
-        cost_estimate=cost(1e6, 5e6),
+        cost_estimate=cost(1, 1),
     )(row_taps, col_taps, after)
 
 
@@ -110,7 +114,7 @@
 
 def early_kernel(ids, one, two, mask_one, mask_two, row_taps, col_taps, after, out, centre, col, row, tall):
     slices = one.shape[0]
-    build_matrices(row_taps, col_taps, col, row)
+    build_matrices(listed(row_taps), listed(col_taps), col, row)
     last = ids[0] == ids[1]
     mask = inner_rows(mask_one[...], mask_two[...], last)
 
@@ -128,17 +132,19 @@
     out[...] = field.astype(jnp.bfloat16)
 
 
-def mend_kernel(ids, mask_one, mask_two, row_taps, col_taps, piece, delta, after, out, col, row, tall):
-    build_matrices(row_taps, col_taps, col, row)
+def mend_kernel(ids, mask_one, mask_two, note, piece, after, out, col, row, tall):
+    terms = note.shape[0] // 2
+    taps = [note[k, :, :TAPS].astype(jnp.bfloat16) for k in range(2 * terms)]
+    build_matrices(taps[:terms], taps[terms:], col, row)
     last = ids[0] == ids[1]
     mask = inner_rows(mask_one[...], mask_two[...], last)
     field = convolve(lambda s: mask, col, row, tall, out.shape[0])
-    shift = jnp.broadcast_to(delta[:, :1], field.shape[1:])
+    shift = jnp.broadcast_to(note[2 * terms][:, :1], field.shape[1:])
     out[...] = (piece[...].astype(jnp.float32) + shift[None] * field).astype(jnp.bfloat16)
 
 
-def early_call(kernel, name, ids, density, valid, row_taps, col_taps, extra, after, out_shape):
-    terms, slices, _ = row_taps.shape
+def early_call(kernel, name, ids, density, valid, terms, extra, after, out_shape):
+    slices = out_shape[0].shape[1]
     cols = valid.shape[1]
     block = LANES // terms - HALO
     last = valid.shape[0] // block - 1
@@ -161,16 +167,16 @@
                 pl.BlockSpec((slices, block, cols), lambda i, ids, f=at(d): (0, f(i, ids), 0)) for d in range(len(cubes))
             ]
             + [pl.BlockSpec((block, cols), lambda i, ids, f=at(d): (f(i, ids), 0)) for d in (0, 1)]
-            + [whole(x) for x in (row_taps, col_taps, *extra)]
+            + [whole(x) for x in extra]
             + [pl.BlockSpec(memory_space=pl.ANY)],
             out_specs=[whole(x) for x in out_shape],
             scratch_shapes=[pltpu.VMEM(shape, jnp.bfloat16) for shape in shapes]
             + [pltpu.VMEM((GROUP * LANES, cols), jnp.bfloat16)],
         ),
         out_shape=out_shape,
-        compiler_params=params(),
-        cost_estimate=cost(3e9, 3e6),
-    )(jnp.stack([ids, jnp.full_like(ids, last)]).astype(jnp.int32), *cubes, valid, valid, row_taps, col_taps, *extra, after)
+        compiler_params=params(60),
+        cost_estimate=cost(1, 1),
+    )(jnp.stack([ids, jnp.full_like(ids, last)]).astype(jnp.int32), *cubes, valid, valid, *extra, after)
 
 
 def sums_kernel(density, valid, after, out, first, last):
@@ -215,31 +221,58 @@
         out_specs=[pl.BlockSpec((slices + 8, LANES), lambda i: (0, 0))]
         + [pl.BlockSpec(edge.shape, lambda i: (0, 0, 0))] * 2,
         out_shape=[jax.ShapeDtypeStruct((slices + 8, LANES), jnp.float32), edge, edge],
-        compiler_params=params(),
-        cost_estimate=cost(2 * density.size, 2 * density.size),
+        compiler_params=params(60),
+        cost_estimate=cost(1, 1),
     )(density, valid, after)
 
 
 def mean_kernel(*refs):
-    sums, centres, out, shifts = refs[:4], refs[4:6], refs[6], refs[7:]
+    sums, out = refs[:4], refs[-1]
     slices = out.shape[0]
     total = sums[0][...] + sums[1][...] + sums[2][...] + sums[3][...]
     total = jnp.sum(total, axis=1, keepdims=True)
-    mean = jnp.broadcast_to(total[:slices] / total[slices : slices + 1], out.shape)
-    out[...] = mean
-    for centre, shift in zip(centres, shifts):
-        shift[...] = centre[...] - mean
-
-
-def means(sums, centres):
-    shape = jax.ShapeDtypeStruct(centres[0].shape, jnp.float32)
-    return pl.pallas_call(
-        mean_kernel, name="means", out_shape=[shape] * 3, compiler_params=params(), cost_estimate=cost(1e4, 1e5)
-    )(*sums, *centres)
+    out[...] = jnp.broadcast_to(total[:slices] / total[slices : slices + 1], out.shape)
+
+
+def means(sums, slices, after):
+    vmem = pl.BlockSpec(memory_space=pltpu.VMEM)
+    return pl.pallas_call(
+        mean_kernel,
+        name="means",
+        in_specs=[vmem] * len(sums) + [pl.BlockSpec(memory_space=pl.ANY)],
+        out_specs=vmem,
+        out_shape=jax.ShapeDtypeStruct((slices, LANES), jnp.float32),
+        compiler_params=params(),
+        cost_estimate=cost(1, 1),
+    )(*sums, after)
+
+
+def notes_kernel(mean, row_taps, col_taps, *refs):
+    terms, slices, taps = row_taps.shape
+    count = len(refs) // 2
+    for centre, note in zip(refs[:count], refs[count:]):
+        note[...] = jnp.zeros_like(note)
+        note[:terms, :, :taps] = row_taps[...].astype(jnp.float32)
+        note[terms : 2 * terms, :, :taps] = col_taps[...].astype(jnp.float32)
+        note[2 * terms] = centre[...] - mean[...]
+
+
+def notes_of(mean, row_taps, col_taps, centres):
+    terms, slices, _ = row_taps.shape
+    note = jax.ShapeDtypeStruct((2 * terms + 1, slices, LANES), jnp.float32)
+    return pl.pallas_call(
+        notes_kernel,
+        name="notes",
+        out_shape=[note] * len(centres),
+        compiler_params=params(),
+        cost_estimate=cost(1, 1),
+    )(mean, row_taps, col_taps, *centres)
 
 
 def filter_kernel(pieces, ids, before, now, after, mask_before, mask_now, mask_after, *refs):
-    (above, below, col, row, mean), outs, (tall, done) = refs[:5], refs[6:-2], refs[-2:]
+    (above, below, col, row, mean), (tall, done) = refs[:5], refs[-2:]
+    count = sum(len(wanted) for wanted in pieces)
+    outs = refs[-2 - count : -2]
     slices, block, cols = now.shape
     step = pl.program_id(0)
     first = ids[step] == 0
@@ -268,7 +301,7 @@
         at += len(wanted)
 
 
-def filter_blocks(ids, pieces, density, valid, above, below, col, row, mean, after):
+def filter_blocks(ids, pieces, density, valid, above, below, col, row, mean, *after):
     slices, rows, cols = density.shape
     block = row.shape[1] // GROUP
     last = rows // block - 1
@@ -293,7 +326,7 @@
             in_specs=[pl.BlockSpec((slices, block, cols), rows_at(d)) for d in (-1, 0, 1)]
             + [pl.BlockSpec((block, cols), mask_at(d)) for d in (-1, 0, 1)]
             + [whole(x) for x in (above, below, col, row, mean)]
-            + [pl.BlockSpec(memory_space=pl.ANY)],
+            + [pl.BlockSpec(memory_space=pl.ANY)] * len(after),
             out_specs=[pl.BlockSpec(shape, lambda i, at: (0, 0, 0)) for shape in shapes],
             scratch_shapes=[
                 pltpu.VMEM((GROUP * LANES, cols), jnp.bfloat16),
@@ -302,7 +335,7 @@
         ),
         out_shape=[jax.ShapeDtypeStruct(shape, jnp.bfloat16) for shape in shapes],
         compiler_params=params(),
-        cost_estimate=cost(count * 2 * 805e6, count * 3e6),
+        cost_estimate=cost(1, 1),
     )(
         jnp.concatenate([ids, jnp.full((1,), last, ids.dtype)]),
         *([density] * 3),
@@ -312,24 +345,25 @@
         col,
         row,
         mean,
-        after,
+        *after,
     )
     out = list(out)
     return [[out.pop(0) for _ in wanted] for wanted in pieces]
 
 
 def project_kernel(count, place, weights, *refs):
-    parts, (amp_out, like_out) = refs[:count], refs[-2:]
+    parts, (amp_out, like_out, token) = refs[:count], refs[-3:]
     zbins = weights.shape[0] // 2
     pencil = jnp.concatenate([x[0] for x in parts], axis=0)
     both = jnp.dot(weights[...], pencil, preferred_element_type=jnp.float32)
     amp = both[:zbins]
     amp_out[...] = amp.astype(jnp.bfloat16)
     like_out[...] = (amp * both[zbins:]).astype(jnp.bfloat16)
-
-
-def project(place, weights, parts, total, earlier):
-    rows, slices, cols = parts[0].shape
+    token[...] = jnp.zeros_like(token)
+
+
+def project(place, weights, parts, rows, total, earlier):
+    _, slices, cols = parts[0][0].shape
     zbins = weights.shape[0] // 2
     count = len(parts)
     shape = jax.ShapeDtypeStruct((zbins, total * cols), jnp.bfloat16)
@@ -340,19 +374,61 @@
             num_scalar_prefetch=1,
             grid=(rows,),
             in_specs=[pl.BlockSpec(weights.shape, lambda i, at: (0, 0))]
-            + [pl.BlockSpec((1, slices, cols), lambda i, at: (i, 0, 0))] * count
+            + [pl.BlockSpec((1, slices, cols), lambda i, at, start=start: (i + start, 0, 0)) for _, start in parts]
             + [pl.BlockSpec(memory_space=pl.ANY)] * len(earlier),
-            out_specs=[pl.BlockSpec((zbins, cols), lambda i, at: (0, i + at[0]))] * 2,
+            out_specs=[pl.BlockSpec((zbins, cols), lambda i, at: (0, i + at[0]))] * 2
+            + [pl.BlockSpec((8, LANES), lambda i, at: (0, 0))],
         ),
-        out_shape=[shape, shape],
+        out_shape=[shape, shape, jax.ShapeDtypeStruct((8, LANES), jnp.float32)],
         input_output_aliases={2 + count + i: i for i in range(len(earlier))},
         compiler_params=params(),
-        cost_estimate=cost(4 * zbins * rows * cols * slices * count, 2 * rows * cols * (slices * count + 2 * zbins)),
-    )(place.reshape(1), weights, *parts, *earlier)
-
-
-EARLY = (4, 6)
-PIECES = ((1, 0, REACH), (0, 0, 5), (0, 5, REACH))
+        cost_estimate=cost(1, 1),
+    )(place.reshape(1), weights, *[x for x, _ in parts], *earlier)
+
+
+def gate_kernel(*refs):
+    pass
+
+
+def gate(x, *earlier):
+    held = pl.BlockSpec(memory_space=pl.ANY)
+    return pl.pallas_call(
+        gate_kernel,
+        name="gate",
+        in_specs=[held] * (1 + len(earlier)),
+        out_specs=held,
+        out_shape=jax.ShapeDtypeStruct(x.shape, x.dtype),
+        input_output_aliases={0: 0},
+        cost_estimate=cost(1, 1),
+    )(x, *earlier)
+
+
+INNER, OUTER, HEAD, TAIL = (1, 0, REACH), (0, 0, REACH), (0, 0, 5), (0, 5, REACH)
+EARLY = (4, 6, 5)
+LATE = (4, 6)
+ORDER = (
+    ("filter", (7, 5, 2), ((6, 0),)),
+    ("send", (7, 0), ((4, 0),)),
+    ("send", (2, 0), ((4, 0),)),
+    ("send", (5, 1), ((4, 0),)),
+    ("filter", (3, 4, 6, 1, 0), ((5, 0),)),
+    ("send", (7, 1), ((5, 0),)),
+    ("send", (2, 1), ((2, 0),)),
+    ("send", (3, 0), ((5, 1), (0, 0))),
+    ("send", (4, "note"), ((5, 1), (0, 0))),
+    ("send", (6, "note"), ((5, 1), (0, 0))),
+    ("send", (5, "note"), ((5, 1), (0, 0))),
+    ("send", (4, 1), ((5, 1), (0, 0))),
+    ("send", (1, 0), ((5, 1), (2, 1))),
+    ("send", (3, 1), ((3, 0),)),
+    ("send", (6, 1), ((7, 0), (0, 0))),
+    ("send", (1, 1), ((3, 0),)),
+    ("project", 0, ()),
+    ("send", (4, 2), ((4, 1), "project 0")),
+    ("send", (6, 2), ((6, 1),)),
+    ("project", 1, ()),
+    ("project", 2, ()),
+)
 
 
 def fast(density, valid, row_taps, col_taps, amp_matrix, like_matrix):
@@ -368,49 +444,58 @@
 
     piece = jax.ShapeDtypeStruct((REACH, slices, cols), jnp.bfloat16)
     centre = jax.ShapeDtypeStruct((slices, LANES), jnp.float32)
-    early, centres, after = [], [], row_taps
-    for k in EARLY:
-        made, about = early_call(
-            early_kernel, "early", me ^ k, density, valid, row_taps, col_taps, (), after, [piece, centre]
+
+    def early(k, after):
+        return early_call(
+            early_kernel, "early", me ^ k, density, valid, terms, (row_taps, col_taps), after, [piece, centre]
         )
-        early.append(made)
-        centres.append(about)
-        after = made
-    own, first, last = masked_sums(density, valid, after)
+
+    made, arrived = {}, {}
+    made[4, 0], about_4 = early(4, row_taps)
+    arrived[4, 0] = swap(made[4, 0], 4)
+    made[6, 0], about_6 = early(6, made[4, 0])
+    own, first, last = masked_sums(density, valid, made[6, 0])
     sums = [own] + [lax.ppermute(own, "tile", [(i, i ^ k) for i in range(tiles)]) for k in range(1, tiles)]
-    above = lax.ppermute(last, "tile", [(i, i + 1) for i in range(tiles - 1)])
-    below = lax.ppermute(first, "tile", [(i + 1, i) for i in range(tiles - 1)])
-    col, row = filter_matrices(row_taps, col_taps, own)
-    mean, *shifts = means(sums, centres)
-
-    filtered = {}
-    after = mean
-    for ks in ((5,), (7, 4, 6, 2, 3, 1, 0)):
-        ids = jnp.stack([me ^ k for k in ks])
-        pieces = [PIECES[1:] if k in EARLY else PIECES for k in ks]
-        got = filter_blocks(ids, pieces, density, valid, above, below, col, row, mean, after)
-        after = got[0][0]
-        for k, made in zip(ks, got):
-            for p, x in zip(range(len(PIECES) - len(made), len(PIECES)), made):
-                filtered[k, p] = x
-    taps = jnp.stack([row_taps, col_taps])
-    arrived = {}
-    for k, made, shift in zip(EARLY, early, shifts):
-        got_taps, got_shift, got = swap(taps, k), swap(shift, k), swap(made, k)
-        (arrived[k, 0],) = early_call(
-            mend_kernel, "mend", me, None, valid, got_taps[0], got_taps[1], (got, got_shift), after, [piece]
-        )
-    for p in range(len(PIECES)):
-        for k in (5, 7, 4, 6, 2, 3, 1):
-            if (k, p) not in arrived:
-                arrived[k, p] = swap(filtered[k, p], k)
-        arrived[0, p] = filtered[0, p]
+    arrived[6, 0] = swap(made[6, 0], 6)
+    mean = means(sums, slices, arrived[4, 0])
+    above = lax.ppermute(gate(last, mean), "tile", [(i, i + 1) for i in range(tiles - 1)])
+    below = lax.ppermute(gate(first, mean), "tile", [(i + 1, i) for i in range(tiles - 1)])
+    made[5, 0], about_5 = early(5, mean)
+    arrived[5, 0] = swap(made[5, 0], 5)
+    col, row = filter_matrices(row_taps, col_taps, made[5, 0])
+    for k, note in zip(EARLY, notes_of(mean, row_taps, col_taps, (about_4, about_6, about_5))):
+        made[k, "note"] = note
+
+    cuts = {k: (INNER, HEAD, TAIL) if k in LATE else (INNER, OUTER) for k in range(peers)}
     weights = jnp.concatenate([amp_matrix, like_matrix], axis=1).T.reshape(-1, peers, slices)
     weights = weights[:, me ^ jnp.arange(peers)].reshape(-1, peers * slices)
     result = []
-    for p, (inner, start, _) in enumerate(PIECES):
-        place = jnp.where((me == peers - 1) != (inner == 1), block - REACH, 0) + start
-        result = project(place, weights, [arrived[k, p] for k in range(peers)], block, result)
+    after = made[5, 0]
+    for what, how, before in ORDER:
+        before = [arrived[x] for x in before]
+        if what == "filter":
+            ids = jnp.stack([me ^ k for k in how])
+            skip = [1 if k in EARLY else 0 for k in how]
+            wanted = [cuts[k][n:] for k, n in zip(how, skip)]
+            got = filter_blocks(ids, wanted, density, valid, above, below, col, row, mean, after, *before)
+            for k, n, parts in zip(how, skip, got):
+                for p, x in enumerate(parts, start=n):
+                    made[k, p] = x
+                    if k == 0:
+                        arrived[k, p] = x
+            after = got[-1][-1]
+        elif what == "send":
+            k, p = how
+            arrived[how] = swap(gate(made[how], *before), k)
+            if p == "note":
+                (arrived[k, 0],) = early_call(
+                    mend_kernel, "mend", me, None, valid, terms, (arrived[how], arrived[k, 0]), after, [piece]
+                )
+        else:
+            inner, start, stop = (INNER, HEAD, TAIL)[how]
+            place = jnp.where((me == peers - 1) != (inner == 1), block - REACH, 0) + start
+            parts = [(arrived[k, how], 0) if k in LATE else (arrived[k, min(how, 1)], start) for k in range(peers)]
+            *result[:], arrived[f"project {how}"] = project(place, weights, parts, stop - start, block, result)
     return tuple(result)
 
 

time: 163 us -> 157 us (0.963)
  waiting for transfers between devices: 39.5 us -> 9.68 us
  local copies, waits for them, and re-layouts: 7.45 us -> 29.7 us
  starting transfers between devices: 60.3 us -> 42.2 us
  Pallas kernels: 52.6 us -> 69.6 us
  other arithmetic: 0.26 us -> 2 us
    ppermute x25 -> x19, waiting for transfers between devices: 39 us -> 5.22 us  [swap(): return lax.ppermute(x, 'cuts', [(i, i ^ k) for i in range(peers)])]
    unnamed x22 -> x122, local copies, waits for them, and re-layouts: 6.7 us -> 28.9 us
    pallas_call x4 -> x6, Pallas kernels: 14 us -> 33.2 us  [early_call(): pl.pallas_call(kernel, name=name, grid_spec=pltpu.PrefetchScalarGridSpec(...]
    ppermute x25 -> x19, starting transfers between devices: 50.6 us -> 34.8 us  [swap(): return lax.ppermute(x, 'cuts', [(i, i ^ k) for i in range(peers)])]
    pallas_call x2, Pallas kernels: 25.7 us -> 21 us  [filter_blocks(): pl.pallas_call(functools.partial(filter_kernel, pieces), name='filter', g...]
    ppermute x3, waiting for transfers between devices: 0.01 us -> 3.36 us  [fast(): lax.ppermute(own, 'tile', [(i, i ^ k) for i in range(tiles)])]
    pallas_call x1, Pallas kernels: 1.58 us -> 4.19 us  [masked_sums(): pl.pallas_call(sums_kernel, name='sums', grid=(rows // step,), in_specs=[...]
    another operation x2 -> x3, other arithmetic: 0.15 us -> 1.9 us  [early_call(): jnp.stack([ids, jnp.full_like(ids, last)]).astype(jnp.int32)]
  transfers between devices with their start and end apart: 30 -> 24, of which waited for: 7 -> 8; matrix products, arithmetic and copies ran while one was open for 1% -> 1% of each run, Pallas kernels for 26% -> 40%
where the time goes in v3:
time: 157 us; the launch traced here: 154 us
  Pallas kernels  69.6 us (44%)
  starting transfers between devices  42.2 us (27%)
  local copies, waits for them, and re-layouts  29.7 us (19%)
  waiting for transfers between devices  9.68 us (6%)
  other arithmetic  2 us (1%)
    ppermute x19, starting transfers between devices, swap(): return lax.ppermute(x, 'cuts', [(i, i ^ k) for i in range(peers)])  34.8 us
    pallas_call x6, Pallas kernels, early_call(): pl.pallas_call(kernel, name=name, grid_spec=pltpu.PrefetchScalarGridSpec(...  33.2 us
    unnamed x122, local copies, waits for them, and re-layouts  28.9 us
    pallas_call x2, Pallas kernels, filter_blocks(): pl.pallas_call(functools.partial(filter_kernel, pieces), name='filter', g...  21 us
    pallas_call x3, Pallas kernels, project(): pl.pallas_call(functools.partial(project_kernel, count), name='project',...  9.64 us
    ppermute x19, waiting for transfers between devices, swap(): return lax.ppermute(x, 'cuts', [(i, i ^ k) for i in range(peers)])  5.22 us
    pallas_call x1, Pallas kernels, masked_sums(): pl.pallas_call(sums_kernel, name='sums', grid=(rows // step,), in_specs=[...  4.19 us
    ppermute x3, starting transfers between devices, fast(): lax.ppermute(own, 'tile', [(i, i ^ k) for i in range(tiles)])  3.49 us
  transfers between devices with their start and end apart: 24, of which 8 were waited for; matrix products, arithmetic and copies ran while one was open for 1% of the time, Pallas kernels for 40%

profile of v3, /device:TPU:0, one launch (start us, length us, event | category | flops | bytes accessed | tf_op | source)
XLA Modules:
  0.0 154.3 jit_solution(12213464691863094126)
XLA Ops:
  1.3 5.9 %early.3 = (bf16[8,16,1024]{2,1,0:T(8,128)(2,1)}, f32[16,128]{1,0:T(8,128)}) custom-call(s32[2]{0:T(128)} %get-tuple-element.74.ids, bf16[16,128,1024]{2,1,0:T(8,128)(2,1)} %after.5, bf16[16,128,1024]{2,1,0:T(8,128)(2,1)} %after.5, s32[128,1024]{1,0:T(8,128)} %mask_two.11, s32[128,1024]{1,0:T(8,128)} %mask_two.11, bf16[4,16,17]{2,1,0:T(8,128)(2,1)} %row_taps.9, ...), custom_call_target="tpu_custom_call" | custom-call | flops 1 | bytes 1 | tf_op jit(solution)/shard_map/early/pallas_call | solution.py:160
  7.2 4.0 %collective-permute-start.3 = (bf16[8,16,1024]{2,1,0:T(8,128)(2,1)}, bf16[8,16,1024]{2,1,0:T(8,128)(2,1)S(1)}, u32[]{:S(2)}, u32[]{:S(2)}) collective-permute-start(bf16[8,16,1024]{2,1,0:T(8,128)(2,1)} %get-tuple-element.38.after), channel_id=1, source_target_pairs={{0,4},{1,5},{2,6},{3,7},{4,0},{5,1},{6,2},{7,3},{8,12},{9,13},{10,... | collective-permute-start | bytes 786440 | tf_op jit(solution)/shard_map/ppermute | solution.py:443
  11.2 5.9 %early.4 = (bf16[8,16,1024]{2,1,0:T(8,128)(2,1)}, f32[16,128]{1,0:T(8,128)}) custom-call(s32[2]{0:T(128)} %get-tuple-element.75.ids, bf16[16,128,1024]{2,1,0:T(8,128)(2,1)} %after.5, bf16[16,128,1024]{2,1,0:T(8,128)(2,1)} %after.5, s32[128,1024]{1,0:T(8,128)} %mask_two.11, s32[128,1024]{1,0:T(8,128)} %mask_two.11, bf16[4,16,17]{2,1,0:T(8,128)(2,1)} %row_taps.9, ...), custom_call_target="tpu_custom_call" | custom-call | flops 1 | bytes 1 | tf_op jit(solution)/shard_map/early/pallas_call | solution.py:160
  17.2 4.2 %sums.1 = (f32[24,128]{1,0:T(8,128)}, bf16[17,8,1024]{2,1,0:T(8,128)(2,1)}, bf16[17,8,1024]{2,1,0:T(8,128)(2,1)}) custom-call(bf16[16,128,1024]{2,1,0:T(8,128)(2,1)} %after.5, s32[128,1024]{1,0:T(8,128)} %mask_two.11, bf16[8,16,1024]{2,1,0:T(8,128)(2,1)} %get-tuple-element.39.after), custom_call_target="tpu_custom_call" | custom-call | flops 1 | bytes 1 | tf_op jit(solution)/shard_map/sums/pallas_call | solution.py:212
  21.4 2.4 %collective-permute-start.2 = (f32[24,128]{1,0:T(8,128)}, f32[24,128]{1,0:T(8,128)S(1)}, u32[]{:S(2)}, u32[]{:S(2)}) collective-permute-start(f32[24,128]{1,0:T(8,128)} %get-tuple-element.41.refs_0_), channel_id=1, source_target_pairs={{0,24},{8,16},{16,8},{24,0},{1,25},{9,17},{17,9},{25,1},{2,26},{10... | collective-permute-start | bytes 36872 | tf_op jit(solution)/shard_map/ppermute | solution.py:458
  29.6 2.5 %collective-permute-start.4 = (bf16[17,8,1024]{2,1,0:T(8,128)(2,1)}, bf16[17,8,1024]{2,1,0:T(8,128)(2,1)S(1)}, u32[]{:S(2)}, u32[]{:S(2)}) collective-permute-start(bf16[17,8,1024]{2,1,0:T(8,128)(2,1)} %gate.18), channel_id=1, source_target_pairs={{0,8},{8,16},{16,24},{1,9},{9,17},{17,25},{2,10},{10,18},{18,26},{... | collective-permute-start | bytes 835592 | tf_op jit(solution)/shard_map/ppermute | solution.py:461
  35.7 6.0 %early.5 = (bf16[8,16,1024]{2,1,0:T(8,128)(2,1)}, f32[16,128]{1,0:T(8,128)}) custom-call(s32[2]{0:T(128)} %pad_add_fusion.1.ids, bf16[16,128,1024]{2,1,0:T(8,128)(2,1)} %after.5, bf16[16,128,1024]{2,1,0:T(8,128)(2,1)} %after.5, s32[128,1024]{1,0:T(8,128)} %mask_two.11, s32[128,1024]{1,0:T(8,128)} %mask_two.11, bf16[4,16,17]{2,1,0:T(8,128)(2,1)} %row_taps.9, ...), custom_call_target="tpu_custom_call" | custom-call | flops 1 | bytes 1 | tf_op jit(solution)/shard_map/early/pallas_call | solution.py:160
  45.3 2.5 %copy-done = bf16[16,128,1024]{2,1,0:T(8,128)(2,1)S(1)} copy-done((bf16[16,128,1024]{2,1,0:T(8,128)(2,1)S(1)}, bf16[16,128,1024]{2,1,0:T(8,128)(2,1)}, u32[]{:S(2)}) %copy-start) | copy-done | bytes 4194328
  48.8 7.9 %filter.2 = (bf16[8,16,1024]{2,1,0:T(8,128)(2,1)S(1)}, bf16[8,16,1024]{2,1,0:T(8,128)(2,1)S(1)}, bf16[8,16,1024]{2,1,0:T(8,128)(2,1)S(1)}, bf16[8,16,1024]{2,1,0:T(8,128)(2,1)S(1)}, bf16[8,16,1024]{2,1,0:T(8,128)(2,1)S(1)}) custom-call(s32[4]{0:T(128)S(1)} %pad_add_fusion.4.ids, bf16[16,128,1024]{2,1,0:T(8,128)(2,1)S(1)} %copy-done, ...), custom_call_target="tpu_custom_call" | custom-call | flops 1 | bytes 1 | tf_op jit(solution)/shard_map/filter/pallas_call | solution.py:320
  59.6 7.1 %collective-permute-start.11 = (bf16[8,16,1024]{2,1,0:T(8,128)(2,1)}, bf16[8,16,1024]{2,1,0:T(8,128)(2,1)S(1)}, u32[]{:S(2)}, u32[]{:S(2)}) collective-permute-start(bf16[8,16,1024]{2,1,0:T(8,128)(2,1)} %gate.23), channel_id=1, source_target_pairs={{0,2},{1,3},{2,0},{3,1},{4,6},{5,7},{6,4},{7,5},{8,10},{9,11},{10,... | collective-permute-start | bytes 786440 | tf_op jit(solution)/shard_map/ppermute | solution.py:443
  66.6 2.1 %collective-permute-start.19 = (bf16[8,16,1024]{2,1,0:T(8,128)(2,1)}, bf16[8,16,1024]{2,1,0:T(8,128)(2,1)S(1)}, u32[]{:S(2)}, u32[]{:S(2)}) collective-permute-start(bf16[8,16,1024]{2,1,0:T(8,128)(2,1)} %gate.31), channel_id=1, source_target_pairs={{0,7},{1,6},{2,5},{3,4},{4,3},{5,2},{6,1},{7,0},{8,15},{9,14},{10,... | collective-permute-start | bytes 786440 | tf_op jit(solution)/shard_map/ppermute | solution.py:443
  68.8 2.3 %copy-done.1 = bf16[16,128,1024]{2,1,0:T(8,128)(2,1)S(1)} copy-done((bf16[16,128,1024]{2,1,0:T(8,128)(2,1)S(1)}, bf16[16,128,1024]{2,1,0:T(8,128)(2,1)}, u32[]{:S(2)}) %copy-start.1) | copy-done | bytes 4194328
  71.1 2.2 %copy-done.4 = bf16[16,256,512]{2,1,0:T(8,128)(2,1)S(1)} copy-done((bf16[16,256,512]{2,1,0:T(8,128)(2,1)S(1)}, bf16[16,256,512]{2,1,0:T(8,128)(2,1)}, u32[]{:S(2)}) %copy-start.4) | copy-done | bytes 4194328
  73.3 13.1 %filter.3 = (bf16[8,16,1024]{2,1,0:T(8,128)(2,1)S(1)}, bf16[8,16,1024]{2,1,0:T(8,128)(2,1)S(1)}, bf16[5,16,1024]{2,1,0:T(8,128)(2,1)S(1)}, bf16[3,16,1024]{2,1,0...) custom-call(s32[6]{0:T(128)S(1)} %concatenate.10.ids, ...), custom_call_target="tpu_custom_call" | custom-call | flops 1 | bytes 1 | tf_op jit(solution)/shard_map/filter/pallas_call | solution.py:320
  102.6 2.7 %collective-permute-start.18 = (f32[9,16,128]{2,1,0:T(8,128)}, f32[9,16,128]{2,1,0:T(8,128)S(1)}, u32[]{:S(2)}, u32[]{:S(2)}) collective-permute-start(f32[9,16,128]{2,1,0:T(8,128)} %gate.30), channel_id=1, source_target_pairs={{0,6},{1,7},{2,4},{3,5},{4,2},{5,3},{6,0},{7,1},{8,14},{9,15},{10,... | collective-permute-start | bytes 221192 | tf_op jit(solution)/shard_map/ppermute | solution.py:443
  107.3 5.7 %collective-permute-start.15 = (bf16[8,16,1024]{2,1,0:T(8,128)(2,1)}, bf16[8,16,1024]{2,1,0:T(8,128)(2,1)S(1)}, u32[]{:S(2)}, u32[]{:S(2)}) collective-permute-start(bf16[8,16,1024]{2,1,0:T(8,128)(2,1)} %gate.27), channel_id=1, source_target_pairs={{0,1},{1,0},{2,3},{3,2},{4,5},{5,4},{6,7},{7,6},{8,9},{9,8},{10,11... | collective-permute-start | bytes 786440 | tf_op jit(solution)/shard_map/ppermute | solution.py:443
  113.1 3.2 %collective-permute-start.23 = (bf16[8,16,1024]{2,1,0:T(8,128)(2,1)}, bf16[8,16,1024]{2,1,0:T(8,128)(2,1)S(1)}, u32[]{:S(2)}, u32[]{:S(2)}) collective-permute-start(bf16[8,16,1024]{2,1,0:T(8,128)(2,1)} %gate.35), channel_id=1, source_target_pairs={{0,7},{1,6},{2,5},{3,4},{4,3},{5,2},{6,1},{7,0},{8,15},{9,14},{10,... | collective-permute-start | bytes 786440 | tf_op jit(solution)/shard_map/ppermute | solution.py:443
  120.1 5.1 %mend.3.refs_4_ = bf16[8,16,1024]{2,1,0:T(8,128)(2,1)} custom-call(s32[2]{0:T(128)} %pad_add_fusion.ids, s32[128,1024]{1,0:T(8,128)} %mask_two.11, s32[128,1024]{1,0:T(8,128)} %mask_two.11, f32[9,16,128]{2,1,0:T(8,128)} %copy-done.57, bf16[8,16,1024]{2,1,0:T(8,128)(2,1)} %copy-done.9, bf16[8,16,1024]{2,1,0:T(8,128)(2,1)} %copy-done.10), custom_call_target="tpu_custom_call" | custom-call | flops 1 | bytes 1 | tf_op jit(solution)/shard_map/mend/pallas_call | solution.py:160
  125.3 5.1 %mend.4.refs_5_ = bf16[8,16,1024]{2,1,0:T(8,128)(2,1)} custom-call(s32[2]{0:T(128)} %pad_add_fusion.ids, s32[128,1024]{1,0:T(8,128)} %mask_two.11, s32[128,1024]{1,0:T(8,128)} %mask_two.11, f32[9,16,128]{2,1,0:T(8,128)} %collective-permute-done.17.note, bf16[8,16,1024]{2,1,0:T(8,128)(2,1)} %copy-done.12, bf16[8,16,1024]{2,1,0:T(8,128)(2,1)} %copy-done.10), custom_call_target="tpu_custom_call" | custom-call | flops 1 | bytes 1 | tf_op jit(solution)/shard_map/mend/pallas_call | solution.py:160
  130.4 5.0 %mend.5.refs_6_ = bf16[8,16,1024]{2,1,0:T(8,128)(2,1)} custom-call(s32[2]{0:T(128)} %pad_add_fusion.ids, s32[128,1024]{1,0:T(8,128)} %mask_two.11, s32[128,1024]{1,0:T(8,128)} %mask_two.11, f32[9,16,128]{2,1,0:T(8,128)} %copy-done.58, bf16[8,16,1024]{2,1,0:T(8,128)(2,1)} %copy-done.20, bf16[8,16,1024]{2,1,0:T(8,128)(2,1)} %copy-done.10), custom_call_target="tpu_custom_call" | custom-call | flops 1 | bytes 1 | tf_op jit(solution)/shard_map/mend/pallas_call | solution.py:160
  135.5 2.1 %collective-permute-start.22 = (bf16[3,16,1024]{2,1,0:T(8,128)(2,1)}, bf16[3,16,1024]{2,1,0:T(8,128)(2,1)S(1)}, u32[]{:S(2)}, u32[]{:S(2)}) collective-permute-start(bf16[3,16,1024]{2,1,0:T(8,128)(2,1)} %gate.34), channel_id=1, source_target_pairs={{0,6},{1,7},{2,4},{3,5},{4,2},{5,3},{6,0},{7,1},{8,14},{9,15},{10,... | collective-permute-start | bytes 294920 | tf_op jit(solution)/shard_map/ppermute | solution.py:443
  139.5 4.5 %project.3 = (bf16[128,16384]{1,0:T(8,128)(2,1)}, bf16[128,16384]{1,0:T(8,128)(2,1)}, f32[8,128]{1,0:T(8,128)S(1)}) custom-call(s32[1]{0:T(128)} %bitcast.14.place, bf16[256,128]{1,0:T(8,128)(2,1)S(1)} %copy.32.weights, bf16[8,16,1024]{2,1,0:T(8,128)(2,1)S(1)} %copy-done.8, bf16[8,16,1024]{2,1,0:T(8,128)(2,1)S(1)} %collective-permute-done.15.refs_1_, ...), custom_call_target="tpu_custom_call" | custom-call | flops 1 | bytes 1 | tf_op jit(solution)/shard_map/project/pallas_call | solution.py:370
  147.1 3.1 %project.4 = (bf16[128,16384]{1,0:T(8,128)(2,1)}, bf16[128,16384]{1,0:T(8,128)(2,1)}, f32[8,128]{1,0:T(8,128)}) custom-call(s32[1]{0:T(128)} %bitcast.15.place, bf16[256,128]{1,0:T(8,128)(2,1)S(1)} %copy.32.weights, bf16[8,16,1024]{2,1,0:T(8,128)(2,1)S(1)} %copy-done.11, ...), custom_call_target="tpu_custom_call", output_to_operand_aliasing={{0}: (10, {}), {1}: (11, {})} | custom-call | flops 1 | bytes 1 | tf_op jit(solution)/shard_map/project/pallas_call | solution.py:370
  152.2 2.1 %project.5 = (bf16[128,16384]{1,0:T(8,128)(2,1)}, bf16[128,16384]{1,0:T(8,128)(2,1)}, f32[8,128]{1,0:T(8,128)}) custom-call(s32[1]{0:T(128)} %bitcast.place, bf16[256,128]{1,0:T(8,128)(2,1)S(1)} %copy.32.weights, bf16[8,16,1024]{2,1,0:T(8,128)(2,1)S(1)} %copy-done.11, ...), custom_call_target="tpu_custom_call", output_to_operand_aliasing={{0}: (10, {}), {1}: (11, {})} | custom-call | flops 1 | bytes 1 | tf_op jit(solution)/shard_map/project/pallas_call | solution.py:370
  (189 shorter events, 46.4 us)
Async XLA Ops:
  7.2 21.0 %collective-permute-start.3 = (bf16[8,16,1024]{2,1,0:T(8,128)(2,1)}, bf16[8,16,1024]{2,1,0:T(8,128)(2,1)S(1)}, u32[]{:S(2)}, u32[]{:S(2)}) collective-permute-start(bf16[8,16,1024]{2,1,0:T(8,128)(2,1)} %get-tuple-element.38.after), channel_id=1, source_target_pairs={{0,4},{1,5},{2,6},{3,7},{4,0},{5,1},{6,2},{7,3},{8,12},{9,13},{10,... | collective-permute-start | bytes 786440 | tf_op jit(solution)/shard_map/ppermute | solution.py:443
  21.4 4.8 %collective-permute-start.2 = (f32[24,128]{1,0:T(8,128)}, f32[24,128]{1,0:T(8,128)S(1)}, u32[]{:S(2)}, u32[]{:S(2)}) collective-permute-start(f32[24,128]{1,0:T(8,128)} %get-tuple-element.41.refs_0_), channel_id=1, source_target_pairs={{0,24},{8,16},{16,8},{24,0},{1,25},{9,17},{17,9},{25,1},{2,26},{10... | collective-permute-start | bytes 36872 | tf_op jit(solution)/shard_map/ppermute | solution.py:458
  23.8 3.9 %collective-permute-start.1 = (f32[24,128]{1,0:T(8,128)}, f32[24,128]{1,0:T(8,128)S(1)}, u32[]{:S(2)}, u32[]{:S(2)}) collective-permute-start(f32[24,128]{1,0:T(8,128)} %get-tuple-element.41.refs_0_), channel_id=1, source_target_pairs={{0,16},{8,24},{16,0},{24,8},{1,17},{9,25},{17,1},{25,9},{2,18},{10... | collective-permute-start | bytes 36872 | tf_op jit(solution)/shard_map/ppermute | solution.py:458
  24.3 3.9 %collective-permute-start = (f32[24,128]{1,0:T(8,128)}, f32[24,128]{1,0:T(8,128)S(1)}, u32[]{:S(2)}, u32[]{:S(2)}) collective-permute-start(f32[24,128]{1,0:T(8,128)} %get-tuple-element.41.refs_0_), channel_id=1, source_target_pairs={{0,8},{8,0},{16,24},{24,16},{1,9},{9,1},{17,25},{25,17},{2,10},{10... | collective-permute-start | bytes 36872 | tf_op jit(solution)/shard_map/ppermute | solution.py:458
  29.6 14.6 %collective-permute-start.4 = (bf16[17,8,1024]{2,1,0:T(8,128)(2,1)}, bf16[17,8,1024]{2,1,0:T(8,128)(2,1)S(1)}, u32[]{:S(2)}, u32[]{:S(2)}) collective-permute-start(bf16[17,8,1024]{2,1,0:T(8,128)(2,1)} %gate.18), channel_id=1, source_target_pairs={{0,8},{8,16},{16,24},{1,9},{9,17},{17,25},{2,10},{10,18},{18,26},{... | collective-permute-start | bytes 835592 | tf_op jit(solution)/shard_map/ppermute | solution.py:461
  32.1 13.2 %collective-permute-start.5 = (bf16[17,8,1024]{2,1,0:T(8,128)(2,1)}, bf16[17,8,1024]{2,1,0:T(8,128)(2,1)S(1)}, u32[]{:S(2)}, u32[]{:S(2)}) collective-permute-start(bf16[17,8,1024]{2,1,0:T(8,128)(2,1)} %gate.19), channel_id=1, source_target_pairs={{8,0},{16,8},{24,16},{9,1},{17,9},{25,17},{10,2},{18,10},{26,18},{... | collective-permute-start | bytes 835592 | tf_op jit(solution)/shard_map/ppermute | solution.py:462
  33.6 10.6 %collective-permute-start.6 = (bf16[8,16,1024]{2,1,0:T(8,128)(2,1)S(1)}, bf16[8,16,1024]{2,1,0:T(8,128)(2,1)S(1)}, u32[]{:S(2)}, u32[]{:S(2)}) collective-permute-start(bf16[8,16,1024]{2,1,0:T(8,128)(2,1)S(1)} %copy-done.56), channel_id=1, source_target_pairs={{0,6},{1,7},{2,4},{3,5},{4,2},{5,3},{6,0},{7,1},{8,14},{9,15},{10,... | collective-permute-start | bytes 786440 | tf_op jit(solution)/shard_map/ppermute | solution.py:443
  41.7 27.1 %collective-permute-start.7 = (bf16[8,16,1024]{2,1,0:T(8,128)(2,1)}, bf16[8,16,1024]{2,1,0:T(8,128)(2,1)S(1)}, u32[]{:S(2)}, u32[]{:S(2)}) collective-permute-start(bf16[8,16,1024]{2,1,0:T(8,128)(2,1)} %get-tuple-element.43.after.refs_5_), channel_id=1, source_target_pairs={{0,5},{1,4},{2,7},{3,6},{4,1},{5,0},{6,3},{7,2},{8,13},{9,12},{10,... | collective-permute-start | bytes 786440 | tf_op jit(solution)/shard_map/ppermute | solution.py:443
  59.6 33.7 %collective-permute-start.11 = (bf16[8,16,1024]{2,1,0:T(8,128)(2,1)}, bf16[8,16,1024]{2,1,0:T(8,128)(2,1)S(1)}, u32[]{:S(2)}, u32[]{:S(2)}) collective-permute-start(bf16[8,16,1024]{2,1,0:T(8,128)(2,1)} %gate.23), channel_id=1, source_target_pairs={{0,2},{1,3},{2,0},{3,1},{4,6},{5,7},{6,4},{7,5},{8,10},{9,11},{10,... | collective-permute-start | bytes 786440 | tf_op jit(solution)/shard_map/ppermute | solution.py:443
  66.6 28.5 %collective-permute-start.8 = (bf16[8,16,1024]{2,1,0:T(8,128)(2,1)}, bf16[8,16,1024]{2,1,0:T(8,128)(2,1)S(1)}, u32[]{:S(2)}, u32[]{:S(2)}) collective-permute-start(bf16[8,16,1024]{2,1,0:T(8,128)(2,1)} %gate.20), channel_id=1, source_target_pairs={{0,5},{1,4},{2,7},{3,6},{4,1},{5,0},{6,3},{7,2},{8,13},{9,12},{10,... | collective-permute-start | bytes 786440 | tf_op jit(solution)/shard_map/ppermute | solution.py:443
  66.6 29.2 %collective-permute-start.19 = (bf16[8,16,1024]{2,1,0:T(8,128)(2,1)}, bf16[8,16,1024]{2,1,0:T(8,128)(2,1)S(1)}, u32[]{:S(2)}, u32[]{:S(2)}) collective-permute-start(bf16[8,16,1024]{2,1,0:T(8,128)(2,1)} %gate.31), channel_id=1, source_target_pairs={{0,7},{1,6},{2,5},{3,4},{4,3},{5,2},{6,1},{7,0},{8,15},{9,14},{10,... | collective-permute-start | bytes 786440 | tf_op jit(solution)/shard_map/ppermute | solution.py:443
  94.0 8.7 %collective-permute-start.12 = (bf16[8,16,1024]{2,1,0:T(8,128)(2,1)}, bf16[8,16,1024]{2,1,0:T(8,128)(2,1)S(1)}, u32[]{:S(2)}, u32[]{:S(2)}) collective-permute-start(bf16[8,16,1024]{2,1,0:T(8,128)(2,1)} %gate.24), channel_id=1, source_target_pairs={{0,2},{1,3},{2,0},{3,1},{4,6},{5,7},{6,4},{7,5},{8,10},{9,11},{10,... | collective-permute-start | bytes 786440 | tf_op jit(solution)/shard_map/ppermute | solution.py:443
  95.8 11.5 %collective-permute-start.9 = (bf16[8,16,1024]{2,1,0:T(8,128)(2,1)}, bf16[8,16,1024]{2,1,0:T(8,128)(2,1)S(1)}, u32[]{:S(2)}, u32[]{:S(2)}) collective-permute-start(bf16[8,16,1024]{2,1,0:T(8,128)(2,1)} %gate.21), channel_id=1, source_target_pairs={{0,3},{1,2},{2,1},{3,0},{4,7},{5,6},{6,5},{7,4},{8,11},{9,10},{10,... | collective-permute-start | bytes 786440 | tf_op jit(solution)/shard_map/ppermute | solution.py:443
  96.5 20.5 %collective-permute-start.21 = (bf16[5,16,1024]{2,1,0:T(8,128)(2,1)}, bf16[5,16,1024]{2,1,0:T(8,128)(2,1)S(1)}, u32[]{:S(2)}, u32[]{:S(2)}) collective-permute-start(bf16[5,16,1024]{2,1,0:T(8,128)(2,1)} %gate.33), channel_id=1, source_target_pairs={{0,6},{1,7},{2,4},{3,5},{4,2},{5,3},{6,0},{7,1},{8,14},{9,15},{10,... | collective-permute-start | bytes 491528 | tf_op jit(solution)/shard_map/ppermute | solution.py:443
  100.6 12.5 %collective-permute-start.16 = (f32[9,16,128]{2,1,0:T(8,128)}, f32[9,16,128]{2,1,0:T(8,128)S(1)}, u32[]{:S(2)}, u32[]{:S(2)}) collective-permute-start(f32[9,16,128]{2,1,0:T(8,128)} %gate.28), channel_id=1, source_target_pairs={{0,4},{1,5},{2,6},{3,7},{4,0},{5,1},{6,2},{7,3},{8,12},{9,13},{10,... | collective-permute-start | bytes 221192 | tf_op jit(solution)/shard_map/ppermute | solution.py:443
  100.9 15.4 %collective-permute-start.17 = (f32[9,16,128]{2,1,0:T(8,128)}, f32[9,16,128]{2,1,0:T(8,128)}, u32[]{:S(2)}, u32[]{:S(2)}) collective-permute-start(f32[9,16,128]{2,1,0:T(8,128)} %gate.29), channel_id=1, source_target_pairs={{0,5},{1,4},{2,7},{3,6},{4,1},{5,0},{6,3},{7,2},{8,13},{9,12},{10,... | collective-permute-start | bytes 221192 | tf_op jit(solution)/shard_map/ppermute | solution.py:443
  102.6 14.2 %collective-permute-start.18 = (f32[9,16,128]{2,1,0:T(8,128)}, f32[9,16,128]{2,1,0:T(8,128)S(1)}, u32[]{:S(2)}, u32[]{:S(2)}) collective-permute-start(f32[9,16,128]{2,1,0:T(8,128)} %gate.30), channel_id=1, source_target_pairs={{0,6},{1,7},{2,4},{3,5},{4,2},{5,3},{6,0},{7,1},{8,14},{9,15},{10,... | collective-permute-start | bytes 221192 | tf_op jit(solution)/shard_map/ppermute | solution.py:443
  107.3 28.2 %collective-permute-start.15 = (bf16[8,16,1024]{2,1,0:T(8,128)(2,1)}, bf16[8,16,1024]{2,1,0:T(8,128)(2,1)S(1)}, u32[]{:S(2)}, u32[]{:S(2)}) collective-permute-start(bf16[8,16,1024]{2,1,0:T(8,128)(2,1)} %gate.27), channel_id=1, source_target_pairs={{0,1},{1,0},{2,3},{3,2},{4,5},{5,4},{6,7},{7,6},{8,9},{9,8},{10,11... | collective-permute-start | bytes 786440 | tf_op jit(solution)/shard_map/ppermute | solution.py:443
  113.1 32.1 %collective-permute-start.23 = (bf16[8,16,1024]{2,1,0:T(8,128)(2,1)}, bf16[8,16,1024]{2,1,0:T(8,128)(2,1)S(1)}, u32[]{:S(2)}, u32[]{:S(2)}) collective-permute-start(bf16[8,16,1024]{2,1,0:T(8,128)(2,1)} %gate.35), channel_id=1, source_target_pairs={{0,7},{1,6},{2,5},{3,4},{4,3},{5,2},{6,1},{7,0},{8,15},{9,14},{10,... | collective-permute-start | bytes 786440 | tf_op jit(solution)/shard_map/ppermute | solution.py:443
  116.3 28.2 %collective-permute-start.14 = (bf16[5,16,1024]{2,1,0:T(8,128)(2,1)}, bf16[5,16,1024]{2,1,0:T(8,128)(2,1)S(1)}, u32[]{:S(2)}, u32[]{:S(2)}) collective-permute-start(bf16[5,16,1024]{2,1,0:T(8,128)(2,1)} %gate.26), channel_id=1, source_target_pairs={{0,4},{1,5},{2,6},{3,7},{4,0},{5,1},{6,2},{7,3},{8,12},{9,13},{10,... | collective-permute-start | bytes 491528 | tf_op jit(solution)/shard_map/ppermute | solution.py:443
  116.8 28.4 %collective-permute-start.10 = (bf16[8,16,1024]{2,1,0:T(8,128)(2,1)}, bf16[8,16,1024]{2,1,0:T(8,128)(2,1)S(1)}, u32[]{:S(2)}, u32[]{:S(2)}) collective-permute-start(bf16[8,16,1024]{2,1,0:T(8,128)(2,1)} %gate.22), channel_id=1, source_target_pairs={{0,1},{1,0},{2,3},{3,2},{4,5},{5,4},{6,7},{7,6},{8,9},{9,8},{10,11... | collective-permute-start | bytes 786440 | tf_op jit(solution)/shard_map/ppermute | solution.py:443
  117.0 28.2 %collective-permute-start.13 = (bf16[8,16,1024]{2,1,0:T(8,128)(2,1)}, bf16[8,16,1024]{2,1,0:T(8,128)(2,1)S(1)}, u32[]{:S(2)}, u32[]{:S(2)}) collective-permute-start(bf16[8,16,1024]{2,1,0:T(8,128)(2,1)} %gate.25), channel_id=1, source_target_pairs={{0,3},{1,2},{2,1},{3,0},{4,7},{5,6},{6,5},{7,4},{8,11},{9,10},{10,... | collective-permute-start | bytes 786440 | tf_op jit(solution)/shard_map/ppermute | solution.py:443
  135.5 14.7 %collective-permute-start.22 = (bf16[3,16,1024]{2,1,0:T(8,128)(2,1)}, bf16[3,16,1024]{2,1,0:T(8,128)(2,1)S(1)}, u32[]{:S(2)}, u32[]{:S(2)}) collective-permute-start(bf16[3,16,1024]{2,1,0:T(8,128)(2,1)} %gate.34), channel_id=1, source_target_pairs={{0,6},{1,7},{2,4},{3,5},{4,2},{5,3},{6,0},{7,1},{8,14},{9,15},{10,... | collective-permute-start | bytes 294920 | tf_op jit(solution)/shard_map/ppermute | solution.py:443
  145.2 7.0 %collective-permute-start.20 = (bf16[3,16,1024]{2,1,0:T(8,128)(2,1)}, bf16[3,16,1024]{2,1,0:T(8,128)(2,1)S(1)}, u32[]{:S(2)}, u32[]{:S(2)}) collective-permute-start(bf16[3,16,1024]{2,1,0:T(8,128)(2,1)} %gate.32), channel_id=1, source_target_pairs={{0,4},{1,5},{2,6},{3,7},{4,0},{5,1},{6,2},{7,3},{8,12},{9,13},{10,... | collective-permute-start | bytes 294920 | tf_op jit(solution)/shard_map/ppermute | solution.py:443
  (61 other events, 507.5 us)

commit v4 on v3

--- a/solution.py
+++ b/solution.py
@@ -15,8 +15,20 @@
 HALO = 2 * REACH
 
 
-def params(mib=40):
+def params(mib=28):
     return pltpu.CompilerParams(vmem_limit_bytes=mib * MIB)
+
+
+def hbm(shape, dtype):
+    return pltpu.HBM(shape, dtype)
+
+
+def held(x):
+    return pltpu.with_memory_space_constraint(x, pltpu.HBM)
+
+
+def anywhere():
+    return pl.BlockSpec(memory_space=pl.ANY)
 
 
 def cost(flops, moved):
@@ -65,24 +77,6 @@
     return (slices, 2 * LANES, terms * LANES), (slices // GROUP, rows * GROUP, GROUP * LANES)
 
 
-def matrices_kernel(row_taps, col_taps, after, col_out, row_out):
-    build_matrices(listed(row_taps), listed(col_taps), col_out, row_out)
-
-
-def filter_matrices(row_taps, col_taps, after):
-    terms, slices, _ = row_taps.shape
-    shapes = matrix_shapes(terms, slices, LANES // terms - HALO)
-    vmem = pl.BlockSpec(memory_space=pltpu.VMEM)
-    return pl.pallas_call(
-        matrices_kernel,
-        name="matrices",
-        in_specs=[vmem, vmem, pl.BlockSpec(memory_space=pl.ANY)],
-        out_shape=[jax.ShapeDtypeStruct(shape, jnp.bfloat16) for shape in shapes],
-        compiler_params=params(),
-        cost_estimate=cost(1, 1),
-    )(row_taps, col_taps, after)
-
-
 def convolve(field, col, row, tall, rows):
     slices, _, wide = col.shape
     terms = wide // LANES
@@ -105,81 +99,7 @@
     return jnp.concatenate(parts, axis=1)
 
 
-def inner_rows(first, second, last):
-    both = jnp.concatenate([first.astype(jnp.float32), second.astype(jnp.float32)], axis=0)
-    rows = both.shape[0] - REACH
-    chosen = jnp.where(last, both[REACH:], both[:rows])
-    return jnp.concatenate([chosen, jnp.zeros((REACH, both.shape[1]), jnp.float32)], axis=0)
-
-
-def early_kernel(ids, one, two, mask_one, mask_two, row_taps, col_taps, after, out, centre, col, row, tall):
-    slices = one.shape[0]
-    build_matrices(listed(row_taps), listed(col_taps), col, row)
-    last = ids[0] == ids[1]
-    mask = inner_rows(mask_one[...], mask_two[...], last)
-
-    def folded(x):
-        x = x.reshape(x.shape[0] // 8, 8, x.shape[1]).sum(axis=0)
-        x = sum(x[:, c : c + LANES] for c in range(0, x.shape[1], LANES))
-        return jnp.sum(x, axis=0, keepdims=True)
-
-    sums = jnp.concatenate([folded(mask * inner_rows(one[s], two[s], last)) for s in range(slices)], axis=0)
-    mean = jnp.sum(sums, axis=1, keepdims=True) / jnp.sum(folded(mask), axis=1, keepdims=True)
-    centre[...] = jnp.broadcast_to(mean, centre.shape)
-    field = convolve(
-        lambda s: mask * (inner_rows(one[s], two[s], last) - mean[s : s + 1]), col, row, tall, out.shape[0]
-    )
-    out[...] = field.astype(jnp.bfloat16)
-
-
-def mend_kernel(ids, mask_one, mask_two, note, piece, after, out, col, row, tall):
-    terms = note.shape[0] // 2
-    taps = [note[k, :, :TAPS].astype(jnp.bfloat16) for k in range(2 * terms)]
-    build_matrices(taps[:terms], taps[terms:], col, row)
-    last = ids[0] == ids[1]
-    mask = inner_rows(mask_one[...], mask_two[...], last)
-    field = convolve(lambda s: mask, col, row, tall, out.shape[0])
-    shift = jnp.broadcast_to(note[2 * terms][:, :1], field.shape[1:])
-    out[...] = (piece[...].astype(jnp.float32) + shift[None] * field).astype(jnp.bfloat16)
-
-
-def early_call(kernel, name, ids, density, valid, terms, extra, after, out_shape):
-    slices = out_shape[0].shape[1]
-    cols = valid.shape[1]
-    block = LANES // terms - HALO
-    last = valid.shape[0] // block - 1
-
-    def at(shift):
-        return lambda i, ids: jnp.minimum(ids[0], last - 1) + shift
-
-    def whole(x):
-        return pl.BlockSpec(x.shape, lambda i, ids: (0,) * x.ndim)
-
-    cubes = [] if density is None else [density] * 2
-    shapes = matrix_shapes(terms, slices, REACH)
-    return pl.pallas_call(
-        kernel,
-        name=name,
-        grid_spec=pltpu.PrefetchScalarGridSpec(
-            num_scalar_prefetch=1,
-            grid=(1,),
-            in_specs=[
-                pl.BlockSpec((slices, block, cols), lambda i, ids, f=at(d): (0, f(i, ids), 0)) for d in range(len(cubes))
-            ]
-            + [pl.BlockSpec((block, cols), lambda i, ids, f=at(d): (f(i, ids), 0)) for d in (0, 1)]
-            + [whole(x) for x in extra]
-            + [pl.BlockSpec(memory_space=pl.ANY)],
-            out_specs=[whole(x) for x in out_shape],
-            scratch_shapes=[pltpu.VMEM(shape, jnp.bfloat16) for shape in shapes]
-            + [pltpu.VMEM((GROUP * LANES, cols), jnp.bfloat16)],
-        ),
-        out_shape=out_shape,
-        compiler_params=params(60),
-        cost_estimate=cost(1, 1),
-    )(jnp.stack([ids, jnp.full_like(ids, last)]).astype(jnp.int32), *cubes, valid, valid, *extra, after)
-
-
-def sums_kernel(density, valid, after, out, first, last):
+def sums_kernel(density, valid, out, first, last):
     slices, rows, cols = density.shape
     step = pl.program_id(0)
 
@@ -205,10 +125,10 @@
         out[s : s + 1, :] += jnp.sum(x, axis=0, keepdims=True)
 
 
-def masked_sums(density, valid, after):
+def masked_sums(density, valid):
     slices, rows, cols = density.shape
     step = 32
-    edge = jax.ShapeDtypeStruct((slices + 1, REACH, cols), jnp.bfloat16)
+    edge = hbm((slices + 1, REACH, cols), jnp.bfloat16)
     return pl.pallas_call(
         sums_kernel,
         name="sums",
@@ -216,14 +136,13 @@
         in_specs=[
             pl.BlockSpec((slices, step, cols), lambda i: (0, i, 0)),
             pl.BlockSpec((step, cols), lambda i: (i, 0)),
-            pl.BlockSpec(memory_space=pl.ANY),
         ],
         out_specs=[pl.BlockSpec((slices + 8, LANES), lambda i: (0, 0))]
-        + [pl.BlockSpec(edge.shape, lambda i: (0, 0, 0))] * 2,
-        out_shape=[jax.ShapeDtypeStruct((slices + 8, LANES), jnp.float32), edge, edge],
-        compiler_params=params(60),
+        + [pl.BlockSpec((slices + 1, REACH, cols), lambda i: (0, 0, 0))] * 2,
+        out_shape=[hbm((slices + 8, LANES), jnp.float32), edge, edge],
+        compiler_params=params(),
         cost_estimate=cost(1, 1),
-    )(density, valid, after)
+    )(held(density), held(valid))
 
 
 def mean_kernel(*refs):
@@ -234,47 +153,27 @@
     out[...] = jnp.broadcast_to(total[:slices] / total[slices : slices + 1], out.shape)
 
 
-def means(sums, slices, after):
-    vmem = pl.BlockSpec(memory_space=pltpu.VMEM)
+def means(sums, slices):
     return pl.pallas_call(
         mean_kernel,
         name="means",
-        in_specs=[vmem] * len(sums) + [pl.BlockSpec(memory_space=pl.ANY)],
-        out_specs=vmem,
         out_shape=jax.ShapeDtypeStruct((slices, LANES), jnp.float32),
         compiler_params=params(),
         cost_estimate=cost(1, 1),
-    )(*sums, after)
-
-
-def notes_kernel(mean, row_taps, col_taps, *refs):
-    terms, slices, taps = row_taps.shape
-    count = len(refs) // 2
-    for centre, note in zip(refs[:count], refs[count:]):
-        note[...] = jnp.zeros_like(note)
-        note[:terms, :, :taps] = row_taps[...].astype(jnp.float32)
-        note[terms : 2 * terms, :, :taps] = col_taps[...].astype(jnp.float32)
-        note[2 * terms] = centre[...] - mean[...]
-
-
-def notes_of(mean, row_taps, col_taps, centres):
-    terms, slices, _ = row_taps.shape
-    note = jax.ShapeDtypeStruct((2 * terms + 1, slices, LANES), jnp.float32)
-    return pl.pallas_call(
-        notes_kernel,
-        name="notes",
-        out_shape=[note] * len(centres),
-        compiler_params=params(),
-        cost_estimate=cost(1, 1),
-    )(mean, row_taps, col_taps, *centres)
+    )(*sums)
 
 
 def filter_kernel(pieces, ids, before, now, after, mask_before, mask_now, mask_after, *refs):
-    (above, below, col, row, mean), (tall, done) = refs[:5], refs[-2:]
+    (above, below, row_taps, col_taps, mean), (tall, done, col, row) = refs[:5], refs[-4:]
     count = sum(len(wanted) for wanted in pieces)
-    outs = refs[-2 - count : -2]
+    outs = refs[-4 - count : -4]
     slices, block, cols = now.shape
     step = pl.program_id(0)
+
+    @pl.when(step == 0)
+    def _():
+        build_matrices(listed(row_taps), listed(col_taps), col, row)
+
     first = ids[step] == 0
     last = ids[step] == ids[pl.num_programs(0)]
     f32 = jnp.float32
@@ -301,9 +200,10 @@
         at += len(wanted)
 
 
-def filter_blocks(ids, pieces, density, valid, above, below, col, row, mean, *after):
-    slices, rows, cols = density.shape
-    block = row.shape[1] // GROUP
+def filter_blocks(ids, pieces, density, valid, above, below, row_taps, col_taps, mean, *after):
+    slices, rows, cols = density.shape
+    terms = row_taps.shape[0]
+    block = LANES // terms - HALO
     last = rows // block - 1
     count = ids.shape[0]
 
@@ -325,25 +225,25 @@
             grid=(count,),
             in_specs=[pl.BlockSpec((slices, block, cols), rows_at(d)) for d in (-1, 0, 1)]
             + [pl.BlockSpec((block, cols), mask_at(d)) for d in (-1, 0, 1)]
-            + [whole(x) for x in (above, below, col, row, mean)]
-            + [pl.BlockSpec(memory_space=pl.ANY)] * len(after),
+            + [whole(x) for x in (above, below, row_taps, col_taps, mean)]
+            + [anywhere()] * len(after),
             out_specs=[pl.BlockSpec(shape, lambda i, at: (0, 0, 0)) for shape in shapes],
             scratch_shapes=[
                 pltpu.VMEM((GROUP * LANES, cols), jnp.bfloat16),
                 pltpu.VMEM((block, slices, cols), jnp.bfloat16),
-            ],
+            ]
+            + [pltpu.VMEM(shape, jnp.bfloat16) for shape in matrix_shapes(terms, slices, block)],
         ),
-        out_shape=[jax.ShapeDtypeStruct(shape, jnp.bfloat16) for shape in shapes],
+        out_shape=[hbm(shape, jnp.bfloat16) for shape in shapes],
         compiler_params=params(),
         cost_estimate=cost(1, 1),
     )(
         jnp.concatenate([ids, jnp.full((1,), last, ids.dtype)]),
-        *([density] * 3),
-        *([valid] * 3),
+        *[held(x) for x in (density, density, density, valid, valid, valid)],
         above,
         below,
-        col,
-        row,
+        row_taps,
+        col_taps,
         mean,
         *after,
     )
@@ -366,7 +266,7 @@
     _, slices, cols = parts[0][0].shape
     zbins = weights.shape[0] // 2
     count = len(parts)
-    shape = jax.ShapeDtypeStruct((zbins, total * cols), jnp.bfloat16)
+    shape = hbm((zbins, total * cols), jnp.bfloat16)
     return pl.pallas_call(
         functools.partial(project_kernel, count),
         name="project",
@@ -375,11 +275,11 @@
             grid=(rows,),
             in_specs=[pl.BlockSpec(weights.shape, lambda i, at: (0, 0))]
             + [pl.BlockSpec((1, slices, cols), lambda i, at, start=start: (i + start, 0, 0)) for _, start in parts]
-            + [pl.BlockSpec(memory_space=pl.ANY)] * len(earlier),
+            + [anywhere()] * len(earlier),
             out_specs=[pl.BlockSpec((zbins, cols), lambda i, at: (0, i + at[0]))] * 2
             + [pl.BlockSpec((8, LANES), lambda i, at: (0, 0))],
         ),
-        out_shape=[shape, shape, jax.ShapeDtypeStruct((8, LANES), jnp.float32)],
+        out_shape=[shape, shape, hbm((8, LANES), jnp.float32)],
         input_output_aliases={2 + count + i: i for i in range(len(earlier))},
         compiler_params=params(),
         cost_estimate=cost(1, 1),
@@ -390,42 +290,40 @@
     pass
 
 
-def gate(x, *earlier):
-    held = pl.BlockSpec(memory_space=pl.ANY)
+def gate(x, *earlier, flops=1):
     return pl.pallas_call(
         gate_kernel,
         name="gate",
-        in_specs=[held] * (1 + len(earlier)),
-        out_specs=held,
-        out_shape=jax.ShapeDtypeStruct(x.shape, x.dtype),
+        in_specs=[anywhere()] * (1 + len(earlier)),
+        out_specs=anywhere(),
+        out_shape=hbm(x.shape, x.dtype),
         input_output_aliases={0: 0},
-        cost_estimate=cost(1, 1),
-    )(x, *earlier)
+        cost_estimate=cost(flops, 1),
+    )(held(x), *earlier)
 
 
 INNER, OUTER, HEAD, TAIL = (1, 0, REACH), (0, 0, REACH), (0, 0, 5), (0, 5, REACH)
-EARLY = (4, 6, 5)
 LATE = (4, 6)
+FILTERS = ((4, (INNER,)),), ((6, (INNER, HEAD, TAIL)), (5, (INNER, OUTER)), (7, (INNER, OUTER)))
 ORDER = (
-    ("filter", (7, 5, 2), ((6, 0),)),
+    ("send", (4, 0), ()),
+    ("send", (6, 0), ((4, 0),)),
+    ("send", (5, 0), ((4, 0),)),
     ("send", (7, 0), ((4, 0),)),
-    ("send", (2, 0), ((4, 0),)),
-    ("send", (5, 1), ((4, 0),)),
-    ("filter", (3, 4, 6, 1, 0), ((5, 0),)),
+    ("filter", ((4, (HEAD, TAIL)), (2, (INNER, OUTER)), (3, (INNER, OUTER)), (1, (INNER, OUTER)), (0, (INNER, OUTER))), ((4, 0),)),
+    ("send", (2, 0), ((6, 0), (0, 0))),
+    ("send", (3, 0), ((6, 0), (0, 0))),
+    ("send", (5, 1), ((6, 0),)),
+    ("send", (2, 1), ((5, 0), (0, 0))),
     ("send", (7, 1), ((5, 0),)),
-    ("send", (2, 1), ((2, 0),)),
-    ("send", (3, 0), ((5, 1), (0, 0))),
-    ("send", (4, "note"), ((5, 1), (0, 0))),
-    ("send", (6, "note"), ((5, 1), (0, 0))),
-    ("send", (5, "note"), ((5, 1), (0, 0))),
-    ("send", (4, 1), ((5, 1), (0, 0))),
-    ("send", (1, 0), ((5, 1), (2, 1))),
-    ("send", (3, 1), ((3, 0),)),
-    ("send", (6, 1), ((7, 0), (0, 0))),
-    ("send", (1, 1), ((3, 0),)),
+    ("send", (4, 1), ((7, 0), (0, 0))),
+    ("send", (3, 1), ((7, 0), (0, 0))),
+    ("send", (1, 0), ((7, 0), (0, 0))),
+    ("send", (6, 1), ((5, 1),)),
+    ("send", (1, 1), ((5, 1), (0, 0))),
     ("project", 0, ()),
-    ("send", (4, 2), ((4, 1), "project 0")),
-    ("send", (6, 2), ((6, 1),)),
+    ("send", (4, 2), ((7, 1), "project 0")),
+    ("send", (6, 2), ((4, 1),)),
     ("project", 1, ()),
     ("project", 2, ()),
 )
@@ -433,7 +331,6 @@
 
 def fast(density, valid, row_taps, col_taps, amp_matrix, like_matrix):
     slices, rows, cols = density.shape
-    terms = row_taps.shape[0]
     peers = lax.axis_size("cuts")
     tiles = lax.axis_size("tile")
     block = rows // peers
@@ -442,55 +339,36 @@
     def swap(x, k):
         return lax.ppermute(x, "cuts", [(i, i ^ k) for i in range(peers)])
 
-    piece = jax.ShapeDtypeStruct((REACH, slices, cols), jnp.bfloat16)
-    centre = jax.ShapeDtypeStruct((slices, LANES), jnp.float32)
-
-    def early(k, after):
-        return early_call(
-            early_kernel, "early", me ^ k, density, valid, terms, (row_taps, col_taps), after, [piece, centre]
-        )
+    own, first, last = masked_sums(density, valid)
+    sums = [own] + [lax.ppermute(own, "tile", [(i, i ^ k) for i in range(tiles)]) for k in range(1, tiles)]
+    above = lax.ppermute(last, "tile", [(i, i + 1) for i in range(tiles - 1)])
+    below = lax.ppermute(first, "tile", [(i + 1, i) for i in range(tiles - 1)])
+    mean = means(sums, slices)
 
     made, arrived = {}, {}
-    made[4, 0], about_4 = early(4, row_taps)
-    arrived[4, 0] = swap(made[4, 0], 4)
-    made[6, 0], about_6 = early(6, made[4, 0])
-    own, first, last = masked_sums(density, valid, made[6, 0])
-    sums = [own] + [lax.ppermute(own, "tile", [(i, i ^ k) for i in range(tiles)]) for k in range(1, tiles)]
-    arrived[6, 0] = swap(made[6, 0], 6)
-    mean = means(sums, slices, arrived[4, 0])
-    above = lax.ppermute(gate(last, mean), "tile", [(i, i + 1) for i in range(tiles - 1)])
-    below = lax.ppermute(gate(first, mean), "tile", [(i + 1, i) for i in range(tiles - 1)])
-    made[5, 0], about_5 = early(5, mean)
-    arrived[5, 0] = swap(made[5, 0], 5)
-    col, row = filter_matrices(row_taps, col_taps, made[5, 0])
-    for k, note in zip(EARLY, notes_of(mean, row_taps, col_taps, (about_4, about_6, about_5))):
-        made[k, "note"] = note
-
-    cuts = {k: (INNER, HEAD, TAIL) if k in LATE else (INNER, OUTER) for k in range(peers)}
+
+    def filter_for(wanted, above, below, *after):
+        ids = jnp.stack([me ^ k for k, _ in wanted])
+        pieces = [cut for _, cut in wanted]
+        got = filter_blocks(ids, pieces, density, valid, above, below, row_taps, col_taps, mean, *after)
+        for (k, cut), parts in zip(wanted, got):
+            for piece, x in zip(cut, parts):
+                p = {INNER: 0, OUTER: 1, HEAD: 1, TAIL: 2}[piece]
+                made[k, p] = x
+                if k == 0:
+                    arrived[k, p] = x
+
+    filter_for(FILTERS[0], last, first)
+    filter_for(FILTERS[1], above, below, made[4, 0])
     weights = jnp.concatenate([amp_matrix, like_matrix], axis=1).T.reshape(-1, peers, slices)
     weights = weights[:, me ^ jnp.arange(peers)].reshape(-1, peers * slices)
     result = []
-    after = made[5, 0]
     for what, how, before in ORDER:
         before = [arrived[x] for x in before]
         if what == "filter":
-            ids = jnp.stack([me ^ k for k in how])
-            skip = [1 if k in EARLY else 0 for k in how]
-            wanted = [cuts[k][n:] for k, n in zip(how, skip)]
-            got = filter_blocks(ids, wanted, density, valid, above, below, col, row, mean, after, *before)
-            for k, n, parts in zip(how, skip, got):
-                for p, x in enumerate(parts, start=n):
-                    made[k, p] = x
-                    if k == 0:
-                        arrived[k, p] = x
-            after = got[-1][-1]
+            filter_for(how, above, below, made[7, 0], *before)
         elif what == "send":
-            k, p = how
-            arrived[how] = swap(gate(made[how], *before), k)
-            if p == "note":
-                (arrived[k, 0],) = early_call(
-                    mend_kernel, "mend", me, None, valid, terms, (arrived[how], arrived[k, 0]), after, [piece]
-                )
+            arrived[how] = swap(gate(made[how], *before) if before else made[how], how[0])
         else:
             inner, start, stop = (INNER, HEAD, TAIL)[how]
             place = jnp.where((me == peers - 1) != (inner == 1), block - REACH, 0) + start

time: 157 us -> 145 us (0.924); the launches traced: 154 us -> 144 us
  waiting for transfers between devices: 9.68 us -> 35.4 us
  Pallas kernels: 69.6 us -> 49.6 us
  local copies, waits for them, and re-layouts: 29.7 us -> 14.7 us
  other arithmetic: 2 us -> 0.17 us
    pallas_call x27 -> x16, Pallas kernels: 34.8 us -> 0.1 us  [the longest x1 0.08 us: means(): pl.pallas_call(mean_kernel, name='means', out_shape=jax.ShapeDtypeStruct(...]
    ppermute x19 -> x16, waiting for transfers between devices: 5.22 us -> 34.6 us  [swap(): return lax.ppermute(x, 'cuts', [(i, i ^ k) for i in range(peers)])]
    unnamed x122 -> x56, local copies, waits for them, and re-layouts: 28.9 us -> 12.5 us
    pallas_call x2 -> x3, Pallas kernels: 21 us -> 34.3 us  [filter_blocks(): pl.pallas_call(functools.partial(filter_kernel, pieces), name='filter', g...]
    ppermute x3, waiting for transfers between devices: 3.36 us -> 0.01 us  [fast(): lax.ppermute(own, 'tile', [(i, i ^ k) for i in range(tiles)])]
    another operation x3 -> x0, other arithmetic: 1.9 us -> none  [early_call(): jnp.stack([ids, jnp.full_like(ids, last)]).astype(jnp.int32)]
    ppermute x19 -> x16, starting transfers between devices: 34.8 us -> 33.8 us  [swap(): return lax.ppermute(x, 'cuts', [(i, i ^ k) for i in range(peers)])]
  transfers between devices with their start and end apart: 24 -> 21, of which waited for: 8 -> 8; matrix products, arithmetic and copies ran while one was open for 1% -> 2% of each run, Pallas kernels for 40% -> 30%
where the time goes in v4:
time: 145 us; the launch traced here: 144 us
  Pallas kernels  49.6 us (34%)
  starting transfers between devices  43.4 us (30%)
  waiting for transfers between devices  35.4 us (24%)
  local copies, waits for them, and re-layouts  14.7 us (10%)
    ppermute x16, waiting for transfers between devices, swap(): return lax.ppermute(x, 'cuts', [(i, i ^ k) for i in range(peers)])  34.6 us
    pallas_call x3, Pallas kernels, filter_blocks(): pl.pallas_call(functools.partial(filter_kernel, pieces), name='filter', g...  34.3 us
    ppermute x16, starting transfers between devices, swap(): return lax.ppermute(x, 'cuts', [(i, i ^ k) for i in range(peers)])  33.8 us
    unnamed x56, local copies, waits for them, and re-layouts  12.5 us
    pallas_call x3, Pallas kernels, project(): pl.pallas_call(functools.partial(project_kernel, count), name='project',...  11 us
    ppermute x3, starting transfers between devices, fast(): lax.ppermute(own, 'tile', [(i, i ^ k) for i in range(tiles)])  4.52 us
    pallas_call x1, Pallas kernels, masked_sums(): pl.pallas_call(sums_kernel, name='sums', grid=(rows // step,), in_specs=[...  4.15 us
    ppermute x1, starting transfers between devices, fast(): above = lax.ppermute(last, 'tile', [(i, i + 1) for i in range(tiles - 1)])  3.81 us
  transfers between devices with their start and end apart: 21, of which 8 were waited for; matrix products, arithmetic and copies ran while one was open for 2% of the time, Pallas kernels for 30%

profile of v4, /device:TPU:0, one launch (start us, length us, event | category | flops | bytes accessed | tf_op | source)
XLA Modules:
  0.0 144.2 jit_solution(9547045735163748622)
XLA Ops:
  0.6 4.2 %sums.1 = (f32[24,128]{1,0:T(8,128)}, bf16[17,8,1024]{2,1,0:T(8,128)(2,1)}, bf16[17,8,1024]{2,1,0:T(8,128)(2,1)}) custom-call(bf16[16,128,1024]{2,1,0:T(8,128)(2,1)} %after.5, s32[128,1024]{1,0:T(8,128)} %mask_after.5), custom_call_target="tpu_custom_call" | custom-call | flops 1 | bytes 1 | tf_op jit(solution)/shard_map/sums/pallas_call | solution.py:132
  4.8 3.9 %collective-permute-start.4 = (f32[24,128]{1,0:T(8,128)}, f32[24,128]{1,0:T(8,128)S(1)}, u32[]{:S(2)}, u32[]{:S(2)}) collective-permute-start(f32[24,128]{1,0:T(8,128)} %get-tuple-element.31.refs_0_), channel_id=1, source_target_pairs={{0,24},{8,16},{16,8},{24,0},{1,25},{9,17},{17,9},{25,1},{2,26},{10... | collective-permute-start | bytes 36872 | tf_op jit(solution)/shard_map/ppermute | solution.py:343
  9.3 3.8 %collective-permute-start = (bf16[17,8,1024]{2,1,0:T(8,128)(2,1)}, bf16[17,8,1024]{2,1,0:T(8,128)(2,1)S(1)}, u32[]{:S(2)}, u32[]{:S(2)}) collective-permute-start(bf16[17,8,1024]{2,1,0:T(8,128)(2,1)} %get-tuple-element.29.refs_0_), channel_id=1, source_target_pairs={{0,8},{8,16},{16,24},{1,9},{9,17},{17,25},{2,10},{10,18},{18,26},{... | collective-permute-start | bytes 835592 | tf_op jit(solution)/shard_map/ppermute | solution.py:344
  13.1 1.3 collective-permute-start.1
  17.3 5.6 %filter.3.refs_5_ = bf16[8,16,1024]{2,1,0:T(8,128)(2,1)} custom-call(s32[2]{0:T(128)S(1)} %pad_add_fusion.1.ids, bf16[16,128,1024]{2,1,0:T(8,128)(2,1)} %after.5, bf16[16,128,1024]{2,1,0:T(8,128)(2,1)} %after.5, bf16[16,128,1024]{2,1,0:T(8,128)(2,1)} %after.5, s32[128,1024]{1,0:T(8,128)} %mask_after.5, s32[128,1024]{1,0:T(8,128)} %mask_after.5, ...), custom_call_target="tpu_custom_call" | custom-call | flops 1 | bytes 1 | tf_op jit(solution)/shard_map/filter/pallas_call | solution.py:220
  22.9 2.6 %collective-permute-start.5 = (bf16[8,16,1024]{2,1,0:T(8,128)(2,1)}, bf16[8,16,1024]{2,1,0:T(8,128)(2,1)S(1)}, u32[]{:S(2)}, u32[]{:S(2)}) collective-permute-start(bf16[8,16,1024]{2,1,0:T(8,128)(2,1)} %filter.3.refs_5_), channel_id=1, source_target_pairs={{0,4},{1,5},{2,6},{3,7},{4,0},{5,1},{6,2},{7,3},{8,12},{9,13},{10,... | collective-permute-start | bytes 786440 | tf_op jit(solution)/shard_map/ppermute | solution.py:340
  27.3 11.8 %filter.4 = (bf16[8,16,1024]{2,1,0:T(8,128)(2,1)}, bf16[5,16,1024]{2,1,0:T(8,128)(2,1)}, bf16[3,16,1024]{2,1,0:T(8,128)(2,1)}, bf16[8,16,1024]{2,1,0:T(8,128)(2,...) custom-call(s32[4]{0:T(128)S(1)} %pad_add_fusion.ids, ...), custom_call_target="tpu_custom_call" | custom-call | flops 1 | bytes 1 | tf_op jit(solution)/shard_map/filter/pallas_call | solution.py:220
  39.8 4.0 %collective-permute-start.6 = (bf16[8,16,1024]{2,1,0:T(8,128)(2,1)}, bf16[8,16,1024]{2,1,0:T(8,128)(2,1)S(1)}, u32[]{:S(2)}, u32[]{:S(2)}) collective-permute-start(bf16[8,16,1024]{2,1,0:T(8,128)(2,1)} %gate.15), channel_id=1, source_target_pairs={{0,6},{1,7},{2,4},{3,5},{4,2},{5,3},{6,0},{7,1},{8,14},{9,15},{10,... | collective-permute-start | bytes 786440 | tf_op jit(solution)/shard_map/ppermute | solution.py:340
  45.8 16.9 %filter.5 = (bf16[5,16,1024]{2,1,0:T(8,128)(2,1)}, bf16[3,16,1024]{2,1,0:T(8,128)(2,1)}, bf16[8,16,1024]{2,1,0:T(8,128)(2,1)}, bf16[8,16,1024]{2,1,0:T(8,128)(2,...) custom-call(s32[6]{0:T(128)S(1)} %concatenate.13.ids, ...), custom_call_target="tpu_custom_call" | custom-call | flops 1 | bytes 1 | tf_op jit(solution)/shard_map/filter/pallas_call | solution.py:220
  63.8 2.4 %collective-permute-start.7 = (bf16[8,16,1024]{2,1,0:T(8,128)(2,1)}, bf16[8,16,1024]{2,1,0:T(8,128)(2,1)S(1)}, u32[]{:S(2)}, u32[]{:S(2)}) collective-permute-start(bf16[8,16,1024]{2,1,0:T(8,128)(2,1)} %gate.16), channel_id=1, source_target_pairs={{0,5},{1,4},{2,7},{3,6},{4,1},{5,0},{6,3},{7,2},{8,13},{9,12},{10,... | collective-permute-start | bytes 786440 | tf_op jit(solution)/shard_map/ppermute | solution.py:340
  66.2 7.3 %collective-permute-done.11.refs_1_.refs_7_ = bf16[8,16,1024]{2,1,0:T(8,128)(2,1)S(1)} collective-permute-done((bf16[8,16,1024]{2,1,0:T(8,128)(2,1)}, bf16[8,16,1024]{2,1,0:T(8,128)(2,1)S(1)}, u32[]{:S(2)}, u32[]{:S(2)}) %collective-permute-start.11) | collective-permute-done | bytes 262176 | tf_op jit(solution)/shard_map/ppermute | solution.py:340
  74.2 14.4 %collective-permute-start.18 = (bf16[5,16,1024]{2,1,0:T(8,128)(2,1)}, bf16[5,16,1024]{2,1,0:T(8,128)(2,1)S(1)}, u32[]{:S(2)}, u32[]{:S(2)}) collective-permute-start(bf16[5,16,1024]{2,1,0:T(8,128)(2,1)} %gate.27), channel_id=1, source_target_pairs={{0,4},{1,5},{2,6},{3,7},{4,0},{5,1},{6,2},{7,3},{8,12},{9,13},{10,... | collective-permute-start | bytes 491528 | tf_op jit(solution)/shard_map/ppermute | solution.py:340
  89.3 6.8 %collective-permute-done.9.refs_1_.refs_5_ = bf16[8,16,1024]{2,1,0:T(8,128)(2,1)S(1)} collective-permute-done((bf16[8,16,1024]{2,1,0:T(8,128)(2,1)}, bf16[8,16,1024]{2,1,0:T(8,128)(2,1)S(1)}, u32[]{:S(2)}, u32[]{:S(2)}) %collective-permute-start.9) | collective-permute-done | bytes 262176 | tf_op jit(solution)/shard_map/ppermute | solution.py:340
  96.8 7.4 %collective-permute-done.18.refs_1_.refs_4_ = bf16[5,16,1024]{2,1,0:T(8,128)(2,1)S(1)} collective-permute-done((bf16[5,16,1024]{2,1,0:T(8,128)(2,1)}, bf16[5,16,1024]{2,1,0:T(8,128)(2,1)S(1)}, u32[]{:S(2)}, u32[]{:S(2)}) %collective-permute-start.18) | collective-permute-done | bytes 163872 | tf_op jit(solution)/shard_map/ppermute | solution.py:340
  104.3 2.0 %collective-permute-start.13 = (bf16[8,16,1024]{2,1,0:T(8,128)(2,1)}, bf16[8,16,1024]{2,1,0:T(8,128)(2,1)S(1)}, u32[]{:S(2)}, u32[]{:S(2)}) collective-permute-start(bf16[8,16,1024]{2,1,0:T(8,128)(2,1)} %gate.22), channel_id=1, source_target_pairs={{0,7},{1,6},{2,5},{3,4},{4,3},{5,2},{6,1},{7,0},{8,15},{9,14},{10,... | collective-permute-start | bytes 786440 | tf_op jit(solution)/shard_map/ppermute | solution.py:340
  107.0 1.7 %collective-permute-done.15.refs_2_ = bf16[8,16,1024]{2,1,0:T(8,128)(2,1)S(1)} collective-permute-done((bf16[8,16,1024]{2,1,0:T(8,128)(2,1)}, bf16[8,16,1024]{2,1,0:T(8,128)(2,1)S(1)}, u32[]{:S(2)}, u32[]{:S(2)}) %collective-permute-start.15) | collective-permute-done | bytes 262176 | tf_op jit(solution)/shard_map/ppermute | solution.py:340
  108.7 7.7 %collective-permute-done.16.refs_3_ = bf16[8,16,1024]{2,1,0:T(8,128)(2,1)S(1)} collective-permute-done((bf16[8,16,1024]{2,1,0:T(8,128)(2,1)}, bf16[8,16,1024]{2,1,0:T(8,128)(2,1)S(1)}, u32[]{:S(2)}, u32[]{:S(2)}) %collective-permute-start.16) | collective-permute-done | bytes 262176 | tf_op jit(solution)/shard_map/ppermute | solution.py:340
  117.1 3.3 %collective-permute-start.8 = (bf16[8,16,1024]{2,1,0:T(8,128)(2,1)}, bf16[8,16,1024]{2,1,0:T(8,128)(2,1)S(1)}, u32[]{:S(2)}, u32[]{:S(2)}) collective-permute-start(bf16[8,16,1024]{2,1,0:T(8,128)(2,1)} %gate.17), channel_id=1, source_target_pairs={{0,1},{1,0},{2,3},{3,2},{4,5},{5,4},{6,7},{7,6},{8,9},{9,8},{10,11... | collective-permute-start | bytes 786440 | tf_op jit(solution)/shard_map/ppermute | solution.py:340
  120.5 1.9 %collective-permute-start.20 = (bf16[5,16,1024]{2,1,0:T(8,128)(2,1)}, bf16[5,16,1024]{2,1,0:T(8,128)(2,1)S(1)}, u32[]{:S(2)}, u32[]{:S(2)}) collective-permute-start(bf16[5,16,1024]{2,1,0:T(8,128)(2,1)} %gate.29), channel_id=1, source_target_pairs={{0,6},{1,7},{2,4},{3,5},{4,2},{5,3},{6,0},{7,1},{8,14},{9,15},{10,... | collective-permute-start | bytes 491528 | tf_op jit(solution)/shard_map/ppermute | solution.py:340
  125.5 5.8 %project.3 = (bf16[128,16384]{1,0:T(8,128)(2,1)}, bf16[128,16384]{1,0:T(8,128)(2,1)}, f32[8,128]{1,0:T(8,128)}) custom-call(s32[1]{0:T(128)} %bitcast.14.place, bf16[256,128]{1,0:T(8,128)(2,1)S(1)} %copy.29.weights, bf16[8,16,1024]{2,1,0:T(8,128)(2,1)S(1)} %copy-done, bf16[8,16,1024]{2,1,0:T(8,128)(2,1)} %collective-permute-done.14.refs_1_, ...), custom_call_target="tpu_custom_call" | custom-call | flops 1 | bytes 1 | tf_op jit(solution)/shard_map/project/pallas_call | solution.py:270
  131.4 2.1 %collective-permute-start.19 = (bf16[3,16,1024]{2,1,0:T(8,128)(2,1)}, bf16[3,16,1024]{2,1,0:T(8,128)(2,1)S(1)}, u32[]{:S(2)}, u32[]{:S(2)}) collective-permute-start(bf16[3,16,1024]{2,1,0:T(8,128)(2,1)} %gate.28), channel_id=1, source_target_pairs={{0,6},{1,7},{2,4},{3,5},{4,2},{5,3},{6,0},{7,1},{8,14},{9,15},{10,... | collective-permute-start | bytes 294920 | tf_op jit(solution)/shard_map/ppermute | solution.py:340
  135.4 3.1 %project.4 = (bf16[128,16384]{1,0:T(8,128)(2,1)}, bf16[128,16384]{1,0:T(8,128)(2,1)}, f32[8,128]{1,0:T(8,128)}) custom-call(s32[1]{0:T(128)} %bitcast.15.place, bf16[256,128]{1,0:T(8,128)(2,1)S(1)} %copy.29.weights, bf16[8,16,1024]{2,1,0:T(8,128)(2,1)S(1)} %copy-done.16, ...), custom_call_target="tpu_custom_call", output_to_operand_aliasing={{0}: (10, {}), {1}: (11, {})} | custom-call | flops 1 | bytes 1 | tf_op jit(solution)/shard_map/project/pallas_call | solution.py:270
  139.0 3.1 %collective-permute-done.17.refs_4_ = bf16[3,16,1024]{2,1,0:T(8,128)(2,1)S(1)} collective-permute-done((bf16[3,16,1024]{2,1,0:T(8,128)(2,1)}, bf16[3,16,1024]{2,1,0:T(8,128)(2,1)S(1)}, u32[]{:S(2)}, u32[]{:S(2)}) %collective-permute-start.17) | collective-permute-done | bytes 98336 | tf_op jit(solution)/shard_map/ppermute | solution.py:340
  142.1 2.1 %project.5 = (bf16[128,16384]{1,0:T(8,128)(2,1)}, bf16[128,16384]{1,0:T(8,128)(2,1)}, f32[8,128]{1,0:T(8,128)}) custom-call(s32[1]{0:T(128)} %bitcast.place, bf16[256,128]{1,0:T(8,128)(2,1)S(1)} %copy.29.weights, bf16[8,16,1024]{2,1,0:T(8,128)(2,1)S(1)} %copy-done.16, ...), custom_call_target="tpu_custom_call", output_to_operand_aliasing={{0}: (10, {}), {1}: (11, {})} | custom-call | flops 1 | bytes 1 | tf_op jit(solution)/shard_map/project/pallas_call | solution.py:270
  (105 shorter events, 17.9 us)
Async XLA Ops:
  4.8 9.7 %collective-permute-start.4 = (f32[24,128]{1,0:T(8,128)}, f32[24,128]{1,0:T(8,128)S(1)}, u32[]{:S(2)}, u32[]{:S(2)}) collective-permute-start(f32[24,128]{1,0:T(8,128)} %get-tuple-element.31.refs_0_), channel_id=1, source_target_pairs={{0,24},{8,16},{16,8},{24,0},{1,25},{9,17},{17,9},{25,1},{2,26},{10... | collective-permute-start | bytes 36872 | tf_op jit(solution)/shard_map/ppermute | solution.py:343
  8.7 5.8 %collective-permute-start.3 = (f32[24,128]{1,0:T(8,128)}, f32[24,128]{1,0:T(8,128)S(1)}, u32[]{:S(2)}, u32[]{:S(2)}) collective-permute-start(f32[24,128]{1,0:T(8,128)} %get-tuple-element.31.refs_0_), channel_id=1, source_target_pairs={{0,16},{8,24},{16,0},{24,8},{1,17},{9,25},{17,1},{25,9},{2,18},{10... | collective-permute-start | bytes 36872 | tf_op jit(solution)/shard_map/ppermute | solution.py:343
  9.2 5.3 %collective-permute-start.2 = (f32[24,128]{1,0:T(8,128)}, f32[24,128]{1,0:T(8,128)S(1)}, u32[]{:S(2)}, u32[]{:S(2)}) collective-permute-start(f32[24,128]{1,0:T(8,128)} %get-tuple-element.31.refs_0_), channel_id=1, source_target_pairs={{0,8},{8,0},{16,24},{24,16},{1,9},{9,1},{17,25},{25,17},{2,10},{10... | collective-permute-start | bytes 36872 | tf_op jit(solution)/shard_map/ppermute | solution.py:343
  9.3 16.2 %collective-permute-start = (bf16[17,8,1024]{2,1,0:T(8,128)(2,1)}, bf16[17,8,1024]{2,1,0:T(8,128)(2,1)S(1)}, u32[]{:S(2)}, u32[]{:S(2)}) collective-permute-start(bf16[17,8,1024]{2,1,0:T(8,128)(2,1)} %get-tuple-element.29.refs_0_), channel_id=1, source_target_pairs={{0,8},{8,16},{16,24},{1,9},{9,17},{17,25},{2,10},{10,18},{18,26},{... | collective-permute-start | bytes 835592 | tf_op jit(solution)/shard_map/ppermute | solution.py:344
  13.1 13.2 %collective-permute-start.1 = (bf16[17,8,1024]{2,1,0:T(8,128)(2,1)}, bf16[17,8,1024]{2,1,0:T(8,128)(2,1)S(1)}, u32[]{:S(2)}, u32[]{:S(2)}) collective-permute-start(bf16[17,8,1024]{2,1,0:T(8,128)(2,1)} %get-tuple-element.30.refs_1_), channel_id=1, source_target_pairs={{8,0},{16,8},{24,16},{9,1},{17,9},{25,17},{10,2},{18,10},{26,18},{... | collective-permute-start | bytes 835592 | tf_op jit(solution)/shard_map/ppermute | solution.py:345
  22.9 16.2 %collective-permute-start.5 = (bf16[8,16,1024]{2,1,0:T(8,128)(2,1)}, bf16[8,16,1024]{2,1,0:T(8,128)(2,1)S(1)}, u32[]{:S(2)}, u32[]{:S(2)}) collective-permute-start(bf16[8,16,1024]{2,1,0:T(8,128)(2,1)} %filter.3.refs_5_), channel_id=1, source_target_pairs={{0,4},{1,5},{2,6},{3,7},{4,0},{5,1},{6,2},{7,3},{8,12},{9,13},{10,... | collective-permute-start | bytes 786440 | tf_op jit(solution)/shard_map/ppermute | solution.py:340
  39.8 23.3 %collective-permute-start.6 = (bf16[8,16,1024]{2,1,0:T(8,128)(2,1)}, bf16[8,16,1024]{2,1,0:T(8,128)(2,1)S(1)}, u32[]{:S(2)}, u32[]{:S(2)}) collective-permute-start(bf16[8,16,1024]{2,1,0:T(8,128)(2,1)} %gate.15), channel_id=1, source_target_pairs={{0,6},{1,7},{2,4},{3,5},{4,2},{5,3},{6,0},{7,1},{8,14},{9,15},{10,... | collective-permute-start | bytes 786440 | tf_op jit(solution)/shard_map/ppermute | solution.py:340
  62.7 43.6 %copy-start.26 = (bf16[128,128]{1,0:T(8,128)(2,1)S(1)}, bf16[128,128]{1,0:T(8,128)(2,1)}, u32[]{:S(2)}) copy-start(bf16[128,128]{1,0:T(8,128)(2,1)} %param.11) | copy-start | bytes 98308
  62.7 43.6 %copy-start.27 = (bf16[128,128]{1,0:T(8,128)(2,1)S(1)}, bf16[128,128]{1,0:T(8,128)(2,1)}, u32[]{:S(2)}) copy-start(bf16[128,128]{1,0:T(8,128)(2,1)} %param.10) | copy-start | bytes 98308
  62.7 10.8 %collective-permute-start.11 = (bf16[8,16,1024]{2,1,0:T(8,128)(2,1)}, bf16[8,16,1024]{2,1,0:T(8,128)(2,1)S(1)}, u32[]{:S(2)}, u32[]{:S(2)}) collective-permute-start(bf16[8,16,1024]{2,1,0:T(8,128)(2,1)} %gate.20), channel_id=1, source_target_pairs={{0,7},{1,6},{2,5},{3,4},{4,3},{5,2},{6,1},{7,0},{8,15},{9,14},{10,... | collective-permute-start | bytes 786440 | tf_op jit(solution)/shard_map/ppermute | solution.py:340
  62.8 33.3 %collective-permute-start.9 = (bf16[8,16,1024]{2,1,0:T(8,128)(2,1)}, bf16[8,16,1024]{2,1,0:T(8,128)(2,1)S(1)}, u32[]{:S(2)}, u32[]{:S(2)}) collective-permute-start(bf16[8,16,1024]{2,1,0:T(8,128)(2,1)} %gate.18), channel_id=1, source_target_pairs={{0,5},{1,4},{2,7},{3,6},{4,1},{5,0},{6,3},{7,2},{8,13},{9,12},{10,... | collective-permute-start | bytes 786440 | tf_op jit(solution)/shard_map/ppermute | solution.py:340
  63.8 42.5 %collective-permute-start.7 = (bf16[8,16,1024]{2,1,0:T(8,128)(2,1)}, bf16[8,16,1024]{2,1,0:T(8,128)(2,1)S(1)}, u32[]{:S(2)}, u32[]{:S(2)}) collective-permute-start(bf16[8,16,1024]{2,1,0:T(8,128)(2,1)} %gate.16), channel_id=1, source_target_pairs={{0,5},{1,4},{2,7},{3,6},{4,1},{5,0},{6,3},{7,2},{8,13},{9,12},{10,... | collective-permute-start | bytes 786440 | tf_op jit(solution)/shard_map/ppermute | solution.py:340
  74.2 30.0 %collective-permute-start.18 = (bf16[5,16,1024]{2,1,0:T(8,128)(2,1)}, bf16[5,16,1024]{2,1,0:T(8,128)(2,1)S(1)}, u32[]{:S(2)}, u32[]{:S(2)}) collective-permute-start(bf16[5,16,1024]{2,1,0:T(8,128)(2,1)} %gate.27), channel_id=1, source_target_pairs={{0,4},{1,5},{2,6},{3,7},{4,0},{5,1},{6,2},{7,3},{8,12},{9,13},{10,... | collective-permute-start | bytes 491528 | tf_op jit(solution)/shard_map/ppermute | solution.py:340
  88.6 20.1 %collective-permute-start.15 = (bf16[8,16,1024]{2,1,0:T(8,128)(2,1)}, bf16[8,16,1024]{2,1,0:T(8,128)(2,1)S(1)}, u32[]{:S(2)}, u32[]{:S(2)}) collective-permute-start(bf16[8,16,1024]{2,1,0:T(8,128)(2,1)} %gate.24), channel_id=1, source_target_pairs={{0,2},{1,3},{2,0},{3,1},{4,6},{5,7},{6,4},{7,5},{8,10},{9,11},{10,... | collective-permute-start | bytes 786440 | tf_op jit(solution)/shard_map/ppermute | solution.py:340
  88.7 27.7 %collective-permute-start.16 = (bf16[8,16,1024]{2,1,0:T(8,128)(2,1)}, bf16[8,16,1024]{2,1,0:T(8,128)(2,1)S(1)}, u32[]{:S(2)}, u32[]{:S(2)}) collective-permute-start(bf16[8,16,1024]{2,1,0:T(8,128)(2,1)} %gate.25), channel_id=1, source_target_pairs={{0,3},{1,2},{2,1},{3,0},{4,7},{5,6},{6,5},{7,4},{8,11},{9,10},{10,... | collective-permute-start | bytes 786440 | tf_op jit(solution)/shard_map/ppermute | solution.py:340
  96.1 24.4 %collective-permute-start.14 = (bf16[8,16,1024]{2,1,0:T(8,128)(2,1)}, bf16[8,16,1024]{2,1,0:T(8,128)(2,1)}, u32[]{:S(2)}, u32[]{:S(2)}) collective-permute-start(bf16[8,16,1024]{2,1,0:T(8,128)(2,1)} %gate.23), channel_id=1, source_target_pairs={{0,1},{1,0},{2,3},{3,2},{4,5},{5,4},{6,7},{7,6},{8,9},{9,8},{10,11... | collective-permute-start | bytes 786440 | tf_op jit(solution)/shard_map/ppermute | solution.py:340
  96.8 36.7 %copy-start.16 = (bf16[8,16,1024]{2,1,0:T(8,128)(2,1)S(1)}, bf16[8,16,1024]{2,1,0:T(8,128)(2,1)}, u32[]{:S(2)}) copy-start(bf16[8,16,1024]{2,1,0:T(8,128)(2,1)} %get-tuple-element.33.refs_0_) | copy-start | bytes 786436
  104.3 27.1 %collective-permute-start.13 = (bf16[8,16,1024]{2,1,0:T(8,128)(2,1)}, bf16[8,16,1024]{2,1,0:T(8,128)(2,1)S(1)}, u32[]{:S(2)}, u32[]{:S(2)}) collective-permute-start(bf16[8,16,1024]{2,1,0:T(8,128)(2,1)} %gate.22), channel_id=1, source_target_pairs={{0,7},{1,6},{2,5},{3,4},{4,3},{5,2},{6,1},{7,0},{8,15},{9,14},{10,... | collective-permute-start | bytes 786440 | tf_op jit(solution)/shard_map/ppermute | solution.py:340
  106.3 27.2 %collective-permute-start.10 = (bf16[8,16,1024]{2,1,0:T(8,128)(2,1)}, bf16[8,16,1024]{2,1,0:T(8,128)(2,1)S(1)}, u32[]{:S(2)}, u32[]{:S(2)}) collective-permute-start(bf16[8,16,1024]{2,1,0:T(8,128)(2,1)} %gate.19), channel_id=1, source_target_pairs={{0,2},{1,3},{2,0},{3,1},{4,6},{5,7},{6,4},{7,5},{8,10},{9,11},{10,... | collective-permute-start | bytes 786440 | tf_op jit(solution)/shard_map/ppermute | solution.py:340
  108.7 24.8 %collective-permute-start.12 = (bf16[8,16,1024]{2,1,0:T(8,128)(2,1)}, bf16[8,16,1024]{2,1,0:T(8,128)(2,1)S(1)}, u32[]{:S(2)}, u32[]{:S(2)}) collective-permute-start(bf16[8,16,1024]{2,1,0:T(8,128)(2,1)} %gate.21), channel_id=1, source_target_pairs={{0,3},{1,2},{2,1},{3,0},{4,7},{5,6},{6,5},{7,4},{8,11},{9,10},{10,... | collective-permute-start | bytes 786440 | tf_op jit(solution)/shard_map/ppermute | solution.py:340
  117.1 16.4 %collective-permute-start.8 = (bf16[8,16,1024]{2,1,0:T(8,128)(2,1)}, bf16[8,16,1024]{2,1,0:T(8,128)(2,1)S(1)}, u32[]{:S(2)}, u32[]{:S(2)}) collective-permute-start(bf16[8,16,1024]{2,1,0:T(8,128)(2,1)} %gate.17), channel_id=1, source_target_pairs={{0,1},{1,0},{2,3},{3,2},{4,5},{5,4},{6,7},{7,6},{8,9},{9,8},{10,11... | collective-permute-start | bytes 786440 | tf_op jit(solution)/shard_map/ppermute | solution.py:340
  120.5 13.0 %collective-permute-start.20 = (bf16[5,16,1024]{2,1,0:T(8,128)(2,1)}, bf16[5,16,1024]{2,1,0:T(8,128)(2,1)S(1)}, u32[]{:S(2)}, u32[]{:S(2)}) collective-permute-start(bf16[5,16,1024]{2,1,0:T(8,128)(2,1)} %gate.29), channel_id=1, source_target_pairs={{0,6},{1,7},{2,4},{3,5},{4,2},{5,3},{6,0},{7,1},{8,14},{9,15},{10,... | collective-permute-start | bytes 491528 | tf_op jit(solution)/shard_map/ppermute | solution.py:340
  131.4 7.7 %collective-permute-start.19 = (bf16[3,16,1024]{2,1,0:T(8,128)(2,1)}, bf16[3,16,1024]{2,1,0:T(8,128)(2,1)S(1)}, u32[]{:S(2)}, u32[]{:S(2)}) collective-permute-start(bf16[3,16,1024]{2,1,0:T(8,128)(2,1)} %gate.28), channel_id=1, source_target_pairs={{0,6},{1,7},{2,4},{3,5},{4,2},{5,3},{6,0},{7,1},{8,14},{9,15},{10,... | collective-permute-start | bytes 294920 | tf_op jit(solution)/shard_map/ppermute | solution.py:340
  133.5 8.6 %collective-permute-start.17 = (bf16[3,16,1024]{2,1,0:T(8,128)(2,1)}, bf16[3,16,1024]{2,1,0:T(8,128)(2,1)S(1)}, u32[]{:S(2)}, u32[]{:S(2)}) collective-permute-start(bf16[3,16,1024]{2,1,0:T(8,128)(2,1)} %gate.26), channel_id=1, source_target_pairs={{0,4},{1,5},{2,6},{3,7},{4,0},{5,1},{6,2},{7,3},{8,12},{9,13},{10,... | collective-permute-start | bytes 294920 | tf_op jit(solution)/shard_map/ppermute | solution.py:340
  (25 other events, 262.4 us)

commit v5 on v4

--- a/solution.py
+++ b/solution.py
@@ -15,7 +15,7 @@
 HALO = 2 * REACH
 
 
-def params(mib=28):
+def params(mib=24):
     return pltpu.CompilerParams(vmem_limit_bytes=mib * MIB)
 
 
@@ -35,21 +35,29 @@
     return pl.CostEstimate(flops=int(flops), bytes_accessed=int(moved), transcendentals=0)
 
 
-def build_matrices(row_taps, col_taps, col_out, row_out):
+def tap_flip():
+    tap = lax.broadcasted_iota(jnp.int32, (TAPS, 2 * LANES), 0)
+    lane = lax.broadcasted_iota(jnp.int32, (TAPS, 2 * LANES), 1)
+    return (lax.rem(tap + lane, 2 * LANES) == 0).astype(jnp.bfloat16)
+
+
+def column_band(taps):
+    band = pltpu.roll(jnp.broadcast_to(taps, (LANES + HALO, 2 * LANES)), 0, 1, stride=1, stride_axis=0)
+    return band[:, :LANES].astype(jnp.bfloat16)
+
+
+def build_columns(col_taps, col_out):
+    terms, slices = len(col_taps), col_taps[0].shape[0]
+    for k in range(terms):
+        base = jnp.dot(col_taps[k], tap_flip(), preferred_element_type=jnp.float32)
+        for s in range(slices):
+            col_out[s, : LANES + HALO, k * LANES : (k + 1) * LANES] = column_band(base[s : s + 1])
+    for s in range(slices):
+        col_out[s, LANES + HALO :, :] = jnp.zeros((LANES - HALO, terms * LANES), jnp.bfloat16)
+
+
+def build_rows(row_taps, row_out):
     terms, slices = len(row_taps), row_taps[0].shape[0]
-    wide = 2 * LANES
-    window = LANES + HALO
-    tap = lax.broadcasted_iota(jnp.int32, (TAPS, wide), 0)
-    lane = lax.broadcasted_iota(jnp.int32, (TAPS, wide), 1)
-    flip = (lax.rem(tap + lane, wide) == 0).astype(jnp.bfloat16)
-    for k in range(terms):
-        base = jnp.dot(col_taps[k], flip, preferred_element_type=jnp.float32)
-        for s in range(slices):
-            rows = jnp.broadcast_to(base[s : s + 1], (window, wide))
-            band = pltpu.roll(rows, 0, 1, stride=1, stride_axis=0)
-            col_out[s, :window, k * LANES : (k + 1) * LANES] = band[:, :LANES].astype(jnp.bfloat16)
-    for s in range(slices):
-        col_out[s, window:, :] = jnp.zeros((wide - window, terms * LANES), jnp.bfloat16)
     high = LANES // terms
     tap = lax.broadcasted_iota(jnp.int32, (TAPS, LANES), 0)
     lane = lax.broadcasted_iota(jnp.int32, (TAPS, LANES), 1)
@@ -172,7 +180,8 @@
 
     @pl.when(step == 0)
     def _():
-        build_matrices(listed(row_taps), listed(col_taps), col, row)
+        build_columns(listed(col_taps), col)
+        build_rows(listed(row_taps), row)
 
     first = ids[step] == 0
     last = ids[step] == ids[pl.num_programs(0)]
@@ -251,6 +260,125 @@
     return [[out.pop(0) for _ in wanted] for wanted in pieces]
 
 
+def band_kernel(pieces, ids, density, valid, above, below, row_taps, col_taps, mean, *refs):
+    (col, row, taps, mask, tall, done, sems) = refs[-7:]
+    count = sum(len(wanted) for wanted in pieces)
+    outs = refs[-7 - count : -7]
+    slices = mean.shape[0]
+    rows, cols = valid.shape
+    terms = row_taps.shape[0]
+    block = done.shape[1]
+    high = block + HALO
+    step = pl.program_id(0)
+    f32 = jnp.float32
+
+    @pl.when(step == 0)
+    def _():
+        for k in range(terms):
+            taps[:, k] = jnp.dot(col_taps[k], tap_flip(), preferred_element_type=f32)
+        col[LANES + HALO :, :] = jnp.zeros((LANES - HALO, terms * LANES), jnp.bfloat16)
+        build_rows(listed(row_taps), row)
+        mask[:REACH] = above[slices].astype(f32)
+        mask[REACH : REACH + rows] = valid[...].astype(f32)
+        mask[REACH + rows :] = below[slices].astype(f32)
+
+    @pl.when(step < slices)
+    def _():
+        mine = taps[step]
+        for k in range(terms):
+            col[: LANES + HALO, k * LANES : (k + 1) * LANES] = column_band(mine[k : k + 1])
+        x = jnp.concatenate([above[step].astype(f32), density[0].astype(f32), below[step].astype(f32)], axis=0)
+        x = mask[...] * (x - mean[pl.ds(step, 1), :][:, :1])
+        x = jnp.concatenate([x, jnp.zeros((rows + HALO, LANES), f32)], axis=1)
+        x = pltpu.roll(x, REACH, 1).astype(jnp.bfloat16)
+        x = jnp.concatenate([x[:, c : c + 2 * LANES] for c in range(0, cols, LANES)], axis=0)
+        y = jnp.dot(x, col[...], preferred_element_type=f32).astype(jnp.bfloat16)
+        for c in range(cols // LANES):
+            for k in range(terms):
+                tall[step * terms + k, :, c * LANES : (c + 1) * LANES] = y[
+                    c * (rows + HALO) : (c + 1) * (rows + HALO), k * LANES : (k + 1) * LANES
+                ]
+
+    def copies(b):
+        at = sum(len(wanted) for wanted in pieces[:b])
+        last = ids[b] == ids[len(pieces)]
+        for p, (inner, start, stop) in enumerate(pieces[b]):
+            here = jnp.where(last != (inner == 1), block - REACH, 0) + start
+            yield pltpu.make_async_copy(done.at[b, pl.ds(here, stop - start)], outs[at + p], sems.at[at + p])
+
+    @pl.when(step >= slices)
+    def _():
+        b = step - slices
+        here = pl.ds(pl.multiple_of(ids[b] * block, block), high)
+        parts = []
+        for g in range(slices // GROUP):
+            slab = tall[g * GROUP * terms : (g + 1) * GROUP * terms, here, :].reshape(GROUP * LANES, cols)
+            z = jnp.dot(row[g], slab, preferred_element_type=f32)
+            parts.append(z.reshape(block, GROUP, cols))
+        done[b] = jnp.concatenate(parts, axis=1).astype(jnp.bfloat16)
+
+    for b in range(len(pieces)):
+
+        @pl.when(step == slices + b)
+        def _():
+            for copy in copies(b):
+                copy.start()
+
+    @pl.when(step == slices + len(pieces) - 1)
+    def _():
+        for b in range(len(pieces)):
+            for copy in copies(b):
+                copy.wait()
+
+
+def filter_band(ids, pieces, density, valid, above, below, row_taps, col_taps, mean, *after):
+    slices, rows, cols = density.shape
+    terms = row_taps.shape[0]
+    block = LANES // terms - HALO
+    count = len(pieces)
+
+    def whole(x):
+        return pl.BlockSpec(x.shape, lambda i, at: (0,) * x.ndim, pipeline_mode=pl.Buffered(1))
+
+    shapes = [(stop - start, slices, cols) for wanted in pieces for _, start, stop in wanted]
+    out = pl.pallas_call(
+        functools.partial(band_kernel, pieces),
+        name="band",
+        grid_spec=pltpu.PrefetchScalarGridSpec(
+            num_scalar_prefetch=1,
+            grid=(slices + count,),
+            in_specs=[pl.BlockSpec((1, rows, cols), lambda i, at: (jnp.minimum(i, slices - 1), 0, 0))]
+            + [whole(x) for x in (valid, above, below, row_taps, col_taps, mean)]
+            + [anywhere()] * len(after),
+            out_specs=[anywhere()] * len(shapes),
+            scratch_shapes=[
+                pltpu.VMEM((2 * LANES, terms * LANES), jnp.bfloat16),
+                pltpu.VMEM((slices // GROUP, block * GROUP, GROUP * LANES), jnp.bfloat16),
+                pltpu.VMEM((slices, terms, 2 * LANES), jnp.float32),
+                pltpu.VMEM((rows + HALO, cols), jnp.float32),
+                pltpu.VMEM((slices * terms, rows + HALO, cols), jnp.bfloat16),
+                pltpu.VMEM((count, block, slices, cols), jnp.bfloat16),
+                pltpu.SemaphoreType.DMA((len(shapes),)),
+            ],
+        ),
+        out_shape=[hbm(shape, jnp.bfloat16) for shape in shapes],
+        compiler_params=params(44),
+        cost_estimate=cost(1, 1),
+    )(
+        jnp.concatenate([ids, jnp.full((1,), rows // block - 1, ids.dtype)]),
+        held(density),
+        held(valid),
+        above,
+        below,
+        row_taps,
+        col_taps,
+        mean,
+        *after,
+    )
+    out = list(out)
+    return [[out.pop(0) for _ in wanted] for wanted in pieces]
+
+
 def project_kernel(count, place, weights, *refs):
     parts, (amp_out, like_out, token) = refs[:count], refs[-3:]
     zbins = weights.shape[0] // 2
@@ -298,35 +426,29 @@
         out_specs=anywhere(),
         out_shape=hbm(x.shape, x.dtype),
         input_output_aliases={0: 0},
+        compiler_params=params(1),
         cost_estimate=cost(flops, 1),
     )(held(x), *earlier)
 
 
 INNER, OUTER, HEAD, TAIL = (1, 0, REACH), (0, 0, REACH), (0, 0, 5), (0, 5, REACH)
-LATE = (4, 6)
-FILTERS = ((4, (INNER,)),), ((6, (INNER, HEAD, TAIL)), (5, (INNER, OUTER)), (7, (INNER, OUTER)))
+LATE = (4, 6, 5, 7)
+FIRST = ((4, (INNER,)), (6, (INNER,)))
+REST = (
+    (5, (INNER, HEAD, TAIL)),
+    (7, (INNER, HEAD, TAIL)),
+    (2, (INNER, OUTER)),
+    (3, (INNER, OUTER)),
+    (4, (HEAD, TAIL)),
+    (6, (HEAD, TAIL)),
+    (1, (INNER, OUTER)),
+    (0, (INNER, OUTER)),
+)
 ORDER = (
-    ("send", (4, 0), ()),
-    ("send", (6, 0), ((4, 0),)),
-    ("send", (5, 0), ((4, 0),)),
-    ("send", (7, 0), ((4, 0),)),
-    ("filter", ((4, (HEAD, TAIL)), (2, (INNER, OUTER)), (3, (INNER, OUTER)), (1, (INNER, OUTER)), (0, (INNER, OUTER))), ((4, 0),)),
-    ("send", (2, 0), ((6, 0), (0, 0))),
-    ("send", (3, 0), ((6, 0), (0, 0))),
-    ("send", (5, 1), ((6, 0),)),
-    ("send", (2, 1), ((5, 0), (0, 0))),
-    ("send", (7, 1), ((5, 0),)),
-    ("send", (4, 1), ((7, 0), (0, 0))),
-    ("send", (3, 1), ((7, 0), (0, 0))),
-    ("send", (1, 0), ((7, 0), (0, 0))),
-    ("send", (6, 1), ((5, 1),)),
-    ("send", (1, 1), ((5, 1), (0, 0))),
-    ("project", 0, ()),
-    ("send", (4, 2), ((7, 1), "project 0")),
-    ("send", (6, 2), ((4, 1),)),
-    ("project", 1, ()),
-    ("project", 2, ()),
+    (4, 0), (6, 0), (5, 0), (2, 0), (7, 0), (3, 0), (4, 1), (2, 1), (6, 1), (1, 0), (5, 1), (3, 1), (7, 1), (1, 1),
+    (4, 2), (6, 2), (5, 2), (7, 2),
 )
+IN_FLIGHT = 4
 
 
 def fast(density, valid, row_taps, col_taps, amp_matrix, like_matrix):
@@ -347,10 +469,10 @@
 
     made, arrived = {}, {}
 
-    def filter_for(wanted, above, below, *after):
+    def filter_for(kernel, wanted, above, below, *after):
         ids = jnp.stack([me ^ k for k, _ in wanted])
         pieces = [cut for _, cut in wanted]
-        got = filter_blocks(ids, pieces, density, valid, above, below, row_taps, col_taps, mean, *after)
+        got = kernel(ids, pieces, density, valid, above, below, row_taps, col_taps, mean, *after)
         for (k, cut), parts in zip(wanted, got):
             for piece, x in zip(cut, parts):
                 p = {INNER: 0, OUTER: 1, HEAD: 1, TAIL: 2}[piece]
@@ -358,22 +480,27 @@
                 if k == 0:
                     arrived[k, p] = x
 
-    filter_for(FILTERS[0], last, first)
-    filter_for(FILTERS[1], above, below, made[4, 0])
+    filter_for(filter_blocks, FIRST, last, first)
+    filter_for(filter_band, REST, above, below, made[4, 0])
     weights = jnp.concatenate([amp_matrix, like_matrix], axis=1).T.reshape(-1, peers, slices)
     weights = weights[:, me ^ jnp.arange(peers)].reshape(-1, peers * slices)
-    result = []
-    for what, how, before in ORDER:
-        before = [arrived[x] for x in before]
-        if what == "filter":
-            filter_for(how, above, below, made[7, 0], *before)
-        elif what == "send":
-            arrived[how] = swap(gate(made[how], *before) if before else made[how], how[0])
-        else:
-            inner, start, stop = (INNER, HEAD, TAIL)[how]
-            place = jnp.where((me == peers - 1) != (inner == 1), block - REACH, 0) + start
-            parts = [(arrived[k, how], 0) if k in LATE else (arrived[k, min(how, 1)], start) for k in range(peers)]
-            *result[:], arrived[f"project {how}"] = project(place, weights, parts, stop - start, block, result)
+    result, tokens = [], []
+
+    def finish(p):
+        inner, start, stop = (INNER, HEAD, TAIL)[p]
+        place = jnp.where((me == peers - 1) != (inner == 1), block - REACH, 0) + start
+        parts = [(arrived[k, p], 0) if k in LATE else (arrived[k, min(p, 1)], start) for k in range(peers)]
+        *result[:], token = project(place, weights, parts, stop - start, block, result)
+        tokens.append(token)
+
+    for at, (k, p) in enumerate(ORDER):
+        before = [arrived[ORDER[at - IN_FLIGHT]]] if at >= IN_FLIGHT else []
+        if at == len(ORDER) - 3:
+            finish(0)
+            before.append(tokens[0])
+        arrived[k, p] = swap(gate(made[k, p], *before) if before else made[k, p], k)
+    finish(1)
+    finish(2)
     return tuple(result)
 
 

time: 145 us -> 132 us (0.910)
  the two profiles are of different devices: /device:TPU:0 before, /device:TPU:13 now
where the time goes in v5:
time: 132 us; the launch traced here: 131 us
  Pallas kernels  46.3 us (35%)
  waiting for transfers between devices  38.9 us (29%)
  starting transfers between devices  37.2 us (28%)
  local copies, waits for them, and re-layouts  7.52 us (6%)
    ppermute x18, waiting for transfers between devices, swap(): return lax.ppermute(x, 'cuts', [(i, i ^ k) for i in range(peers)])  38.9 us
    ppermute x18, starting transfers between devices, swap(): return lax.ppermute(x, 'cuts', [(i, i ^ k) for i in range(peers)])  28.4 us
    pallas_call x1, Pallas kernels, filter_band(): pl.pallas_call(functools.partial(band_kernel, pieces), name='band', grid_...  23.1 us
    pallas_call x3, Pallas kernels, project(): pl.pallas_call(functools.partial(project_kernel, count), name='project',...  9.64 us
    pallas_call x1, Pallas kernels, filter_blocks(): pl.pallas_call(functools.partial(filter_kernel, pieces), name='filter', g...  9.31 us
    unnamed x26, local copies, waits for them, and re-layouts  6.77 us
    pallas_call x1, Pallas kernels, masked_sums(): pl.pallas_call(sums_kernel, name='sums', grid=(rows // step,), in_specs=[...  4.16 us
    ppermute x1, starting transfers between devices, fast(): above = lax.ppermute(last, 'tile', [(i, i + 1) for i in range(tiles - 1)])  3.11 us
  transfers between devices with their start and end apart: 23, of which 8 were waited for; matrix products, arithmetic and copies ran while one was open for 1% of the time, Pallas kernels for 31%

profile of v5, /device:TPU:13, one launch (start us, length us, event | category | flops | bytes accessed | tf_op | source)
XLA Modules:
  0.0 130.8 jit_solution(7741617542888892921)
XLA Ops:
  0.6 4.2 %sums.1 = (f32[24,128]{1,0:T(8,128)}, bf16[17,8,1024]{2,1,0:T(8,128)(2,1)}, bf16[17,8,1024]{2,1,0:T(8,128)(2,1)}) custom-call(bf16[16,128,1024]{2,1,0:T(8,128)(2,1)} %density.3, s32[128,1024]{1,0:T(8,128)} %valid.3), custom_call_target="tpu_custom_call" | custom-call | flops 1 | bytes 1 | tf_op jit(solution)/shard_map/sums/pallas_call | solution.py:140
  4.8 1.2 collective-permute-start.4
  6.0 1.2 collective-permute-start.3
  7.5 3.1 %collective-permute-start = (bf16[17,8,1024]{2,1,0:T(8,128)(2,1)}, bf16[17,8,1024]{2,1,0:T(8,128)(2,1)S(1)}, u32[]{:S(2)}, u32[]{:S(2)}) collective-permute-start(bf16[17,8,1024]{2,1,0:T(8,128)(2,1)} %get-tuple-element.32.refs_0_), channel_id=1, source_target_pairs={{0,8},{8,16},{16,24},{1,9},{9,17},{17,25},{2,10},{10,18},{18,26},{... | collective-permute-start | bytes 835592 | tf_op jit(solution)/shard_map/ppermute | solution.py:466
  10.6 3.1 %collective-permute-start.1 = (bf16[17,8,1024]{2,1,0:T(8,128)(2,1)}, bf16[17,8,1024]{2,1,0:T(8,128)(2,1)S(1)}, u32[]{:S(2)}, u32[]{:S(2)}) collective-permute-start(bf16[17,8,1024]{2,1,0:T(8,128)(2,1)} %get-tuple-element.33.refs_1_), channel_id=1, source_target_pairs={{8,0},{16,8},{24,16},{9,1},{17,9},{25,17},{10,2},{18,10},{26,18},{... | collective-permute-start | bytes 835592 | tf_op jit(solution)/shard_map/ppermute | solution.py:467
  16.5 9.3 %filter.1 = (bf16[8,16,1024]{2,1,0:T(8,128)(2,1)}, bf16[8,16,1024]{2,1,0:T(8,128)(2,1)}) custom-call(s32[3]{0:T(128)S(1)} %pad_add_fusion.ids, bf16[16,128,1024]{2,1,0:T(8,128)(2,1)} %density.3, bf16[16,128,1024]{2,1,0:T(8,128)(2,1)} %density.3, bf16[16,128,1024]{2,1,0:T(8,128)(2,1)} %density.3, s32[128,1024]{1,0:T(8,128)} %valid.3, s32[128,1024]{1,0:T(8,128)} %valid.3, ...), custom_call_target="tpu_custom_call" | custom-call | flops 1 | bytes 1 | tf_op jit(solution)/shard_map/filter/pallas_call | solution.py:229
  28.8 23.1 %band.1 = (bf16[8,16,1024]{2,1,0:T(8,128)(2,1)}, bf16[5,16,1024]{2,1,0:T(8,128)(2,1)}, bf16[3,16,1024]{2,1,0:T(8,128)(2,1)}, bf16[8,16,1024]{2,1,0:T(8,128)(2,1)...) custom-call(s32[9]{0:T(128)S(1)} %concatenate.10.ids, ...), custom_call_target="tpu_custom_call" | custom-call | flops 1 | bytes 1 | tf_op jit(solution)/shard_map/band/pallas_call | solution.py:344
  51.9 3.4 %collective-permute-start.6 = (bf16[8,16,1024]{2,1,0:T(8,128)(2,1)}, bf16[8,16,1024]{2,1,0:T(8,128)(2,1)S(1)}, u32[]{:S(2)}, u32[]{:S(2)}) collective-permute-start(bf16[8,16,1024]{2,1,0:T(8,128)(2,1)} %gate.14), channel_id=1, source_target_pairs={{0,3},{1,2},{2,1},{3,0},{4,7},{5,6},{6,5},{7,4},{8,11},{9,10},{10,... | collective-permute-start | bytes 786440 | tf_op jit(solution)/shard_map/ppermute | solution.py:462
  55.8 1.1 collective-permute-start.17
  57.0 2.2 %collective-permute-start.12 = (bf16[8,16,1024]{2,1,0:T(8,128)(2,1)}, bf16[8,16,1024]{2,1,0:T(8,128)(2,1)S(1)}, u32[]{:S(2)}, u32[]{:S(2)}) collective-permute-start(bf16[8,16,1024]{2,1,0:T(8,128)(2,1)} %get-tuple-element.47), channel_id=1, source_target_pairs={{0,5},{1,4},{2,7},{3,6},{4,1},{5,0},{6,3},{7,2},{8,13},{9,12},{10,... | collective-permute-start | bytes 786440 | tf_op jit(solution)/shard_map/ppermute | solution.py:462
  59.2 3.3 %collective-permute-done.6.refs_1_.refs_3_ = bf16[8,16,1024]{2,1,0:T(8,128)(2,1)S(1)} collective-permute-done((bf16[8,16,1024]{2,1,0:T(8,128)(2,1)}, bf16[8,16,1024]{2,1,0:T(8,128)(2,1)S(1)}, u32[]{:S(2)}, u32[]{:S(2)}) %collective-permute-start.6) | collective-permute-done | bytes 262176 | tf_op jit(solution)/shard_map/ppermute | solution.py:462
  63.3 13.4 %collective-permute-done.9.refs_1_.refs_2_ = bf16[8,16,1024]{2,1,0:T(8,128)(2,1)S(1)} collective-permute-done((bf16[8,16,1024]{2,1,0:T(8,128)(2,1)}, bf16[8,16,1024]{2,1,0:T(8,128)(2,1)S(1)}, u32[]{:S(2)}, u32[]{:S(2)}) %collective-permute-start.9) | collective-permute-done | bytes 262176 | tf_op jit(solution)/shard_map/ppermute | solution.py:462
  76.7 2.1 %collective-permute-start.10 = (bf16[8,16,1024]{2,1,0:T(8,128)(2,1)}, bf16[8,16,1024]{2,1,0:T(8,128)(2,1)S(1)}, u32[]{:S(2)}, u32[]{:S(2)}) collective-permute-start(bf16[8,16,1024]{2,1,0:T(8,128)(2,1)} %gate.17), channel_id=1, source_target_pairs={{0,2},{1,3},{2,0},{3,1},{4,6},{5,7},{6,4},{7,5},{8,10},{9,11},{10,... | collective-permute-start | bytes 786440 | tf_op jit(solution)/shard_map/ppermute | solution.py:462
  79.8 3.3 %collective-permute-start.13 = (bf16[5,16,1024]{2,1,0:T(8,128)(2,1)}, bf16[5,16,1024]{2,1,0:T(8,128)(2,1)S(1)}, u32[]{:S(2)}, u32[]{:S(2)}) collective-permute-start(bf16[5,16,1024]{2,1,0:T(8,128)(2,1)} %gate.19), channel_id=1, source_target_pairs={{0,4},{1,5},{2,6},{3,7},{4,0},{5,1},{6,2},{7,3},{8,12},{9,13},{10,... | collective-permute-start | bytes 491528 | tf_op jit(solution)/shard_map/ppermute | solution.py:462
  83.1 7.7 %collective-permute-done.10.refs_1_.refs_2_ = bf16[8,16,1024]{2,1,0:T(8,128)(2,1)S(1)} collective-permute-done((bf16[8,16,1024]{2,1,0:T(8,128)(2,1)}, bf16[8,16,1024]{2,1,0:T(8,128)(2,1)S(1)}, u32[]{:S(2)}, u32[]{:S(2)}) %collective-permute-start.10) | collective-permute-done | bytes 262176 | tf_op jit(solution)/shard_map/ppermute | solution.py:462
  90.8 2.7 %collective-permute-start.11 = (bf16[8,16,1024]{2,1,0:T(8,128)(2,1)}, bf16[8,16,1024]{2,1,0:T(8,128)(2,1)S(1)}, u32[]{:S(2)}, u32[]{:S(2)}) collective-permute-start(bf16[8,16,1024]{2,1,0:T(8,128)(2,1)} %gate.18), channel_id=1, source_target_pairs={{0,3},{1,2},{2,1},{3,0},{4,7},{5,6},{6,5},{7,4},{8,11},{9,10},{10,... | collective-permute-start | bytes 786440 | tf_op jit(solution)/shard_map/ppermute | solution.py:462
  95.2 3.5 %collective-permute-start.14 = (bf16[5,16,1024]{2,1,0:T(8,128)(2,1)}, bf16[5,16,1024]{2,1,0:T(8,128)(2,1)S(1)}, u32[]{:S(2)}, u32[]{:S(2)}) collective-permute-start(bf16[5,16,1024]{2,1,0:T(8,128)(2,1)} %gate.20), channel_id=1, source_target_pairs={{0,5},{1,4},{2,7},{3,6},{4,1},{5,0},{6,3},{7,2},{8,13},{9,12},{10,... | collective-permute-start | bytes 491528 | tf_op jit(solution)/shard_map/ppermute | solution.py:462
  100.5 4.5 %project.3 = (bf16[128,16384]{1,0:T(8,128)(2,1)}, bf16[128,16384]{1,0:T(8,128)(2,1)}, f32[8,128]{1,0:T(8,128)}) custom-call(s32[1]{0:T(128)} %bitcast.14.place, bf16[256,128]{1,0:T(8,128)(2,1)S(1)} %copy.28.weights, bf16[8,16,1024]{2,1,0:T(8,128)(2,1)S(1)} %copy-done.5, bf16[8,16,1024]{2,1,0:T(8,128)(2,1)S(1)} %collective-permute-done.7.refs_1_, ...), custom_call_target="tpu_custom_call" | custom-call | flops 1 | bytes 1 | tf_op jit(solution)/shard_map/project/pallas_call | solution.py:398
  105.5 6.2 %collective-permute-done.14.refs_1_.refs_5_ = bf16[5,16,1024]{2,1,0:T(8,128)(2,1)S(1)} collective-permute-done((bf16[5,16,1024]{2,1,0:T(8,128)(2,1)}, bf16[5,16,1024]{2,1,0:T(8,128)(2,1)S(1)}, u32[]{:S(2)}, u32[]{:S(2)}) %collective-permute-start.14) | collective-permute-done | bytes 163872 | tf_op jit(solution)/shard_map/ppermute | solution.py:462
  111.7 3.0 %collective-permute-start.15 = (bf16[3,16,1024]{2,1,0:T(8,128)(2,1)}, bf16[3,16,1024]{2,1,0:T(8,128)(2,1)S(1)}, u32[]{:S(2)}, u32[]{:S(2)}) collective-permute-start(bf16[3,16,1024]{2,1,0:T(8,128)(2,1)} %gate.21), channel_id=1, source_target_pairs={{0,4},{1,5},{2,6},{3,7},{4,0},{5,1},{6,2},{7,3},{8,12},{9,13},{10,... | collective-permute-start | bytes 294920 | tf_op jit(solution)/shard_map/ppermute | solution.py:462
  118.4 3.1 %project.4 = (bf16[128,16384]{1,0:T(8,128)(2,1)}, bf16[128,16384]{1,0:T(8,128)(2,1)}, f32[8,128]{1,0:T(8,128)}) custom-call(s32[1]{0:T(128)} %bitcast.15.place, bf16[256,128]{1,0:T(8,128)(2,1)S(1)} %copy.28.weights, bf16[8,16,1024]{2,1,0:T(8,128)(2,1)S(1)} %copy-done, ...), custom_call_target="tpu_custom_call", output_to_operand_aliasing={{0}: (10, {}), {1}: (11, {})} | custom-call | flops 1 | bytes 1 | tf_op jit(solution)/shard_map/project/pallas_call | solution.py:398
  122.3 4.3 %collective-permute-done.22.refs_7_ = bf16[3,16,1024]{2,1,0:T(8,128)(2,1)S(1)} collective-permute-done((bf16[3,16,1024]{2,1,0:T(8,128)(2,1)}, bf16[3,16,1024]{2,1,0:T(8,128)(2,1)S(1)}, u32[]{:S(2)}, u32[]{:S(2)}) %collective-permute-start.22) | collective-permute-done | bytes 98336 | tf_op jit(solution)/shard_map/ppermute | solution.py:462
  126.6 2.1 %collective-permute-done.21.refs_6_ = bf16[3,16,1024]{2,1,0:T(8,128)(2,1)S(1)} collective-permute-done((bf16[3,16,1024]{2,1,0:T(8,128)(2,1)}, bf16[3,16,1024]{2,1,0:T(8,128)(2,1)S(1)}, u32[]{:S(2)}, u32[]{:S(2)}) %collective-permute-start.21) | collective-permute-done | bytes 98336 | tf_op jit(solution)/shard_map/ppermute | solution.py:462
  128.7 2.1 %project.5 = (bf16[128,16384]{1,0:T(8,128)(2,1)}, bf16[128,16384]{1,0:T(8,128)(2,1)}, f32[8,128]{1,0:T(8,128)}) custom-call(s32[1]{0:T(128)} %bitcast.place, bf16[256,128]{1,0:T(8,128)(2,1)S(1)} %copy.28.weights, bf16[8,16,1024]{2,1,0:T(8,128)(2,1)S(1)} %copy-done, ...), custom_call_target="tpu_custom_call", output_to_operand_aliasing={{0}: (10, {}), {1}: (11, {})} | custom-call | flops 1 | bytes 1 | tf_op jit(solution)/shard_map/project/pallas_call | solution.py:398
  (76 shorter events, 16.8 us)
Async XLA Ops:
  4.8 8.9 %collective-permute-start.4 = (f32[24,128]{1,0:T(8,128)}, f32[24,128]{1,0:T(8,128)S(1)}, u32[]{:S(2)}, u32[]{:S(2)}) collective-permute-start(f32[24,128]{1,0:T(8,128)} %get-tuple-element.34.refs_0_), channel_id=1, source_target_pairs={{0,24},{8,16},{16,8},{24,0},{1,25},{9,17},{17,9},{25,1},{2,26},{10... | collective-permute-start | bytes 36872 | tf_op jit(solution)/shard_map/ppermute | solution.py:465
  6.0 7.8 %collective-permute-start.3 = (f32[24,128]{1,0:T(8,128)}, f32[24,128]{1,0:T(8,128)S(1)}, u32[]{:S(2)}, u32[]{:S(2)}) collective-permute-start(f32[24,128]{1,0:T(8,128)} %get-tuple-element.34.refs_0_), channel_id=1, source_target_pairs={{0,16},{8,24},{16,0},{24,8},{1,17},{9,25},{17,1},{25,9},{2,18},{10... | collective-permute-start | bytes 36872 | tf_op jit(solution)/shard_map/ppermute | solution.py:465
  7.2 6.5 %collective-permute-start.2 = (f32[24,128]{1,0:T(8,128)}, f32[24,128]{1,0:T(8,128)S(1)}, u32[]{:S(2)}, u32[]{:S(2)}) collective-permute-start(f32[24,128]{1,0:T(8,128)} %get-tuple-element.34.refs_0_), channel_id=1, source_target_pairs={{0,8},{8,0},{16,24},{24,16},{1,9},{9,1},{17,25},{25,17},{2,10},{10... | collective-permute-start | bytes 36872 | tf_op jit(solution)/shard_map/ppermute | solution.py:465
  7.5 20.3 %collective-permute-start = (bf16[17,8,1024]{2,1,0:T(8,128)(2,1)}, bf16[17,8,1024]{2,1,0:T(8,128)(2,1)S(1)}, u32[]{:S(2)}, u32[]{:S(2)}) collective-permute-start(bf16[17,8,1024]{2,1,0:T(8,128)(2,1)} %get-tuple-element.32.refs_0_), channel_id=1, source_target_pairs={{0,8},{8,16},{16,24},{1,9},{9,17},{17,25},{2,10},{10,18},{18,26},{... | collective-permute-start | bytes 835592 | tf_op jit(solution)/shard_map/ppermute | solution.py:466
  10.6 17.2 %collective-permute-start.1 = (bf16[17,8,1024]{2,1,0:T(8,128)(2,1)}, bf16[17,8,1024]{2,1,0:T(8,128)(2,1)S(1)}, u32[]{:S(2)}, u32[]{:S(2)}) collective-permute-start(bf16[17,8,1024]{2,1,0:T(8,128)(2,1)} %get-tuple-element.33.refs_1_), channel_id=1, source_target_pairs={{8,0},{16,8},{24,16},{9,1},{17,9},{25,17},{10,2},{18,10},{26,18},{... | collective-permute-start | bytes 835592 | tf_op jit(solution)/shard_map/ppermute | solution.py:467
  25.8 26.1 %collective-permute-start.5 = (bf16[8,16,1024]{2,1,0:T(8,128)(2,1)}, bf16[8,16,1024]{2,1,0:T(8,128)(2,1)S(1)}, u32[]{:S(2)}, u32[]{:S(2)}) collective-permute-start(bf16[8,16,1024]{2,1,0:T(8,128)(2,1)} %get-tuple-element.40), channel_id=1, source_target_pairs={{0,6},{1,7},{2,4},{3,5},{4,2},{5,3},{6,0},{7,1},{8,14},{9,15},{10,... | collective-permute-start | bytes 786440 | tf_op jit(solution)/shard_map/ppermute | solution.py:462
  26.6 29.2 %collective-permute-start.16 = (bf16[8,16,1024]{2,1,0:T(8,128)(2,1)}, bf16[8,16,1024]{2,1,0:T(8,128)(2,1)S(1)}, u32[]{:S(2)}, u32[]{:S(2)}) collective-permute-start(bf16[8,16,1024]{2,1,0:T(8,128)(2,1)} %get-tuple-element.35.refs_0_), channel_id=1, source_target_pairs={{0,4},{1,5},{2,6},{3,7},{4,0},{5,1},{6,2},{7,3},{8,12},{9,13},{10,... | collective-permute-start | bytes 786440 | tf_op jit(solution)/shard_map/ppermute | solution.py:462
  51.9 46.9 %copy-start.11 = (bf16[128,128]{1,0:T(8,128)(2,1)S(1)}, bf16[128,128]{1,0:T(8,128)(2,1)}, u32[]{:S(2)}) copy-start(bf16[128,128]{1,0:T(8,128)(2,1)} %param.11) | copy-start | bytes 98308
  51.9 10.5 %collective-permute-start.6 = (bf16[8,16,1024]{2,1,0:T(8,128)(2,1)}, bf16[8,16,1024]{2,1,0:T(8,128)(2,1)S(1)}, u32[]{:S(2)}, u32[]{:S(2)}) collective-permute-start(bf16[8,16,1024]{2,1,0:T(8,128)(2,1)} %gate.14), channel_id=1, source_target_pairs={{0,3},{1,2},{2,1},{3,0},{4,7},{5,6},{6,5},{7,4},{8,11},{9,10},{10,... | collective-permute-start | bytes 786440 | tf_op jit(solution)/shard_map/ppermute | solution.py:462
  55.3 21.3 %collective-permute-start.9 = (bf16[8,16,1024]{2,1,0:T(8,128)(2,1)}, bf16[8,16,1024]{2,1,0:T(8,128)(2,1)S(1)}, u32[]{:S(2)}, u32[]{:S(2)}) collective-permute-start(bf16[8,16,1024]{2,1,0:T(8,128)(2,1)} %get-tuple-element.42), channel_id=1, source_target_pairs={{0,2},{1,3},{2,0},{3,1},{4,6},{5,7},{6,4},{7,5},{8,10},{9,11},{10,... | collective-permute-start | bytes 786440 | tf_op jit(solution)/shard_map/ppermute | solution.py:462
  55.8 22.9 %collective-permute-start.17 = (bf16[8,16,1024]{2,1,0:T(8,128)(2,1)}, bf16[8,16,1024]{2,1,0:T(8,128)(2,1)S(1)}, u32[]{:S(2)}, u32[]{:S(2)}) collective-permute-start(bf16[8,16,1024]{2,1,0:T(8,128)(2,1)} %gate.22), channel_id=1, source_target_pairs={{0,7},{1,6},{2,5},{3,4},{4,3},{5,2},{6,1},{7,0},{8,15},{9,14},{10,... | collective-permute-start | bytes 786440 | tf_op jit(solution)/shard_map/ppermute | solution.py:462
  57.0 22.8 %collective-permute-start.12 = (bf16[8,16,1024]{2,1,0:T(8,128)(2,1)}, bf16[8,16,1024]{2,1,0:T(8,128)(2,1)S(1)}, u32[]{:S(2)}, u32[]{:S(2)}) collective-permute-start(bf16[8,16,1024]{2,1,0:T(8,128)(2,1)} %get-tuple-element.47), channel_id=1, source_target_pairs={{0,5},{1,4},{2,7},{3,6},{4,1},{5,0},{6,3},{7,2},{8,13},{9,12},{10,... | collective-permute-start | bytes 786440 | tf_op jit(solution)/shard_map/ppermute | solution.py:462
  62.5 20.6 %collective-permute-start.7 = (bf16[8,16,1024]{2,1,0:T(8,128)(2,1)}, bf16[8,16,1024]{2,1,0:T(8,128)(2,1)S(1)}, u32[]{:S(2)}, u32[]{:S(2)}) collective-permute-start(bf16[8,16,1024]{2,1,0:T(8,128)(2,1)} %gate.15), channel_id=1, source_target_pairs={{0,1},{1,0},{2,3},{3,2},{4,5},{5,4},{6,7},{7,6},{8,9},{9,8},{10,11... | collective-permute-start | bytes 786440 | tf_op jit(solution)/shard_map/ppermute | solution.py:462
  76.7 14.2 %collective-permute-start.10 = (bf16[8,16,1024]{2,1,0:T(8,128)(2,1)}, bf16[8,16,1024]{2,1,0:T(8,128)(2,1)S(1)}, u32[]{:S(2)}, u32[]{:S(2)}) collective-permute-start(bf16[8,16,1024]{2,1,0:T(8,128)(2,1)} %gate.17), channel_id=1, source_target_pairs={{0,2},{1,3},{2,0},{3,1},{4,6},{5,7},{6,4},{7,5},{8,10},{9,11},{10,... | collective-permute-start | bytes 786440 | tf_op jit(solution)/shard_map/ppermute | solution.py:462
  78.8 14.8 %collective-permute-start.18 = (bf16[5,16,1024]{2,1,0:T(8,128)(2,1)}, bf16[5,16,1024]{2,1,0:T(8,128)(2,1)S(1)}, u32[]{:S(2)}, u32[]{:S(2)}) collective-permute-start(bf16[5,16,1024]{2,1,0:T(8,128)(2,1)} %gate.23), channel_id=1, source_target_pairs={{0,6},{1,7},{2,4},{3,5},{4,2},{5,3},{6,0},{7,1},{8,14},{9,15},{10,... | collective-permute-start | bytes 491528 | tf_op jit(solution)/shard_map/ppermute | solution.py:462
  79.8 14.8 %collective-permute-start.13 = (bf16[5,16,1024]{2,1,0:T(8,128)(2,1)}, bf16[5,16,1024]{2,1,0:T(8,128)(2,1)S(1)}, u32[]{:S(2)}, u32[]{:S(2)}) collective-permute-start(bf16[5,16,1024]{2,1,0:T(8,128)(2,1)} %gate.19), channel_id=1, source_target_pairs={{0,4},{1,5},{2,6},{3,7},{4,0},{5,1},{6,2},{7,3},{8,12},{9,13},{10,... | collective-permute-start | bytes 491528 | tf_op jit(solution)/shard_map/ppermute | solution.py:462
  83.1 31.7 %collective-permute-start.8 = (bf16[8,16,1024]{2,1,0:T(8,128)(2,1)}, bf16[8,16,1024]{2,1,0:T(8,128)(2,1)S(1)}, u32[]{:S(2)}, u32[]{:S(2)}) collective-permute-start(bf16[8,16,1024]{2,1,0:T(8,128)(2,1)} %gate.16), channel_id=1, source_target_pairs={{0,1},{1,0},{2,3},{3,2},{4,5},{5,4},{6,7},{7,6},{8,9},{9,8},{10,11... | collective-permute-start | bytes 786440 | tf_op jit(solution)/shard_map/ppermute | solution.py:462
  90.8 24.8 %collective-permute-start.11 = (bf16[8,16,1024]{2,1,0:T(8,128)(2,1)}, bf16[8,16,1024]{2,1,0:T(8,128)(2,1)S(1)}, u32[]{:S(2)}, u32[]{:S(2)}) collective-permute-start(bf16[8,16,1024]{2,1,0:T(8,128)(2,1)} %gate.18), channel_id=1, source_target_pairs={{0,3},{1,2},{2,1},{3,0},{4,7},{5,6},{6,5},{7,4},{8,11},{9,10},{10,... | collective-permute-start | bytes 786440 | tf_op jit(solution)/shard_map/ppermute | solution.py:462
  93.5 11.4 %collective-permute-start.19 = (bf16[5,16,1024]{2,1,0:T(8,128)(2,1)}, bf16[5,16,1024]{2,1,0:T(8,128)(2,1)S(1)}, u32[]{:S(2)}, u32[]{:S(2)}) collective-permute-start(bf16[5,16,1024]{2,1,0:T(8,128)(2,1)} %gate.24), channel_id=1, source_target_pairs={{0,7},{1,6},{2,5},{3,4},{4,3},{5,2},{6,1},{7,0},{8,15},{9,14},{10,... | collective-permute-start | bytes 491528 | tf_op jit(solution)/shard_map/ppermute | solution.py:462
  95.2 16.5 %collective-permute-start.14 = (bf16[5,16,1024]{2,1,0:T(8,128)(2,1)}, bf16[5,16,1024]{2,1,0:T(8,128)(2,1)S(1)}, u32[]{:S(2)}, u32[]{:S(2)}) collective-permute-start(bf16[5,16,1024]{2,1,0:T(8,128)(2,1)} %gate.20), channel_id=1, source_target_pairs={{0,5},{1,4},{2,7},{3,6},{4,1},{5,0},{6,3},{7,2},{8,13},{9,12},{10,... | collective-permute-start | bytes 491528 | tf_op jit(solution)/shard_map/ppermute | solution.py:462
  104.9 16.6 %collective-permute-start.20 = (bf16[3,16,1024]{2,1,0:T(8,128)(2,1)}, bf16[3,16,1024]{2,1,0:T(8,128)(2,1)S(1)}, u32[]{:S(2)}, u32[]{:S(2)}) collective-permute-start(bf16[3,16,1024]{2,1,0:T(8,128)(2,1)} %gate.25), channel_id=1, source_target_pairs={{0,5},{1,4},{2,7},{3,6},{4,1},{5,0},{6,3},{7,2},{8,13},{9,12},{10,... | collective-permute-start | bytes 294920 | tf_op jit(solution)/shard_map/ppermute | solution.py:462
  111.7 10.6 %collective-permute-start.15 = (bf16[3,16,1024]{2,1,0:T(8,128)(2,1)}, bf16[3,16,1024]{2,1,0:T(8,128)(2,1)S(1)}, u32[]{:S(2)}, u32[]{:S(2)}) collective-permute-start(bf16[3,16,1024]{2,1,0:T(8,128)(2,1)} %gate.21), channel_id=1, source_target_pairs={{0,4},{1,5},{2,6},{3,7},{4,0},{5,1},{6,2},{7,3},{8,12},{9,13},{10,... | collective-permute-start | bytes 294920 | tf_op jit(solution)/shard_map/ppermute | solution.py:462
  114.8 11.9 %collective-permute-start.22 = (bf16[3,16,1024]{2,1,0:T(8,128)(2,1)}, bf16[3,16,1024]{2,1,0:T(8,128)(2,1)S(1)}, u32[]{:S(2)}, u32[]{:S(2)}) collective-permute-start(bf16[3,16,1024]{2,1,0:T(8,128)(2,1)} %gate.27), channel_id=1, source_target_pairs={{0,7},{1,6},{2,5},{3,4},{4,3},{5,2},{6,1},{7,0},{8,15},{9,14},{10,... | collective-permute-start | bytes 294920 | tf_op jit(solution)/shard_map/ppermute | solution.py:462
  116.3 12.4 %collective-permute-start.21 = (bf16[3,16,1024]{2,1,0:T(8,128)(2,1)}, bf16[3,16,1024]{2,1,0:T(8,128)(2,1)S(1)}, u32[]{:S(2)}, u32[]{:S(2)}) collective-permute-start(bf16[3,16,1024]{2,1,0:T(8,128)(2,1)} %gate.26), channel_id=1, source_target_pairs={{0,6},{1,7},{2,4},{3,5},{4,2},{5,3},{6,0},{7,1},{8,14},{9,15},{10,... | collective-permute-start | bytes 294920 | tf_op jit(solution)/shard_map/ppermute | solution.py:462
  (12 other events, 120.2 us)

commit v6 on v5

--- a/solution.py
+++ b/solution.py
@@ -11,6 +11,8 @@
 TAPS = 2 * REACH + 1
 LANES = 128
 GROUP = 8
+PER = 4
+PAIR = 2
 MIB = 1024 * 1024
 HALO = 2 * REACH
 
@@ -136,7 +138,7 @@
 def masked_sums(density, valid):
     slices, rows, cols = density.shape
     step = 32
-    edge = hbm((slices + 1, REACH, cols), jnp.bfloat16)
+    edge = jax.ShapeDtypeStruct((slices + 1, REACH, cols), jnp.bfloat16)
     return pl.pallas_call(
         sums_kernel,
         name="sums",
@@ -147,10 +149,10 @@
         ],
         out_specs=[pl.BlockSpec((slices + 8, LANES), lambda i: (0, 0))]
         + [pl.BlockSpec((slices + 1, REACH, cols), lambda i: (0, 0, 0))] * 2,
-        out_shape=[hbm((slices + 8, LANES), jnp.float32), edge, edge],
+        out_shape=[jax.ShapeDtypeStruct((slices + 8, LANES), jnp.float32), edge, edge],
         compiler_params=params(),
         cost_estimate=cost(1, 1),
-    )(held(density), held(valid))
+    )(density, valid)
 
 
 def mean_kernel(*refs):
@@ -248,7 +250,8 @@
         cost_estimate=cost(1, 1),
     )(
         jnp.concatenate([ids, jnp.full((1,), last, ids.dtype)]),
-        *[held(x) for x in (density, density, density, valid, valid, valid)],
+        *([density] * 3),
+        *([valid] * 3),
         above,
         below,
         row_taps,
@@ -276,28 +279,32 @@
     def _():
         for k in range(terms):
             taps[:, k] = jnp.dot(col_taps[k], tap_flip(), preferred_element_type=f32)
-        col[LANES + HALO :, :] = jnp.zeros((LANES - HALO, terms * LANES), jnp.bfloat16)
+        col[:, LANES + HALO :, :] = jnp.zeros((PER, LANES - HALO, terms * LANES), jnp.bfloat16)
         build_rows(listed(row_taps), row)
         mask[:REACH] = above[slices].astype(f32)
         mask[REACH : REACH + rows] = valid[...].astype(f32)
         mask[REACH + rows :] = below[slices].astype(f32)
 
-    @pl.when(step < slices)
+    steps = slices // PER
+
+    @pl.when(step < steps)
     def _():
-        mine = taps[step]
-        for k in range(terms):
-            col[: LANES + HALO, k * LANES : (k + 1) * LANES] = column_band(mine[k : k + 1])
-        x = jnp.concatenate([above[step].astype(f32), density[0].astype(f32), below[step].astype(f32)], axis=0)
-        x = mask[...] * (x - mean[pl.ds(step, 1), :][:, :1])
-        x = jnp.concatenate([x, jnp.zeros((rows + HALO, LANES), f32)], axis=1)
-        x = pltpu.roll(x, REACH, 1).astype(jnp.bfloat16)
-        x = jnp.concatenate([x[:, c : c + 2 * LANES] for c in range(0, cols, LANES)], axis=0)
-        y = jnp.dot(x, col[...], preferred_element_type=f32).astype(jnp.bfloat16)
-        for c in range(cols // LANES):
+        for j in range(PER):
+            s = step * PER + j
+            mine = taps[s]
             for k in range(terms):
-                tall[step * terms + k, :, c * LANES : (c + 1) * LANES] = y[
-                    c * (rows + HALO) : (c + 1) * (rows + HALO), k * LANES : (k + 1) * LANES
-                ]
+                col[j, : LANES + HALO, k * LANES : (k + 1) * LANES] = column_band(mine[k : k + 1])
+            x = jnp.concatenate([above[s].astype(f32), density[j].astype(f32), below[s].astype(f32)], axis=0)
+            x = mask[...] * (x - mean[pl.ds(s, 1), :][:, :1])
+            x = jnp.concatenate([x, jnp.zeros((rows + HALO, LANES), f32)], axis=1)
+            x = pltpu.roll(x, REACH, 1).astype(jnp.bfloat16)
+            x = jnp.concatenate([x[:, c : c + 2 * LANES] for c in range(0, cols, LANES)], axis=0)
+            y = jnp.dot(x, col[j], preferred_element_type=f32).astype(jnp.bfloat16)
+            for c in range(cols // LANES):
+                for k in range(terms):
+                    tall[s * terms + k, :, c * LANES : (c + 1) * LANES] = y[
+                        c * (rows + HALO) : (c + 1) * (rows + HALO), k * LANES : (k + 1) * LANES
+                    ]
 
     def copies(b):
         at = sum(len(wanted) for wanted in pieces[:b])
@@ -306,25 +313,27 @@
             here = jnp.where(last != (inner == 1), block - REACH, 0) + start
             yield pltpu.make_async_copy(done.at[b, pl.ds(here, stop - start)], outs[at + p], sems.at[at + p])
 
-    @pl.when(step >= slices)
+    @pl.when(step >= steps)
     def _():
-        b = step - slices
-        here = pl.ds(pl.multiple_of(ids[b] * block, block), high)
-        parts = []
-        for g in range(slices // GROUP):
-            slab = tall[g * GROUP * terms : (g + 1) * GROUP * terms, here, :].reshape(GROUP * LANES, cols)
-            z = jnp.dot(row[g], slab, preferred_element_type=f32)
-            parts.append(z.reshape(block, GROUP, cols))
-        done[b] = jnp.concatenate(parts, axis=1).astype(jnp.bfloat16)
-
-    for b in range(len(pieces)):
-
-        @pl.when(step == slices + b)
+        for j in range(PAIR):
+            b = (step - steps) * PAIR + j
+            here = pl.ds(pl.multiple_of(ids[b] * block, block), high)
+            parts = []
+            for g in range(slices // GROUP):
+                slab = tall[g * GROUP * terms : (g + 1) * GROUP * terms, here, :].reshape(GROUP * LANES, cols)
+                z = jnp.dot(row[g], slab, preferred_element_type=f32)
+                parts.append(z.reshape(block, GROUP, cols))
+            done[b] = jnp.concatenate(parts, axis=1).astype(jnp.bfloat16)
+
+    for n in range(len(pieces) // PAIR):
+
+        @pl.when(step == steps + n)
         def _():
-            for copy in copies(b):
-                copy.start()
-
-    @pl.when(step == slices + len(pieces) - 1)
+            for b in range(n * PAIR, (n + 1) * PAIR):
+                for copy in copies(b):
+                    copy.start()
+
+    @pl.when(step == pl.num_programs(0) - 1)
     def _():
         for b in range(len(pieces)):
             for copy in copies(b):
@@ -346,13 +355,13 @@
         name="band",
         grid_spec=pltpu.PrefetchScalarGridSpec(
             num_scalar_prefetch=1,
-            grid=(slices + count,),
-            in_specs=[pl.BlockSpec((1, rows, cols), lambda i, at: (jnp.minimum(i, slices - 1), 0, 0))]
+            grid=(slices // PER + count // PAIR,),
+            in_specs=[pl.BlockSpec((PER, rows, cols), lambda i, at: (jnp.minimum(i, slices // PER - 1), 0, 0))]
             + [whole(x) for x in (valid, above, below, row_taps, col_taps, mean)]
             + [anywhere()] * len(after),
             out_specs=[anywhere()] * len(shapes),
             scratch_shapes=[
-                pltpu.VMEM((2 * LANES, terms * LANES), jnp.bfloat16),
+                pltpu.VMEM((PER, 2 * LANES, terms * LANES), jnp.bfloat16),
                 pltpu.VMEM((slices // GROUP, block * GROUP, GROUP * LANES), jnp.bfloat16),
                 pltpu.VMEM((slices, terms, 2 * LANES), jnp.float32),
                 pltpu.VMEM((rows + HALO, cols), jnp.float32),
@@ -366,8 +375,8 @@
         cost_estimate=cost(1, 1),
     )(
         jnp.concatenate([ids, jnp.full((1,), rows // block - 1, ids.dtype)]),
-        held(density),
-        held(valid),
+        density,
+        valid,
         above,
         below,
         row_taps,
@@ -433,9 +442,9 @@
 
 INNER, OUTER, HEAD, TAIL = (1, 0, REACH), (0, 0, REACH), (0, 0, 5), (0, 5, REACH)
 LATE = (4, 6, 5, 7)
-FIRST = ((4, (INNER,)), (6, (INNER,)))
+FIRST = ((4,), (6, 5))
 REST = (
-    (5, (INNER, HEAD, TAIL)),
+    (5, (HEAD, TAIL)),
     (7, (INNER, HEAD, TAIL)),
     (2, (INNER, OUTER)),
     (3, (INNER, OUTER)),
@@ -445,10 +454,10 @@
     (0, (INNER, OUTER)),
 )
 ORDER = (
-    (4, 0), (6, 0), (5, 0), (2, 0), (7, 0), (3, 0), (4, 1), (2, 1), (6, 1), (1, 0), (5, 1), (3, 1), (7, 1), (1, 1),
+    (4, 0), (6, 0), (5, 0), (7, 0), (2, 0), (4, 1), (3, 0), (6, 1), (2, 1), (5, 1), (1, 0), (7, 1), (3, 1), (1, 1),
     (4, 2), (6, 2), (5, 2), (7, 2),
 )
-IN_FLIGHT = 4
+WAITS = {3: 1, 4: 1, 5: 2, 6: 2, **{at: at - 4 for at in range(7, len(ORDER))}}
 
 
 def fast(density, valid, row_taps, col_taps, amp_matrix, like_matrix):
@@ -463,8 +472,6 @@
 
     own, first, last = masked_sums(density, valid)
     sums = [own] + [lax.ppermute(own, "tile", [(i, i ^ k) for i in range(tiles)]) for k in range(1, tiles)]
-    above = lax.ppermute(last, "tile", [(i, i + 1) for i in range(tiles - 1)])
-    below = lax.ppermute(first, "tile", [(i + 1, i) for i in range(tiles - 1)])
     mean = means(sums, slices)
 
     made, arrived = {}, {}
@@ -480,8 +487,15 @@
                 if k == 0:
                     arrived[k, p] = x
 
-    filter_for(filter_blocks, FIRST, last, first)
-    filter_for(filter_band, REST, above, below, made[4, 0])
+    above = lax.ppermute(last, "tile", [(i, i + 1) for i in range(tiles - 1)])
+    below = lax.ppermute(first, "tile", [(i + 1, i) for i in range(tiles - 1)])
+    after = ()
+    for ks in FIRST:
+        filter_for(filter_blocks, [(k, (INNER,)) for k in ks], last, first, *after)
+        after = (made[ks[0], 0],)
+        for k in ks:
+            arrived[k, 0] = swap(made[k, 0], k)
+    filter_for(filter_band, REST, above, below, *after, gate(mean, arrived[4, 0]))
     weights = jnp.concatenate([amp_matrix, like_matrix], axis=1).T.reshape(-1, peers, slices)
     weights = weights[:, me ^ jnp.arange(peers)].reshape(-1, peers * slices)
     result, tokens = [], []
@@ -494,7 +508,9 @@
         tokens.append(token)
 
     for at, (k, p) in enumerate(ORDER):
-        before = [arrived[ORDER[at - IN_FLIGHT]]] if at >= IN_FLIGHT else []
+        if (k, p) in arrived:
+            continue
+        before = [arrived[ORDER[WAITS[at]]]] if at in WAITS else []
         if at == len(ORDER) - 3:
             finish(0)
             before.append(tokens[0])

time: 132 us -> 134 us (1.015)
  the two profiles are of different devices: /device:TPU:13 before, /device:TPU:0 now
where the time goes in v6:
time: 134 us; the launch traced here: 133 us
  starting transfers between devices  46.5 us (35%)
  Pallas kernels  39 us (29%)
  waiting for transfers between devices  32 us (24%)
  local copies, waits for them, and re-layouts  14.7 us (11%)
    ppermute x18, starting transfers between devices, swap(): return lax.ppermute(x, 'cuts', [(i, i ^ k) for i in range(peers)])  36.8 us
    ppermute x18, waiting for transfers between devices, swap(): return lax.ppermute(x, 'cuts', [(i, i ^ k) for i in range(peers)])  32 us
    pallas_call x1, Pallas kernels, filter_band(): pl.pallas_call(functools.partial(band_kernel, pieces), name='band', grid_...  15.8 us
    unnamed x35, local copies, waits for them, and re-layouts  14 us
    pallas_call x2, Pallas kernels, filter_blocks(): pl.pallas_call(functools.partial(filter_kernel, pieces), name='filter', g...  11.9 us
    pallas_call x3, Pallas kernels, project(): pl.pallas_call(functools.partial(project_kernel, count), name='project',...  9.64 us
    ppermute x3, starting transfers between devices, fast(): lax.ppermute(own, 'tile', [(i, i ^ k) for i in range(tiles)])  4.6 us
    ppermute x1, starting transfers between devices, fast(): above = lax.ppermute(last, 'tile', [(i, i + 1) for i in range(tiles - 1)])  3.8 us
  transfers between devices with their start and end apart: 23, of which 8 were waited for; matrix products, arithmetic and copies ran while one was open for 1% of the time, Pallas kernels for 27%

profile of v6, /device:TPU:0, one launch (start us, length us, event | category | flops | bytes accessed | tf_op | source)
XLA Modules:
  0.0 133.3 jit_solution(18233329527193853553)
XLA Ops:
  0.6 2.2 %copy-done = bf16[16,128,1024]{2,1,0:T(8,128)(2,1)S(1)} copy-done((bf16[16,128,1024]{2,1,0:T(8,128)(2,1)S(1)}, bf16[16,128,1024]{2,1,0:T(8,128)(2,1)}, u32[]{:S(2)}) %copy-start) | copy-done | bytes 4194328
  5.4 4.0 %collective-permute-start.4 = (f32[24,128]{1,0:T(8,128)S(1)}, f32[24,128]{1,0:T(8,128)S(1)}, u32[]{:S(2)}, u32[]{:S(2)}) collective-permute-start(f32[24,128]{1,0:T(8,128)S(1)} %get-tuple-element.33.refs_0_), channel_id=1, source_target_pairs={{0,24},{8,16},{16,8},{24,0},{1,25},{9,17},{17,9},{25,1},{2,26},{10... | collective-permute-start | bytes 36872 | tf_op jit(solution)/shard_map/ppermute | solution.py:474
  10.1 3.8 %collective-permute-start = (bf16[17,8,1024]{2,1,0:T(8,128)(2,1)S(1)}, bf16[17,8,1024]{2,1,0:T(8,128)(2,1)S(1)}, u32[]{:S(2)}, u32[]{:S(2)}) collective-permute-start(bf16[17,8,1024]{2,1,0:T(8,128)(2,1)S(1)} %get-tuple-element.31.refs_0_), channel_id=1, source_target_pairs={{0,8},{8,16},{16,24},{1,9},{9,17},{17,25},{2,10},{10,18},{18,26},{... | collective-permute-start | bytes 835592 | tf_op jit(solution)/shard_map/ppermute | solution.py:490
  15.4 2.2 %copy-done.1 = bf16[16,128,1024]{2,1,0:T(8,128)(2,1)S(1)} copy-done((bf16[16,128,1024]{2,1,0:T(8,128)(2,1)S(1)}, bf16[16,128,1024]{2,1,0:T(8,128)(2,1)}, u32[]{:S(2)}) %copy-start.1) | copy-done | bytes 4194328
  17.5 4.2 %filter.2.refs_5_ = bf16[8,16,1024]{2,1,0:T(8,128)(2,1)} custom-call(s32[2]{0:T(128)S(1)} %pad_add_fusion.1.ids, bf16[16,128,1024]{2,1,0:T(8,128)(2,1)S(1)} %copy-done.1, bf16[16,128,1024]{2,1,0:T(8,128)(2,1)S(1)} %copy-done.1, bf16[16,128,1024]{2,1,0:T(8,128)(2,1)S(1)} %copy-done.1, s32[128,1024]{1,0:T(8,128)S(1)} %copy-done.4, s32[128,1024]{1,0:T(8,128)S(1)} %copy-done.4, ...), custom_call_target="tpu_custom_call" | custom-call | flops 1 | bytes 1 | tf_op jit(solution)/shard_map/filter/pallas_call | solution.py:231
  21.8 2.6 %collective-permute-start.5 = (bf16[8,16,1024]{2,1,0:T(8,128)(2,1)}, bf16[8,16,1024]{2,1,0:T(8,128)(2,1)S(1)}, u32[]{:S(2)}, u32[]{:S(2)}) collective-permute-start(bf16[8,16,1024]{2,1,0:T(8,128)(2,1)} %filter.2.refs_5_), channel_id=1, source_target_pairs={{0,4},{1,5},{2,6},{3,7},{4,0},{5,1},{6,2},{7,3},{8,12},{9,13},{10,... | collective-permute-start | bytes 786440 | tf_op jit(solution)/shard_map/ppermute | solution.py:471
  25.4 7.6 %filter.3 = (bf16[8,16,1024]{2,1,0:T(8,128)(2,1)}, bf16[8,16,1024]{2,1,0:T(8,128)(2,1)}) custom-call(s32[3]{0:T(128)S(1)} %pad_add_fusion.ids, bf16[16,128,1024]{2,1,0:T(8,128)(2,1)S(1)} %copy-done.1, bf16[16,128,1024]{2,1,0:T(8,128)(2,1)S(1)} %copy-done.1, bf16[16,128,1024]{2,1,0:T(8,128)(2,1)S(1)} %copy-done.1, s32[128,1024]{1,0:T(8,128)S(1)} %copy-done.4, ...), custom_call_target="tpu_custom_call" | custom-call | flops 1 | bytes 1 | tf_op jit(solution)/shard_map/filter/pallas_call | solution.py:231
  35.5 2.2 %copy-done.2 = bf16[16,128,1024]{2,1,0:T(8,128)(2,1)S(1)} copy-done((bf16[16,128,1024]{2,1,0:T(8,128)(2,1)S(1)}, bf16[16,128,1024]{2,1,0:T(8,128)(2,1)}, u32[]{:S(2)}) %copy-start.2) | copy-done | bytes 4194328
  39.4 15.8 %band.1 = (bf16[5,16,1024]{2,1,0:T(8,128)(2,1)}, bf16[3,16,1024]{2,1,0:T(8,128)(2,1)}, bf16[8,16,1024]{2,1,0:T(8,128)(2,1)}, bf16[5,16,1024]{2,1,0:T(8,128)(2,1)...) custom-call(s32[9]{0:T(128)S(1)} %concatenate.13.ids, ...), custom_call_target="tpu_custom_call" | custom-call | flops 1 | bytes 1 | tf_op jit(solution)/shard_map/band/pallas_call | solution.py:353
  55.3 12.1 %collective-permute-start.11 = (bf16[8,16,1024]{2,1,0:T(8,128)(2,1)}, bf16[8,16,1024]{2,1,0:T(8,128)(2,1)S(1)}, u32[]{:S(2)}, u32[]{:S(2)}) collective-permute-start(bf16[8,16,1024]{2,1,0:T(8,128)(2,1)} %gate.20), channel_id=1, source_target_pairs={{0,2},{1,3},{2,0},{3,1},{4,6},{5,7},{6,4},{7,5},{8,10},{9,11},{10,... | collective-permute-start | bytes 786440 | tf_op jit(solution)/shard_map/ppermute | solution.py:471
  67.3 3.3 %collective-permute-start.7 = (bf16[5,16,1024]{2,1,0:T(8,128)(2,1)}, bf16[5,16,1024]{2,1,0:T(8,128)(2,1)S(1)}, u32[]{:S(2)}, u32[]{:S(2)}) collective-permute-start(bf16[5,16,1024]{2,1,0:T(8,128)(2,1)} %gate.17), channel_id=1, source_target_pairs={{0,4},{1,5},{2,6},{3,7},{4,0},{5,1},{6,2},{7,3},{8,12},{9,13},{10,... | collective-permute-start | bytes 491528 | tf_op jit(solution)/shard_map/ppermute | solution.py:471
  71.0 7.2 %collective-permute-done.11.refs_1_.refs_2_ = bf16[8,16,1024]{2,1,0:T(8,128)(2,1)S(1)} collective-permute-done((bf16[8,16,1024]{2,1,0:T(8,128)(2,1)}, bf16[8,16,1024]{2,1,0:T(8,128)(2,1)S(1)}, u32[]{:S(2)}, u32[]{:S(2)}) %collective-permute-start.11) | collective-permute-done | bytes 262176 | tf_op jit(solution)/shard_map/ppermute | solution.py:471
  78.2 2.8 %collective-permute-start.8 = (bf16[5,16,1024]{2,1,0:T(8,128)(2,1)}, bf16[5,16,1024]{2,1,0:T(8,128)(2,1)S(1)}, u32[]{:S(2)}, u32[]{:S(2)}) collective-permute-start(bf16[5,16,1024]{2,1,0:T(8,128)(2,1)} %gate.18), channel_id=1, source_target_pairs={{0,5},{1,4},{2,7},{3,6},{4,1},{5,0},{6,3},{7,2},{8,13},{9,12},{10,... | collective-permute-start | bytes 491528 | tf_op jit(solution)/shard_map/ppermute | solution.py:471
  81.0 4.3 %collective-permute-done.18.refs_1_.refs_7_ = bf16[8,16,1024]{2,1,0:T(8,128)(2,1)S(1)} collective-permute-done((bf16[8,16,1024]{2,1,0:T(8,128)(2,1)}, bf16[8,16,1024]{2,1,0:T(8,128)(2,1)S(1)}, u32[]{:S(2)}, u32[]{:S(2)}) %collective-permute-start.18) | collective-permute-done | bytes 262176 | tf_op jit(solution)/shard_map/ppermute | solution.py:471
  85.3 3.5 %collective-permute-start.19 = (bf16[5,16,1024]{2,1,0:T(8,128)(2,1)}, bf16[5,16,1024]{2,1,0:T(8,128)(2,1)S(1)}, u32[]{:S(2)}, u32[]{:S(2)}) collective-permute-start(bf16[5,16,1024]{2,1,0:T(8,128)(2,1)} %gate.28), channel_id=1, source_target_pairs={{0,6},{1,7},{2,4},{3,5},{4,2},{5,3},{6,0},{7,1},{8,14},{9,15},{10,... | collective-permute-start | bytes 491528 | tf_op jit(solution)/shard_map/ppermute | solution.py:471
  90.3 8.0 %collective-permute-done.8.refs_1_.refs_5_ = bf16[5,16,1024]{2,1,0:T(8,128)(2,1)S(1)} collective-permute-done((bf16[5,16,1024]{2,1,0:T(8,128)(2,1)}, bf16[5,16,1024]{2,1,0:T(8,128)(2,1)S(1)}, u32[]{:S(2)}, u32[]{:S(2)}) %collective-permute-start.8) | collective-permute-done | bytes 163872 | tf_op jit(solution)/shard_map/ppermute | solution.py:471
  98.4 3.0 %collective-permute-start.13 = (bf16[8,16,1024]{2,1,0:T(8,128)(2,1)}, bf16[8,16,1024]{2,1,0:T(8,128)(2,1)S(1)}, u32[]{:S(2)}, u32[]{:S(2)}) collective-permute-start(bf16[8,16,1024]{2,1,0:T(8,128)(2,1)} %gate.22), channel_id=1, source_target_pairs={{0,3},{1,2},{2,1},{3,0},{4,7},{5,6},{6,5},{7,4},{8,11},{9,10},{10,... | collective-permute-start | bytes 786440 | tf_op jit(solution)/shard_map/ppermute | solution.py:471
  101.4 2.8 %collective-permute-done.19.refs_1_.refs_6_ = bf16[5,16,1024]{2,1,0:T(8,128)(2,1)S(1)} collective-permute-done((bf16[5,16,1024]{2,1,0:T(8,128)(2,1)}, bf16[5,16,1024]{2,1,0:T(8,128)(2,1)S(1)}, u32[]{:S(2)}, u32[]{:S(2)}) %collective-permute-start.19) | collective-permute-done | bytes 163872 | tf_op jit(solution)/shard_map/ppermute | solution.py:471
  107.6 4.4 %project.3 = (bf16[128,16384]{1,0:T(8,128)(2,1)}, bf16[128,16384]{1,0:T(8,128)(2,1)}, f32[8,128]{1,0:T(8,128)}) custom-call(s32[1]{0:T(128)} %bitcast.14.place, bf16[256,128]{1,0:T(8,128)(2,1)S(1)} %copy.30.weights, bf16[8,16,1024]{2,1,0:T(8,128)(2,1)S(1)} %copy-done.9, bf16[8,16,1024]{2,1,0:T(8,128)(2,1)S(1)} %collective-permute-done.15.refs_1_, ...), custom_call_target="tpu_custom_call" | custom-call | flops 1 | bytes 1 | tf_op jit(solution)/shard_map/project/pallas_call | solution.py:407
  112.1 2.6 %collective-permute-start.22 = (bf16[3,16,1024]{2,1,0:T(8,128)(2,1)}, bf16[3,16,1024]{2,1,0:T(8,128)(2,1)S(1)}, u32[]{:S(2)}, u32[]{:S(2)}) collective-permute-start(bf16[3,16,1024]{2,1,0:T(8,128)(2,1)} %gate.31), channel_id=1, source_target_pairs={{0,7},{1,6},{2,5},{3,4},{4,3},{5,2},{6,1},{7,0},{8,15},{9,14},{10,... | collective-permute-start | bytes 294920 | tf_op jit(solution)/shard_map/ppermute | solution.py:471
  115.6 1.6 %collective-permute-start.21 = (bf16[3,16,1024]{2,1,0:T(8,128)(2,1)}, bf16[3,16,1024]{2,1,0:T(8,128)(2,1)S(1)}, u32[]{:S(2)}, u32[]{:S(2)}) collective-permute-start(bf16[3,16,1024]{2,1,0:T(8,128)(2,1)} %gate.30), channel_id=1, source_target_pairs={{0,6},{1,7},{2,4},{3,5},{4,2},{5,3},{6,0},{7,1},{8,14},{9,15},{10,... | collective-permute-start | bytes 294920 | tf_op jit(solution)/shard_map/ppermute | solution.py:471
  119.7 3.1 %project.4 = (bf16[128,16384]{1,0:T(8,128)(2,1)}, bf16[128,16384]{1,0:T(8,128)(2,1)}, f32[8,128]{1,0:T(8,128)}) custom-call(s32[1]{0:T(128)} %bitcast.15.place, bf16[256,128]{1,0:T(8,128)(2,1)S(1)} %copy.30.weights, bf16[8,16,1024]{2,1,0:T(8,128)(2,1)S(1)} %copy-done.6, ...), custom_call_target="tpu_custom_call", output_to_operand_aliasing={{0}: (10, {}), {1}: (11, {})} | custom-call | flops 1 | bytes 1 | tf_op jit(solution)/shard_map/project/pallas_call | solution.py:407
  122.8 8.5 %collective-permute-done.17.refs_5_ = bf16[3,16,1024]{2,1,0:T(8,128)(2,1)S(1)} collective-permute-done((bf16[3,16,1024]{2,1,0:T(8,128)(2,1)}, bf16[3,16,1024]{2,1,0:T(8,128)(2,1)S(1)}, u32[]{:S(2)}, u32[]{:S(2)}) %collective-permute-start.17) | collective-permute-done | bytes 98336 | tf_op jit(solution)/shard_map/ppermute | solution.py:471
  131.3 2.1 %project.5 = (bf16[128,16384]{1,0:T(8,128)(2,1)}, bf16[128,16384]{1,0:T(8,128)(2,1)}, f32[8,128]{1,0:T(8,128)}) custom-call(s32[1]{0:T(128)} %bitcast.place, bf16[256,128]{1,0:T(8,128)(2,1)S(1)} %copy.30.weights, bf16[8,16,1024]{2,1,0:T(8,128)(2,1)S(1)} %copy-done.6, ...), custom_call_target="tpu_custom_call", output_to_operand_aliasing={{0}: (10, {}), {1}: (11, {})} | custom-call | flops 1 | bytes 1 | tf_op jit(solution)/shard_map/project/pallas_call | solution.py:407
  (89 shorter events, 18.5 us)
Async XLA Ops:
  5.4 9.8 %collective-permute-start.4 = (f32[24,128]{1,0:T(8,128)S(1)}, f32[24,128]{1,0:T(8,128)S(1)}, u32[]{:S(2)}, u32[]{:S(2)}) collective-permute-start(f32[24,128]{1,0:T(8,128)S(1)} %get-tuple-element.33.refs_0_), channel_id=1, source_target_pairs={{0,24},{8,16},{16,8},{24,0},{1,25},{9,17},{17,9},{25,1},{2,26},{10... | collective-permute-start | bytes 36872 | tf_op jit(solution)/shard_map/ppermute | solution.py:474
  9.4 5.8 %collective-permute-start.3 = (f32[24,128]{1,0:T(8,128)S(1)}, f32[24,128]{1,0:T(8,128)S(1)}, u32[]{:S(2)}, u32[]{:S(2)}) collective-permute-start(f32[24,128]{1,0:T(8,128)S(1)} %get-tuple-element.33.refs_0_), channel_id=1, source_target_pairs={{0,16},{8,24},{16,0},{24,8},{1,17},{9,25},{17,1},{25,9},{2,18},{10... | collective-permute-start | bytes 36872 | tf_op jit(solution)/shard_map/ppermute | solution.py:474
  9.9 5.3 %collective-permute-start.2 = (f32[24,128]{1,0:T(8,128)S(1)}, f32[24,128]{1,0:T(8,128)S(1)}, u32[]{:S(2)}, u32[]{:S(2)}) collective-permute-start(f32[24,128]{1,0:T(8,128)S(1)} %get-tuple-element.33.refs_0_), channel_id=1, source_target_pairs={{0,8},{8,0},{16,24},{24,16},{1,9},{9,1},{17,25},{25,17},{2,10},{10... | collective-permute-start | bytes 36872 | tf_op jit(solution)/shard_map/ppermute | solution.py:474
  10.1 25.5 %collective-permute-start = (bf16[17,8,1024]{2,1,0:T(8,128)(2,1)S(1)}, bf16[17,8,1024]{2,1,0:T(8,128)(2,1)S(1)}, u32[]{:S(2)}, u32[]{:S(2)}) collective-permute-start(bf16[17,8,1024]{2,1,0:T(8,128)(2,1)S(1)} %get-tuple-element.31.refs_0_), channel_id=1, source_target_pairs={{0,8},{8,16},{16,24},{1,9},{9,17},{17,25},{2,10},{10,18},{18,26},{... | collective-permute-start | bytes 835592 | tf_op jit(solution)/shard_map/ppermute | solution.py:490
  13.9 21.7 %collective-permute-start.1 = (bf16[17,8,1024]{2,1,0:T(8,128)(2,1)S(1)}, bf16[17,8,1024]{2,1,0:T(8,128)(2,1)S(1)}, u32[]{:S(2)}, u32[]{:S(2)}) collective-permute-start(bf16[17,8,1024]{2,1,0:T(8,128)(2,1)S(1)} %get-tuple-element.32.refs_1_), channel_id=1, source_target_pairs={{8,0},{16,8},{24,16},{9,1},{17,9},{25,17},{10,2},{18,10},{26,18},{... | collective-permute-start | bytes 835592 | tf_op jit(solution)/shard_map/ppermute | solution.py:491
  21.8 13.7 %collective-permute-start.5 = (bf16[8,16,1024]{2,1,0:T(8,128)(2,1)}, bf16[8,16,1024]{2,1,0:T(8,128)(2,1)S(1)}, u32[]{:S(2)}, u32[]{:S(2)}) collective-permute-start(bf16[8,16,1024]{2,1,0:T(8,128)(2,1)} %filter.2.refs_5_), channel_id=1, source_target_pairs={{0,4},{1,5},{2,6},{3,7},{4,0},{5,1},{6,2},{7,3},{8,12},{9,13},{10,... | collective-permute-start | bytes 786440 | tf_op jit(solution)/shard_map/ppermute | solution.py:471
  33.0 22.2 %collective-permute-start.10 = (bf16[8,16,1024]{2,1,0:T(8,128)(2,1)}, bf16[8,16,1024]{2,1,0:T(8,128)(2,1)S(1)}, u32[]{:S(2)}, u32[]{:S(2)}) collective-permute-start(bf16[8,16,1024]{2,1,0:T(8,128)(2,1)} %get-tuple-element.34.refs_0_), channel_id=1, source_target_pairs={{0,6},{1,7},{2,4},{3,5},{4,2},{5,3},{6,0},{7,1},{8,14},{9,15},{10,... | collective-permute-start | bytes 786440 | tf_op jit(solution)/shard_map/ppermute | solution.py:471
  34.4 33.0 %collective-permute-start.6 = (bf16[8,16,1024]{2,1,0:T(8,128)(2,1)}, bf16[8,16,1024]{2,1,0:T(8,128)(2,1)S(1)}, u32[]{:S(2)}, u32[]{:S(2)}) collective-permute-start(bf16[8,16,1024]{2,1,0:T(8,128)(2,1)} %get-tuple-element.39), channel_id=1, source_target_pairs={{0,5},{1,4},{2,7},{3,6},{4,1},{5,0},{6,3},{7,2},{8,13},{9,12},{10,... | collective-permute-start | bytes 786440 | tf_op jit(solution)/shard_map/ppermute | solution.py:471
  55.2 50.6 %copy-start.15 = (bf16[128,128]{1,0:T(8,128)(2,1)S(1)}, bf16[128,128]{1,0:T(8,128)(2,1)}, u32[]{:S(2)}) copy-start(bf16[128,128]{1,0:T(8,128)(2,1)} %param.11) | copy-start | bytes 98308
  55.3 22.9 %collective-permute-start.11 = (bf16[8,16,1024]{2,1,0:T(8,128)(2,1)}, bf16[8,16,1024]{2,1,0:T(8,128)(2,1)S(1)}, u32[]{:S(2)}, u32[]{:S(2)}) collective-permute-start(bf16[8,16,1024]{2,1,0:T(8,128)(2,1)} %gate.20), channel_id=1, source_target_pairs={{0,2},{1,3},{2,0},{3,1},{4,6},{5,7},{6,4},{7,5},{8,10},{9,11},{10,... | collective-permute-start | bytes 786440 | tf_op jit(solution)/shard_map/ppermute | solution.py:471
  67.3 10.8 %collective-permute-start.7 = (bf16[5,16,1024]{2,1,0:T(8,128)(2,1)}, bf16[5,16,1024]{2,1,0:T(8,128)(2,1)S(1)}, u32[]{:S(2)}, u32[]{:S(2)}) collective-permute-start(bf16[5,16,1024]{2,1,0:T(8,128)(2,1)} %gate.17), channel_id=1, source_target_pairs={{0,4},{1,5},{2,6},{3,7},{4,0},{5,1},{6,2},{7,3},{8,12},{9,13},{10,... | collective-permute-start | bytes 491528 | tf_op jit(solution)/shard_map/ppermute | solution.py:471
  70.6 14.6 %collective-permute-start.18 = (bf16[8,16,1024]{2,1,0:T(8,128)(2,1)}, bf16[8,16,1024]{2,1,0:T(8,128)(2,1)S(1)}, u32[]{:S(2)}, u32[]{:S(2)}) collective-permute-start(bf16[8,16,1024]{2,1,0:T(8,128)(2,1)} %gate.27), channel_id=1, source_target_pairs={{0,7},{1,6},{2,5},{3,4},{4,3},{5,2},{6,1},{7,0},{8,15},{9,14},{10,... | collective-permute-start | bytes 786440 | tf_op jit(solution)/shard_map/ppermute | solution.py:471
  70.6 18.6 %collective-permute-start.14 = (bf16[8,16,1024]{2,1,0:T(8,128)(2,1)}, bf16[8,16,1024]{2,1,0:T(8,128)(2,1)S(1)}, u32[]{:S(2)}, u32[]{:S(2)}) collective-permute-start(bf16[8,16,1024]{2,1,0:T(8,128)(2,1)} %gate.23), channel_id=1, source_target_pairs={{0,3},{1,2},{2,1},{3,0},{4,7},{5,6},{6,5},{7,4},{8,11},{9,10},{10,... | collective-permute-start | bytes 786440 | tf_op jit(solution)/shard_map/ppermute | solution.py:471
  78.2 20.2 %collective-permute-start.12 = (bf16[8,16,1024]{2,1,0:T(8,128)(2,1)}, bf16[8,16,1024]{2,1,0:T(8,128)(2,1)S(1)}, u32[]{:S(2)}, u32[]{:S(2)}) collective-permute-start(bf16[8,16,1024]{2,1,0:T(8,128)(2,1)} %gate.21), channel_id=1, source_target_pairs={{0,2},{1,3},{2,0},{3,1},{4,6},{5,7},{6,4},{7,5},{8,10},{9,11},{10,... | collective-permute-start | bytes 786440 | tf_op jit(solution)/shard_map/ppermute | solution.py:471
  78.2 20.2 %collective-permute-start.8 = (bf16[5,16,1024]{2,1,0:T(8,128)(2,1)}, bf16[5,16,1024]{2,1,0:T(8,128)(2,1)S(1)}, u32[]{:S(2)}, u32[]{:S(2)}) collective-permute-start(bf16[5,16,1024]{2,1,0:T(8,128)(2,1)} %gate.18), channel_id=1, source_target_pairs={{0,5},{1,4},{2,7},{3,6},{4,1},{5,0},{6,3},{7,2},{8,13},{9,12},{10,... | collective-permute-start | bytes 491528 | tf_op jit(solution)/shard_map/ppermute | solution.py:471
  85.3 19.0 %collective-permute-start.19 = (bf16[5,16,1024]{2,1,0:T(8,128)(2,1)}, bf16[5,16,1024]{2,1,0:T(8,128)(2,1)S(1)}, u32[]{:S(2)}, u32[]{:S(2)}) collective-permute-start(bf16[5,16,1024]{2,1,0:T(8,128)(2,1)} %gate.28), channel_id=1, source_target_pairs={{0,6},{1,7},{2,4},{3,5},{4,2},{5,3},{6,0},{7,1},{8,14},{9,15},{10,... | collective-permute-start | bytes 491528 | tf_op jit(solution)/shard_map/ppermute | solution.py:471
  89.2 17.4 %collective-permute-start.15 = (bf16[8,16,1024]{2,1,0:T(8,128)(2,1)}, bf16[8,16,1024]{2,1,0:T(8,128)(2,1)S(1)}, u32[]{:S(2)}, u32[]{:S(2)}) collective-permute-start(bf16[8,16,1024]{2,1,0:T(8,128)(2,1)} %gate.24), channel_id=1, source_target_pairs={{0,1},{1,0},{2,3},{3,2},{4,5},{5,4},{6,7},{7,6},{8,9},{9,8},{10,11... | collective-permute-start | bytes 786440 | tf_op jit(solution)/shard_map/ppermute | solution.py:471
  98.4 13.7 %collective-permute-start.9 = (bf16[8,16,1024]{2,1,0:T(8,128)(2,1)}, bf16[8,16,1024]{2,1,0:T(8,128)(2,1)S(1)}, u32[]{:S(2)}, u32[]{:S(2)}) collective-permute-start(bf16[8,16,1024]{2,1,0:T(8,128)(2,1)} %gate.19), channel_id=1, source_target_pairs={{0,1},{1,0},{2,3},{3,2},{4,5},{5,4},{6,7},{7,6},{8,9},{9,8},{10,11... | collective-permute-start | bytes 786440 | tf_op jit(solution)/shard_map/ppermute | solution.py:471
  98.4 18.8 %collective-permute-start.13 = (bf16[8,16,1024]{2,1,0:T(8,128)(2,1)}, bf16[8,16,1024]{2,1,0:T(8,128)(2,1)S(1)}, u32[]{:S(2)}, u32[]{:S(2)}) collective-permute-start(bf16[8,16,1024]{2,1,0:T(8,128)(2,1)} %gate.22), channel_id=1, source_target_pairs={{0,3},{1,2},{2,1},{3,0},{4,7},{5,6},{6,5},{7,4},{8,11},{9,10},{10,... | collective-permute-start | bytes 786440 | tf_op jit(solution)/shard_map/ppermute | solution.py:471
  104.9 10.0 %collective-permute-start.20 = (bf16[5,16,1024]{2,1,0:T(8,128)(2,1)}, bf16[5,16,1024]{2,1,0:T(8,128)(2,1)S(1)}, u32[]{:S(2)}, u32[]{:S(2)}) collective-permute-start(bf16[5,16,1024]{2,1,0:T(8,128)(2,1)} %gate.29), channel_id=1, source_target_pairs={{0,7},{1,6},{2,5},{3,4},{4,3},{5,2},{6,1},{7,0},{8,15},{9,14},{10,... | collective-permute-start | bytes 491528 | tf_op jit(solution)/shard_map/ppermute | solution.py:471
  106.6 16.2 %collective-permute-start.16 = (bf16[3,16,1024]{2,1,0:T(8,128)(2,1)}, bf16[3,16,1024]{2,1,0:T(8,128)(2,1)S(1)}, u32[]{:S(2)}, u32[]{:S(2)}) collective-permute-start(bf16[3,16,1024]{2,1,0:T(8,128)(2,1)} %gate.25), channel_id=1, source_target_pairs={{0,4},{1,5},{2,6},{3,7},{4,0},{5,1},{6,2},{7,3},{8,12},{9,13},{10,... | collective-permute-start | bytes 294920 | tf_op jit(solution)/shard_map/ppermute | solution.py:471
  112.1 10.7 %collective-permute-start.22 = (bf16[3,16,1024]{2,1,0:T(8,128)(2,1)}, bf16[3,16,1024]{2,1,0:T(8,128)(2,1)S(1)}, u32[]{:S(2)}, u32[]{:S(2)}) collective-permute-start(bf16[3,16,1024]{2,1,0:T(8,128)(2,1)} %gate.31), channel_id=1, source_target_pairs={{0,7},{1,6},{2,5},{3,4},{4,3},{5,2},{6,1},{7,0},{8,15},{9,14},{10,... | collective-permute-start | bytes 294920 | tf_op jit(solution)/shard_map/ppermute | solution.py:471
  115.6 7.2 %collective-permute-start.21 = (bf16[3,16,1024]{2,1,0:T(8,128)(2,1)}, bf16[3,16,1024]{2,1,0:T(8,128)(2,1)S(1)}, u32[]{:S(2)}, u32[]{:S(2)}) collective-permute-start(bf16[3,16,1024]{2,1,0:T(8,128)(2,1)} %gate.30), channel_id=1, source_target_pairs={{0,6},{1,7},{2,4},{3,5},{4,2},{5,3},{6,0},{7,1},{8,14},{9,15},{10,... | collective-permute-start | bytes 294920 | tf_op jit(solution)/shard_map/ppermute | solution.py:471
  117.2 14.1 %collective-permute-start.17 = (bf16[3,16,1024]{2,1,0:T(8,128)(2,1)}, bf16[3,16,1024]{2,1,0:T(8,128)(2,1)S(1)}, u32[]{:S(2)}, u32[]{:S(2)}) collective-permute-start(bf16[3,16,1024]{2,1,0:T(8,128)(2,1)} %gate.26), channel_id=1, source_target_pairs={{0,5},{1,4},{2,7},{3,6},{4,1},{5,0},{6,3},{7,2},{8,13},{9,12},{10,... | collective-permute-start | bytes 294920 | tf_op jit(solution)/shard_map/ppermute | solution.py:471
  (16 other events, 131.9 us)

commit v7 on v6

--- a/solution.py
+++ b/solution.py
@@ -13,6 +13,8 @@
 GROUP = 8
 PER = 4
 PAIR = 2
+CHUNKS = 8
+BEFORE_BAND = 2e9
 MIB = 1024 * 1024
 HALO = 2 * REACH
 
@@ -109,50 +111,56 @@
     return jnp.concatenate(parts, axis=1)
 
 
-def sums_kernel(density, valid, out, first, last):
-    slices, rows, cols = density.shape
-    step = pl.program_id(0)
-
-    @pl.when(step == 0)
-    def _():
-        out[...] = jnp.zeros_like(out)
-        first[:slices] = density[:, :REACH]
-        first[slices] = valid[:REACH].astype(jnp.bfloat16)
-
-    @pl.when(step == pl.num_programs(0) - 1)
-    def _():
-        last[:slices] = density[:, rows - REACH :]
-        last[slices] = valid[rows - REACH :].astype(jnp.bfloat16)
-
-    mask = valid[...] != 0
-    for s in range(slices + 1):
-        if s < slices:
-            x = jnp.where(mask, density[s].astype(jnp.float32), 0.0)
-        else:
-            x = jnp.where(mask, 1.0, 0.0)
-        x = x.reshape(rows // 8, 8, cols).sum(axis=0)
-        x = sum(x[:, c : c + LANES] for c in range(0, cols, LANES))
-        out[s : s + 1, :] += jnp.sum(x, axis=0, keepdims=True)
+def sums_kernel(density, valid, out, first, last, cube, plane, sems):
+    slices, rows, cols = cube.shape
+    step = rows // CHUNKS
+
+    def copies(i):
+        at = pl.ds(pl.multiple_of(i * step, step), step)
+        yield pltpu.make_async_copy(density.at[:, at], cube.at[:, at], sems.at[i])
+        yield pltpu.make_async_copy(valid.at[at], plane.at[at], sems.at[CHUNKS + i])
+
+    for i in range(CHUNKS):
+        for copy in copies(i):
+            copy.start()
+    out[...] = jnp.zeros_like(out)
+
+    def body(i, _):
+        for copy in copies(i):
+            copy.wait()
+        at = pl.ds(pl.multiple_of(i * step, step), step)
+        mask = plane[at] != 0
+        for s in range(slices + 1):
+            x = cube[s, at].astype(jnp.float32) if s < slices else jnp.ones((step, cols), jnp.float32)
+            x = jnp.where(mask, x, 0.0).reshape(step // 8, 8, cols).sum(axis=0)
+            x = sum(x[:, c : c + LANES] for c in range(0, cols, LANES))
+            out[s : s + 1, :] += jnp.sum(x, axis=0, keepdims=True)
+        return 0
+
+    lax.fori_loop(0, CHUNKS, body, 0)
+    first[:slices] = cube[:, :REACH]
+    first[slices] = plane[:REACH].astype(jnp.bfloat16)
+    last[:slices] = cube[:, rows - REACH :]
+    last[slices] = plane[rows - REACH :].astype(jnp.bfloat16)
 
 
 def masked_sums(density, valid):
     slices, rows, cols = density.shape
-    step = 32
-    edge = jax.ShapeDtypeStruct((slices + 1, REACH, cols), jnp.bfloat16)
+    edge = hbm((slices + 1, REACH, cols), jnp.bfloat16)
     return pl.pallas_call(
         sums_kernel,
         name="sums",
-        grid=(rows // step,),
-        in_specs=[
-            pl.BlockSpec((slices, step, cols), lambda i: (0, i, 0)),
-            pl.BlockSpec((step, cols), lambda i: (i, 0)),
+        in_specs=[anywhere()] * 2,
+        out_specs=[pl.BlockSpec(memory_space=pltpu.VMEM)] * 3,
+        out_shape=[hbm((slices + 8, LANES), jnp.float32), edge, edge],
+        scratch_shapes=[
+            pltpu.VMEM(density.shape, jnp.bfloat16),
+            pltpu.VMEM(valid.shape, jnp.int32),
+            pltpu.SemaphoreType.DMA((2 * CHUNKS,)),
         ],
-        out_specs=[pl.BlockSpec((slices + 8, LANES), lambda i: (0, 0))]
-        + [pl.BlockSpec((slices + 1, REACH, cols), lambda i: (0, 0, 0))] * 2,
-        out_shape=[jax.ShapeDtypeStruct((slices + 8, LANES), jnp.float32), edge, edge],
         compiler_params=params(),
         cost_estimate=cost(1, 1),
-    )(density, valid)
+    )(held(density), held(valid))
 
 
 def mean_kernel(*refs):
@@ -173,87 +181,76 @@
     )(*sums)
 
 
-def filter_kernel(pieces, ids, before, now, after, mask_before, mask_now, mask_after, *refs):
-    (above, below, row_taps, col_taps, mean), (tall, done, col, row) = refs[:5], refs[-4:]
-    count = sum(len(wanted) for wanted in pieces)
-    outs = refs[-4 - count : -4]
-    slices, block, cols = now.shape
-    step = pl.program_id(0)
-
-    @pl.when(step == 0)
-    def _():
-        build_columns(listed(col_taps), col)
-        build_rows(listed(row_taps), row)
-
-    first = ids[step] == 0
-    last = ids[step] == ids[pl.num_programs(0)]
-    f32 = jnp.float32
-    top = jnp.where(first, above[slices].astype(f32), mask_before[REACH:, :].astype(f32))
-    bottom = jnp.where(last, below[slices].astype(f32), mask_after[:REACH, :].astype(f32))
-    mask = jnp.concatenate([top, mask_now[...].astype(f32), bottom], axis=0)
-
-    def field(s):
-        top = jnp.where(first, above[s].astype(f32), before[s].astype(f32)[REACH:])
-        bottom = jnp.where(last, below[s].astype(f32), after[s].astype(f32)[:REACH])
-        x = jnp.concatenate([top, now[s].astype(f32), bottom], axis=0)
-        return mask * (x - mean[s : s + 1, :1])
-
-    done[...] = convolve(field, col, row, tall, block).astype(jnp.bfloat16)
-    at = 0
+def inner_rows(both, last):
+    both = both.astype(jnp.float32)
+    rows = both.shape[0] - REACH
+    chosen = jnp.where(last, both[REACH:], both[:rows])
+    return jnp.concatenate([chosen, jnp.zeros((REACH, both.shape[1]), jnp.float32)], axis=0)
+
+
+def inner_kernel(pieces, ids, density, valid, row_taps, col_taps, mean, *refs):
+    (col, row, tall, cube, plane, sems) = refs[-6:]
+    count, slices, high, _ = cube.shape
+    outs = list(refs[-6 - sum(len(wanted) for wanted in pieces) : -6])
+    block = high // 2
+    copies = []
+    for b in range(count):
+        here = pl.ds(pl.multiple_of(jnp.minimum(ids[b], ids[count] - 1) * block, block), high)
+        copies.append(pltpu.make_async_copy(density.at[:, here], cube.at[b], sems.at[2 * b]))
+        copies.append(pltpu.make_async_copy(valid.at[here], plane.at[b], sems.at[2 * b + 1]))
+    for copy in copies:
+        copy.start()
+    build_columns(listed(col_taps), col)
+    build_rows(listed(row_taps), row)
+    for copy in copies:
+        copy.wait()
     for b, wanted in enumerate(pieces):
-
-        @pl.when(step == b)
-        def _():
-            for p, (inner, start, stop) in enumerate(wanted):
-                here = jnp.where(last != (inner == 1), block - REACH, 0) + start
-                outs[at + p][...] = done[pl.ds(here, stop - start)]
-
-        at += len(wanted)
-
-
-def filter_blocks(ids, pieces, density, valid, above, below, row_taps, col_taps, mean, *after):
+        last = ids[b] == ids[count]
+        mask = inner_rows(plane[b], last)
+        field = convolve(
+            lambda s, b=b, last=last, mask=mask: mask * (inner_rows(cube[b, s], last) - mean[s : s + 1, :1]),
+            col,
+            row,
+            tall,
+            REACH,
+        ).astype(jnp.bfloat16)
+        for _, start, stop in wanted:
+            outs.pop(0)[...] = field[start:stop]
+
+
+def filter_inner(ids, pieces, density, valid, row_taps, col_taps, mean, *after):
     slices, rows, cols = density.shape
     terms = row_taps.shape[0]
-    block = LANES // terms - HALO
-    last = rows // block - 1
+    high = LANES // terms
     count = ids.shape[0]
 
-    def rows_at(shift):
-        return lambda i, at: (0, jnp.clip(at[i] + shift, 0, last), 0)
-
-    def mask_at(shift):
-        return lambda i, at: (jnp.clip(at[i] + shift, 0, last), 0)
-
     def whole(x):
-        return pl.BlockSpec(x.shape, lambda i, at: (0,) * x.ndim, pipeline_mode=pl.Buffered(1))
+        return pl.BlockSpec(x.shape, lambda i, at: (0,) * x.ndim)
 
     shapes = [(stop - start, slices, cols) for wanted in pieces for _, start, stop in wanted]
     out = pl.pallas_call(
-        functools.partial(filter_kernel, pieces),
-        name="filter",
+        functools.partial(inner_kernel, pieces),
+        name="inner",
         grid_spec=pltpu.PrefetchScalarGridSpec(
             num_scalar_prefetch=1,
-            grid=(count,),
-            in_specs=[pl.BlockSpec((slices, block, cols), rows_at(d)) for d in (-1, 0, 1)]
-            + [pl.BlockSpec((block, cols), mask_at(d)) for d in (-1, 0, 1)]
-            + [whole(x) for x in (above, below, row_taps, col_taps, mean)]
-            + [anywhere()] * len(after),
+            grid=(1,),
+            in_specs=[anywhere()] * 2 + [whole(x) for x in (row_taps, col_taps, mean)] + [anywhere()] * len(after),
             out_specs=[pl.BlockSpec(shape, lambda i, at: (0, 0, 0)) for shape in shapes],
-            scratch_shapes=[
+            scratch_shapes=[pltpu.VMEM(x, jnp.bfloat16) for x in matrix_shapes(terms, slices, REACH)]
+            + [
                 pltpu.VMEM((GROUP * LANES, cols), jnp.bfloat16),
-                pltpu.VMEM((block, slices, cols), jnp.bfloat16),
-            ]
-            + [pltpu.VMEM(shape, jnp.bfloat16) for shape in matrix_shapes(terms, slices, block)],
+                pltpu.VMEM((count, slices, high, cols), jnp.bfloat16),
+                pltpu.VMEM((count, high, cols), jnp.int32),
+                pltpu.SemaphoreType.DMA((2 * count,)),
+            ],
         ),
         out_shape=[hbm(shape, jnp.bfloat16) for shape in shapes],
         compiler_params=params(),
         cost_estimate=cost(1, 1),
     )(
-        jnp.concatenate([ids, jnp.full((1,), last, ids.dtype)]),
-        *([density] * 3),
-        *([valid] * 3),
-        above,
-        below,
+        jnp.concatenate([ids, jnp.full((1,), rows // (high - HALO) - 1, ids.dtype)]),
+        held(density),
+        held(valid),
         row_taps,
         col_taps,
         mean,
@@ -375,8 +372,8 @@
         cost_estimate=cost(1, 1),
     )(
         jnp.concatenate([ids, jnp.full((1,), rows // block - 1, ids.dtype)]),
-        density,
-        valid,
+        held(density),
+        held(valid),
         above,
         below,
         row_taps,
@@ -440,24 +437,40 @@
     )(held(x), *earlier)
 
 
-INNER, OUTER, HEAD, TAIL = (1, 0, REACH), (0, 0, REACH), (0, 0, 5), (0, 5, REACH)
-LATE = (4, 6, 5, 7)
-FIRST = ((4,), (6, 5))
+INNER, OUTER = (1, 0, REACH), (0, 0, REACH)
+GROUPS = (1, 0, 5), (1, 5, REACH), (0, 0, 5), (0, 5, REACH)
+FIRST = (((4, GROUPS[:2]),), ((6, (INNER,)), (5, (INNER,))))
 REST = (
-    (5, (HEAD, TAIL)),
-    (7, (INNER, HEAD, TAIL)),
+    (5, GROUPS[2:]),
+    (7, (INNER, *GROUPS[2:])),
     (2, (INNER, OUTER)),
     (3, (INNER, OUTER)),
-    (4, (HEAD, TAIL)),
-    (6, (HEAD, TAIL)),
+    (4, GROUPS[2:]),
+    (6, GROUPS[2:]),
     (1, (INNER, OUTER)),
     (0, (INNER, OUTER)),
 )
 ORDER = (
-    (4, 0), (6, 0), (5, 0), (7, 0), (2, 0), (4, 1), (3, 0), (6, 1), (2, 1), (5, 1), (1, 0), (7, 1), (3, 1), (1, 1),
-    (4, 2), (6, 2), (5, 2), (7, 2),
+    (4, GROUPS[0], None),
+    (6, INNER, None),
+    (5, INNER, None),
+    (4, GROUPS[1], None),
+    (7, INNER, 3),
+    (2, INNER, 3),
+    (4, GROUPS[2], 1),
+    (3, INNER, 1),
+    (6, GROUPS[2], 2),
+    (2, OUTER, 2),
+    (5, GROUPS[2], 6),
+    (1, INNER, 7),
+    (7, GROUPS[2], 8),
+    (3, OUTER, 9),
+    (1, OUTER, 10),
+    (4, GROUPS[3], 11),
+    (6, GROUPS[3], 12),
+    (5, GROUPS[3], 13),
+    (7, GROUPS[3], 14),
 )
-WAITS = {3: 1, 4: 1, 5: 2, 6: 2, **{at: at - 4 for at in range(7, len(ORDER))}}
 
 
 def fast(density, valid, row_taps, col_taps, amp_matrix, like_matrix):
@@ -476,47 +489,62 @@
 
     made, arrived = {}, {}
 
-    def filter_for(kernel, wanted, above, below, *after):
-        ids = jnp.stack([me ^ k for k, _ in wanted])
-        pieces = [cut for _, cut in wanted]
-        got = kernel(ids, pieces, density, valid, above, below, row_taps, col_taps, mean, *after)
+    above = lax.ppermute(last, "tile", [(i, i + 1) for i in range(tiles - 1)])
+    below = lax.ppermute(first, "tile", [(i + 1, i) for i in range(tiles - 1)])
+    def ids(wanted):
+        return jnp.stack([me ^ k for k, _ in wanted])
+
+    def keep(wanted, got):
         for (k, cut), parts in zip(wanted, got):
             for piece, x in zip(cut, parts):
-                p = {INNER: 0, OUTER: 1, HEAD: 1, TAIL: 2}[piece]
-                made[k, p] = x
-                if k == 0:
-                    arrived[k, p] = x
-
-    above = lax.ppermute(last, "tile", [(i, i + 1) for i in range(tiles - 1)])
-    below = lax.ppermute(first, "tile", [(i + 1, i) for i in range(tiles - 1)])
+                made[k, piece] = x
+
+    def send(k, piece, *before):
+        x = made[k, piece]
+        arrived[k, piece] = swap(gate(x, *before) if before else x, k)
+
+    inputs = row_taps, col_taps, mean
     after = ()
-    for ks in FIRST:
-        filter_for(filter_blocks, [(k, (INNER,)) for k in ks], last, first, *after)
-        after = (made[ks[0], 0],)
-        for k in ks:
-            arrived[k, 0] = swap(made[k, 0], k)
-    filter_for(filter_band, REST, above, below, *after, gate(mean, arrived[4, 0]))
+    for wanted in FIRST:
+        got = filter_inner(ids(wanted), [cut for _, cut in wanted], density, valid, *inputs, *after)
+        keep(wanted, got)
+        after = (got[0][0],)
+    first_piece = ORDER[0][:2]
+    send(*first_piece)
+    got = filter_band(
+        ids(REST), [cut for _, cut in REST], density, valid, above, below, *inputs, *after, gate(mean, arrived[first_piece], flops=BEFORE_BAND)
+    )
+    keep(REST, got)
+    for piece in (INNER, OUTER):
+        arrived[0, piece] = made[0, piece]
+
     weights = jnp.concatenate([amp_matrix, like_matrix], axis=1).T.reshape(-1, peers, slices)
     weights = weights[:, me ^ jnp.arange(peers)].reshape(-1, peers * slices)
     result, tokens = [], []
 
-    def finish(p):
-        inner, start, stop = (INNER, HEAD, TAIL)[p]
+    def finish(group):
+        inner, start, stop = group
         place = jnp.where((me == peers - 1) != (inner == 1), block - REACH, 0) + start
-        parts = [(arrived[k, p], 0) if k in LATE else (arrived[k, min(p, 1)], start) for k in range(peers)]
+        parts = []
+        for k in range(peers):
+            for piece in (group, INNER, OUTER):
+                if (k, piece) in arrived and piece[0] == inner:
+                    parts.append((arrived[k, piece], start - piece[1]))
+                    break
         *result[:], token = project(place, weights, parts, stop - start, block, result)
         tokens.append(token)
 
-    for at, (k, p) in enumerate(ORDER):
-        if (k, p) in arrived:
+    for at, (k, piece, wait) in enumerate(ORDER):
+        if (k, piece) in arrived:
             continue
-        before = [arrived[ORDER[WAITS[at]]]] if at in WAITS else []
+        before = [] if wait is None else [arrived[ORDER[wait][:2]]]
         if at == len(ORDER) - 3:
-            finish(0)
-            before.append(tokens[0])
-        arrived[k, p] = swap(gate(made[k, p], *before) if before else made[k, p], k)
-    finish(1)
-    finish(2)
+            finish(GROUPS[0])
+            finish(GROUPS[1])
+            before.append(tokens[1])
+        send(k, piece, *before)
+    finish(GROUPS[2])
+    finish(GROUPS[3])
     return tuple(result)
 
 

time: 134 us -> 126 us (0.940)
  starting transfers between devices: 46.5 us -> 35 us
  local copies, waits for them, and re-layouts: 14.7 us -> 5.31 us
  Pallas kernels: 39 us -> 46.4 us
  waiting for transfers between devices: 32 us -> 36.3 us
    ppermute x18 -> x19, starting transfers between devices: 36.8 us -> 25.3 us  [swap(): return lax.ppermute(x, 'cuts', [(i, i ^ k) for i in range(peers)])]
    unnamed x35 -> x29, local copies, waits for them, and re-layouts: 14 us -> 4.56 us
    pallas_call x3, Pallas kernels: 13.4 us -> 18.4 us  [the longest x2 15 us: filter_inner(): pl.pallas_call(functools.partial(inner_kernel, pieces), name='inner', gri...]
    ppermute x18 -> x19, waiting for transfers between devices: 32 us -> 36.3 us  [swap(): return lax.ppermute(x, 'cuts', [(i, i ^ k) for i in range(peers)])]
    pallas_call x1, Pallas kernels: 15.8 us -> 17.5 us  [filter_band(): pl.pallas_call(functools.partial(band_kernel, pieces), name='band', grid_...]
    pallas_call x3 -> x4, Pallas kernels: 9.64 us -> 10.4 us  [project(): pl.pallas_call(functools.partial(project_kernel, count), name='project',...]
  transfers between devices with their start and end apart: 23 -> 24, of which waited for: 8 -> 10; matrix products, arithmetic and copies ran while one was open for 1% -> 1% of each run, Pallas kernels for 27% -> 33%
where the time goes in v7:
time: 126 us; the launch traced here: 124 us
  Pallas kernels  46.4 us (37%)
  waiting for transfers between devices  36.3 us (29%)
  starting transfers between devices  35 us (28%)
  local copies, waits for them, and re-layouts  5.31 us (4%)
    ppermute x19, waiting for transfers between devices, swap(): return lax.ppermute(x, 'cuts', [(i, i ^ k) for i in range(peers)])  36.3 us
    ppermute x19, starting transfers between devices, swap(): return lax.ppermute(x, 'cuts', [(i, i ^ k) for i in range(peers)])  25.3 us
    pallas_call x1, Pallas kernels, filter_band(): pl.pallas_call(functools.partial(band_kernel, pieces), name='band', grid_...  17.5 us
    pallas_call x2, Pallas kernels, filter_inner(): pl.pallas_call(functools.partial(inner_kernel, pieces), name='inner', gri...  15 us
    pallas_call x4, Pallas kernels, project(): pl.pallas_call(functools.partial(project_kernel, count), name='project',...  10.4 us
    unnamed x29, local copies, waits for them, and re-layouts  4.56 us
    ppermute x3, starting transfers between devices, fast(): lax.ppermute(own, 'tile', [(i, i ^ k) for i in range(tiles)])  4.54 us
    ppermute x1, starting transfers between devices, fast(): above = lax.ppermute(last, 'tile', [(i, i + 1) for i in range(tiles - 1)])  3.86 us
  transfers between devices with their start and end apart: 24, of which 10 were waited for; matrix products, arithmetic and copies ran while one was open for 1% of the time, Pallas kernels for 33%

profile of v7, /device:TPU:0, one launch (start us, length us, event | category | flops | bytes accessed | tf_op | source)
XLA Modules:
  0.0 124.1 jit_solution(14117039633653650561)
XLA Ops:
  0.6 3.4 %sums.1 = (f32[24,128]{1,0:T(8,128)}, bf16[17,8,1024]{2,1,0:T(8,128)(2,1)}, bf16[17,8,1024]{2,1,0:T(8,128)(2,1)}) custom-call(bf16[16,128,1024]{2,1,0:T(8,128)(2,1)} %density.7, s32[128,1024]{1,0:T(8,128)} %valid.7), custom_call_target="tpu_custom_call" | custom-call | flops 1 | bytes 1 | tf_op jit(solution)/shard_map/sums/pallas_call | solution.py:150
  4.0 3.0 %collective-permute-start.2 = (f32[24,128]{1,0:T(8,128)}, f32[24,128]{1,0:T(8,128)S(1)}, u32[]{:S(2)}, u32[]{:S(2)}) collective-permute-start(f32[24,128]{1,0:T(8,128)} %get-tuple-element.37.refs_0_), channel_id=1, source_target_pairs={{0,8},{8,0},{16,24},{24,16},{1,9},{9,1},{17,25},{25,17},{2,10},{10... | collective-permute-start | bytes 36872 | tf_op jit(solution)/shard_map/ppermute | solution.py:487
  8.6 3.9 %collective-permute-start = (bf16[17,8,1024]{2,1,0:T(8,128)(2,1)}, bf16[17,8,1024]{2,1,0:T(8,128)(2,1)S(1)}, u32[]{:S(2)}, u32[]{:S(2)}) collective-permute-start(bf16[17,8,1024]{2,1,0:T(8,128)(2,1)} %get-tuple-element.35), channel_id=1, source_target_pairs={{0,8},{8,16},{16,24},{1,9},{9,17},{17,25},{2,10},{10,18},{18,26},{... | collective-permute-start | bytes 835592 | tf_op jit(solution)/shard_map/ppermute | solution.py:492
  14.6 6.2 %inner.2 = (bf16[5,16,1024]{2,1,0:T(8,128)(2,1)}, bf16[3,16,1024]{2,1,0:T(8,128)(2,1)}) custom-call(s32[2]{0:T(128)S(1)} %pad_add_fusion.1.ids, bf16[16,128,1024]{2,1,0:T(8,128)(2,1)} %density.7, s32[128,1024]{1,0:T(8,128)} %valid.7, bf16[4,16,17]{2,1,0:T(8,128)(2,1)S(1)} %copy-done.6, bf16[4,16,17]{2,1,0:T(8,128)(2,1)S(1)} %copy-done.7, ...), custom_call_target="tpu_custom_call" | custom-call | flops 1 | bytes 1 | tf_op jit(solution)/shard_map/inner/pallas_call | solution.py:231
  20.8 2.7 %collective-permute-start.5 = (bf16[5,16,1024]{2,1,0:T(8,128)(2,1)}, bf16[5,16,1024]{2,1,0:T(8,128)(2,1)S(1)}, u32[]{:S(2)}, u32[]{:S(2)}) collective-permute-start(bf16[5,16,1024]{2,1,0:T(8,128)(2,1)} %get-tuple-element.38.refs_0_), channel_id=1, source_target_pairs={{0,4},{1,5},{2,6},{3,7},{4,0},{5,1},{6,2},{7,3},{8,12},{9,13},{10,... | collective-permute-start | bytes 491528 | tf_op jit(solution)/shard_map/ppermute | solution.py:484
  24.5 8.9 %inner.3 = (bf16[8,16,1024]{2,1,0:T(8,128)(2,1)}, bf16[8,16,1024]{2,1,0:T(8,128)(2,1)}) custom-call(s32[3]{0:T(128)S(1)} %pad_add_fusion.ids, bf16[16,128,1024]{2,1,0:T(8,128)(2,1)} %density.7, s32[128,1024]{1,0:T(8,128)} %valid.7, bf16[4,16,17]{2,1,0:T(8,128)(2,1)S(1)} %copy-done.6, bf16[4,16,17]{2,1,0:T(8,128)(2,1)S(1)} %copy-done.7, ...), custom_call_target="tpu_custom_call" | custom-call | flops 1 | bytes 1 | tf_op jit(solution)/shard_map/inner/pallas_call | solution.py:231
  36.2 17.5 %band.1 = (bf16[5,16,1024]{2,1,0:T(8,128)(2,1)}, bf16[3,16,1024]{2,1,0:T(8,128)(2,1)}, bf16[8,16,1024]{2,1,0:T(8,128)(2,1)}, bf16[5,16,1024]{2,1,0:T(8,128)(2,1)...) custom-call(s32[9]{0:T(128)S(1)} %concatenate.13.ids, ...), custom_call_target="tpu_custom_call" | custom-call | flops 1 | bytes 1 | tf_op jit(solution)/shard_map/band/pallas_call | solution.py:350
  59.9 5.4 %collective-permute-done.7.refs_1_.refs_4_ = bf16[5,16,1024]{2,1,0:T(8,128)(2,1)S(1)} collective-permute-done((bf16[5,16,1024]{2,1,0:T(8,128)(2,1)}, bf16[5,16,1024]{2,1,0:T(8,128)(2,1)S(1)}, u32[]{:S(2)}, u32[]{:S(2)}) %collective-permute-start.7) | collective-permute-done | bytes 163872 | tf_op jit(solution)/shard_map/ppermute | solution.py:484
  65.2 2.8 %collective-permute-start.17 = (bf16[5,16,1024]{2,1,0:T(8,128)(2,1)}, bf16[5,16,1024]{2,1,0:T(8,128)(2,1)S(1)}, u32[]{:S(2)}, u32[]{:S(2)}) collective-permute-start(bf16[5,16,1024]{2,1,0:T(8,128)(2,1)} %gate.26), channel_id=1, source_target_pairs={{0,6},{1,7},{2,4},{3,5},{4,2},{5,3},{6,0},{7,1},{8,14},{9,15},{10,... | collective-permute-start | bytes 491528 | tf_op jit(solution)/shard_map/ppermute | solution.py:484
  68.0 5.4 %collective-permute-done.19.refs_1_.refs_4_ = bf16[3,16,1024]{2,1,0:T(8,128)(2,1)S(1)} collective-permute-done((bf16[3,16,1024]{2,1,0:T(8,128)(2,1)S(1)}, bf16[3,16,1024]{2,1,0:T(8,128)(2,1)S(1)}, u32[]{:S(2)}, u32[]{:S(2)}) %collective-permute-start.19) | collective-permute-done | bytes 98336 | tf_op jit(solution)/shard_map/ppermute | solution.py:484
  74.9 3.1 %collective-permute-start.21 = (bf16[8,16,1024]{2,1,0:T(8,128)(2,1)}, bf16[8,16,1024]{2,1,0:T(8,128)(2,1)S(1)}, u32[]{:S(2)}, u32[]{:S(2)}) collective-permute-start(bf16[8,16,1024]{2,1,0:T(8,128)(2,1)} %gate.29), channel_id=1, source_target_pairs={{0,7},{1,6},{2,5},{3,4},{4,3},{5,2},{6,1},{7,0},{8,15},{9,14},{10,... | collective-permute-start | bytes 786440 | tf_op jit(solution)/shard_map/ppermute | solution.py:484
  78.0 2.4 %collective-permute-done.11.refs_1_.refs_2_ = bf16[8,16,1024]{2,1,0:T(8,128)(2,1)S(1)} collective-permute-done((bf16[8,16,1024]{2,1,0:T(8,128)(2,1)}, bf16[8,16,1024]{2,1,0:T(8,128)(2,1)S(1)}, u32[]{:S(2)}, u32[]{:S(2)}) %collective-permute-start.11) | collective-permute-done | bytes 262176 | tf_op jit(solution)/shard_map/ppermute | solution.py:484
  81.6 2.1 %collective-permute-start.9 = (bf16[8,16,1024]{2,1,0:T(8,128)(2,1)}, bf16[8,16,1024]{2,1,0:T(8,128)(2,1)S(1)}, u32[]{:S(2)}, u32[]{:S(2)}) collective-permute-start(bf16[8,16,1024]{2,1,0:T(8,128)(2,1)} %gate.19), channel_id=1, source_target_pairs={{0,1},{1,0},{2,3},{3,2},{4,5},{5,4},{6,7},{7,6},{8,9},{9,8},{10,11... | collective-permute-start | bytes 786440 | tf_op jit(solution)/shard_map/ppermute | solution.py:484
  83.7 9.3 %collective-permute-done.20.refs_2_ = bf16[8,16,1024]{2,1,0:T(8,128)(2,1)S(1)} collective-permute-done((bf16[8,16,1024]{2,1,0:T(8,128)(2,1)}, bf16[8,16,1024]{2,1,0:T(8,128)(2,1)S(1)}, u32[]{:S(2)}, u32[]{:S(2)}) %collective-permute-start.20) | collective-permute-done | bytes 262176 | tf_op jit(solution)/shard_map/ppermute | solution.py:484
  95.1 3.1 %project.4 = (bf16[128,16384]{1,0:T(8,128)(2,1)}, bf16[128,16384]{1,0:T(8,128)(2,1)}, f32[8,128]{1,0:T(8,128)}) custom-call(s32[1]{0:T(128)} %bitcast.15.place, bf16[256,128]{1,0:T(8,128)(2,1)S(1)} %copy.33.weights, bf16[8,16,1024]{2,1,0:T(8,128)(2,1)S(1)} %copy-done.1, bf16[8,16,1024]{2,1,0:T(8,128)(2,1)S(1)} %collective-permute-done.14.refs_1_, ...), custom_call_target="tpu_custom_call" | custom-call | flops 1 | bytes 1 | tf_op jit(solution)/shard_map/project/pallas_call | solution.py:404
  98.3 2.1 %project.5 = (bf16[128,16384]{1,0:T(8,128)(2,1)}, bf16[128,16384]{1,0:T(8,128)(2,1)}, f32[8,128]{1,0:T(8,128)}) custom-call(s32[1]{0:T(128)} %bitcast.14.place, bf16[256,128]{1,0:T(8,128)(2,1)S(1)} %copy.33.weights, bf16[8,16,1024]{2,1,0:T(8,128)(2,1)S(1)} %copy-done.1, ...), custom_call_target="tpu_custom_call", output_to_operand_aliasing={{0}: (10, {}), {1}: (11, {})} | custom-call | flops 1 | bytes 1 | tf_op jit(solution)/shard_map/project/pallas_call | solution.py:404
  100.3 2.8 %collective-permute-done.18.refs_1_.refs_7_ = bf16[5,16,1024]{2,1,0:T(8,128)(2,1)S(1)} collective-permute-done((bf16[5,16,1024]{2,1,0:T(8,128)(2,1)}, bf16[5,16,1024]{2,1,0:T(8,128)(2,1)S(1)}, u32[]{:S(2)}, u32[]{:S(2)}) %collective-permute-start.18) | collective-permute-done | bytes 163872 | tf_op jit(solution)/shard_map/ppermute | solution.py:484
  103.8 2.4 %collective-permute-start.22 = (bf16[3,16,1024]{2,1,0:T(8,128)(2,1)}, bf16[3,16,1024]{2,1,0:T(8,128)(2,1)S(1)}, u32[]{:S(2)}, u32[]{:S(2)}) collective-permute-start(bf16[3,16,1024]{2,1,0:T(8,128)(2,1)} %gate.30), channel_id=1, source_target_pairs={{0,6},{1,7},{2,4},{3,5},{4,2},{5,3},{6,0},{7,1},{8,14},{9,15},{10,... | collective-permute-start | bytes 294920 | tf_op jit(solution)/shard_map/ppermute | solution.py:484
  106.2 2.0 %collective-permute-start.15 = (bf16[3,16,1024]{2,1,0:T(8,128)(2,1)}, bf16[3,16,1024]{2,1,0:T(8,128)(2,1)S(1)}, u32[]{:S(2)}, u32[]{:S(2)}) collective-permute-start(bf16[3,16,1024]{2,1,0:T(8,128)(2,1)} %gate.24), channel_id=1, source_target_pairs={{0,4},{1,5},{2,6},{3,7},{4,0},{5,1},{6,2},{7,3},{8,12},{9,13},{10,... | collective-permute-start | bytes 294920 | tf_op jit(solution)/shard_map/ppermute | solution.py:484
  108.3 1.8 %collective-permute-start.23 = (bf16[3,16,1024]{2,1,0:T(8,128)(2,1)}, bf16[3,16,1024]{2,1,0:T(8,128)(2,1)S(1)}, u32[]{:S(2)}, u32[]{:S(2)}) collective-permute-start(bf16[3,16,1024]{2,1,0:T(8,128)(2,1)} %gate.31), channel_id=1, source_target_pairs={{0,7},{1,6},{2,5},{3,4},{4,3},{5,2},{6,1},{7,0},{8,15},{9,14},{10,... | collective-permute-start | bytes 294920 | tf_op jit(solution)/shard_map/ppermute | solution.py:484
  110.9 3.1 %project.6 = (bf16[128,16384]{1,0:T(8,128)(2,1)}, bf16[128,16384]{1,0:T(8,128)(2,1)}, f32[8,128]{1,0:T(8,128)}) custom-call(s32[1]{0:T(128)} %bitcast.16.place, bf16[256,128]{1,0:T(8,128)(2,1)S(1)} %copy.33.weights, bf16[8,16,1024]{2,1,0:T(8,128)(2,1)S(1)} %copy-done, ...), custom_call_target="tpu_custom_call", output_to_operand_aliasing={{0}: (10, {}), {1}: (11, {})} | custom-call | flops 1 | bytes 1 | tf_op jit(solution)/shard_map/project/pallas_call | solution.py:404
  114.1 5.6 %collective-permute-done.16.refs_5_ = bf16[3,16,1024]{2,1,0:T(8,128)(2,1)S(1)} collective-permute-done((bf16[3,16,1024]{2,1,0:T(8,128)(2,1)}, bf16[3,16,1024]{2,1,0:T(8,128)(2,1)S(1)}, u32[]{:S(2)}, u32[]{:S(2)}) %collective-permute-start.16) | collective-permute-done | bytes 98336 | tf_op jit(solution)/shard_map/ppermute | solution.py:484
  119.6 2.4 %collective-permute-done.15.refs_4_ = bf16[3,16,1024]{2,1,0:T(8,128)(2,1)S(1)} collective-permute-done((bf16[3,16,1024]{2,1,0:T(8,128)(2,1)}, bf16[3,16,1024]{2,1,0:T(8,128)(2,1)S(1)}, u32[]{:S(2)}, u32[]{:S(2)}) %collective-permute-start.15) | collective-permute-done | bytes 98336 | tf_op jit(solution)/shard_map/ppermute | solution.py:484
  122.0 2.1 %project.7 = (bf16[128,16384]{1,0:T(8,128)(2,1)}, bf16[128,16384]{1,0:T(8,128)(2,1)}, f32[8,128]{1,0:T(8,128)}) custom-call(s32[1]{0:T(128)} %bitcast.place, bf16[256,128]{1,0:T(8,128)(2,1)S(1)} %copy.33.weights, bf16[8,16,1024]{2,1,0:T(8,128)(2,1)S(1)} %copy-done, ...), custom_call_target="tpu_custom_call", output_to_operand_aliasing={{0}: (10, {}), {1}: (11, {})} | custom-call | flops 1 | bytes 1 | tf_op jit(solution)/shard_map/project/pallas_call | solution.py:404
  (86 shorter events, 20.1 us)
Async XLA Ops:
  4.0 9.8 %collective-permute-start.2 = (f32[24,128]{1,0:T(8,128)}, f32[24,128]{1,0:T(8,128)S(1)}, u32[]{:S(2)}, u32[]{:S(2)}) collective-permute-start(f32[24,128]{1,0:T(8,128)} %get-tuple-element.37.refs_0_), channel_id=1, source_target_pairs={{0,8},{8,0},{16,24},{24,16},{1,9},{9,1},{17,25},{25,17},{2,10},{10... | collective-permute-start | bytes 36872 | tf_op jit(solution)/shard_map/ppermute | solution.py:487
  7.0 6.8 %collective-permute-start.3 = (f32[24,128]{1,0:T(8,128)}, f32[24,128]{1,0:T(8,128)S(1)}, u32[]{:S(2)}, u32[]{:S(2)}) collective-permute-start(f32[24,128]{1,0:T(8,128)} %get-tuple-element.37.refs_0_), channel_id=1, source_target_pairs={{0,16},{8,24},{16,0},{24,8},{1,17},{9,25},{17,1},{25,9},{2,18},{10... | collective-permute-start | bytes 36872 | tf_op jit(solution)/shard_map/ppermute | solution.py:487
  8.6 5.3 %collective-permute-start.4 = (f32[24,128]{1,0:T(8,128)}, f32[24,128]{1,0:T(8,128)S(1)}, u32[]{:S(2)}, u32[]{:S(2)}) collective-permute-start(f32[24,128]{1,0:T(8,128)} %get-tuple-element.37.refs_0_), channel_id=1, source_target_pairs={{0,24},{8,16},{16,8},{24,0},{1,25},{9,17},{17,9},{25,1},{2,26},{10... | collective-permute-start | bytes 36872 | tf_op jit(solution)/shard_map/ppermute | solution.py:487
  8.6 26.8 %collective-permute-start = (bf16[17,8,1024]{2,1,0:T(8,128)(2,1)}, bf16[17,8,1024]{2,1,0:T(8,128)(2,1)S(1)}, u32[]{:S(2)}, u32[]{:S(2)}) collective-permute-start(bf16[17,8,1024]{2,1,0:T(8,128)(2,1)} %get-tuple-element.35), channel_id=1, source_target_pairs={{0,8},{8,16},{16,24},{1,9},{9,17},{17,25},{2,10},{10,18},{18,26},{... | collective-permute-start | bytes 835592 | tf_op jit(solution)/shard_map/ppermute | solution.py:492
  12.4 23.0 %collective-permute-start.1 = (bf16[17,8,1024]{2,1,0:T(8,128)(2,1)}, bf16[17,8,1024]{2,1,0:T(8,128)(2,1)S(1)}, u32[]{:S(2)}, u32[]{:S(2)}) collective-permute-start(bf16[17,8,1024]{2,1,0:T(8,128)(2,1)} %get-tuple-element.36), channel_id=1, source_target_pairs={{8,0},{16,8},{24,16},{9,1},{17,9},{25,17},{10,2},{18,10},{26,18},{... | collective-permute-start | bytes 835592 | tf_op jit(solution)/shard_map/ppermute | solution.py:493
  20.8 14.6 %collective-permute-start.5 = (bf16[5,16,1024]{2,1,0:T(8,128)(2,1)}, bf16[5,16,1024]{2,1,0:T(8,128)(2,1)S(1)}, u32[]{:S(2)}, u32[]{:S(2)}) collective-permute-start(bf16[5,16,1024]{2,1,0:T(8,128)(2,1)} %get-tuple-element.38.refs_0_), channel_id=1, source_target_pairs={{0,4},{1,5},{2,6},{3,7},{4,0},{5,1},{6,2},{7,3},{8,12},{9,13},{10,... | collective-permute-start | bytes 491528 | tf_op jit(solution)/shard_map/ppermute | solution.py:484
  33.3 20.4 %collective-permute-start.6 = (bf16[8,16,1024]{2,1,0:T(8,128)(2,1)}, bf16[8,16,1024]{2,1,0:T(8,128)(2,1)S(1)}, u32[]{:S(2)}, u32[]{:S(2)}) collective-permute-start(bf16[8,16,1024]{2,1,0:T(8,128)(2,1)} %get-tuple-element.39.refs_0_), channel_id=1, source_target_pairs={{0,6},{1,7},{2,4},{3,5},{4,2},{5,3},{6,0},{7,1},{8,14},{9,15},{10,... | collective-permute-start | bytes 786440 | tf_op jit(solution)/shard_map/ppermute | solution.py:484
  34.7 22.4 %collective-permute-start.10 = (bf16[8,16,1024]{2,1,0:T(8,128)(2,1)}, bf16[8,16,1024]{2,1,0:T(8,128)(2,1)S(1)}, u32[]{:S(2)}, u32[]{:S(2)}) collective-permute-start(bf16[8,16,1024]{2,1,0:T(8,128)(2,1)} %get-tuple-element.45), channel_id=1, source_target_pairs={{0,5},{1,4},{2,7},{3,6},{4,1},{5,0},{6,3},{7,2},{8,13},{9,12},{10,... | collective-permute-start | bytes 786440 | tf_op jit(solution)/shard_map/ppermute | solution.py:484
  53.7 11.5 %collective-permute-start.7 = (bf16[5,16,1024]{2,1,0:T(8,128)(2,1)}, bf16[5,16,1024]{2,1,0:T(8,128)(2,1)S(1)}, u32[]{:S(2)}, u32[]{:S(2)}) collective-permute-start(bf16[5,16,1024]{2,1,0:T(8,128)(2,1)} %gate.17), channel_id=1, source_target_pairs={{0,4},{1,5},{2,6},{3,7},{4,0},{5,1},{6,2},{7,3},{8,12},{9,13},{10,... | collective-permute-start | bytes 491528 | tf_op jit(solution)/shard_map/ppermute | solution.py:484
  55.5 19.5 %collective-permute-start.13 = (bf16[8,16,1024]{2,1,0:T(8,128)(2,1)}, bf16[8,16,1024]{2,1,0:T(8,128)(2,1)S(1)}, u32[]{:S(2)}, u32[]{:S(2)}) collective-permute-start(bf16[8,16,1024]{2,1,0:T(8,128)(2,1)} %gate.22), channel_id=1, source_target_pairs={{0,3},{1,2},{2,1},{3,0},{4,7},{5,6},{6,5},{7,4},{8,11},{9,10},{10,... | collective-permute-start | bytes 786440 | tf_op jit(solution)/shard_map/ppermute | solution.py:484
  57.2 23.2 %collective-permute-start.11 = (bf16[8,16,1024]{2,1,0:T(8,128)(2,1)}, bf16[8,16,1024]{2,1,0:T(8,128)(2,1)S(1)}, u32[]{:S(2)}, u32[]{:S(2)}) collective-permute-start(bf16[8,16,1024]{2,1,0:T(8,128)(2,1)} %gate.20), channel_id=1, source_target_pairs={{0,2},{1,3},{2,0},{3,1},{4,6},{5,7},{6,4},{7,5},{8,10},{9,11},{10,... | collective-permute-start | bytes 786440 | tf_op jit(solution)/shard_map/ppermute | solution.py:484
  58.2 15.3 %collective-permute-start.19 = (bf16[3,16,1024]{2,1,0:T(8,128)(2,1)S(1)}, bf16[3,16,1024]{2,1,0:T(8,128)(2,1)S(1)}, u32[]{:S(2)}, u32[]{:S(2)}) collective-permute-start(bf16[3,16,1024]{2,1,0:T(8,128)(2,1)S(1)} %copy-done.13), channel_id=1, source_target_pairs={{0,4},{1,5},{2,6},{3,7},{4,0},{5,1},{6,2},{7,3},{8,12},{9,13},{10,... | collective-permute-start | bytes 294920 | tf_op jit(solution)/shard_map/ppermute | solution.py:484
  65.2 15.2 %collective-permute-start.8 = (bf16[5,16,1024]{2,1,0:T(8,128)(2,1)}, bf16[5,16,1024]{2,1,0:T(8,128)(2,1)S(1)}, u32[]{:S(2)}, u32[]{:S(2)}) collective-permute-start(bf16[5,16,1024]{2,1,0:T(8,128)(2,1)} %gate.18), channel_id=1, source_target_pairs={{0,5},{1,4},{2,7},{3,6},{4,1},{5,0},{6,3},{7,2},{8,13},{9,12},{10,... | collective-permute-start | bytes 491528 | tf_op jit(solution)/shard_map/ppermute | solution.py:484
  65.2 16.3 %collective-permute-start.17 = (bf16[5,16,1024]{2,1,0:T(8,128)(2,1)}, bf16[5,16,1024]{2,1,0:T(8,128)(2,1)S(1)}, u32[]{:S(2)}, u32[]{:S(2)}) collective-permute-start(bf16[5,16,1024]{2,1,0:T(8,128)(2,1)} %gate.26), channel_id=1, source_target_pairs={{0,6},{1,7},{2,4},{3,5},{4,2},{5,3},{6,0},{7,1},{8,14},{9,15},{10,... | collective-permute-start | bytes 491528 | tf_op jit(solution)/shard_map/ppermute | solution.py:484
  73.4 19.5 %collective-permute-start.20 = (bf16[8,16,1024]{2,1,0:T(8,128)(2,1)}, bf16[8,16,1024]{2,1,0:T(8,128)(2,1)S(1)}, u32[]{:S(2)}, u32[]{:S(2)}) collective-permute-start(bf16[8,16,1024]{2,1,0:T(8,128)(2,1)} %gate.28), channel_id=1, source_target_pairs={{0,2},{1,3},{2,0},{3,1},{4,6},{5,7},{6,4},{7,5},{8,10},{9,11},{10,... | collective-permute-start | bytes 786440 | tf_op jit(solution)/shard_map/ppermute | solution.py:484
  74.9 20.2 %collective-permute-start.21 = (bf16[8,16,1024]{2,1,0:T(8,128)(2,1)}, bf16[8,16,1024]{2,1,0:T(8,128)(2,1)S(1)}, u32[]{:S(2)}, u32[]{:S(2)}) collective-permute-start(bf16[8,16,1024]{2,1,0:T(8,128)(2,1)} %gate.29), channel_id=1, source_target_pairs={{0,7},{1,6},{2,5},{3,4},{4,3},{5,2},{6,1},{7,0},{8,15},{9,14},{10,... | collective-permute-start | bytes 786440 | tf_op jit(solution)/shard_map/ppermute | solution.py:484
  80.4 14.7 %collective-permute-start.14 = (bf16[8,16,1024]{2,1,0:T(8,128)(2,1)}, bf16[8,16,1024]{2,1,0:T(8,128)(2,1)S(1)}, u32[]{:S(2)}, u32[]{:S(2)}) collective-permute-start(bf16[8,16,1024]{2,1,0:T(8,128)(2,1)} %gate.23), channel_id=1, source_target_pairs={{0,1},{1,0},{2,3},{3,2},{4,5},{5,4},{6,7},{7,6},{8,9},{9,8},{10,11... | collective-permute-start | bytes 786440 | tf_op jit(solution)/shard_map/ppermute | solution.py:484
  80.4 25.8 %collective-permute-start.12 = (bf16[8,16,1024]{2,1,0:T(8,128)(2,1)}, bf16[8,16,1024]{2,1,0:T(8,128)(2,1)S(1)}, u32[]{:S(2)}, u32[]{:S(2)}) collective-permute-start(bf16[8,16,1024]{2,1,0:T(8,128)(2,1)} %gate.21), channel_id=1, source_target_pairs={{0,3},{1,2},{2,1},{3,0},{4,7},{5,6},{6,5},{7,4},{8,11},{9,10},{10,... | collective-permute-start | bytes 786440 | tf_op jit(solution)/shard_map/ppermute | solution.py:484
  81.6 26.7 %collective-permute-start.9 = (bf16[8,16,1024]{2,1,0:T(8,128)(2,1)}, bf16[8,16,1024]{2,1,0:T(8,128)(2,1)S(1)}, u32[]{:S(2)}, u32[]{:S(2)}) collective-permute-start(bf16[8,16,1024]{2,1,0:T(8,128)(2,1)} %gate.19), channel_id=1, source_target_pairs={{0,1},{1,0},{2,3},{3,2},{4,5},{5,4},{6,7},{7,6},{8,9},{9,8},{10,11... | collective-permute-start | bytes 786440 | tf_op jit(solution)/shard_map/ppermute | solution.py:484
  93.0 10.2 %collective-permute-start.18 = (bf16[5,16,1024]{2,1,0:T(8,128)(2,1)}, bf16[5,16,1024]{2,1,0:T(8,128)(2,1)S(1)}, u32[]{:S(2)}, u32[]{:S(2)}) collective-permute-start(bf16[5,16,1024]{2,1,0:T(8,128)(2,1)} %gate.27), channel_id=1, source_target_pairs={{0,7},{1,6},{2,5},{3,4},{4,3},{5,2},{6,1},{7,0},{8,15},{9,14},{10,... | collective-permute-start | bytes 491528 | tf_op jit(solution)/shard_map/ppermute | solution.py:484
  103.8 10.2 %collective-permute-start.22 = (bf16[3,16,1024]{2,1,0:T(8,128)(2,1)}, bf16[3,16,1024]{2,1,0:T(8,128)(2,1)S(1)}, u32[]{:S(2)}, u32[]{:S(2)}) collective-permute-start(bf16[3,16,1024]{2,1,0:T(8,128)(2,1)} %gate.30), channel_id=1, source_target_pairs={{0,6},{1,7},{2,4},{3,5},{4,2},{5,3},{6,0},{7,1},{8,14},{9,15},{10,... | collective-permute-start | bytes 294920 | tf_op jit(solution)/shard_map/ppermute | solution.py:484
  106.2 13.4 %collective-permute-start.16 = (bf16[3,16,1024]{2,1,0:T(8,128)(2,1)}, bf16[3,16,1024]{2,1,0:T(8,128)(2,1)S(1)}, u32[]{:S(2)}, u32[]{:S(2)}) collective-permute-start(bf16[3,16,1024]{2,1,0:T(8,128)(2,1)} %gate.25), channel_id=1, source_target_pairs={{0,5},{1,4},{2,7},{3,6},{4,1},{5,0},{6,3},{7,2},{8,13},{9,12},{10,... | collective-permute-start | bytes 294920 | tf_op jit(solution)/shard_map/ppermute | solution.py:484
  106.2 15.8 %collective-permute-start.15 = (bf16[3,16,1024]{2,1,0:T(8,128)(2,1)}, bf16[3,16,1024]{2,1,0:T(8,128)(2,1)S(1)}, u32[]{:S(2)}, u32[]{:S(2)}) collective-permute-start(bf16[3,16,1024]{2,1,0:T(8,128)(2,1)} %gate.24), channel_id=1, source_target_pairs={{0,4},{1,5},{2,6},{3,7},{4,0},{5,1},{6,2},{7,3},{8,12},{9,13},{10,... | collective-permute-start | bytes 294920 | tf_op jit(solution)/shard_map/ppermute | solution.py:484
  108.3 13.7 %collective-permute-start.23 = (bf16[3,16,1024]{2,1,0:T(8,128)(2,1)}, bf16[3,16,1024]{2,1,0:T(8,128)(2,1)S(1)}, u32[]{:S(2)}, u32[]{:S(2)}) collective-permute-start(bf16[3,16,1024]{2,1,0:T(8,128)(2,1)} %gate.31), channel_id=1, source_target_pairs={{0,7},{1,6},{2,5},{3,4},{4,3},{5,2},{6,1},{7,0},{8,15},{9,14},{10,... | collective-permute-start | bytes 294920 | tf_op jit(solution)/shard_map/ppermute | solution.py:484
  (14 other events, 190.8 us)

commit v8 on v7

--- a/solution.py
+++ b/solution.py
@@ -388,11 +388,13 @@
 def project_kernel(count, place, weights, *refs):
     parts, (amp_out, like_out, token) = refs[:count], refs[-3:]
     zbins = weights.shape[0] // 2
-    pencil = jnp.concatenate([x[0] for x in parts], axis=0)
-    both = jnp.dot(weights[...], pencil, preferred_element_type=jnp.float32)
-    amp = both[:zbins]
-    amp_out[...] = amp.astype(jnp.bfloat16)
-    like_out[...] = (amp * both[zbins:]).astype(jnp.bfloat16)
+    rows, _, cols = parts[0].shape
+    for r in range(rows):
+        pencil = jnp.concatenate([x[r] for x in parts], axis=0)
+        both = jnp.dot(weights[...], pencil, preferred_element_type=jnp.float32)
+        amp = both[:zbins]
+        amp_out[:, r * cols : (r + 1) * cols] = amp.astype(jnp.bfloat16)
+        like_out[:, r * cols : (r + 1) * cols] = (amp * both[zbins:]).astype(jnp.bfloat16)
     token[...] = jnp.zeros_like(token)
 
 
@@ -406,11 +408,14 @@
         name="project",
         grid_spec=pltpu.PrefetchScalarGridSpec(
             num_scalar_prefetch=1,
-            grid=(rows,),
+            grid=(rows // PAIR,),
             in_specs=[pl.BlockSpec(weights.shape, lambda i, at: (0, 0))]
-            + [pl.BlockSpec((1, slices, cols), lambda i, at, start=start: (i + start, 0, 0)) for _, start in parts]
+            + [
+                pl.BlockSpec((PAIR, slices, cols), lambda i, at, start=start: (i + start // PAIR, 0, 0))
+                for _, start in parts
+            ]
             + [anywhere()] * len(earlier),
-            out_specs=[pl.BlockSpec((zbins, cols), lambda i, at: (0, i + at[0]))] * 2
+            out_specs=[pl.BlockSpec((zbins, PAIR * cols), lambda i, at: (0, i + at[0] // PAIR))] * 2
             + [pl.BlockSpec((8, LANES), lambda i, at: (0, 0))],
         ),
         out_shape=[shape, shape, hbm((8, LANES), jnp.float32)],
@@ -438,38 +443,37 @@
 
 
 INNER, OUTER = (1, 0, REACH), (0, 0, REACH)
-GROUPS = (1, 0, 5), (1, 5, REACH), (0, 0, 5), (0, 5, REACH)
-FIRST = (((4, GROUPS[:2]),), ((6, (INNER,)), (5, (INNER,))))
+HEAD, TAIL = (0, 0, 6), (0, 6, REACH)
+FIRST = (((4, (INNER,)),), ((6, (INNER,)), (5, (INNER,))))
 REST = (
-    (5, GROUPS[2:]),
-    (7, (INNER, *GROUPS[2:])),
+    (5, (HEAD, TAIL)),
+    (7, (INNER, HEAD, TAIL)),
     (2, (INNER, OUTER)),
     (3, (INNER, OUTER)),
-    (4, GROUPS[2:]),
-    (6, GROUPS[2:]),
+    (4, (HEAD, TAIL)),
+    (6, (HEAD, TAIL)),
     (1, (INNER, OUTER)),
     (0, (INNER, OUTER)),
 )
 ORDER = (
-    (4, GROUPS[0], None),
+    (4, INNER, None),
     (6, INNER, None),
     (5, INNER, None),
-    (4, GROUPS[1], None),
-    (7, INNER, 3),
-    (2, INNER, 3),
-    (4, GROUPS[2], 1),
+    (7, INNER, 0),
+    (2, INNER, 0),
+    (4, HEAD, 1),
     (3, INNER, 1),
-    (6, GROUPS[2], 2),
+    (6, HEAD, 2),
     (2, OUTER, 2),
-    (5, GROUPS[2], 6),
-    (1, INNER, 7),
-    (7, GROUPS[2], 8),
-    (3, OUTER, 9),
-    (1, OUTER, 10),
-    (4, GROUPS[3], 11),
-    (6, GROUPS[3], 12),
-    (5, GROUPS[3], 13),
-    (7, GROUPS[3], 14),
+    (5, HEAD, 5),
+    (1, INNER, 6),
+    (7, HEAD, 7),
+    (3, OUTER, 8),
+    (1, OUTER, 9),
+    (4, TAIL, 10),
+    (6, TAIL, 11),
+    (5, TAIL, 12),
+    (7, TAIL, 13),
 )
 
 
@@ -484,7 +488,7 @@
         return lax.ppermute(x, "cuts", [(i, i ^ k) for i in range(peers)])
 
     own, first, last = masked_sums(density, valid)
-    sums = [own] + [lax.ppermute(own, "tile", [(i, i ^ k) for i in range(tiles)]) for k in range(1, tiles)]
+    sums = [held(own)] + [lax.ppermute(own, "tile", [(i, i ^ k) for i in range(tiles)]) for k in range(1, tiles)]
     mean = means(sums, slices)
 
     made, arrived = {}, {}
@@ -508,7 +512,7 @@
     for wanted in FIRST:
         got = filter_inner(ids(wanted), [cut for _, cut in wanted], density, valid, *inputs, *after)
         keep(wanted, got)
-        after = (got[0][0],)
+        after = (held(got[0][0]),)
     first_piece = ORDER[0][:2]
     send(*first_piece)
     got = filter_band(
@@ -539,12 +543,11 @@
             continue
         before = [] if wait is None else [arrived[ORDER[wait][:2]]]
         if at == len(ORDER) - 3:
-            finish(GROUPS[0])
-            finish(GROUPS[1])
-            before.append(tokens[1])
+            finish(INNER)
+            before.append(tokens[0])
         send(k, piece, *before)
-    finish(GROUPS[2])
-    finish(GROUPS[3])
+    finish(HEAD)
+    finish(TAIL)
     return tuple(result)
 
 

time: 126 us -> 127 us (level)
  waiting for transfers between devices: 36.3 us -> 41.9 us
  local copies, waits for them, and re-layouts: 5.31 us -> 2.75 us
  starting transfers between devices: 35 us -> 32.6 us
    ppermute x3, waiting for transfers between devices: 0.01 us -> 3.69 us  [fast(): lax.ppermute(own, 'tile', [(i, i ^ k) for i in range(tiles)])]
    unnamed x29 -> x21, local copies, waits for them, and re-layouts: 4.56 us -> 2 us
    ppermute x19 -> x18, waiting for transfers between devices: 36.3 us -> 38 us  [swap(): return lax.ppermute(x, 'cuts', [(i, i ^ k) for i in range(peers)])]
    ppermute x1, starting transfers between devices: 3.86 us -> 2.45 us  [fast(): above = lax.ppermute(last, 'tile', [(i, i + 1) for i in range(tiles - 1)])]
    ppermute x19 -> x18, starting transfers between devices: 25.3 us -> 24.1 us  [swap(): return lax.ppermute(x, 'cuts', [(i, i ^ k) for i in range(peers)])]
    pallas_call x4 -> x3, Pallas kernels: 10.4 us -> 9.37 us  [project(): pl.pallas_call(functools.partial(project_kernel, count), name='project',...]
  transfers between devices with their start and end apart: 24 -> 23, of which waited for: 10 -> 10; matrix products, arithmetic and copies ran while one was open for 1% -> 1% of each run, Pallas kernels for 33% -> 27%
where the time goes in v8:
time: 127 us; the launch traced here: 124 us
  Pallas kernels  45.9 us (36%)
  waiting for transfers between devices  41.9 us (33%)
  starting transfers between devices  32.6 us (26%)
  local copies, waits for them, and re-layouts  2.75 us (2%)
    ppermute x18, waiting for transfers between devices, swap(): return lax.ppermute(x, 'cuts', [(i, i ^ k) for i in range(peers)])  38 us
    ppermute x18, starting transfers between devices, swap(): return lax.ppermute(x, 'cuts', [(i, i ^ k) for i in range(peers)])  24.1 us
    pallas_call x1, Pallas kernels, filter_band(): pl.pallas_call(functools.partial(band_kernel, pieces), name='band', grid_...  17.3 us
    pallas_call x2, Pallas kernels, filter_inner(): pl.pallas_call(functools.partial(inner_kernel, pieces), name='inner', gri...  15 us
    pallas_call x3, Pallas kernels, project(): pl.pallas_call(functools.partial(project_kernel, count), name='project',...  9.37 us
    ppermute x3, starting transfers between devices, fast(): lax.ppermute(own, 'tile', [(i, i ^ k) for i in range(tiles)])  4.6 us
    ppermute x3, waiting for transfers between devices, fast(): lax.ppermute(own, 'tile', [(i, i ^ k) for i in range(tiles)])  3.69 us
    pallas_call x1, Pallas kernels, masked_sums(): pl.pallas_call(sums_kernel, name='sums', in_specs=[anywhere()] * 2, out_s...  3.38 us
  transfers between devices with their start and end apart: 23, of which 10 were waited for; matrix products, arithmetic and copies ran while one was open for 1% of the time, Pallas kernels for 27%

profile of v8, /device:TPU:0, one launch (start us, length us, event | category | flops | bytes accessed | tf_op | source)
XLA Modules:
  0.0 124.2 jit_solution(2167094224803347701)
XLA Ops:
  0.6 3.4 %sums.1 = (f32[24,128]{1,0:T(8,128)}, bf16[17,8,1024]{2,1,0:T(8,128)(2,1)}, bf16[17,8,1024]{2,1,0:T(8,128)(2,1)}) custom-call(bf16[16,128,1024]{2,1,0:T(8,128)(2,1)} %density.7, s32[128,1024]{1,0:T(8,128)} %valid.7), custom_call_target="tpu_custom_call" | custom-call | flops 1 | bytes 1 | tf_op jit(solution)/shard_map/sums/pallas_call | solution.py:150
  4.1 4.0 %collective-permute-start.4 = (f32[24,128]{1,0:T(8,128)}, f32[24,128]{1,0:T(8,128)S(1)}, u32[]{:S(2)}, u32[]{:S(2)}) collective-permute-start(f32[24,128]{1,0:T(8,128)} %get-tuple-element.33.refs_0_), channel_id=1, source_target_pairs={{0,24},{8,16},{16,8},{24,0},{1,25},{9,17},{17,9},{25,1},{2,26},{10... | collective-permute-start | bytes 36872 | tf_op jit(solution)/shard_map/ppermute | solution.py:491
  9.9 2.0 %collective-permute-done.3.refs_2_ = f32[24,128]{1,0:T(8,128)S(1)} collective-permute-done((f32[24,128]{1,0:T(8,128)}, f32[24,128]{1,0:T(8,128)S(1)}, u32[]{:S(2)}, u32[]{:S(2)}) %collective-permute-start.3) | collective-permute-done | bytes 12320 | tf_op jit(solution)/shard_map/ppermute | solution.py:491
  13.2 6.2 %inner.2.refs_0_ = bf16[8,16,1024]{2,1,0:T(8,128)(2,1)} custom-call(s32[2]{0:T(128)S(1)} %pad_add_fusion.1.ids, bf16[16,128,1024]{2,1,0:T(8,128)(2,1)} %density.7, s32[128,1024]{1,0:T(8,128)} %valid.7, bf16[4,16,17]{2,1,0:T(8,128)(2,1)S(1)} %copy-done.2, bf16[4,16,17]{2,1,0:T(8,128)(2,1)S(1)} %copy-done.3, f32[16,128]{1,0:T(8,128)S(1)} %means.1.mean), custom_call_target="tpu_custom_call" | custom-call | flops 1 | bytes 1 | tf_op jit(solution)/shard_map/inner/pallas_call | solution.py:231
  19.4 2.6 %collective-permute-start.5 = (bf16[8,16,1024]{2,1,0:T(8,128)(2,1)}, bf16[8,16,1024]{2,1,0:T(8,128)(2,1)S(1)}, u32[]{:S(2)}, u32[]{:S(2)}) collective-permute-start(bf16[8,16,1024]{2,1,0:T(8,128)(2,1)} %inner.2.refs_0_), channel_id=1, source_target_pairs={{0,4},{1,5},{2,6},{3,7},{4,0},{5,1},{6,2},{7,3},{8,12},{9,13},{10,... | collective-permute-start | bytes 786440 | tf_op jit(solution)/shard_map/ppermute | solution.py:488
  22.1 2.4 %collective-permute-start = (bf16[17,8,1024]{2,1,0:T(8,128)(2,1)S(1)}, bf16[17,8,1024]{2,1,0:T(8,128)(2,1)S(1)}, u32[]{:S(2)}, u32[]{:S(2)}) collective-permute-start(bf16[17,8,1024]{2,1,0:T(8,128)(2,1)S(1)} %copy-done.9), channel_id=1, source_target_pairs={{0,8},{8,16},{16,24},{1,9},{9,17},{17,25},{2,10},{10,18},{18,26},{... | collective-permute-start | bytes 835592 | tf_op jit(solution)/shard_map/ppermute | solution.py:496
  24.5 1.5 %collective-permute-start.1 = (bf16[17,8,1024]{2,1,0:T(8,128)(2,1)S(1)}, bf16[17,8,1024]{2,1,0:T(8,128)(2,1)S(1)}, u32[]{:S(2)}, u32[]{:S(2)}) collective-permute-start(bf16[17,8,1024]{2,1,0:T(8,128)(2,1)S(1)} %copy-done.8), channel_id=1, source_target_pairs={{8,0},{16,8},{24,16},{9,1},{17,9},{25,17},{10,2},{18,10},{26,18},{... | collective-permute-start | bytes 835592 | tf_op jit(solution)/shard_map/ppermute | solution.py:497
  26.1 8.8 %inner.3 = (bf16[8,16,1024]{2,1,0:T(8,128)(2,1)}, bf16[8,16,1024]{2,1,0:T(8,128)(2,1)}) custom-call(s32[3]{0:T(128)S(1)} %pad_add_fusion.ids, bf16[16,128,1024]{2,1,0:T(8,128)(2,1)} %density.7, s32[128,1024]{1,0:T(8,128)} %valid.7, bf16[4,16,17]{2,1,0:T(8,128)(2,1)S(1)} %copy-done.2, bf16[4,16,17]{2,1,0:T(8,128)(2,1)S(1)} %copy-done.3, ...), custom_call_target="tpu_custom_call" | custom-call | flops 1 | bytes 1 | tf_op jit(solution)/shard_map/inner/pallas_call | solution.py:231
  34.9 1.4 %collective-permute-start.6 = (bf16[8,16,1024]{2,1,0:T(8,128)(2,1)}, bf16[8,16,1024]{2,1,0:T(8,128)(2,1)S(1)}, u32[]{:S(2)}, u32[]{:S(2)}) collective-permute-start(bf16[8,16,1024]{2,1,0:T(8,128)(2,1)} %get-tuple-element.34.refs_0_), channel_id=1, source_target_pairs={{0,6},{1,7},{2,4},{3,5},{4,2},{5,3},{6,0},{7,1},{8,14},{9,15},{10,... | collective-permute-start | bytes 786440 | tf_op jit(solution)/shard_map/ppermute | solution.py:488
  38.0 17.3 %band.1 = (bf16[6,16,1024]{2,1,0:T(8,128)(2,1)}, bf16[2,16,1024]{2,1,0:T(8,128)(2,1)}, bf16[8,16,1024]{2,1,0:T(8,128)(2,1)}, bf16[6,16,1024]{2,1,0:T(8,128)(2,1)...) custom-call(s32[9]{0:T(128)S(1)} %concatenate.13.ids, ...), custom_call_target="tpu_custom_call" | custom-call | flops 1 | bytes 1 | tf_op jit(solution)/shard_map/band/pallas_call | solution.py:350
  55.3 2.6 %collective-permute-start.13 = (bf16[8,16,1024]{2,1,0:T(8,128)(2,1)}, bf16[8,16,1024]{2,1,0:T(8,128)(2,1)S(1)}, u32[]{:S(2)}, u32[]{:S(2)}) collective-permute-start(bf16[8,16,1024]{2,1,0:T(8,128)(2,1)} %gate.22), channel_id=1, source_target_pairs={{0,3},{1,2},{2,1},{3,0},{4,7},{5,6},{6,5},{7,4},{8,11},{9,10},{10,... | collective-permute-start | bytes 786440 | tf_op jit(solution)/shard_map/ppermute | solution.py:488
  58.1 1.8 %collective-permute-start.11 = (bf16[8,16,1024]{2,1,0:T(8,128)(2,1)}, bf16[8,16,1024]{2,1,0:T(8,128)(2,1)S(1)}, u32[]{:S(2)}, u32[]{:S(2)}) collective-permute-start(bf16[8,16,1024]{2,1,0:T(8,128)(2,1)} %gate.20), channel_id=1, source_target_pairs={{0,2},{1,3},{2,0},{3,1},{4,6},{5,7},{6,4},{7,5},{8,10},{9,11},{10,... | collective-permute-start | bytes 786440 | tf_op jit(solution)/shard_map/ppermute | solution.py:488
  59.8 9.4 %collective-permute-done.7.refs_1_.refs_4_ = bf16[6,16,1024]{2,1,0:T(8,128)(2,1)S(1)} collective-permute-done((bf16[6,16,1024]{2,1,0:T(8,128)(2,1)}, bf16[6,16,1024]{2,1,0:T(8,128)(2,1)S(1)}, u32[]{:S(2)}, u32[]{:S(2)}) %collective-permute-start.7) | collective-permute-done | bytes 196640 | tf_op jit(solution)/shard_map/ppermute | solution.py:488
  70.6 3.1 %collective-permute-start.14 = (bf16[8,16,1024]{2,1,0:T(8,128)(2,1)}, bf16[8,16,1024]{2,1,0:T(8,128)(2,1)S(1)}, u32[]{:S(2)}, u32[]{:S(2)}) collective-permute-start(bf16[8,16,1024]{2,1,0:T(8,128)(2,1)} %gate.23), channel_id=1, source_target_pairs={{0,1},{1,0},{2,3},{3,2},{4,5},{5,4},{6,7},{7,6},{8,9},{9,8},{10,11... | collective-permute-start | bytes 786440 | tf_op jit(solution)/shard_map/ppermute | solution.py:488
  73.7 2.2 %collective-permute-start.20 = (bf16[8,16,1024]{2,1,0:T(8,128)(2,1)}, bf16[8,16,1024]{2,1,0:T(8,128)(2,1)}, u32[]{:S(2)}, u32[]{:S(2)}) collective-permute-start(bf16[8,16,1024]{2,1,0:T(8,128)(2,1)} %gate.29), channel_id=1, source_target_pairs={{0,7},{1,6},{2,5},{3,4},{4,3},{5,2},{6,1},{7,0},{8,15},{9,14},{10,... | collective-permute-start | bytes 786440 | tf_op jit(solution)/shard_map/ppermute | solution.py:488
  76.5 14.3 %collective-permute-done.8.refs_1_.refs_5_ = bf16[6,16,1024]{2,1,0:T(8,128)(2,1)S(1)} collective-permute-done((bf16[6,16,1024]{2,1,0:T(8,128)(2,1)}, bf16[6,16,1024]{2,1,0:T(8,128)(2,1)S(1)}, u32[]{:S(2)}, u32[]{:S(2)}) %collective-permute-start.8) | collective-permute-done | bytes 196640 | tf_op jit(solution)/shard_map/ppermute | solution.py:488
  90.8 1.7 %collective-permute-start.9 = (bf16[8,16,1024]{2,1,0:T(8,128)(2,1)}, bf16[8,16,1024]{2,1,0:T(8,128)(2,1)S(1)}, u32[]{:S(2)}, u32[]{:S(2)}) collective-permute-start(bf16[8,16,1024]{2,1,0:T(8,128)(2,1)} %gate.19), channel_id=1, source_target_pairs={{0,1},{1,0},{2,3},{3,2},{4,5},{5,4},{6,7},{7,6},{8,9},{9,8},{10,11... | collective-permute-start | bytes 786440 | tf_op jit(solution)/shard_map/ppermute | solution.py:488
  94.3 12.4 %collective-permute-done.12.refs_1_.refs_3_ = bf16[8,16,1024]{2,1,0:T(8,128)(2,1)S(1)} collective-permute-done((bf16[8,16,1024]{2,1,0:T(8,128)(2,1)}, bf16[8,16,1024]{2,1,0:T(8,128)(2,1)S(1)}, u32[]{:S(2)}, u32[]{:S(2)}) %collective-permute-start.12) | collective-permute-done | bytes 262176 | tf_op jit(solution)/shard_map/ppermute | solution.py:488
  106.6 2.4 %collective-permute-start.16 = (bf16[2,16,1024]{2,1,0:T(8,128)(2,1)}, bf16[2,16,1024]{2,1,0:T(8,128)(2,1)}, u32[]{:S(2)}, u32[]{:S(2)}) collective-permute-start(bf16[2,16,1024]{2,1,0:T(8,128)(2,1)} %gate.25), channel_id=1, source_target_pairs={{0,5},{1,4},{2,7},{3,6},{4,1},{5,0},{6,3},{7,2},{8,13},{9,12},{10,... | collective-permute-start | bytes 196616 | tf_op jit(solution)/shard_map/ppermute | solution.py:488
  109.0 4.5 %project.3 = (bf16[128,16384]{1,0:T(8,128)(2,1)}, bf16[128,16384]{1,0:T(8,128)(2,1)}, f32[8,128]{1,0:T(8,128)}) custom-call(s32[1]{0:T(128)} %bitcast.14.place, bf16[256,128]{1,0:T(8,128)(2,1)S(1)} %copy.30.weights, bf16[8,16,1024]{2,1,0:T(8,128)(2,1)S(1)} %copy-done.1, bf16[8,16,1024]{2,1,0:T(8,128)(2,1)S(1)} %collective-permute-done.14.refs_1_, ...), custom_call_target="tpu_custom_call" | custom-call | flops 1 | bytes 1 | tf_op jit(solution)/shard_map/project/pallas_call | solution.py:406
  114.2 1.5 %collective-permute-start.21 = (bf16[2,16,1024]{2,1,0:T(8,128)(2,1)}, bf16[2,16,1024]{2,1,0:T(8,128)(2,1)S(1)}, u32[]{:S(2)}, u32[]{:S(2)}) collective-permute-start(bf16[2,16,1024]{2,1,0:T(8,128)(2,1)} %gate.30), channel_id=1, source_target_pairs={{0,6},{1,7},{2,4},{3,5},{4,2},{5,3},{6,0},{7,1},{8,14},{9,15},{10,... | collective-permute-start | bytes 196616 | tf_op jit(solution)/shard_map/ppermute | solution.py:488
  115.7 2.3 %collective-permute-start.22 = (bf16[2,16,1024]{2,1,0:T(8,128)(2,1)}, bf16[2,16,1024]{2,1,0:T(8,128)(2,1)S(1)}, u32[]{:S(2)}, u32[]{:S(2)}) collective-permute-start(bf16[2,16,1024]{2,1,0:T(8,128)(2,1)} %gate.31), channel_id=1, source_target_pairs={{0,7},{1,6},{2,5},{3,4},{4,3},{5,2},{6,1},{7,0},{8,15},{9,14},{10,... | collective-permute-start | bytes 196616 | tf_op jit(solution)/shard_map/ppermute | solution.py:488
  118.0 2.7 %project.4 = (bf16[128,16384]{1,0:T(8,128)(2,1)}, bf16[128,16384]{1,0:T(8,128)(2,1)}, f32[8,128]{1,0:T(8,128)}) custom-call(s32[1]{0:T(128)} %bitcast.15.place, bf16[256,128]{1,0:T(8,128)(2,1)S(1)} %copy.30.weights, bf16[8,16,1024]{2,1,0:T(8,128)(2,1)S(1)} %copy-done, ...), custom_call_target="tpu_custom_call", output_to_operand_aliasing={{0}: (10, {}), {1}: (11, {})} | custom-call | flops 1 | bytes 1 | tf_op jit(solution)/shard_map/project/pallas_call | solution.py:406
  122.0 2.2 %project.5 = (bf16[128,16384]{1,0:T(8,128)(2,1)}, bf16[128,16384]{1,0:T(8,128)(2,1)}, f32[8,128]{1,0:T(8,128)}) custom-call(s32[1]{0:T(128)} %bitcast.place, bf16[256,128]{1,0:T(8,128)(2,1)S(1)} %copy.30.weights, bf16[8,16,1024]{2,1,0:T(8,128)(2,1)S(1)} %copy-done, ...), custom_call_target="tpu_custom_call", output_to_operand_aliasing={{0}: (10, {}), {1}: (11, {})} | custom-call | flops 1 | bytes 1 | tf_op jit(solution)/shard_map/project/pallas_call | solution.py:406
  (75 shorter events, 10.8 us)
Async XLA Ops:
  4.1 5.8 %collective-permute-start.4 = (f32[24,128]{1,0:T(8,128)}, f32[24,128]{1,0:T(8,128)S(1)}, u32[]{:S(2)}, u32[]{:S(2)}) collective-permute-start(f32[24,128]{1,0:T(8,128)} %get-tuple-element.33.refs_0_), channel_id=1, source_target_pairs={{0,24},{8,16},{16,8},{24,0},{1,25},{9,17},{17,9},{25,1},{2,26},{10... | collective-permute-start | bytes 36872 | tf_op jit(solution)/shard_map/ppermute | solution.py:491
  8.0 3.9 %collective-permute-start.3 = (f32[24,128]{1,0:T(8,128)}, f32[24,128]{1,0:T(8,128)S(1)}, u32[]{:S(2)}, u32[]{:S(2)}) collective-permute-start(f32[24,128]{1,0:T(8,128)} %get-tuple-element.33.refs_0_), channel_id=1, source_target_pairs={{0,16},{8,24},{16,0},{24,8},{1,17},{9,25},{17,1},{25,9},{2,18},{10... | collective-permute-start | bytes 36872 | tf_op jit(solution)/shard_map/ppermute | solution.py:491
  8.5 3.9 %collective-permute-start.2 = (f32[24,128]{1,0:T(8,128)}, f32[24,128]{1,0:T(8,128)S(1)}, u32[]{:S(2)}, u32[]{:S(2)}) collective-permute-start(f32[24,128]{1,0:T(8,128)} %get-tuple-element.33.refs_0_), channel_id=1, source_target_pairs={{0,8},{8,0},{16,24},{24,16},{1,9},{9,1},{17,25},{25,17},{2,10},{10... | collective-permute-start | bytes 36872 | tf_op jit(solution)/shard_map/ppermute | solution.py:491
  19.4 17.6 %collective-permute-start.5 = (bf16[8,16,1024]{2,1,0:T(8,128)(2,1)}, bf16[8,16,1024]{2,1,0:T(8,128)(2,1)S(1)}, u32[]{:S(2)}, u32[]{:S(2)}) collective-permute-start(bf16[8,16,1024]{2,1,0:T(8,128)(2,1)} %inner.2.refs_0_), channel_id=1, source_target_pairs={{0,4},{1,5},{2,6},{3,7},{4,0},{5,1},{6,2},{7,3},{8,12},{9,13},{10,... | collective-permute-start | bytes 786440 | tf_op jit(solution)/shard_map/ppermute | solution.py:488
  22.1 15.0 %collective-permute-start = (bf16[17,8,1024]{2,1,0:T(8,128)(2,1)S(1)}, bf16[17,8,1024]{2,1,0:T(8,128)(2,1)S(1)}, u32[]{:S(2)}, u32[]{:S(2)}) collective-permute-start(bf16[17,8,1024]{2,1,0:T(8,128)(2,1)S(1)} %copy-done.9), channel_id=1, source_target_pairs={{0,8},{8,16},{16,24},{1,9},{9,17},{17,25},{2,10},{10,18},{18,26},{... | collective-permute-start | bytes 835592 | tf_op jit(solution)/shard_map/ppermute | solution.py:496
  24.5 12.8 %collective-permute-start.1 = (bf16[17,8,1024]{2,1,0:T(8,128)(2,1)S(1)}, bf16[17,8,1024]{2,1,0:T(8,128)(2,1)S(1)}, u32[]{:S(2)}, u32[]{:S(2)}) collective-permute-start(bf16[17,8,1024]{2,1,0:T(8,128)(2,1)S(1)} %copy-done.8), channel_id=1, source_target_pairs={{8,0},{16,8},{24,16},{9,1},{17,9},{25,17},{10,2},{18,10},{26,18},{... | collective-permute-start | bytes 835592 | tf_op jit(solution)/shard_map/ppermute | solution.py:497
  34.9 20.4 %collective-permute-start.6 = (bf16[8,16,1024]{2,1,0:T(8,128)(2,1)}, bf16[8,16,1024]{2,1,0:T(8,128)(2,1)S(1)}, u32[]{:S(2)}, u32[]{:S(2)}) collective-permute-start(bf16[8,16,1024]{2,1,0:T(8,128)(2,1)} %get-tuple-element.34.refs_0_), channel_id=1, source_target_pairs={{0,6},{1,7},{2,4},{3,5},{4,2},{5,3},{6,0},{7,1},{8,14},{9,15},{10,... | collective-permute-start | bytes 786440 | tf_op jit(solution)/shard_map/ppermute | solution.py:488
  37.0 21.0 %collective-permute-start.10 = (bf16[8,16,1024]{2,1,0:T(8,128)(2,1)}, bf16[8,16,1024]{2,1,0:T(8,128)(2,1)S(1)}, u32[]{:S(2)}, u32[]{:S(2)}) collective-permute-start(bf16[8,16,1024]{2,1,0:T(8,128)(2,1)} %get-tuple-element.40), channel_id=1, source_target_pairs={{0,5},{1,4},{2,7},{3,6},{4,1},{5,0},{6,3},{7,2},{8,13},{9,12},{10,... | collective-permute-start | bytes 786440 | tf_op jit(solution)/shard_map/ppermute | solution.py:488
  55.3 15.2 %collective-permute-start.13 = (bf16[8,16,1024]{2,1,0:T(8,128)(2,1)}, bf16[8,16,1024]{2,1,0:T(8,128)(2,1)S(1)}, u32[]{:S(2)}, u32[]{:S(2)}) collective-permute-start(bf16[8,16,1024]{2,1,0:T(8,128)(2,1)} %gate.22), channel_id=1, source_target_pairs={{0,3},{1,2},{2,1},{3,0},{4,7},{5,6},{6,5},{7,4},{8,11},{9,10},{10,... | collective-permute-start | bytes 786440 | tf_op jit(solution)/shard_map/ppermute | solution.py:488
  57.9 11.3 %collective-permute-start.7 = (bf16[6,16,1024]{2,1,0:T(8,128)(2,1)}, bf16[6,16,1024]{2,1,0:T(8,128)(2,1)S(1)}, u32[]{:S(2)}, u32[]{:S(2)}) collective-permute-start(bf16[6,16,1024]{2,1,0:T(8,128)(2,1)} %gate.17), channel_id=1, source_target_pairs={{0,4},{1,5},{2,6},{3,7},{4,0},{5,1},{6,2},{7,3},{8,12},{9,13},{10,... | collective-permute-start | bytes 589832 | tf_op jit(solution)/shard_map/ppermute | solution.py:488
  58.0 51.0 %copy-start.1 = (bf16[8,16,1024]{2,1,0:T(8,128)(2,1)S(1)}, bf16[8,16,1024]{2,1,0:T(8,128)(2,1)}, u32[]{:S(2)}) copy-start(bf16[8,16,1024]{2,1,0:T(8,128)(2,1)} %get-tuple-element.49.refs_0_) | copy-start | bytes 786436
  58.1 18.5 %collective-permute-start.11 = (bf16[8,16,1024]{2,1,0:T(8,128)(2,1)}, bf16[8,16,1024]{2,1,0:T(8,128)(2,1)S(1)}, u32[]{:S(2)}, u32[]{:S(2)}) collective-permute-start(bf16[8,16,1024]{2,1,0:T(8,128)(2,1)} %gate.20), channel_id=1, source_target_pairs={{0,2},{1,3},{2,0},{3,1},{4,6},{5,7},{6,4},{7,5},{8,10},{9,11},{10,... | collective-permute-start | bytes 786440 | tf_op jit(solution)/shard_map/ppermute | solution.py:488
  69.2 21.6 %collective-permute-start.8 = (bf16[6,16,1024]{2,1,0:T(8,128)(2,1)}, bf16[6,16,1024]{2,1,0:T(8,128)(2,1)S(1)}, u32[]{:S(2)}, u32[]{:S(2)}) collective-permute-start(bf16[6,16,1024]{2,1,0:T(8,128)(2,1)} %gate.18), channel_id=1, source_target_pairs={{0,5},{1,4},{2,7},{3,6},{4,1},{5,0},{6,3},{7,2},{8,13},{9,12},{10,... | collective-permute-start | bytes 589832 | tf_op jit(solution)/shard_map/ppermute | solution.py:488
  69.2 21.6 %collective-permute-start.17 = (bf16[6,16,1024]{2,1,0:T(8,128)(2,1)}, bf16[6,16,1024]{2,1,0:T(8,128)(2,1)S(1)}, u32[]{:S(2)}, u32[]{:S(2)}) collective-permute-start(bf16[6,16,1024]{2,1,0:T(8,128)(2,1)} %gate.26), channel_id=1, source_target_pairs={{0,6},{1,7},{2,4},{3,5},{4,2},{5,3},{6,0},{7,1},{8,14},{9,15},{10,... | collective-permute-start | bytes 589832 | tf_op jit(solution)/shard_map/ppermute | solution.py:488
  70.6 21.9 %collective-permute-start.14 = (bf16[8,16,1024]{2,1,0:T(8,128)(2,1)}, bf16[8,16,1024]{2,1,0:T(8,128)(2,1)S(1)}, u32[]{:S(2)}, u32[]{:S(2)}) collective-permute-start(bf16[8,16,1024]{2,1,0:T(8,128)(2,1)} %gate.23), channel_id=1, source_target_pairs={{0,1},{1,0},{2,3},{3,2},{4,5},{5,4},{6,7},{7,6},{8,9},{9,8},{10,11... | collective-permute-start | bytes 786440 | tf_op jit(solution)/shard_map/ppermute | solution.py:488
  73.7 33.0 %collective-permute-start.20 = (bf16[8,16,1024]{2,1,0:T(8,128)(2,1)}, bf16[8,16,1024]{2,1,0:T(8,128)(2,1)}, u32[]{:S(2)}, u32[]{:S(2)}) collective-permute-start(bf16[8,16,1024]{2,1,0:T(8,128)(2,1)} %gate.29), channel_id=1, source_target_pairs={{0,7},{1,6},{2,5},{3,4},{4,3},{5,2},{6,1},{7,0},{8,15},{9,14},{10,... | collective-permute-start | bytes 786440 | tf_op jit(solution)/shard_map/ppermute | solution.py:488
  76.5 32.5 %collective-permute-start.19 = (bf16[8,16,1024]{2,1,0:T(8,128)(2,1)}, bf16[8,16,1024]{2,1,0:T(8,128)(2,1)}, u32[]{:S(2)}, u32[]{:S(2)}) collective-permute-start(bf16[8,16,1024]{2,1,0:T(8,128)(2,1)} %gate.28), channel_id=1, source_target_pairs={{0,2},{1,3},{2,0},{3,1},{4,6},{5,7},{6,4},{7,5},{8,10},{9,11},{10,... | collective-permute-start | bytes 786440 | tf_op jit(solution)/shard_map/ppermute | solution.py:488
  90.8 15.8 %collective-permute-start.12 = (bf16[8,16,1024]{2,1,0:T(8,128)(2,1)}, bf16[8,16,1024]{2,1,0:T(8,128)(2,1)S(1)}, u32[]{:S(2)}, u32[]{:S(2)}) collective-permute-start(bf16[8,16,1024]{2,1,0:T(8,128)(2,1)} %gate.21), channel_id=1, source_target_pairs={{0,3},{1,2},{2,1},{3,0},{4,7},{5,6},{6,5},{7,4},{8,11},{9,10},{10,... | collective-permute-start | bytes 786440 | tf_op jit(solution)/shard_map/ppermute | solution.py:488
  90.8 24.9 %collective-permute-start.9 = (bf16[8,16,1024]{2,1,0:T(8,128)(2,1)}, bf16[8,16,1024]{2,1,0:T(8,128)(2,1)S(1)}, u32[]{:S(2)}, u32[]{:S(2)}) collective-permute-start(bf16[8,16,1024]{2,1,0:T(8,128)(2,1)} %gate.19), channel_id=1, source_target_pairs={{0,1},{1,0},{2,3},{3,2},{4,5},{5,4},{6,7},{7,6},{8,9},{9,8},{10,11... | collective-permute-start | bytes 786440 | tf_op jit(solution)/shard_map/ppermute | solution.py:488
  92.5 21.0 %collective-permute-start.18 = (bf16[6,16,1024]{2,1,0:T(8,128)(2,1)}, bf16[6,16,1024]{2,1,0:T(8,128)(2,1)S(1)}, u32[]{:S(2)}, u32[]{:S(2)}) collective-permute-start(bf16[6,16,1024]{2,1,0:T(8,128)(2,1)} %gate.27), channel_id=1, source_target_pairs={{0,7},{1,6},{2,5},{3,4},{4,3},{5,2},{6,1},{7,0},{8,15},{9,14},{10,... | collective-permute-start | bytes 589832 | tf_op jit(solution)/shard_map/ppermute | solution.py:488
  106.6 14.1 %collective-permute-start.15 = (bf16[2,16,1024]{2,1,0:T(8,128)(2,1)}, bf16[2,16,1024]{2,1,0:T(8,128)(2,1)S(1)}, u32[]{:S(2)}, u32[]{:S(2)}) collective-permute-start(bf16[2,16,1024]{2,1,0:T(8,128)(2,1)} %gate.24), channel_id=1, source_target_pairs={{0,4},{1,5},{2,6},{3,7},{4,0},{5,1},{6,2},{7,3},{8,12},{9,13},{10,... | collective-permute-start | bytes 196616 | tf_op jit(solution)/shard_map/ppermute | solution.py:488
  106.6 14.1 %collective-permute-start.16 = (bf16[2,16,1024]{2,1,0:T(8,128)(2,1)}, bf16[2,16,1024]{2,1,0:T(8,128)(2,1)}, u32[]{:S(2)}, u32[]{:S(2)}) collective-permute-start(bf16[2,16,1024]{2,1,0:T(8,128)(2,1)} %gate.25), channel_id=1, source_target_pairs={{0,5},{1,4},{2,7},{3,6},{4,1},{5,0},{6,3},{7,2},{8,13},{9,12},{10,... | collective-permute-start | bytes 196616 | tf_op jit(solution)/shard_map/ppermute | solution.py:488
  114.2 7.0 %collective-permute-start.21 = (bf16[2,16,1024]{2,1,0:T(8,128)(2,1)}, bf16[2,16,1024]{2,1,0:T(8,128)(2,1)S(1)}, u32[]{:S(2)}, u32[]{:S(2)}) collective-permute-start(bf16[2,16,1024]{2,1,0:T(8,128)(2,1)} %gate.30), channel_id=1, source_target_pairs={{0,6},{1,7},{2,4},{3,5},{4,2},{5,3},{6,0},{7,1},{8,14},{9,15},{10,... | collective-permute-start | bytes 196616 | tf_op jit(solution)/shard_map/ppermute | solution.py:488
  115.7 6.3 %collective-permute-start.22 = (bf16[2,16,1024]{2,1,0:T(8,128)(2,1)}, bf16[2,16,1024]{2,1,0:T(8,128)(2,1)S(1)}, u32[]{:S(2)}, u32[]{:S(2)}) collective-permute-start(bf16[2,16,1024]{2,1,0:T(8,128)(2,1)} %gate.31), channel_id=1, source_target_pairs={{0,7},{1,6},{2,5},{3,4},{4,3},{5,2},{6,1},{7,0},{8,15},{9,14},{10,... | collective-permute-start | bytes 196616 | tf_op jit(solution)/shard_map/ppermute | solution.py:488
  (9 other events, 185.9 us)

commit v9 on v8

--- a/solution.py
+++ b/solution.py
@@ -29,6 +29,10 @@
 
 def held(x):
     return pltpu.with_memory_space_constraint(x, pltpu.HBM)
+
+
+def resident(x):
+    return pltpu.with_memory_space_constraint(x, pltpu.VMEM)
 
 
 def anywhere():
@@ -152,7 +156,7 @@
         name="sums",
         in_specs=[anywhere()] * 2,
         out_specs=[pl.BlockSpec(memory_space=pltpu.VMEM)] * 3,
-        out_shape=[hbm((slices + 8, LANES), jnp.float32), edge, edge],
+        out_shape=[jax.ShapeDtypeStruct((slices + 8, LANES), jnp.float32), edge, edge],
         scratch_shapes=[
             pltpu.VMEM(density.shape, jnp.bfloat16),
             pltpu.VMEM(valid.shape, jnp.int32),
@@ -171,14 +175,17 @@
     out[...] = jnp.broadcast_to(total[:slices] / total[slices : slices + 1], out.shape)
 
 
-def means(sums, slices):
+def means(sums, slices, after):
+    vmem = pl.BlockSpec(memory_space=pltpu.VMEM)
     return pl.pallas_call(
         mean_kernel,
         name="means",
+        in_specs=[vmem] * len(sums) + [anywhere()],
+        out_specs=vmem,
         out_shape=jax.ShapeDtypeStruct((slices, LANES), jnp.float32),
-        compiler_params=params(),
+        compiler_params=params(1),
         cost_estimate=cost(1, 1),
-    )(*sums)
+    )(*sums, resident(after))
 
 
 def inner_rows(both, last):
@@ -188,23 +195,59 @@
     return jnp.concatenate([chosen, jnp.zeros((REACH, both.shape[1]), jnp.float32)], axis=0)
 
 
-def inner_kernel(pieces, ids, density, valid, row_taps, col_taps, mean, *refs):
-    (col, row, tall, cube, plane, sems) = refs[-6:]
-    count, slices, high, _ = cube.shape
-    outs = list(refs[-6 - sum(len(wanted) for wanted in pieces) : -6])
-    block = high // 2
-    copies = []
-    for b in range(count):
-        here = pl.ds(pl.multiple_of(jnp.minimum(ids[b], ids[count] - 1) * block, block), high)
-        copies.append(pltpu.make_async_copy(density.at[:, here], cube.at[b], sems.at[2 * b]))
-        copies.append(pltpu.make_async_copy(valid.at[here], plane.at[b], sems.at[2 * b + 1]))
+def window_copies(ids, b, last, density, valid, cube, plane, sems):
+    high = plane.shape[1]
+    here = pl.ds(pl.multiple_of(jnp.minimum(ids[b], last - 1) * (high // 2), high // 2), high)
+    return [
+        pltpu.make_async_copy(density.at[:, here], cube.at[b], sems.at[2 * b]),
+        pltpu.make_async_copy(valid.at[here], plane.at[b], sems.at[2 * b + 1]),
+    ]
+
+
+def ready_kernel(ids, density, valid, row_taps, col_taps, after, col, row, cube, plane, sems):
+    copies = window_copies(ids, 0, ids[1], density, valid, cube, plane, sems)
     for copy in copies:
         copy.start()
     build_columns(listed(col_taps), col)
     build_rows(listed(row_taps), row)
     for copy in copies:
         copy.wait()
+
+
+def make_ready(ids, density, valid, row_taps, col_taps, after):
+    slices, rows, cols = density.shape
+    terms = row_taps.shape[0]
+    high = LANES // terms
+    vmem = pl.BlockSpec(memory_space=pltpu.VMEM)
+    shapes = *matrix_shapes(terms, slices, high - HALO), (1, slices, high, cols)
+    return pl.pallas_call(
+        ready_kernel,
+        name="ready",
+        in_specs=[pl.BlockSpec(memory_space=pltpu.SMEM)] + [anywhere()] * 2 + [vmem] * 2 + [anywhere()],
+        out_specs=[vmem] * 4,
+        out_shape=[pltpu.VMEM(shape, jnp.bfloat16) for shape in shapes] + [pltpu.VMEM((1, high, cols), jnp.int32)],
+        scratch_shapes=[pltpu.SemaphoreType.DMA((2,))],
+        compiler_params=params(),
+        cost_estimate=cost(1, 1),
+    )(jnp.stack([ids, jnp.full_like(ids, rows // (high - HALO) - 1)]), held(density), held(valid), row_taps, col_taps, after)
+
+
+def inner_kernel(pieces, loaded, ids, *refs):
+    count = len(pieces)
+    outs = sum(len(wanted) for wanted in pieces)
+    if loaded:
+        (cube, plane, col, row, mean), tall = refs[:5], refs[-1]
+        outs = list(refs[-1 - outs : -1])
+    else:
+        (density, valid, col, row, mean), (tall, cube, plane, sems) = refs[:5], refs[-4:]
+        outs = list(refs[-4 - outs : -4])
+        copies = [window_copies(ids, b, ids[count], density, valid, cube, plane, sems) for b in range(count)]
+        for copy in sum(copies, []):
+            copy.start()
     for b, wanted in enumerate(pieces):
+        if not loaded:
+            for copy in copies[b]:
+                copy.wait()
         last = ids[b] == ids[count]
         mask = inner_rows(plane[b], last)
         field = convolve(
@@ -218,41 +261,39 @@
             outs.pop(0)[...] = field[start:stop]
 
 
-def filter_inner(ids, pieces, density, valid, row_taps, col_taps, mean, *after):
+def filter_inner(ids, pieces, density, valid, ready, mean, *after):
     slices, rows, cols = density.shape
-    terms = row_taps.shape[0]
-    high = LANES // terms
+    col, row, cube, plane = ready
+    high = plane.shape[1]
     count = ids.shape[0]
-
-    def whole(x):
-        return pl.BlockSpec(x.shape, lambda i, at: (0,) * x.ndim)
-
+    loaded = not after
+    vmem = pl.BlockSpec(memory_space=pltpu.VMEM)
     shapes = [(stop - start, slices, cols) for wanted in pieces for _, start, stop in wanted]
+    field = [resident(cube), resident(plane)] if loaded else [held(density), held(valid)]
+    scratch = [pltpu.VMEM((GROUP * LANES, cols), jnp.bfloat16)]
+    if not loaded:
+        scratch += [
+            pltpu.VMEM((count, slices, high, cols), jnp.bfloat16),
+            pltpu.VMEM((count, high, cols), jnp.int32),
+            pltpu.SemaphoreType.DMA((2 * count,)),
+        ]
     out = pl.pallas_call(
-        functools.partial(inner_kernel, pieces),
+        functools.partial(inner_kernel, pieces, loaded),
         name="inner",
-        grid_spec=pltpu.PrefetchScalarGridSpec(
-            num_scalar_prefetch=1,
-            grid=(1,),
-            in_specs=[anywhere()] * 2 + [whole(x) for x in (row_taps, col_taps, mean)] + [anywhere()] * len(after),
-            out_specs=[pl.BlockSpec(shape, lambda i, at: (0, 0, 0)) for shape in shapes],
-            scratch_shapes=[pltpu.VMEM(x, jnp.bfloat16) for x in matrix_shapes(terms, slices, REACH)]
-            + [
-                pltpu.VMEM((GROUP * LANES, cols), jnp.bfloat16),
-                pltpu.VMEM((count, slices, high, cols), jnp.bfloat16),
-                pltpu.VMEM((count, high, cols), jnp.int32),
-                pltpu.SemaphoreType.DMA((2 * count,)),
-            ],
-        ),
+        in_specs=[pl.BlockSpec(memory_space=pltpu.SMEM)]
+        + [vmem if loaded else anywhere()] * 2
+        + [vmem] * 3
+        + [anywhere()] * len(after),
+        out_specs=[vmem] * len(shapes),
         out_shape=[hbm(shape, jnp.bfloat16) for shape in shapes],
+        scratch_shapes=scratch,
         compiler_params=params(),
         cost_estimate=cost(1, 1),
     )(
         jnp.concatenate([ids, jnp.full((1,), rows // (high - HALO) - 1, ids.dtype)]),
-        held(density),
-        held(valid),
-        row_taps,
-        col_taps,
+        *field,
+        resident(col),
+        resident(row),
         mean,
         *after,
     )
@@ -260,13 +301,13 @@
     return [[out.pop(0) for _ in wanted] for wanted in pieces]
 
 
-def band_kernel(pieces, ids, density, valid, above, below, row_taps, col_taps, mean, *refs):
-    (col, row, taps, mask, tall, done, sems) = refs[-7:]
+def band_kernel(pieces, ids, density, valid, above, below, col, row, mean, *refs):
+    (mask, tall, done, sems) = refs[-4:]
     count = sum(len(wanted) for wanted in pieces)
-    outs = refs[-7 - count : -7]
+    outs = refs[-4 - count : -4]
     slices = mean.shape[0]
     rows, cols = valid.shape
-    terms = row_taps.shape[0]
+    terms = col.shape[2] // LANES
     block = done.shape[1]
     high = block + HALO
     step = pl.program_id(0)
@@ -274,10 +315,6 @@
 
     @pl.when(step == 0)
     def _():
-        for k in range(terms):
-            taps[:, k] = jnp.dot(col_taps[k], tap_flip(), preferred_element_type=f32)
-        col[:, LANES + HALO :, :] = jnp.zeros((PER, LANES - HALO, terms * LANES), jnp.bfloat16)
-        build_rows(listed(row_taps), row)
         mask[:REACH] = above[slices].astype(f32)
         mask[REACH : REACH + rows] = valid[...].astype(f32)
         mask[REACH + rows :] = below[slices].astype(f32)
@@ -288,15 +325,12 @@
     def _():
         for j in range(PER):
             s = step * PER + j
-            mine = taps[s]
-            for k in range(terms):
-                col[j, : LANES + HALO, k * LANES : (k + 1) * LANES] = column_band(mine[k : k + 1])
             x = jnp.concatenate([above[s].astype(f32), density[j].astype(f32), below[s].astype(f32)], axis=0)
             x = mask[...] * (x - mean[pl.ds(s, 1), :][:, :1])
             x = jnp.concatenate([x, jnp.zeros((rows + HALO, LANES), f32)], axis=1)
             x = pltpu.roll(x, REACH, 1).astype(jnp.bfloat16)
             x = jnp.concatenate([x[:, c : c + 2 * LANES] for c in range(0, cols, LANES)], axis=0)
-            y = jnp.dot(x, col[j], preferred_element_type=f32).astype(jnp.bfloat16)
+            y = jnp.dot(x, col[s], preferred_element_type=f32).astype(jnp.bfloat16)
             for c in range(cols // LANES):
                 for k in range(terms):
                     tall[s * terms + k, :, c * LANES : (c + 1) * LANES] = y[
@@ -337,9 +371,10 @@
                 copy.wait()
 
 
-def filter_band(ids, pieces, density, valid, above, below, row_taps, col_taps, mean, *after):
+def filter_band(ids, pieces, density, valid, above, below, ready, mean, *after):
     slices, rows, cols = density.shape
-    terms = row_taps.shape[0]
+    col, row = ready[:2]
+    terms = col.shape[2] // LANES
     block = LANES // terms - HALO
     count = len(pieces)
 
@@ -354,13 +389,12 @@
             num_scalar_prefetch=1,
             grid=(slices // PER + count // PAIR,),
             in_specs=[pl.BlockSpec((PER, rows, cols), lambda i, at: (jnp.minimum(i, slices // PER - 1), 0, 0))]
-            + [whole(x) for x in (valid, above, below, row_taps, col_taps, mean)]
+            + [whole(x) for x in (valid, above, below)]
+            + [pl.BlockSpec(memory_space=pltpu.VMEM)] * 2
+            + [whole(mean)]
             + [anywhere()] * len(after),
             out_specs=[anywhere()] * len(shapes),
             scratch_shapes=[
-                pltpu.VMEM((PER, 2 * LANES, terms * LANES), jnp.bfloat16),
-                pltpu.VMEM((slices // GROUP, block * GROUP, GROUP * LANES), jnp.bfloat16),
-                pltpu.VMEM((slices, terms, 2 * LANES), jnp.float32),
                 pltpu.VMEM((rows + HALO, cols), jnp.float32),
                 pltpu.VMEM((slices * terms, rows + HALO, cols), jnp.bfloat16),
                 pltpu.VMEM((count, block, slices, cols), jnp.bfloat16),
@@ -376,8 +410,8 @@
         held(valid),
         above,
         below,
-        row_taps,
-        col_taps,
+        resident(col),
+        resident(row),
         mean,
         *after,
     )
@@ -460,20 +494,20 @@
     (6, INNER, None),
     (5, INNER, None),
     (7, INNER, 0),
-    (2, INNER, 0),
+    (2, INNER, 1),
     (4, HEAD, 1),
-    (3, INNER, 1),
+    (3, INNER, 2),
     (6, HEAD, 2),
-    (2, OUTER, 2),
-    (5, HEAD, 5),
+    (2, OUTER, 4),
+    (5, HEAD, 3),
     (1, INNER, 6),
-    (7, HEAD, 7),
-    (3, OUTER, 8),
-    (1, OUTER, 9),
-    (4, TAIL, 10),
-    (6, TAIL, 11),
-    (5, TAIL, 12),
-    (7, TAIL, 13),
+    (7, HEAD, 5),
+    (3, OUTER, 6),
+    (1, OUTER, 10),
+    (4, TAIL, 7),
+    (6, TAIL, 9),
+    (5, TAIL, 11),
+    (7, TAIL, 14),
 )
 
 
@@ -488,8 +522,9 @@
         return lax.ppermute(x, "cuts", [(i, i ^ k) for i in range(peers)])
 
     own, first, last = masked_sums(density, valid)
-    sums = [held(own)] + [lax.ppermute(own, "tile", [(i, i ^ k) for i in range(tiles)]) for k in range(1, tiles)]
-    mean = means(sums, slices)
+    sums = [own] + [lax.ppermute(own, "tile", [(i, i ^ k) for i in range(tiles)]) for k in range(1, tiles)]
+    ready = make_ready(me ^ ORDER[0][0], density, valid, row_taps, col_taps, own)
+    mean = means(sums, slices, ready[0])
 
     made, arrived = {}, {}
 
@@ -507,16 +542,15 @@
         x = made[k, piece]
         arrived[k, piece] = swap(gate(x, *before) if before else x, k)
 
-    inputs = row_taps, col_taps, mean
     after = ()
     for wanted in FIRST:
-        got = filter_inner(ids(wanted), [cut for _, cut in wanted], density, valid, *inputs, *after)
+        got = filter_inner(ids(wanted), [cut for _, cut in wanted], density, valid, ready, mean, *after)
         keep(wanted, got)
         after = (held(got[0][0]),)
     first_piece = ORDER[0][:2]
     send(*first_piece)
     got = filter_band(
-        ids(REST), [cut for _, cut in REST], density, valid, above, below, *inputs, *after, gate(mean, arrived[first_piece], flops=BEFORE_BAND)
+        ids(REST), [cut for _, cut in REST], density, valid, above, below, ready, mean, *after, gate(mean, arrived[first_piece], flops=BEFORE_BAND)
     )
     keep(REST, got)
     for piece in (INNER, OUTER):

time: 127 us -> 120 us (0.945)
  waiting for transfers between devices: 41.9 us -> 12.4 us
  starting transfers between devices: 32.6 us -> 51.6 us
  local copies, waits for them, and re-layouts: 2.75 us -> 9.02 us
  Pallas kernels: 45.9 us -> 43 us
  other arithmetic: 0.18 us -> 1.58 us
    ppermute x18, waiting for transfers between devices: 38 us -> 12 us  [swap(): return lax.ppermute(x, 'cuts', [(i, i ^ k) for i in range(peers)])]
    ppermute x18, starting transfers between devices: 24.1 us -> 42.1 us  [swap(): return lax.ppermute(x, 'cuts', [(i, i ^ k) for i in range(peers)])]
    unnamed x21 -> x29, local copies, waits for them, and re-layouts: 2 us -> 5.97 us
    ppermute x3, waiting for transfers between devices: 3.69 us -> 0.32 us  [fast(): lax.ppermute(own, 'tile', [(i, i ^ k) for i in range(tiles)])]
    pallas_call x3 -> x4, Pallas kernels: 15.8 us -> 14 us  [the longest x2 10.8 us: filter_inner(): pl.pallas_call(functools.partial(inner_kernel, pieces, loaded), name='inn...]
    gather x1, local copies, waits for them, and re-layouts: 0.55 us -> 2.02 us  [fast(): weights = weights[:, me ^ jnp.arange(peers)].reshape(-1, peers * slices)]
    concatenate x1, other arithmetic: 0.01 us -> 1.41 us  [fast(): jnp.concatenate([amp_matrix, like_matrix], axis=1)]
  transfers between devices with their start and end apart: 23 -> 23, of which waited for: 10 -> 6; matrix products, arithmetic and copies ran while one was open for 1% -> 4% of each run, Pallas kernels for 27% -> 28%
where the time goes in v9:
time: 120 us; the launch traced here: 118 us
  starting transfers between devices  51.6 us (43%)
  Pallas kernels  43 us (36%)
  waiting for transfers between devices  12.4 us (10%)
  local copies, waits for them, and re-layouts  9.02 us (8%)
  other arithmetic  1.58 us (1%)
    ppermute x18, starting transfers between devices, swap(): return lax.ppermute(x, 'cuts', [(i, i ^ k) for i in range(peers)])  42.1 us
    pallas_call x1, Pallas kernels, filter_band(): pl.pallas_call(functools.partial(band_kernel, pieces), name='band', grid_...  16.6 us
    ppermute x18, waiting for transfers between devices, swap(): return lax.ppermute(x, 'cuts', [(i, i ^ k) for i in range(peers)])  12 us
    pallas_call x2, Pallas kernels, filter_inner(): pl.pallas_call(functools.partial(inner_kernel, pieces, loaded), name='inn...  10.8 us
    pallas_call x3, Pallas kernels, project(): pl.pallas_call(functools.partial(project_kernel, count), name='project',...  8.96 us
    unnamed x29, local copies, waits for them, and re-layouts  5.97 us
    ppermute x3, starting transfers between devices, fast(): lax.ppermute(own, 'tile', [(i, i ^ k) for i in range(tiles)])  4.6 us
    ppermute x1, starting transfers between devices, fast(): above = lax.ppermute(last, 'tile', [(i, i + 1) for i in range(tiles - 1)])  3.4 us
  transfers between devices with their start and end apart: 23, of which 6 were waited for; matrix products, arithmetic and copies ran while one was open for 4% of the time, Pallas kernels for 28%

profile of v9, /device:TPU:0, one launch (start us, length us, event | category | flops | bytes accessed | tf_op | source)
XLA Modules:
  0.0 118.4 jit_solution(17605350331969218089)
XLA Ops:
  0.6 3.4 %sums.1 = (f32[24,128]{1,0:T(8,128)S(1)}, bf16[17,8,1024]{2,1,0:T(8,128)(2,1)}, bf16[17,8,1024]{2,1,0:T(8,128)(2,1)}) custom-call(bf16[16,128,1024]{2,1,0:T(8,128)(2,1)} %density.5, s32[128,1024]{1,0:T(8,128)} %valid.5), custom_call_target="tpu_custom_call" | custom-call | flops 1 | bytes 1 | tf_op jit(solution)/shard_map/sums/pallas_call | solution.py:154
  4.0 4.0 %collective-permute-start.4 = (f32[24,128]{1,0:T(8,128)S(1)}, f32[24,128]{1,0:T(8,128)S(1)}, u32[]{:S(2)}, u32[]{:S(2)}) collective-permute-start(f32[24,128]{1,0:T(8,128)S(1)} %get-tuple-element.37.after.refs_0_), channel_id=1, source_target_pairs={{0,24},{8,16},{16,8},{24,0},{1,25},{9,17},{17,9},{25,1},{2,26},{10... | collective-permute-start | bytes 36872 | tf_op jit(solution)/shard_map/ppermute | solution.py:525
  8.7 3.1 %ready.1 = (bf16[16,256,512]{2,1,0:T(8,128)(2,1)S(1)}, bf16[2,128,1024]{2,1,0:T(8,128)(2,1)S(1)}, bf16[1,16,32,1024]{3,2,1,0:T(8,128)(2,1)S(1)}, s32[1,32,1024]{2,1,0:T(8,128)S(1)}) custom-call(s32[2]{0:T(128)S(1)} %pad_add_fusion.ids, bf16[16,128,1024]{2,1,0:T(8,128)(2,1)} %density.5, s32[128,1024]{1,0:T(8,128)} %valid.5, bf16[4,16,17]{2,1,0:T(8,128)(2,1)S(1)} %copy-done.9, ...), custom_call_target="tpu_custom_call" | custom-call | flops 1 | bytes 1 | tf_op jit(solution)/shard_map/ready/pallas_call | solution.py:223
  12.3 3.6 %inner.2.refs_5_ = bf16[8,16,1024]{2,1,0:T(8,128)(2,1)} custom-call(s32[2]{0:T(128)S(1)} %pad_add_fusion.ids, bf16[1,16,32,1024]{3,2,1,0:T(8,128)(2,1)S(1)} %get-tuple-element.40.refs_0_, s32[1,32,1024]{2,1,0:T(8,128)S(1)} %get-tuple-element.41.refs_1_, bf16[16,256,512]{2,1,0:T(8,128)(2,1)S(1)} %get-tuple-element.38.refs_4_.refs_2_.col, ...), custom_call_target="tpu_custom_call" | custom-call | flops 1 | bytes 1 | tf_op jit(solution)/shard_map/inner/pallas_call | solution.py:280
  15.9 2.7 %collective-permute-start.5 = (bf16[8,16,1024]{2,1,0:T(8,128)(2,1)}, bf16[8,16,1024]{2,1,0:T(8,128)(2,1)S(1)}, u32[]{:S(2)}, u32[]{:S(2)}) collective-permute-start(bf16[8,16,1024]{2,1,0:T(8,128)(2,1)} %inner.2.refs_5_), channel_id=1, source_target_pairs={{0,4},{1,5},{2,6},{3,7},{4,0},{5,1},{6,2},{7,3},{8,12},{9,13},{10,... | collective-permute-start | bytes 786440 | tf_op jit(solution)/shard_map/ppermute | solution.py:522
  18.6 3.4 %collective-permute-start = (bf16[17,8,1024]{2,1,0:T(8,128)(2,1)S(1)}, bf16[17,8,1024]{2,1,0:T(8,128)(2,1)S(1)}, u32[]{:S(2)}, u32[]{:S(2)}) collective-permute-start(bf16[17,8,1024]{2,1,0:T(8,128)(2,1)S(1)} %copy-done.13), channel_id=1, source_target_pairs={{0,8},{8,16},{16,24},{1,9},{9,17},{17,25},{2,10},{10,18},{18,26},{... | collective-permute-start | bytes 835592 | tf_op jit(solution)/shard_map/ppermute | solution.py:531
  23.6 2.2 %copy-done.1 = bf16[16,256,512]{2,1,0:T(8,128)(2,1)S(1)} copy-done((bf16[16,256,512]{2,1,0:T(8,128)(2,1)S(1)}, bf16[16,256,512]{2,1,0:T(8,128)(2,1)}, u32[]{:S(2)}) %copy-start.1) | copy-done | bytes 4194328
  25.8 7.2 %inner.3 = (bf16[8,16,1024]{2,1,0:T(8,128)(2,1)}, bf16[8,16,1024]{2,1,0:T(8,128)(2,1)}) custom-call(s32[3]{0:T(128)S(1)} %pad_add_fusion.1.ids, bf16[16,128,1024]{2,1,0:T(8,128)(2,1)} %density.5, s32[128,1024]{1,0:T(8,128)} %valid.5, bf16[16,256,512]{2,1,0:T(8,128)(2,1)S(1)} %copy-done.1, bf16[2,128,1024]{2,1,0:T(8,128)(2,1)S(1)} %get-tuple-element.39.refs_3_.row, ...), custom_call_target="tpu_custom_call" | custom-call | flops 1 | bytes 1 | tf_op jit(solution)/shard_map/inner/pallas_call | solution.py:280
  33.8 2.0 %collective-permute-start.10 = (bf16[8,16,1024]{2,1,0:T(8,128)(2,1)}, bf16[8,16,1024]{2,1,0:T(8,128)(2,1)S(1)}, u32[]{:S(2)}, u32[]{:S(2)}) collective-permute-start(bf16[8,16,1024]{2,1,0:T(8,128)(2,1)} %get-tuple-element.42.refs_0_), channel_id=1, source_target_pairs={{0,6},{1,7},{2,4},{3,5},{4,2},{5,3},{6,0},{7,1},{8,14},{9,15},{10,... | collective-permute-start | bytes 786440 | tf_op jit(solution)/shard_map/ppermute | solution.py:522
  36.5 16.6 %band.1 = (bf16[6,16,1024]{2,1,0:T(8,128)(2,1)}, bf16[2,16,1024]{2,1,0:T(8,128)(2,1)}, bf16[8,16,1024]{2,1,0:T(8,128)(2,1)}, bf16[6,16,1024]{2,1,0:T(8,128)(2,1)...) custom-call(s32[9]{0:T(128)S(1)} %concatenate.11.ids, ...), custom_call_target="tpu_custom_call" | custom-call | flops 1 | bytes 1 | tf_op jit(solution)/shard_map/band/pallas_call | solution.py:385
  54.4 2.5 %collective-permute-start.14 = (bf16[6,16,1024]{2,1,0:T(8,128)(2,1)}, bf16[6,16,1024]{2,1,0:T(8,128)(2,1)S(1)}, u32[]{:S(2)}, u32[]{:S(2)}) collective-permute-start(bf16[6,16,1024]{2,1,0:T(8,128)(2,1)} %gate.23), channel_id=1, source_target_pairs={{0,6},{1,7},{2,4},{3,5},{4,2},{5,3},{6,0},{7,1},{8,14},{9,15},{10,... | collective-permute-start | bytes 589832 | tf_op jit(solution)/shard_map/ppermute | solution.py:522
  56.8 3.1 %collective-permute-start.16 = (bf16[6,16,1024]{2,1,0:T(8,128)(2,1)}, bf16[6,16,1024]{2,1,0:T(8,128)(2,1)S(1)}, u32[]{:S(2)}, u32[]{:S(2)}) collective-permute-start(bf16[6,16,1024]{2,1,0:T(8,128)(2,1)} %gate.25), channel_id=1, source_target_pairs={{0,4},{1,5},{2,6},{3,7},{4,0},{5,1},{6,2},{7,3},{8,12},{9,13},{10,... | collective-permute-start | bytes 589832 | tf_op jit(solution)/shard_map/ppermute | solution.py:522
  61.4 7.1 %collective-permute-start.8 = (bf16[8,16,1024]{2,1,0:T(8,128)(2,1)}, bf16[8,16,1024]{2,1,0:T(8,128)(2,1)S(1)}, u32[]{:S(2)}, u32[]{:S(2)}) collective-permute-start(bf16[8,16,1024]{2,1,0:T(8,128)(2,1)} %gate.18), channel_id=1, source_target_pairs={{0,1},{1,0},{2,3},{3,2},{4,5},{5,4},{6,7},{7,6},{8,9},{9,8},{10,11... | collective-permute-start | bytes 786440 | tf_op jit(solution)/shard_map/ppermute | solution.py:522
  68.5 10.7 %collective-permute-start.15 = (bf16[2,16,1024]{2,1,0:T(8,128)(2,1)}, bf16[2,16,1024]{2,1,0:T(8,128)(2,1)S(1)}, u32[]{:S(2)}, u32[]{:S(2)}) collective-permute-start(bf16[2,16,1024]{2,1,0:T(8,128)(2,1)} %gate.24), channel_id=1, source_target_pairs={{0,4},{1,5},{2,6},{3,7},{4,0},{5,1},{6,2},{7,3},{8,12},{9,13},{10,... | collective-permute-start | bytes 196616 | tf_op jit(solution)/shard_map/ppermute | solution.py:522
  79.1 2.9 %collective-permute-done.16.refs_1_.refs_4_ = bf16[6,16,1024]{2,1,0:T(8,128)(2,1)S(1)} collective-permute-done((bf16[6,16,1024]{2,1,0:T(8,128)(2,1)}, bf16[6,16,1024]{2,1,0:T(8,128)(2,1)S(1)}, u32[]{:S(2)}, u32[]{:S(2)}) %collective-permute-start.16) | collective-permute-done | bytes 196640 | tf_op jit(solution)/shard_map/ppermute | solution.py:522
  83.0 6.8 %collective-permute-start.20 = (bf16[6,16,1024]{2,1,0:T(8,128)(2,1)}, bf16[6,16,1024]{2,1,0:T(8,128)(2,1)}, u32[]{:S(2)}, u32[]{:S(2)}) collective-permute-start(bf16[6,16,1024]{2,1,0:T(8,128)(2,1)} %gate.29), channel_id=1, source_target_pairs={{0,5},{1,4},{2,7},{3,6},{4,1},{5,0},{6,3},{7,2},{8,13},{9,12},{10,... | collective-permute-start | bytes 589832 | tf_op jit(solution)/shard_map/ppermute | solution.py:522
  91.9 2.0 %gather_fusion = bf16[8,256,16]{1,2,0:T(8,128)(2,1)} fusion(bf16[256,8,16]{0,2,1:T(8,128)(2,1)} %bitcast.20, s32[1024]{0:T(1024)S(1)} %pad_clamp_fusion), kind=kCustom, calls=%fused_computation | custom fusion | bytes 131104 | tf_op jit(solution)/shard_map/gather | solution.py:560
  95.7 2.2 %collective-permute-start.22 = (bf16[2,16,1024]{2,1,0:T(8,128)(2,1)}, bf16[2,16,1024]{2,1,0:T(8,128)(2,1)}, u32[]{:S(2)}, u32[]{:S(2)}) collective-permute-start(bf16[2,16,1024]{2,1,0:T(8,128)(2,1)} %gate.31), channel_id=1, source_target_pairs={{0,7},{1,6},{2,5},{3,4},{4,3},{5,2},{6,1},{7,0},{8,15},{9,14},{10,... | collective-permute-start | bytes 196616 | tf_op jit(solution)/shard_map/ppermute | solution.py:522
  98.8 3.2 %project.3 = (bf16[128,16384]{1,0:T(8,128)(2,1)}, bf16[128,16384]{1,0:T(8,128)(2,1)}, f32[8,128]{1,0:T(8,128)}) custom-call(s32[1]{0:T(128)} %bitcast.14.place, bf16[256,128]{1,0:T(8,128)(2,1)S(1)} %copy.30.weights, bf16[8,16,1024]{2,1,0:T(8,128)(2,1)S(1)} %copy-done.7, bf16[8,16,1024]{2,1,0:T(8,128)(2,1)S(1)} %collective-permute-done.8.refs_1_, ...), custom_call_target="tpu_custom_call" | custom-call | flops 1 | bytes 1 | tf_op jit(solution)/shard_map/project/pallas_call | solution.py:440
  102.0 6.0 %collective-permute-done.20.refs_1_.refs_5_ = bf16[6,16,1024]{2,1,0:T(8,128)(2,1)} collective-permute-done((bf16[6,16,1024]{2,1,0:T(8,128)(2,1)}, bf16[6,16,1024]{2,1,0:T(8,128)(2,1)}, u32[]{:S(2)}, u32[]{:S(2)}) %collective-permute-start.20) | collective-permute-done | bytes 196640 | tf_op jit(solution)/shard_map/ppermute | solution.py:522
  108.8 2.1 %collective-permute-start.21 = (bf16[2,16,1024]{2,1,0:T(8,128)(2,1)}, bf16[2,16,1024]{2,1,0:T(8,128)(2,1)S(1)}, u32[]{:S(2)}, u32[]{:S(2)}) collective-permute-start(bf16[2,16,1024]{2,1,0:T(8,128)(2,1)} %gate.30), channel_id=1, source_target_pairs={{0,6},{1,7},{2,4},{3,5},{4,2},{5,3},{6,0},{7,1},{8,14},{9,15},{10,... | collective-permute-start | bytes 196616 | tf_op jit(solution)/shard_map/ppermute | solution.py:522
  111.0 3.6 %project.4 = (bf16[128,16384]{1,0:T(8,128)(2,1)}, bf16[128,16384]{1,0:T(8,128)(2,1)}, f32[8,128]{1,0:T(8,128)}) custom-call(s32[1]{0:T(128)} %bitcast.15.place, bf16[256,128]{1,0:T(8,128)(2,1)S(1)} %copy.30.weights, bf16[8,16,1024]{2,1,0:T(8,128)(2,1)S(1)} %copy-done.3, ...), custom_call_target="tpu_custom_call", output_to_operand_aliasing={{0}: (10, {}), {1}: (11, {})} | custom-call | flops 1 | bytes 1 | tf_op jit(solution)/shard_map/project/pallas_call | solution.py:440
  114.6 1.5 %collective-permute-done.18.refs_5_ = bf16[2,16,1024]{2,1,0:T(8,128)(2,1)S(1)} collective-permute-done((bf16[2,16,1024]{2,1,0:T(8,128)(2,1)}, bf16[2,16,1024]{2,1,0:T(8,128)(2,1)S(1)}, u32[]{:S(2)}, u32[]{:S(2)}) %collective-permute-start.18) | collective-permute-done | bytes 65568 | tf_op jit(solution)/shard_map/ppermute | solution.py:522
  116.2 2.2 %project.5 = (bf16[128,16384]{1,0:T(8,128)(2,1)}, bf16[128,16384]{1,0:T(8,128)(2,1)}, f32[8,128]{1,0:T(8,128)}) custom-call(s32[1]{0:T(128)} %bitcast.place, bf16[256,128]{1,0:T(8,128)(2,1)S(1)} %copy.30.weights, bf16[8,16,1024]{2,1,0:T(8,128)(2,1)S(1)} %copy-done.3, ...), custom_call_target="tpu_custom_call", output_to_operand_aliasing={{0}: (10, {}), {1}: (11, {})} | custom-call | flops 1 | bytes 1 | tf_op jit(solution)/shard_map/project/pallas_call | solution.py:440
  (84 shorter events, 13.5 us)
Async XLA Ops:
  4.0 7.8 %collective-permute-start.4 = (f32[24,128]{1,0:T(8,128)S(1)}, f32[24,128]{1,0:T(8,128)S(1)}, u32[]{:S(2)}, u32[]{:S(2)}) collective-permute-start(f32[24,128]{1,0:T(8,128)S(1)} %get-tuple-element.37.after.refs_0_), channel_id=1, source_target_pairs={{0,24},{8,16},{16,8},{24,0},{1,25},{9,17},{17,9},{25,1},{2,26},{10... | collective-permute-start | bytes 36872 | tf_op jit(solution)/shard_map/ppermute | solution.py:525
  8.0 3.9 %collective-permute-start.3 = (f32[24,128]{1,0:T(8,128)S(1)}, f32[24,128]{1,0:T(8,128)S(1)}, u32[]{:S(2)}, u32[]{:S(2)}) collective-permute-start(f32[24,128]{1,0:T(8,128)S(1)} %get-tuple-element.37.after.refs_0_), channel_id=1, source_target_pairs={{0,16},{8,24},{16,0},{24,8},{1,17},{9,25},{17,1},{25,9},{2,18},{10... | collective-permute-start | bytes 36872 | tf_op jit(solution)/shard_map/ppermute | solution.py:525
  8.5 3.7 %collective-permute-start.2 = (f32[24,128]{1,0:T(8,128)S(1)}, f32[24,128]{1,0:T(8,128)S(1)}, u32[]{:S(2)}, u32[]{:S(2)}) collective-permute-start(f32[24,128]{1,0:T(8,128)S(1)} %get-tuple-element.37.after.refs_0_), channel_id=1, source_target_pairs={{0,8},{8,0},{16,24},{24,16},{1,9},{9,1},{17,25},{25,17},{2,10},{10... | collective-permute-start | bytes 36872 | tf_op jit(solution)/shard_map/ppermute | solution.py:525
  15.9 19.8 %collective-permute-start.5 = (bf16[8,16,1024]{2,1,0:T(8,128)(2,1)}, bf16[8,16,1024]{2,1,0:T(8,128)(2,1)S(1)}, u32[]{:S(2)}, u32[]{:S(2)}) collective-permute-start(bf16[8,16,1024]{2,1,0:T(8,128)(2,1)} %inner.2.refs_5_), channel_id=1, source_target_pairs={{0,4},{1,5},{2,6},{3,7},{4,0},{5,1},{6,2},{7,3},{8,12},{9,13},{10,... | collective-permute-start | bytes 786440 | tf_op jit(solution)/shard_map/ppermute | solution.py:522
  18.6 17.1 %collective-permute-start = (bf16[17,8,1024]{2,1,0:T(8,128)(2,1)S(1)}, bf16[17,8,1024]{2,1,0:T(8,128)(2,1)S(1)}, u32[]{:S(2)}, u32[]{:S(2)}) collective-permute-start(bf16[17,8,1024]{2,1,0:T(8,128)(2,1)S(1)} %copy-done.13), channel_id=1, source_target_pairs={{0,8},{8,16},{16,24},{1,9},{9,17},{17,25},{2,10},{10,18},{18,26},{... | collective-permute-start | bytes 835592 | tf_op jit(solution)/shard_map/ppermute | solution.py:531
  22.1 13.7 %collective-permute-start.1 = (bf16[17,8,1024]{2,1,0:T(8,128)(2,1)S(1)}, bf16[17,8,1024]{2,1,0:T(8,128)(2,1)S(1)}, u32[]{:S(2)}, u32[]{:S(2)}) collective-permute-start(bf16[17,8,1024]{2,1,0:T(8,128)(2,1)S(1)} %copy-done.12), channel_id=1, source_target_pairs={{8,0},{16,8},{24,16},{9,1},{17,9},{25,17},{10,2},{18,10},{26,18},{... | collective-permute-start | bytes 835592 | tf_op jit(solution)/shard_map/ppermute | solution.py:532
  33.0 20.8 %collective-permute-start.6 = (bf16[8,16,1024]{2,1,0:T(8,128)(2,1)}, bf16[8,16,1024]{2,1,0:T(8,128)(2,1)S(1)}, u32[]{:S(2)}, u32[]{:S(2)}) collective-permute-start(bf16[8,16,1024]{2,1,0:T(8,128)(2,1)} %get-tuple-element.47), channel_id=1, source_target_pairs={{0,5},{1,4},{2,7},{3,6},{4,1},{5,0},{6,3},{7,2},{8,13},{9,12},{10,... | collective-permute-start | bytes 786440 | tf_op jit(solution)/shard_map/ppermute | solution.py:522
  33.8 23.1 %collective-permute-start.10 = (bf16[8,16,1024]{2,1,0:T(8,128)(2,1)}, bf16[8,16,1024]{2,1,0:T(8,128)(2,1)S(1)}, u32[]{:S(2)}, u32[]{:S(2)}) collective-permute-start(bf16[8,16,1024]{2,1,0:T(8,128)(2,1)} %get-tuple-element.42.refs_0_), channel_id=1, source_target_pairs={{0,6},{1,7},{2,4},{3,5},{4,2},{5,3},{6,0},{7,1},{8,14},{9,15},{10,... | collective-permute-start | bytes 786440 | tf_op jit(solution)/shard_map/ppermute | solution.py:522
  53.8 7.6 %collective-permute-start.7 = (bf16[8,16,1024]{2,1,0:T(8,128)(2,1)}, bf16[8,16,1024]{2,1,0:T(8,128)(2,1)S(1)}, u32[]{:S(2)}, u32[]{:S(2)}) collective-permute-start(bf16[8,16,1024]{2,1,0:T(8,128)(2,1)} %gate.17), channel_id=1, source_target_pairs={{0,3},{1,2},{2,1},{3,0},{4,7},{5,6},{6,5},{7,4},{8,11},{9,10},{10,... | collective-permute-start | bytes 786440 | tf_op jit(solution)/shard_map/ppermute | solution.py:522
  54.4 14.1 %collective-permute-start.14 = (bf16[6,16,1024]{2,1,0:T(8,128)(2,1)}, bf16[6,16,1024]{2,1,0:T(8,128)(2,1)S(1)}, u32[]{:S(2)}, u32[]{:S(2)}) collective-permute-start(bf16[6,16,1024]{2,1,0:T(8,128)(2,1)} %gate.23), channel_id=1, source_target_pairs={{0,6},{1,7},{2,4},{3,5},{4,2},{5,3},{6,0},{7,1},{8,14},{9,15},{10,... | collective-permute-start | bytes 589832 | tf_op jit(solution)/shard_map/ppermute | solution.py:522
  56.8 25.2 %collective-permute-start.16 = (bf16[6,16,1024]{2,1,0:T(8,128)(2,1)}, bf16[6,16,1024]{2,1,0:T(8,128)(2,1)S(1)}, u32[]{:S(2)}, u32[]{:S(2)}) collective-permute-start(bf16[6,16,1024]{2,1,0:T(8,128)(2,1)} %gate.25), channel_id=1, source_target_pairs={{0,4},{1,5},{2,6},{3,7},{4,0},{5,1},{6,2},{7,3},{8,12},{9,13},{10,... | collective-permute-start | bytes 589832 | tf_op jit(solution)/shard_map/ppermute | solution.py:522
  60.0 22.1 %collective-permute-start.19 = (bf16[8,16,1024]{2,1,0:T(8,128)(2,1)}, bf16[8,16,1024]{2,1,0:T(8,128)(2,1)S(1)}, u32[]{:S(2)}, u32[]{:S(2)}) collective-permute-start(bf16[8,16,1024]{2,1,0:T(8,128)(2,1)} %gate.28), channel_id=1, source_target_pairs={{0,7},{1,6},{2,5},{3,4},{4,3},{5,2},{6,1},{7,0},{8,15},{9,14},{10,... | collective-permute-start | bytes 786440 | tf_op jit(solution)/shard_map/ppermute | solution.py:522
  60.6 22.4 %collective-permute-start.11 = (bf16[8,16,1024]{2,1,0:T(8,128)(2,1)}, bf16[8,16,1024]{2,1,0:T(8,128)(2,1)S(1)}, u32[]{:S(2)}, u32[]{:S(2)}) collective-permute-start(bf16[8,16,1024]{2,1,0:T(8,128)(2,1)} %gate.20), channel_id=1, source_target_pairs={{0,2},{1,3},{2,0},{3,1},{4,6},{5,7},{6,4},{7,5},{8,10},{9,11},{10,... | collective-permute-start | bytes 786440 | tf_op jit(solution)/shard_map/ppermute | solution.py:522
  61.4 49.6 %copy-start.3 = (bf16[8,16,1024]{2,1,0:T(8,128)(2,1)S(1)}, bf16[8,16,1024]{2,1,0:T(8,128)(2,1)}, u32[]{:S(2)}) copy-start(bf16[8,16,1024]{2,1,0:T(8,128)(2,1)} %get-tuple-element.43.refs_0_) | copy-start | bytes 786436
  61.4 28.4 %collective-permute-start.8 = (bf16[8,16,1024]{2,1,0:T(8,128)(2,1)}, bf16[8,16,1024]{2,1,0:T(8,128)(2,1)S(1)}, u32[]{:S(2)}, u32[]{:S(2)}) collective-permute-start(bf16[8,16,1024]{2,1,0:T(8,128)(2,1)} %gate.18), channel_id=1, source_target_pairs={{0,1},{1,0},{2,3},{3,2},{4,5},{5,4},{6,7},{7,6},{8,9},{9,8},{10,11... | collective-permute-start | bytes 786440 | tf_op jit(solution)/shard_map/ppermute | solution.py:522
  68.5 21.8 %collective-permute-start.15 = (bf16[2,16,1024]{2,1,0:T(8,128)(2,1)}, bf16[2,16,1024]{2,1,0:T(8,128)(2,1)S(1)}, u32[]{:S(2)}, u32[]{:S(2)}) collective-permute-start(bf16[2,16,1024]{2,1,0:T(8,128)(2,1)} %gate.24), channel_id=1, source_target_pairs={{0,4},{1,5},{2,6},{3,7},{4,0},{5,1},{6,2},{7,3},{8,12},{9,13},{10,... | collective-permute-start | bytes 196616 | tf_op jit(solution)/shard_map/ppermute | solution.py:522
  82.1 26.8 %collective-permute-start.13 = (bf16[8,16,1024]{2,1,0:T(8,128)(2,1)}, bf16[8,16,1024]{2,1,0:T(8,128)(2,1)S(1)}, u32[]{:S(2)}, u32[]{:S(2)}) collective-permute-start(bf16[8,16,1024]{2,1,0:T(8,128)(2,1)} %gate.22), channel_id=1, source_target_pairs={{0,3},{1,2},{2,1},{3,0},{4,7},{5,6},{6,5},{7,4},{8,11},{9,10},{10,... | collective-permute-start | bytes 786440 | tf_op jit(solution)/shard_map/ppermute | solution.py:522
  82.1 13.6 %collective-permute-start.17 = (bf16[6,16,1024]{2,1,0:T(8,128)(2,1)}, bf16[6,16,1024]{2,1,0:T(8,128)(2,1)S(1)}, u32[]{:S(2)}, u32[]{:S(2)}) collective-permute-start(bf16[6,16,1024]{2,1,0:T(8,128)(2,1)} %gate.26), channel_id=1, source_target_pairs={{0,7},{1,6},{2,5},{3,4},{4,3},{5,2},{6,1},{7,0},{8,15},{9,14},{10,... | collective-permute-start | bytes 589832 | tf_op jit(solution)/shard_map/ppermute | solution.py:522
  83.0 25.1 %collective-permute-start.20 = (bf16[6,16,1024]{2,1,0:T(8,128)(2,1)}, bf16[6,16,1024]{2,1,0:T(8,128)(2,1)}, u32[]{:S(2)}, u32[]{:S(2)}) collective-permute-start(bf16[6,16,1024]{2,1,0:T(8,128)(2,1)} %gate.29), channel_id=1, source_target_pairs={{0,5},{1,4},{2,7},{3,6},{4,1},{5,0},{6,3},{7,2},{8,13},{9,12},{10,... | collective-permute-start | bytes 589832 | tf_op jit(solution)/shard_map/ppermute | solution.py:522
  89.7 21.2 %collective-permute-start.12 = (bf16[8,16,1024]{2,1,0:T(8,128)(2,1)}, bf16[8,16,1024]{2,1,0:T(8,128)(2,1)S(1)}, u32[]{:S(2)}, u32[]{:S(2)}) collective-permute-start(bf16[8,16,1024]{2,1,0:T(8,128)(2,1)} %gate.21), channel_id=1, source_target_pairs={{0,2},{1,3},{2,0},{3,1},{4,6},{5,7},{6,4},{7,5},{8,10},{9,11},{10,... | collective-permute-start | bytes 786440 | tf_op jit(solution)/shard_map/ppermute | solution.py:522
  90.3 20.6 %collective-permute-start.9 = (bf16[8,16,1024]{2,1,0:T(8,128)(2,1)}, bf16[8,16,1024]{2,1,0:T(8,128)(2,1)S(1)}, u32[]{:S(2)}, u32[]{:S(2)}) collective-permute-start(bf16[8,16,1024]{2,1,0:T(8,128)(2,1)} %gate.19), channel_id=1, source_target_pairs={{0,1},{1,0},{2,3},{3,2},{4,5},{5,4},{6,7},{7,6},{8,9},{9,8},{10,11... | collective-permute-start | bytes 786440 | tf_op jit(solution)/shard_map/ppermute | solution.py:522
  95.7 18.9 %collective-permute-start.22 = (bf16[2,16,1024]{2,1,0:T(8,128)(2,1)}, bf16[2,16,1024]{2,1,0:T(8,128)(2,1)}, u32[]{:S(2)}, u32[]{:S(2)}) collective-permute-start(bf16[2,16,1024]{2,1,0:T(8,128)(2,1)} %gate.31), channel_id=1, source_target_pairs={{0,7},{1,6},{2,5},{3,4},{4,3},{5,2},{6,1},{7,0},{8,15},{9,14},{10,... | collective-permute-start | bytes 196616 | tf_op jit(solution)/shard_map/ppermute | solution.py:522
  108.0 8.1 %collective-permute-start.18 = (bf16[2,16,1024]{2,1,0:T(8,128)(2,1)}, bf16[2,16,1024]{2,1,0:T(8,128)(2,1)S(1)}, u32[]{:S(2)}, u32[]{:S(2)}) collective-permute-start(bf16[2,16,1024]{2,1,0:T(8,128)(2,1)} %gate.27), channel_id=1, source_target_pairs={{0,5},{1,4},{2,7},{3,6},{4,1},{5,0},{6,3},{7,2},{8,13},{9,12},{10,... | collective-permute-start | bytes 196616 | tf_op jit(solution)/shard_map/ppermute | solution.py:522
  108.8 7.3 %collective-permute-start.21 = (bf16[2,16,1024]{2,1,0:T(8,128)(2,1)}, bf16[2,16,1024]{2,1,0:T(8,128)(2,1)S(1)}, u32[]{:S(2)}, u32[]{:S(2)}) collective-permute-start(bf16[2,16,1024]{2,1,0:T(8,128)(2,1)} %gate.30), channel_id=1, source_target_pairs={{0,6},{1,7},{2,4},{3,5},{4,2},{5,3},{6,0},{7,1},{8,14},{9,15},{10,... | collective-permute-start | bytes 196616 | tf_op jit(solution)/shard_map/ppermute | solution.py:522
  (13 other events, 53.2 us)

commit v10 on v9

--- a/solution.py
+++ b/solution.py
@@ -19,7 +19,7 @@
 HALO = 2 * REACH
 
 
-def params(mib=24):
+def params(mib=44):
     return pltpu.CompilerParams(vmem_limit_bytes=mib * MIB)
 
 
@@ -150,13 +150,13 @@
 
 def masked_sums(density, valid):
     slices, rows, cols = density.shape
-    edge = hbm((slices + 1, REACH, cols), jnp.bfloat16)
+    edge = pltpu.VMEM((slices + 1, REACH, cols), jnp.bfloat16)
     return pl.pallas_call(
         sums_kernel,
         name="sums",
         in_specs=[anywhere()] * 2,
         out_specs=[pl.BlockSpec(memory_space=pltpu.VMEM)] * 3,
-        out_shape=[jax.ShapeDtypeStruct((slices + 8, LANES), jnp.float32), edge, edge],
+        out_shape=[pltpu.VMEM((slices + 8, LANES), jnp.float32), edge, edge],
         scratch_shapes=[
             pltpu.VMEM(density.shape, jnp.bfloat16),
             pltpu.VMEM(valid.shape, jnp.int32),
@@ -168,8 +168,9 @@
 
 
 def mean_kernel(*refs):
-    sums, out = refs[:4], refs[-1]
+    sums, (out, token) = refs[:4], refs[-2:]
     slices = out.shape[0]
+    token[...] = jnp.zeros_like(token)
     total = sums[0][...] + sums[1][...] + sums[2][...] + sums[3][...]
     total = jnp.sum(total, axis=1, keepdims=True)
     out[...] = jnp.broadcast_to(total[:slices] / total[slices : slices + 1], out.shape)
@@ -181,9 +182,9 @@
         mean_kernel,
         name="means",
         in_specs=[vmem] * len(sums) + [anywhere()],
-        out_specs=vmem,
-        out_shape=jax.ShapeDtypeStruct((slices, LANES), jnp.float32),
-        compiler_params=params(1),
+        out_specs=[vmem] * 2,
+        out_shape=[pltpu.VMEM((slices, LANES), jnp.float32), hbm((8, LANES), jnp.float32)],
+        compiler_params=params(),
         cost_estimate=cost(1, 1),
     )(*sums, resident(after))
 
@@ -285,7 +286,7 @@
         + [vmem] * 3
         + [anywhere()] * len(after),
         out_specs=[vmem] * len(shapes),
-        out_shape=[hbm(shape, jnp.bfloat16) for shape in shapes],
+        out_shape=[pltpu.VMEM(shape, jnp.bfloat16) for shape in shapes],
         scratch_shapes=scratch,
         compiler_params=params(),
         cost_estimate=cost(1, 1),
@@ -402,7 +403,7 @@
             ],
         ),
         out_shape=[hbm(shape, jnp.bfloat16) for shape in shapes],
-        compiler_params=params(44),
+        compiler_params=params(),
         cost_estimate=cost(1, 1),
     )(
         jnp.concatenate([ids, jnp.full((1,), rows // block - 1, ids.dtype)]),
@@ -471,7 +472,7 @@
         out_specs=anywhere(),
         out_shape=hbm(x.shape, x.dtype),
         input_output_aliases={0: 0},
-        compiler_params=params(1),
+        compiler_params=params(),
         cost_estimate=cost(flops, 1),
     )(held(x), *earlier)
 
@@ -524,7 +525,7 @@
     own, first, last = masked_sums(density, valid)
     sums = [own] + [lax.ppermute(own, "tile", [(i, i ^ k) for i in range(tiles)]) for k in range(1, tiles)]
     ready = make_ready(me ^ ORDER[0][0], density, valid, row_taps, col_taps, own)
-    mean = means(sums, slices, ready[0])
+    mean, token = means(sums, slices, ready[0])
 
     made, arrived = {}, {}
 
@@ -546,11 +547,11 @@
     for wanted in FIRST:
         got = filter_inner(ids(wanted), [cut for _, cut in wanted], density, valid, ready, mean, *after)
         keep(wanted, got)
-        after = (held(got[0][0]),)
+        after = (resident(got[0][0]),)
     first_piece = ORDER[0][:2]
     send(*first_piece)
     got = filter_band(
-        ids(REST), [cut for _, cut in REST], density, valid, above, below, ready, mean, *after, gate(mean, arrived[first_piece], flops=BEFORE_BAND)
+        ids(REST), [cut for _, cut in REST], density, valid, above, below, ready, mean, *after, held(gate(token, arrived[first_piece], flops=BEFORE_BAND))
     )
     keep(REST, got)
     for piece in (INNER, OUTER):

time: 120 us -> 118 us (0.983)
  starting transfers between devices: 51.6 us -> 55 us
  waiting for transfers between devices: 12.4 us -> 9.96 us
  Pallas kernels: 43 us -> 41.6 us
  local copies, waits for them, and re-layouts: 9.02 us -> 7.73 us
    ppermute x18, starting transfers between devices: 42.1 us -> 45.6 us  [swap(): return lax.ppermute(x, 'cuts', [(i, i ^ k) for i in range(peers)])]
    ppermute x18, waiting for transfers between devices: 12 us -> 9.41 us  [swap(): return lax.ppermute(x, 'cuts', [(i, i ^ k) for i in range(peers)])]
    pallas_call x2, Pallas kernels: 10.8 us -> 9.42 us  [filter_inner(): pl.pallas_call(functools.partial(inner_kernel, pieces, loaded), name='inn...]
    unnamed x29 -> x22, local copies, waits for them, and re-layouts: 5.97 us -> 4.67 us
  transfers between devices with their start and end apart: 23 -> 23, of which waited for: 6 -> 9; matrix products, arithmetic and copies ran while one was open for 4% -> 4% of each run, Pallas kernels for 28% -> 28%
where the time goes in v10:
time: 118 us; the launch traced here: 117 us
  starting transfers between devices  55 us (47%)
  Pallas kernels  41.6 us (35%)
  waiting for transfers between devices  9.96 us (8%)
  local copies, waits for them, and re-layouts  7.73 us (7%)
  other arithmetic  1.58 us (1%)
    ppermute x18, starting transfers between devices, swap(): return lax.ppermute(x, 'cuts', [(i, i ^ k) for i in range(peers)])  45.6 us
    pallas_call x1, Pallas kernels, filter_band(): pl.pallas_call(functools.partial(band_kernel, pieces), name='band', grid_...  16.6 us
    pallas_call x2, Pallas kernels, filter_inner(): pl.pallas_call(functools.partial(inner_kernel, pieces, loaded), name='inn...  9.42 us
    ppermute x18, waiting for transfers between devices, swap(): return lax.ppermute(x, 'cuts', [(i, i ^ k) for i in range(peers)])  9.41 us
    pallas_call x3, Pallas kernels, project(): pl.pallas_call(functools.partial(project_kernel, count), name='project',...  8.95 us
    unnamed x22, local copies, waits for them, and re-layouts  4.67 us
    ppermute x3, starting transfers between devices, fast(): lax.ppermute(own, 'tile', [(i, i ^ k) for i in range(tiles)])  4.6 us
    ppermute x1, starting transfers between devices, fast(): above = lax.ppermute(last, 'tile', [(i, i + 1) for i in range(tiles - 1)])  3.4 us
  transfers between devices with their start and end apart: 23, of which 9 were waited for; matrix products, arithmetic and copies ran while one was open for 4% of the time, Pallas kernels for 28%

profile of v10, /device:TPU:0, one launch (start us, length us, event | category | flops | bytes accessed | tf_op | source)
XLA Modules:
  0.0 116.7 jit_solution(11787283511504213453)
XLA Ops:
  0.6 2.6 %sums.1 = (f32[24,128]{1,0:T(8,128)S(1)}, bf16[17,8,1024]{2,1,0:T(8,128)(2,1)S(1)}, bf16[17,8,1024]{2,1,0:T(8,128)(2,1)S(1)}) custom-call(bf16[16,128,1024]{2,1,0:T(8,128)(2,1)} %density.5, s32[128,1024]{1,0:T(8,128)} %valid.5), custom_call_target="tpu_custom_call" | custom-call | flops 1 | bytes 1 | tf_op jit(solution)/shard_map/sums/pallas_call | solution.py:154
  3.3 4.0 %collective-permute-start.4 = (f32[24,128]{1,0:T(8,128)S(1)}, f32[24,128]{1,0:T(8,128)S(1)}, u32[]{:S(2)}, u32[]{:S(2)}) collective-permute-start(f32[24,128]{1,0:T(8,128)S(1)} %get-tuple-element.39.after.refs_0_), channel_id=1, source_target_pairs={{0,24},{8,16},{16,8},{24,0},{1,25},{9,17},{17,9},{25,1},{2,26},{10... | collective-permute-start | bytes 36872 | tf_op jit(solution)/shard_map/ppermute | solution.py:526
  7.9 3.1 %ready.1 = (bf16[16,256,512]{2,1,0:T(8,128)(2,1)S(1)}, bf16[2,128,1024]{2,1,0:T(8,128)(2,1)S(1)}, bf16[1,16,32,1024]{3,2,1,0:T(8,128)(2,1)S(1)}, s32[1,32,1024]{2,1,0:T(8,128)S(1)}) custom-call(s32[2]{0:T(128)S(1)} %pad_add_fusion.ids, bf16[16,128,1024]{2,1,0:T(8,128)(2,1)} %density.5, s32[128,1024]{1,0:T(8,128)} %valid.5, bf16[4,16,17]{2,1,0:T(8,128)(2,1)S(1)} %copy-done.8, ...), custom_call_target="tpu_custom_call" | custom-call | flops 1 | bytes 1 | tf_op jit(solution)/shard_map/ready/pallas_call | solution.py:224
  12.3 2.9 %inner.2.refs_5_ = bf16[8,16,1024]{2,1,0:T(8,128)(2,1)S(1)} custom-call(s32[2]{0:T(128)S(1)} %pad_add_fusion.ids, bf16[1,16,32,1024]{3,2,1,0:T(8,128)(2,1)S(1)} %get-tuple-element.43.refs_0_, s32[1,32,1024]{2,1,0:T(8,128)S(1)} %get-tuple-element.44.refs_1_, bf16[16,256,512]{2,1,0:T(8,128)(2,1)S(1)} %get-tuple-element.40.refs_4_.refs_2_.col, ...), custom_call_target="tpu_custom_call" | custom-call | flops 1 | bytes 1 | tf_op jit(solution)/shard_map/inner/pallas_call | solution.py:281
  15.2 2.5 %collective-permute-start.5 = (bf16[8,16,1024]{2,1,0:T(8,128)(2,1)S(1)}, bf16[8,16,1024]{2,1,0:T(8,128)(2,1)S(1)}, u32[]{:S(2)}, u32[]{:S(2)}) collective-permute-start(bf16[8,16,1024]{2,1,0:T(8,128)(2,1)S(1)} %inner.2.refs_5_), channel_id=1, source_target_pairs={{0,4},{1,5},{2,6},{3,7},{4,0},{5,1},{6,2},{7,3},{8,12},{9,13},{10,... | collective-permute-start | bytes 786440 | tf_op jit(solution)/shard_map/ppermute | solution.py:523
  17.8 3.4 %collective-permute-start = (bf16[17,8,1024]{2,1,0:T(8,128)(2,1)S(1)}, bf16[17,8,1024]{2,1,0:T(8,128)(2,1)S(1)}, u32[]{:S(2)}, u32[]{:S(2)}) collective-permute-start(bf16[17,8,1024]{2,1,0:T(8,128)(2,1)S(1)} %get-tuple-element.37), channel_id=1, source_target_pairs={{0,8},{8,16},{16,24},{1,9},{9,17},{17,25},{2,10},{10,18},{18,26},{... | collective-permute-start | bytes 835592 | tf_op jit(solution)/shard_map/ppermute | solution.py:532
  22.7 2.2 %copy-done.1 = bf16[16,256,512]{2,1,0:T(8,128)(2,1)S(1)} copy-done((bf16[16,256,512]{2,1,0:T(8,128)(2,1)S(1)}, bf16[16,256,512]{2,1,0:T(8,128)(2,1)}, u32[]{:S(2)}) %copy-start.1) | copy-done | bytes 4194328
  24.9 6.5 %inner.3 = (bf16[8,16,1024]{2,1,0:T(8,128)(2,1)S(1)}, bf16[8,16,1024]{2,1,0:T(8,128)(2,1)S(1)}) custom-call(s32[3]{0:T(128)S(1)} %pad_add_fusion.1.ids, bf16[16,128,1024]{2,1,0:T(8,128)(2,1)} %density.5, s32[128,1024]{1,0:T(8,128)} %valid.5, bf16[16,256,512]{2,1,0:T(8,128)(2,1)S(1)} %copy-done.1, bf16[2,128,1024]{2,1,0:T(8,128)(2,1)S(1)} %get-tuple-element.41.refs_3_.row, ...), custom_call_target="tpu_custom_call" | custom-call | flops 1 | bytes 1 | tf_op jit(solution)/shard_map/inner/pallas_call | solution.py:281
  31.6 2.0 %collective-permute-start.10 = (bf16[8,16,1024]{2,1,0:T(8,128)(2,1)S(1)}, bf16[8,16,1024]{2,1,0:T(8,128)(2,1)S(1)}, u32[]{:S(2)}, u32[]{:S(2)}) collective-permute-start(bf16[8,16,1024]{2,1,0:T(8,128)(2,1)S(1)} %get-tuple-element.45.refs_0_), channel_id=1, source_target_pairs={{0,6},{1,7},{2,4},{3,5},{4,2},{5,3},{6,0},{7,1},{8,14},{9,15},{10,... | collective-permute-start | bytes 786440 | tf_op jit(solution)/shard_map/ppermute | solution.py:523
  33.8 16.6 %band.1 = (bf16[6,16,1024]{2,1,0:T(8,128)(2,1)}, bf16[2,16,1024]{2,1,0:T(8,128)(2,1)}, bf16[8,16,1024]{2,1,0:T(8,128)(2,1)}, bf16[6,16,1024]{2,1,0:T(8,128)(2,1)...) custom-call(s32[9]{0:T(128)S(1)} %concatenate.11.ids, ...), custom_call_target="tpu_custom_call" | custom-call | flops 1 | bytes 1 | tf_op jit(solution)/shard_map/band/pallas_call | solution.py:386
  50.5 1.5 %collective-permute-done.6.refs_1_.refs_5_ = bf16[8,16,1024]{2,1,0:T(8,128)(2,1)S(1)} collective-permute-done((bf16[8,16,1024]{2,1,0:T(8,128)(2,1)S(1)}, bf16[8,16,1024]{2,1,0:T(8,128)(2,1)S(1)}, u32[]{:S(2)}, u32[]{:S(2)}) %collective-permute-start.6) | collective-permute-done | bytes 262176 | tf_op jit(solution)/shard_map/ppermute | solution.py:523
  52.1 2.5 %collective-permute-start.14 = (bf16[6,16,1024]{2,1,0:T(8,128)(2,1)}, bf16[6,16,1024]{2,1,0:T(8,128)(2,1)S(1)}, u32[]{:S(2)}, u32[]{:S(2)}) collective-permute-start(bf16[6,16,1024]{2,1,0:T(8,128)(2,1)} %gate.23), channel_id=1, source_target_pairs={{0,6},{1,7},{2,4},{3,5},{4,2},{5,3},{6,0},{7,1},{8,14},{9,15},{10,... | collective-permute-start | bytes 589832 | tf_op jit(solution)/shard_map/ppermute | solution.py:523
  54.6 3.6 %collective-permute-start.16 = (bf16[6,16,1024]{2,1,0:T(8,128)(2,1)}, bf16[6,16,1024]{2,1,0:T(8,128)(2,1)S(1)}, u32[]{:S(2)}, u32[]{:S(2)}) collective-permute-start(bf16[6,16,1024]{2,1,0:T(8,128)(2,1)} %gate.25), channel_id=1, source_target_pairs={{0,4},{1,5},{2,6},{3,7},{4,0},{5,1},{6,2},{7,3},{8,12},{9,13},{10,... | collective-permute-start | bytes 589832 | tf_op jit(solution)/shard_map/ppermute | solution.py:523
  58.8 2.5 %collective-permute-done.7.refs_1_.refs_3_ = bf16[8,16,1024]{2,1,0:T(8,128)(2,1)S(1)} collective-permute-done((bf16[8,16,1024]{2,1,0:T(8,128)(2,1)}, bf16[8,16,1024]{2,1,0:T(8,128)(2,1)S(1)}, u32[]{:S(2)}, u32[]{:S(2)}) %collective-permute-start.7) | collective-permute-done | bytes 262176 | tf_op jit(solution)/shard_map/ppermute | solution.py:523
  61.4 4.3 %collective-permute-start.8 = (bf16[8,16,1024]{2,1,0:T(8,128)(2,1)}, bf16[8,16,1024]{2,1,0:T(8,128)(2,1)S(1)}, u32[]{:S(2)}, u32[]{:S(2)}) collective-permute-start(bf16[8,16,1024]{2,1,0:T(8,128)(2,1)} %gate.18), channel_id=1, source_target_pairs={{0,1},{1,0},{2,3},{3,2},{4,5},{5,4},{6,7},{7,6},{8,9},{9,8},{10,11... | collective-permute-start | bytes 786440 | tf_op jit(solution)/shard_map/ppermute | solution.py:523
  66.2 10.6 %collective-permute-start.15 = (bf16[2,16,1024]{2,1,0:T(8,128)(2,1)}, bf16[2,16,1024]{2,1,0:T(8,128)(2,1)S(1)}, u32[]{:S(2)}, u32[]{:S(2)}) collective-permute-start(bf16[2,16,1024]{2,1,0:T(8,128)(2,1)} %gate.24), channel_id=1, source_target_pairs={{0,4},{1,5},{2,6},{3,7},{4,0},{5,1},{6,2},{7,3},{8,12},{9,13},{10,... | collective-permute-start | bytes 196616 | tf_op jit(solution)/shard_map/ppermute | solution.py:523
  76.8 2.8 %collective-permute-done.16.refs_1_.refs_4_ = bf16[6,16,1024]{2,1,0:T(8,128)(2,1)S(1)} collective-permute-done((bf16[6,16,1024]{2,1,0:T(8,128)(2,1)}, bf16[6,16,1024]{2,1,0:T(8,128)(2,1)S(1)}, u32[]{:S(2)}, u32[]{:S(2)}) %collective-permute-start.16) | collective-permute-done | bytes 196640 | tf_op jit(solution)/shard_map/ppermute | solution.py:523
  81.0 6.6 %collective-permute-start.20 = (bf16[6,16,1024]{2,1,0:T(8,128)(2,1)}, bf16[6,16,1024]{2,1,0:T(8,128)(2,1)}, u32[]{:S(2)}, u32[]{:S(2)}) collective-permute-start(bf16[6,16,1024]{2,1,0:T(8,128)(2,1)} %gate.29), channel_id=1, source_target_pairs={{0,5},{1,4},{2,7},{3,6},{4,1},{5,0},{6,3},{7,2},{8,13},{9,12},{10,... | collective-permute-start | bytes 589832 | tf_op jit(solution)/shard_map/ppermute | solution.py:523
  89.9 2.0 %gather_fusion = bf16[8,256,16]{1,2,0:T(8,128)(2,1)} fusion(bf16[256,8,16]{0,2,1:T(8,128)(2,1)} %bitcast.20, s32[1024]{0:T(1024)S(1)} %pad_clamp_fusion), kind=kCustom, calls=%fused_computation | custom fusion | bytes 131104 | tf_op jit(solution)/shard_map/gather | solution.py:561
  93.7 9.8 %collective-permute-start.22 = (bf16[2,16,1024]{2,1,0:T(8,128)(2,1)}, bf16[2,16,1024]{2,1,0:T(8,128)(2,1)}, u32[]{:S(2)}, u32[]{:S(2)}) collective-permute-start(bf16[2,16,1024]{2,1,0:T(8,128)(2,1)} %gate.31), channel_id=1, source_target_pairs={{0,7},{1,6},{2,5},{3,4},{4,3},{5,2},{6,1},{7,0},{8,15},{9,14},{10,... | collective-permute-start | bytes 196616 | tf_op jit(solution)/shard_map/ppermute | solution.py:523
  104.4 3.2 %project.3 = (bf16[128,16384]{1,0:T(8,128)(2,1)}, bf16[128,16384]{1,0:T(8,128)(2,1)}, f32[8,128]{1,0:T(8,128)}) custom-call(s32[1]{0:T(128)} %bitcast.14.place, bf16[256,128]{1,0:T(8,128)(2,1)S(1)} %copy.30.weights, bf16[8,16,1024]{2,1,0:T(8,128)(2,1)S(1)} %copy-done.7, bf16[8,16,1024]{2,1,0:T(8,128)(2,1)S(1)} %collective-permute-done.8.refs_1_, ...), custom_call_target="tpu_custom_call" | custom-call | flops 1 | bytes 1 | tf_op jit(solution)/shard_map/project/pallas_call | solution.py:441
  109.1 3.6 %project.4 = (bf16[128,16384]{1,0:T(8,128)(2,1)}, bf16[128,16384]{1,0:T(8,128)(2,1)}, f32[8,128]{1,0:T(8,128)}) custom-call(s32[1]{0:T(128)} %bitcast.15.place, bf16[256,128]{1,0:T(8,128)(2,1)S(1)} %copy.30.weights, bf16[8,16,1024]{2,1,0:T(8,128)(2,1)S(1)} %copy-done.3, ...), custom_call_target="tpu_custom_call", output_to_operand_aliasing={{0}: (10, {}), {1}: (11, {})} | custom-call | flops 1 | bytes 1 | tf_op jit(solution)/shard_map/project/pallas_call | solution.py:441
  112.9 1.7 %collective-permute-done.21.refs_6_ = bf16[2,16,1024]{2,1,0:T(8,128)(2,1)S(1)} collective-permute-done((bf16[2,16,1024]{2,1,0:T(8,128)(2,1)}, bf16[2,16,1024]{2,1,0:T(8,128)(2,1)S(1)}, u32[]{:S(2)}, u32[]{:S(2)}) %collective-permute-start.21) | collective-permute-done | bytes 65568 | tf_op jit(solution)/shard_map/ppermute | solution.py:523
  114.5 2.2 %project.5 = (bf16[128,16384]{1,0:T(8,128)(2,1)}, bf16[128,16384]{1,0:T(8,128)(2,1)}, f32[8,128]{1,0:T(8,128)}) custom-call(s32[1]{0:T(128)} %bitcast.place, bf16[256,128]{1,0:T(8,128)(2,1)S(1)} %copy.30.weights, bf16[8,16,1024]{2,1,0:T(8,128)(2,1)S(1)} %copy-done.3, ...), custom_call_target="tpu_custom_call", output_to_operand_aliasing={{0}: (10, {}), {1}: (11, {})} | custom-call | flops 1 | bytes 1 | tf_op jit(solution)/shard_map/project/pallas_call | solution.py:441
  (77 shorter events, 13.2 us)
Async XLA Ops:
  3.3 7.8 %collective-permute-start.4 = (f32[24,128]{1,0:T(8,128)S(1)}, f32[24,128]{1,0:T(8,128)S(1)}, u32[]{:S(2)}, u32[]{:S(2)}) collective-permute-start(f32[24,128]{1,0:T(8,128)S(1)} %get-tuple-element.39.after.refs_0_), channel_id=1, source_target_pairs={{0,24},{8,16},{16,8},{24,0},{1,25},{9,17},{17,9},{25,1},{2,26},{10... | collective-permute-start | bytes 36872 | tf_op jit(solution)/shard_map/ppermute | solution.py:526
  7.2 3.9 %collective-permute-start.3 = (f32[24,128]{1,0:T(8,128)S(1)}, f32[24,128]{1,0:T(8,128)S(1)}, u32[]{:S(2)}, u32[]{:S(2)}) collective-permute-start(f32[24,128]{1,0:T(8,128)S(1)} %get-tuple-element.39.after.refs_0_), channel_id=1, source_target_pairs={{0,16},{8,24},{16,0},{24,8},{1,17},{9,25},{17,1},{25,9},{2,18},{10... | collective-permute-start | bytes 36872 | tf_op jit(solution)/shard_map/ppermute | solution.py:526
  7.7 3.7 %collective-permute-start.2 = (f32[24,128]{1,0:T(8,128)S(1)}, f32[24,128]{1,0:T(8,128)S(1)}, u32[]{:S(2)}, u32[]{:S(2)}) collective-permute-start(f32[24,128]{1,0:T(8,128)S(1)} %get-tuple-element.39.after.refs_0_), channel_id=1, source_target_pairs={{0,8},{8,0},{16,24},{24,16},{1,9},{9,1},{17,25},{25,17},{2,10},{10... | collective-permute-start | bytes 36872 | tf_op jit(solution)/shard_map/ppermute | solution.py:526
  15.2 18.4 %collective-permute-start.5 = (bf16[8,16,1024]{2,1,0:T(8,128)(2,1)S(1)}, bf16[8,16,1024]{2,1,0:T(8,128)(2,1)S(1)}, u32[]{:S(2)}, u32[]{:S(2)}) collective-permute-start(bf16[8,16,1024]{2,1,0:T(8,128)(2,1)S(1)} %inner.2.refs_5_), channel_id=1, source_target_pairs={{0,4},{1,5},{2,6},{3,7},{4,0},{5,1},{6,2},{7,3},{8,12},{9,13},{10,... | collective-permute-start | bytes 786440 | tf_op jit(solution)/shard_map/ppermute | solution.py:523
  17.8 15.9 %collective-permute-start = (bf16[17,8,1024]{2,1,0:T(8,128)(2,1)S(1)}, bf16[17,8,1024]{2,1,0:T(8,128)(2,1)S(1)}, u32[]{:S(2)}, u32[]{:S(2)}) collective-permute-start(bf16[17,8,1024]{2,1,0:T(8,128)(2,1)S(1)} %get-tuple-element.37), channel_id=1, source_target_pairs={{0,8},{8,16},{16,24},{1,9},{9,17},{17,25},{2,10},{10,18},{18,26},{... | collective-permute-start | bytes 835592 | tf_op jit(solution)/shard_map/ppermute | solution.py:532
  21.2 12.7 %collective-permute-start.1 = (bf16[17,8,1024]{2,1,0:T(8,128)(2,1)S(1)}, bf16[17,8,1024]{2,1,0:T(8,128)(2,1)S(1)}, u32[]{:S(2)}, u32[]{:S(2)}) collective-permute-start(bf16[17,8,1024]{2,1,0:T(8,128)(2,1)S(1)} %get-tuple-element.38), channel_id=1, source_target_pairs={{8,0},{16,8},{24,16},{9,1},{17,9},{25,17},{10,2},{18,10},{26,18},{... | collective-permute-start | bytes 835592 | tf_op jit(solution)/shard_map/ppermute | solution.py:533
  31.4 20.6 %collective-permute-start.6 = (bf16[8,16,1024]{2,1,0:T(8,128)(2,1)S(1)}, bf16[8,16,1024]{2,1,0:T(8,128)(2,1)S(1)}, u32[]{:S(2)}, u32[]{:S(2)}) collective-permute-start(bf16[8,16,1024]{2,1,0:T(8,128)(2,1)S(1)} %get-tuple-element.51), channel_id=1, source_target_pairs={{0,5},{1,4},{2,7},{3,6},{4,1},{5,0},{6,3},{7,2},{8,13},{9,12},{10,... | collective-permute-start | bytes 786440 | tf_op jit(solution)/shard_map/ppermute | solution.py:523
  31.6 23.0 %collective-permute-start.10 = (bf16[8,16,1024]{2,1,0:T(8,128)(2,1)S(1)}, bf16[8,16,1024]{2,1,0:T(8,128)(2,1)S(1)}, u32[]{:S(2)}, u32[]{:S(2)}) collective-permute-start(bf16[8,16,1024]{2,1,0:T(8,128)(2,1)S(1)} %get-tuple-element.45.refs_0_), channel_id=1, source_target_pairs={{0,6},{1,7},{2,4},{3,5},{4,2},{5,3},{6,0},{7,1},{8,14},{9,15},{10,... | collective-permute-start | bytes 786440 | tf_op jit(solution)/shard_map/ppermute | solution.py:523
  52.0 9.3 %collective-permute-start.7 = (bf16[8,16,1024]{2,1,0:T(8,128)(2,1)}, bf16[8,16,1024]{2,1,0:T(8,128)(2,1)S(1)}, u32[]{:S(2)}, u32[]{:S(2)}) collective-permute-start(bf16[8,16,1024]{2,1,0:T(8,128)(2,1)} %gate.17), channel_id=1, source_target_pairs={{0,3},{1,2},{2,1},{3,0},{4,7},{5,6},{6,5},{7,4},{8,11},{9,10},{10,... | collective-permute-start | bytes 786440 | tf_op jit(solution)/shard_map/ppermute | solution.py:523
  52.1 14.1 %collective-permute-start.14 = (bf16[6,16,1024]{2,1,0:T(8,128)(2,1)}, bf16[6,16,1024]{2,1,0:T(8,128)(2,1)S(1)}, u32[]{:S(2)}, u32[]{:S(2)}) collective-permute-start(bf16[6,16,1024]{2,1,0:T(8,128)(2,1)} %gate.23), channel_id=1, source_target_pairs={{0,6},{1,7},{2,4},{3,5},{4,2},{5,3},{6,0},{7,1},{8,14},{9,15},{10,... | collective-permute-start | bytes 589832 | tf_op jit(solution)/shard_map/ppermute | solution.py:523
  54.6 25.0 %collective-permute-start.16 = (bf16[6,16,1024]{2,1,0:T(8,128)(2,1)}, bf16[6,16,1024]{2,1,0:T(8,128)(2,1)S(1)}, u32[]{:S(2)}, u32[]{:S(2)}) collective-permute-start(bf16[6,16,1024]{2,1,0:T(8,128)(2,1)} %gate.25), channel_id=1, source_target_pairs={{0,4},{1,5},{2,6},{3,7},{4,0},{5,1},{6,2},{7,3},{8,12},{9,13},{10,... | collective-permute-start | bytes 589832 | tf_op jit(solution)/shard_map/ppermute | solution.py:523
  58.2 21.4 %collective-permute-start.19 = (bf16[8,16,1024]{2,1,0:T(8,128)(2,1)}, bf16[8,16,1024]{2,1,0:T(8,128)(2,1)S(1)}, u32[]{:S(2)}, u32[]{:S(2)}) collective-permute-start(bf16[8,16,1024]{2,1,0:T(8,128)(2,1)} %gate.28), channel_id=1, source_target_pairs={{0,7},{1,6},{2,5},{3,4},{4,3},{5,2},{6,1},{7,0},{8,15},{9,14},{10,... | collective-permute-start | bytes 786440 | tf_op jit(solution)/shard_map/ppermute | solution.py:523
  58.8 22.2 %collective-permute-start.11 = (bf16[8,16,1024]{2,1,0:T(8,128)(2,1)}, bf16[8,16,1024]{2,1,0:T(8,128)(2,1)S(1)}, u32[]{:S(2)}, u32[]{:S(2)}) collective-permute-start(bf16[8,16,1024]{2,1,0:T(8,128)(2,1)} %gate.20), channel_id=1, source_target_pairs={{0,2},{1,3},{2,0},{3,1},{4,6},{5,7},{6,4},{7,5},{8,10},{9,11},{10,... | collective-permute-start | bytes 786440 | tf_op jit(solution)/shard_map/ppermute | solution.py:523
  61.3 47.7 %copy-start.3 = (bf16[8,16,1024]{2,1,0:T(8,128)(2,1)S(1)}, bf16[8,16,1024]{2,1,0:T(8,128)(2,1)}, u32[]{:S(2)}) copy-start(bf16[8,16,1024]{2,1,0:T(8,128)(2,1)} %get-tuple-element.47.refs_0_) | copy-start | bytes 786436
  61.4 26.2 %collective-permute-start.8 = (bf16[8,16,1024]{2,1,0:T(8,128)(2,1)}, bf16[8,16,1024]{2,1,0:T(8,128)(2,1)S(1)}, u32[]{:S(2)}, u32[]{:S(2)}) collective-permute-start(bf16[8,16,1024]{2,1,0:T(8,128)(2,1)} %gate.18), channel_id=1, source_target_pairs={{0,1},{1,0},{2,3},{3,2},{4,5},{5,4},{6,7},{7,6},{8,9},{9,8},{10,11... | collective-permute-start | bytes 786440 | tf_op jit(solution)/shard_map/ppermute | solution.py:523
  66.2 22.1 %collective-permute-start.15 = (bf16[2,16,1024]{2,1,0:T(8,128)(2,1)}, bf16[2,16,1024]{2,1,0:T(8,128)(2,1)S(1)}, u32[]{:S(2)}, u32[]{:S(2)}) collective-permute-start(bf16[2,16,1024]{2,1,0:T(8,128)(2,1)} %gate.24), channel_id=1, source_target_pairs={{0,4},{1,5},{2,6},{3,7},{4,0},{5,1},{6,2},{7,3},{8,12},{9,13},{10,... | collective-permute-start | bytes 196616 | tf_op jit(solution)/shard_map/ppermute | solution.py:523
  79.6 28.7 %collective-permute-start.13 = (bf16[8,16,1024]{2,1,0:T(8,128)(2,1)}, bf16[8,16,1024]{2,1,0:T(8,128)(2,1)S(1)}, u32[]{:S(2)}, u32[]{:S(2)}) collective-permute-start(bf16[8,16,1024]{2,1,0:T(8,128)(2,1)} %gate.22), channel_id=1, source_target_pairs={{0,3},{1,2},{2,1},{3,0},{4,7},{5,6},{6,5},{7,4},{8,11},{9,10},{10,... | collective-permute-start | bytes 786440 | tf_op jit(solution)/shard_map/ppermute | solution.py:523
  79.6 14.1 %collective-permute-start.17 = (bf16[6,16,1024]{2,1,0:T(8,128)(2,1)}, bf16[6,16,1024]{2,1,0:T(8,128)(2,1)S(1)}, u32[]{:S(2)}, u32[]{:S(2)}) collective-permute-start(bf16[6,16,1024]{2,1,0:T(8,128)(2,1)} %gate.26), channel_id=1, source_target_pairs={{0,7},{1,6},{2,5},{3,4},{4,3},{5,2},{6,1},{7,0},{8,15},{9,14},{10,... | collective-permute-start | bytes 589832 | tf_op jit(solution)/shard_map/ppermute | solution.py:523
  81.0 26.5 %collective-permute-start.20 = (bf16[6,16,1024]{2,1,0:T(8,128)(2,1)}, bf16[6,16,1024]{2,1,0:T(8,128)(2,1)}, u32[]{:S(2)}, u32[]{:S(2)}) collective-permute-start(bf16[6,16,1024]{2,1,0:T(8,128)(2,1)} %gate.29), channel_id=1, source_target_pairs={{0,5},{1,4},{2,7},{3,6},{4,1},{5,0},{6,3},{7,2},{8,13},{9,12},{10,... | collective-permute-start | bytes 589832 | tf_op jit(solution)/shard_map/ppermute | solution.py:523
  87.6 21.4 %collective-permute-start.12 = (bf16[8,16,1024]{2,1,0:T(8,128)(2,1)}, bf16[8,16,1024]{2,1,0:T(8,128)(2,1)S(1)}, u32[]{:S(2)}, u32[]{:S(2)}) collective-permute-start(bf16[8,16,1024]{2,1,0:T(8,128)(2,1)} %gate.21), channel_id=1, source_target_pairs={{0,2},{1,3},{2,0},{3,1},{4,6},{5,7},{6,4},{7,5},{8,10},{9,11},{10,... | collective-permute-start | bytes 786440 | tf_op jit(solution)/shard_map/ppermute | solution.py:523
  88.3 20.8 %collective-permute-start.9 = (bf16[8,16,1024]{2,1,0:T(8,128)(2,1)}, bf16[8,16,1024]{2,1,0:T(8,128)(2,1)S(1)}, u32[]{:S(2)}, u32[]{:S(2)}) collective-permute-start(bf16[8,16,1024]{2,1,0:T(8,128)(2,1)} %gate.19), channel_id=1, source_target_pairs={{0,1},{1,0},{2,3},{3,2},{4,5},{5,4},{6,7},{7,6},{8,9},{9,8},{10,11... | collective-permute-start | bytes 786440 | tf_op jit(solution)/shard_map/ppermute | solution.py:523
  93.7 19.0 %collective-permute-start.22 = (bf16[2,16,1024]{2,1,0:T(8,128)(2,1)}, bf16[2,16,1024]{2,1,0:T(8,128)(2,1)}, u32[]{:S(2)}, u32[]{:S(2)}) collective-permute-start(bf16[2,16,1024]{2,1,0:T(8,128)(2,1)} %gate.31), channel_id=1, source_target_pairs={{0,7},{1,6},{2,5},{3,4},{4,3},{5,2},{6,1},{7,0},{8,15},{9,14},{10,... | collective-permute-start | bytes 196616 | tf_op jit(solution)/shard_map/ppermute | solution.py:523
  107.6 5.3 %collective-permute-start.18 = (bf16[2,16,1024]{2,1,0:T(8,128)(2,1)}, bf16[2,16,1024]{2,1,0:T(8,128)(2,1)S(1)}, u32[]{:S(2)}, u32[]{:S(2)}) collective-permute-start(bf16[2,16,1024]{2,1,0:T(8,128)(2,1)} %gate.27), channel_id=1, source_target_pairs={{0,5},{1,4},{2,7},{3,6},{4,1},{5,0},{6,3},{7,2},{8,13},{9,12},{10,... | collective-permute-start | bytes 196616 | tf_op jit(solution)/shard_map/ppermute | solution.py:523
  108.3 6.3 %collective-permute-start.21 = (bf16[2,16,1024]{2,1,0:T(8,128)(2,1)}, bf16[2,16,1024]{2,1,0:T(8,128)(2,1)S(1)}, u32[]{:S(2)}, u32[]{:S(2)}) collective-permute-start(bf16[2,16,1024]{2,1,0:T(8,128)(2,1)} %gate.30), channel_id=1, source_target_pairs={{0,6},{1,7},{2,4},{3,5},{4,2},{5,3},{6,0},{7,1},{8,14},{9,15},{10,... | collective-permute-start | bytes 196616 | tf_op jit(solution)/shard_map/ppermute | solution.py:523
  (10 other events, 34.7 us)

commit v11 on v10

--- a/solution.py
+++ b/solution.py
@@ -19,7 +19,7 @@
 HALO = 2 * REACH
 
 
-def params(mib=44):
+def params(mib=33):
     return pltpu.CompilerParams(vmem_limit_bytes=mib * MIB)
 
 
@@ -183,7 +183,7 @@
         name="means",
         in_specs=[vmem] * len(sums) + [anywhere()],
         out_specs=[vmem] * 2,
-        out_shape=[pltpu.VMEM((slices, LANES), jnp.float32), hbm((8, LANES), jnp.float32)],
+        out_shape=[pltpu.VMEM((slices, LANES), jnp.float32), pltpu.VMEM((8, LANES), jnp.float32)],
         compiler_params=params(),
         cost_estimate=cost(1, 1),
     )(*sums, resident(after))
@@ -464,17 +464,17 @@
     pass
 
 
-def gate(x, *earlier, flops=1):
+def gate(x, *earlier, flops=1, space=pltpu.HBM):
     return pl.pallas_call(
         gate_kernel,
         name="gate",
         in_specs=[anywhere()] * (1 + len(earlier)),
         out_specs=anywhere(),
-        out_shape=hbm(x.shape, x.dtype),
+        out_shape=space(x.shape, x.dtype),
         input_output_aliases={0: 0},
         compiler_params=params(),
         cost_estimate=cost(flops, 1),
-    )(held(x), *earlier)
+    )(pltpu.with_memory_space_constraint(x, space), *earlier)
 
 
 INNER, OUTER = (1, 0, REACH), (0, 0, REACH)
@@ -551,7 +551,7 @@
     first_piece = ORDER[0][:2]
     send(*first_piece)
     got = filter_band(
-        ids(REST), [cut for _, cut in REST], density, valid, above, below, ready, mean, *after, held(gate(token, arrived[first_piece], flops=BEFORE_BAND))
+        ids(REST), [cut for _, cut in REST], density, valid, above, below, ready, mean, *after, resident(gate(token, arrived[first_piece], flops=BEFORE_BAND, space=pltpu.VMEM))
     )
     keep(REST, got)
     for piece in (INNER, OUTER):

time: 118 us -> 117 us (level)
  transfers between devices with their start and end apart: 23 -> 23, of which waited for: 9 -> 8; matrix products, arithmetic and copies ran while one was open for 4% -> 4% of each run, Pallas kernels for 28% -> 28%
where the time goes in v11:
time: 117 us; the launch traced here: 116 us
  starting transfers between devices  55.3 us (47%)
  Pallas kernels  40.8 us (35%)
  waiting for transfers between devices  9.58 us (8%)
  local copies, waits for them, and re-layouts  7.73 us (7%)
  other arithmetic  1.58 us (1%)
    ppermute x18, starting transfers between devices, swap(): return lax.ppermute(x, 'cuts', [(i, i ^ k) for i in range(peers)])  45.9 us
    pallas_call x1, Pallas kernels, filter_band(): pl.pallas_call(functools.partial(band_kernel, pieces), name='band', grid_...  16.6 us
    pallas_call x2, Pallas kernels, filter_inner(): pl.pallas_call(functools.partial(inner_kernel, pieces, loaded), name='inn...  9.41 us
    ppermute x18, waiting for transfers between devices, swap(): return lax.ppermute(x, 'cuts', [(i, i ^ k) for i in range(peers)])  9.03 us
    pallas_call x3, Pallas kernels, project(): pl.pallas_call(functools.partial(project_kernel, count), name='project',...  8.95 us
    unnamed x22, local copies, waits for them, and re-layouts  4.67 us
    ppermute x3, starting transfers between devices, fast(): lax.ppermute(own, 'tile', [(i, i ^ k) for i in range(tiles)])  4.6 us
    ppermute x1, starting transfers between devices, fast(): above = lax.ppermute(last, 'tile', [(i, i + 1) for i in range(tiles - 1)])  3.41 us
  transfers between devices with their start and end apart: 23, of which 8 were waited for; matrix products, arithmetic and copies ran while one was open for 4% of the time, Pallas kernels for 28%

profile of v11, /device:TPU:0, one launch (start us, length us, event | category | flops | bytes accessed | tf_op | source)
XLA Modules:
  0.0 115.9 jit_solution(10721454722700601172)
XLA Ops:
  0.6 2.6 %sums.1 = (f32[24,128]{1,0:T(8,128)S(1)}, bf16[17,8,1024]{2,1,0:T(8,128)(2,1)S(1)}, bf16[17,8,1024]{2,1,0:T(8,128)(2,1)S(1)}) custom-call(bf16[16,128,1024]{2,1,0:T(8,128)(2,1)} %density.5, s32[128,1024]{1,0:T(8,128)} %valid.5), custom_call_target="tpu_custom_call" | custom-call | flops 1 | bytes 1 | tf_op jit(solution)/shard_map/sums/pallas_call | solution.py:154
  3.3 4.0 %collective-permute-start.4 = (f32[24,128]{1,0:T(8,128)S(1)}, f32[24,128]{1,0:T(8,128)S(1)}, u32[]{:S(2)}, u32[]{:S(2)}) collective-permute-start(f32[24,128]{1,0:T(8,128)S(1)} %get-tuple-element.39.after.refs_0_), channel_id=1, source_target_pairs={{0,24},{8,16},{16,8},{24,0},{1,25},{9,17},{17,9},{25,1},{2,26},{10... | collective-permute-start | bytes 36872 | tf_op jit(solution)/shard_map/ppermute | solution.py:526
  7.9 3.1 %ready.1 = (bf16[16,256,512]{2,1,0:T(8,128)(2,1)S(1)}, bf16[2,128,1024]{2,1,0:T(8,128)(2,1)S(1)}, bf16[1,16,32,1024]{3,2,1,0:T(8,128)(2,1)S(1)}, s32[1,32,1024]{2,1,0:T(8,128)S(1)}) custom-call(s32[2]{0:T(128)S(1)} %pad_add_fusion.ids, bf16[16,128,1024]{2,1,0:T(8,128)(2,1)} %density.5, s32[128,1024]{1,0:T(8,128)} %valid.5, bf16[4,16,17]{2,1,0:T(8,128)(2,1)S(1)} %copy-done.8, ...), custom_call_target="tpu_custom_call" | custom-call | flops 1 | bytes 1 | tf_op jit(solution)/shard_map/ready/pallas_call | solution.py:224
  11.5 2.9 %inner.2.refs_5_ = bf16[8,16,1024]{2,1,0:T(8,128)(2,1)S(1)} custom-call(s32[2]{0:T(128)S(1)} %pad_add_fusion.ids, bf16[1,16,32,1024]{3,2,1,0:T(8,128)(2,1)S(1)} %get-tuple-element.43.refs_0_, s32[1,32,1024]{2,1,0:T(8,128)S(1)} %get-tuple-element.44.refs_1_, bf16[16,256,512]{2,1,0:T(8,128)(2,1)S(1)} %get-tuple-element.40.refs_4_.refs_2_.col, ...), custom_call_target="tpu_custom_call" | custom-call | flops 1 | bytes 1 | tf_op jit(solution)/shard_map/inner/pallas_call | solution.py:281
  14.4 2.7 %collective-permute-start.5 = (bf16[8,16,1024]{2,1,0:T(8,128)(2,1)S(1)}, bf16[8,16,1024]{2,1,0:T(8,128)(2,1)S(1)}, u32[]{:S(2)}, u32[]{:S(2)}) collective-permute-start(bf16[8,16,1024]{2,1,0:T(8,128)(2,1)S(1)} %inner.2.refs_5_), channel_id=1, source_target_pairs={{0,4},{1,5},{2,6},{3,7},{4,0},{5,1},{6,2},{7,3},{8,12},{9,13},{10,... | collective-permute-start | bytes 786440 | tf_op jit(solution)/shard_map/ppermute | solution.py:523
  17.2 3.4 %collective-permute-start = (bf16[17,8,1024]{2,1,0:T(8,128)(2,1)S(1)}, bf16[17,8,1024]{2,1,0:T(8,128)(2,1)S(1)}, u32[]{:S(2)}, u32[]{:S(2)}) collective-permute-start(bf16[17,8,1024]{2,1,0:T(8,128)(2,1)S(1)} %get-tuple-element.37), channel_id=1, source_target_pairs={{0,8},{8,16},{16,24},{1,9},{9,17},{17,25},{2,10},{10,18},{18,26},{... | collective-permute-start | bytes 835592 | tf_op jit(solution)/shard_map/ppermute | solution.py:532
  20.6 1.5 %collective-permute-start.1 = (bf16[17,8,1024]{2,1,0:T(8,128)(2,1)S(1)}, bf16[17,8,1024]{2,1,0:T(8,128)(2,1)S(1)}, u32[]{:S(2)}, u32[]{:S(2)}) collective-permute-start(bf16[17,8,1024]{2,1,0:T(8,128)(2,1)S(1)} %get-tuple-element.38), channel_id=1, source_target_pairs={{8,0},{16,8},{24,16},{9,1},{17,9},{25,17},{10,2},{18,10},{26,18},{... | collective-permute-start | bytes 835592 | tf_op jit(solution)/shard_map/ppermute | solution.py:533
  22.2 2.2 %copy-done.1 = bf16[16,256,512]{2,1,0:T(8,128)(2,1)S(1)} copy-done((bf16[16,256,512]{2,1,0:T(8,128)(2,1)S(1)}, bf16[16,256,512]{2,1,0:T(8,128)(2,1)}, u32[]{:S(2)}) %copy-start.1) | copy-done | bytes 4194328
  24.3 6.5 %inner.3 = (bf16[8,16,1024]{2,1,0:T(8,128)(2,1)S(1)}, bf16[8,16,1024]{2,1,0:T(8,128)(2,1)S(1)}) custom-call(s32[3]{0:T(128)S(1)} %pad_add_fusion.1.ids, bf16[16,128,1024]{2,1,0:T(8,128)(2,1)} %density.5, s32[128,1024]{1,0:T(8,128)} %valid.5, bf16[16,256,512]{2,1,0:T(8,128)(2,1)S(1)} %copy-done.1, bf16[2,128,1024]{2,1,0:T(8,128)(2,1)S(1)} %get-tuple-element.41.refs_3_.row, ...), custom_call_target="tpu_custom_call" | custom-call | flops 1 | bytes 1 | tf_op jit(solution)/shard_map/inner/pallas_call | solution.py:281
  31.0 2.0 %collective-permute-start.10 = (bf16[8,16,1024]{2,1,0:T(8,128)(2,1)S(1)}, bf16[8,16,1024]{2,1,0:T(8,128)(2,1)S(1)}, u32[]{:S(2)}, u32[]{:S(2)}) collective-permute-start(bf16[8,16,1024]{2,1,0:T(8,128)(2,1)S(1)} %get-tuple-element.45.refs_0_), channel_id=1, source_target_pairs={{0,6},{1,7},{2,4},{3,5},{4,2},{5,3},{6,0},{7,1},{8,14},{9,15},{10,... | collective-permute-start | bytes 786440 | tf_op jit(solution)/shard_map/ppermute | solution.py:523
  33.3 16.6 %band.1 = (bf16[6,16,1024]{2,1,0:T(8,128)(2,1)}, bf16[2,16,1024]{2,1,0:T(8,128)(2,1)}, bf16[8,16,1024]{2,1,0:T(8,128)(2,1)}, bf16[6,16,1024]{2,1,0:T(8,128)(2,1)...) custom-call(s32[9]{0:T(128)S(1)} %concatenate.11.ids, ...), custom_call_target="tpu_custom_call" | custom-call | flops 1 | bytes 1 | tf_op jit(solution)/shard_map/band/pallas_call | solution.py:386
  49.9 1.5 %collective-permute-done.6.refs_1_.refs_5_ = bf16[8,16,1024]{2,1,0:T(8,128)(2,1)S(1)} collective-permute-done((bf16[8,16,1024]{2,1,0:T(8,128)(2,1)S(1)}, bf16[8,16,1024]{2,1,0:T(8,128)(2,1)S(1)}, u32[]{:S(2)}, u32[]{:S(2)}) %collective-permute-start.6) | collective-permute-done | bytes 262176 | tf_op jit(solution)/shard_map/ppermute | solution.py:523
  51.5 2.5 %collective-permute-start.14 = (bf16[6,16,1024]{2,1,0:T(8,128)(2,1)}, bf16[6,16,1024]{2,1,0:T(8,128)(2,1)S(1)}, u32[]{:S(2)}, u32[]{:S(2)}) collective-permute-start(bf16[6,16,1024]{2,1,0:T(8,128)(2,1)} %gate.23), channel_id=1, source_target_pairs={{0,6},{1,7},{2,4},{3,5},{4,2},{5,3},{6,0},{7,1},{8,14},{9,15},{10,... | collective-permute-start | bytes 589832 | tf_op jit(solution)/shard_map/ppermute | solution.py:523
  54.0 3.6 %collective-permute-start.16 = (bf16[6,16,1024]{2,1,0:T(8,128)(2,1)}, bf16[6,16,1024]{2,1,0:T(8,128)(2,1)S(1)}, u32[]{:S(2)}, u32[]{:S(2)}) collective-permute-start(bf16[6,16,1024]{2,1,0:T(8,128)(2,1)} %gate.25), channel_id=1, source_target_pairs={{0,4},{1,5},{2,6},{3,7},{4,0},{5,1},{6,2},{7,3},{8,12},{9,13},{10,... | collective-permute-start | bytes 589832 | tf_op jit(solution)/shard_map/ppermute | solution.py:523
  58.3 2.6 %collective-permute-done.7.refs_1_.refs_3_ = bf16[8,16,1024]{2,1,0:T(8,128)(2,1)S(1)} collective-permute-done((bf16[8,16,1024]{2,1,0:T(8,128)(2,1)}, bf16[8,16,1024]{2,1,0:T(8,128)(2,1)S(1)}, u32[]{:S(2)}, u32[]{:S(2)}) %collective-permute-start.7) | collective-permute-done | bytes 262176 | tf_op jit(solution)/shard_map/ppermute | solution.py:523
  60.8 4.2 %collective-permute-start.8 = (bf16[8,16,1024]{2,1,0:T(8,128)(2,1)}, bf16[8,16,1024]{2,1,0:T(8,128)(2,1)S(1)}, u32[]{:S(2)}, u32[]{:S(2)}) collective-permute-start(bf16[8,16,1024]{2,1,0:T(8,128)(2,1)} %gate.18), channel_id=1, source_target_pairs={{0,1},{1,0},{2,3},{3,2},{4,5},{5,4},{6,7},{7,6},{8,9},{9,8},{10,11... | collective-permute-start | bytes 786440 | tf_op jit(solution)/shard_map/ppermute | solution.py:523
  65.6 10.6 %collective-permute-start.15 = (bf16[2,16,1024]{2,1,0:T(8,128)(2,1)}, bf16[2,16,1024]{2,1,0:T(8,128)(2,1)S(1)}, u32[]{:S(2)}, u32[]{:S(2)}) collective-permute-start(bf16[2,16,1024]{2,1,0:T(8,128)(2,1)} %gate.24), channel_id=1, source_target_pairs={{0,4},{1,5},{2,6},{3,7},{4,0},{5,1},{6,2},{7,3},{8,12},{9,13},{10,... | collective-permute-start | bytes 196616 | tf_op jit(solution)/shard_map/ppermute | solution.py:523
  76.2 2.8 %collective-permute-done.16.refs_1_.refs_4_ = bf16[6,16,1024]{2,1,0:T(8,128)(2,1)S(1)} collective-permute-done((bf16[6,16,1024]{2,1,0:T(8,128)(2,1)}, bf16[6,16,1024]{2,1,0:T(8,128)(2,1)S(1)}, u32[]{:S(2)}, u32[]{:S(2)}) %collective-permute-start.16) | collective-permute-done | bytes 196640 | tf_op jit(solution)/shard_map/ppermute | solution.py:523
  80.5 6.6 %collective-permute-start.20 = (bf16[6,16,1024]{2,1,0:T(8,128)(2,1)}, bf16[6,16,1024]{2,1,0:T(8,128)(2,1)}, u32[]{:S(2)}, u32[]{:S(2)}) collective-permute-start(bf16[6,16,1024]{2,1,0:T(8,128)(2,1)} %gate.29), channel_id=1, source_target_pairs={{0,5},{1,4},{2,7},{3,6},{4,1},{5,0},{6,3},{7,2},{8,13},{9,12},{10,... | collective-permute-start | bytes 589832 | tf_op jit(solution)/shard_map/ppermute | solution.py:523
  89.3 2.0 %gather_fusion = bf16[8,256,16]{1,2,0:T(8,128)(2,1)} fusion(bf16[256,8,16]{0,2,1:T(8,128)(2,1)} %bitcast.20, s32[1024]{0:T(1024)S(1)} %pad_clamp_fusion), kind=kCustom, calls=%fused_computation | custom fusion | bytes 131104 | tf_op jit(solution)/shard_map/gather | solution.py:561
  93.1 9.5 %collective-permute-start.22 = (bf16[2,16,1024]{2,1,0:T(8,128)(2,1)}, bf16[2,16,1024]{2,1,0:T(8,128)(2,1)}, u32[]{:S(2)}, u32[]{:S(2)}) collective-permute-start(bf16[2,16,1024]{2,1,0:T(8,128)(2,1)} %gate.31), channel_id=1, source_target_pairs={{0,7},{1,6},{2,5},{3,4},{4,3},{5,2},{6,1},{7,0},{8,15},{9,14},{10,... | collective-permute-start | bytes 196616 | tf_op jit(solution)/shard_map/ppermute | solution.py:523
  103.5 3.2 %project.3 = (bf16[128,16384]{1,0:T(8,128)(2,1)}, bf16[128,16384]{1,0:T(8,128)(2,1)}, f32[8,128]{1,0:T(8,128)}) custom-call(s32[1]{0:T(128)} %bitcast.14.place, bf16[256,128]{1,0:T(8,128)(2,1)S(1)} %copy.30.weights, bf16[8,16,1024]{2,1,0:T(8,128)(2,1)S(1)} %copy-done.7, bf16[8,16,1024]{2,1,0:T(8,128)(2,1)S(1)} %collective-permute-done.8.refs_1_, ...), custom_call_target="tpu_custom_call" | custom-call | flops 1 | bytes 1 | tf_op jit(solution)/shard_map/project/pallas_call | solution.py:441
  108.6 3.6 %project.4 = (bf16[128,16384]{1,0:T(8,128)(2,1)}, bf16[128,16384]{1,0:T(8,128)(2,1)}, f32[8,128]{1,0:T(8,128)}) custom-call(s32[1]{0:T(128)} %bitcast.15.place, bf16[256,128]{1,0:T(8,128)(2,1)S(1)} %copy.30.weights, bf16[8,16,1024]{2,1,0:T(8,128)(2,1)S(1)} %copy-done.3, ...), custom_call_target="tpu_custom_call", output_to_operand_aliasing={{0}: (10, {}), {1}: (11, {})} | custom-call | flops 1 | bytes 1 | tf_op jit(solution)/shard_map/project/pallas_call | solution.py:441
  113.7 2.2 %project.5 = (bf16[128,16384]{1,0:T(8,128)(2,1)}, bf16[128,16384]{1,0:T(8,128)(2,1)}, f32[8,128]{1,0:T(8,128)}) custom-call(s32[1]{0:T(128)} %bitcast.place, bf16[256,128]{1,0:T(8,128)(2,1)S(1)} %copy.30.weights, bf16[8,16,1024]{2,1,0:T(8,128)(2,1)S(1)} %copy-done.3, ...), custom_call_target="tpu_custom_call", output_to_operand_aliasing={{0}: (10, {}), {1}: (11, {})} | custom-call | flops 1 | bytes 1 | tf_op jit(solution)/shard_map/project/pallas_call | solution.py:441
  (77 shorter events, 12.7 us)
Async XLA Ops:
  3.3 7.8 %collective-permute-start.4 = (f32[24,128]{1,0:T(8,128)S(1)}, f32[24,128]{1,0:T(8,128)S(1)}, u32[]{:S(2)}, u32[]{:S(2)}) collective-permute-start(f32[24,128]{1,0:T(8,128)S(1)} %get-tuple-element.39.after.refs_0_), channel_id=1, source_target_pairs={{0,24},{8,16},{16,8},{24,0},{1,25},{9,17},{17,9},{25,1},{2,26},{10... | collective-permute-start | bytes 36872 | tf_op jit(solution)/shard_map/ppermute | solution.py:526
  7.2 3.9 %collective-permute-start.3 = (f32[24,128]{1,0:T(8,128)S(1)}, f32[24,128]{1,0:T(8,128)S(1)}, u32[]{:S(2)}, u32[]{:S(2)}) collective-permute-start(f32[24,128]{1,0:T(8,128)S(1)} %get-tuple-element.39.after.refs_0_), channel_id=1, source_target_pairs={{0,16},{8,24},{16,0},{24,8},{1,17},{9,25},{17,1},{25,9},{2,18},{10... | collective-permute-start | bytes 36872 | tf_op jit(solution)/shard_map/ppermute | solution.py:526
  7.7 3.7 %collective-permute-start.2 = (f32[24,128]{1,0:T(8,128)S(1)}, f32[24,128]{1,0:T(8,128)S(1)}, u32[]{:S(2)}, u32[]{:S(2)}) collective-permute-start(f32[24,128]{1,0:T(8,128)S(1)} %get-tuple-element.39.after.refs_0_), channel_id=1, source_target_pairs={{0,8},{8,0},{16,24},{24,16},{1,9},{9,1},{17,25},{25,17},{2,10},{10... | collective-permute-start | bytes 36872 | tf_op jit(solution)/shard_map/ppermute | solution.py:526
  14.4 18.6 %collective-permute-start.5 = (bf16[8,16,1024]{2,1,0:T(8,128)(2,1)S(1)}, bf16[8,16,1024]{2,1,0:T(8,128)(2,1)S(1)}, u32[]{:S(2)}, u32[]{:S(2)}) collective-permute-start(bf16[8,16,1024]{2,1,0:T(8,128)(2,1)S(1)} %inner.2.refs_5_), channel_id=1, source_target_pairs={{0,4},{1,5},{2,6},{3,7},{4,0},{5,1},{6,2},{7,3},{8,12},{9,13},{10,... | collective-permute-start | bytes 786440 | tf_op jit(solution)/shard_map/ppermute | solution.py:523
  17.2 15.9 %collective-permute-start = (bf16[17,8,1024]{2,1,0:T(8,128)(2,1)S(1)}, bf16[17,8,1024]{2,1,0:T(8,128)(2,1)S(1)}, u32[]{:S(2)}, u32[]{:S(2)}) collective-permute-start(bf16[17,8,1024]{2,1,0:T(8,128)(2,1)S(1)} %get-tuple-element.37), channel_id=1, source_target_pairs={{0,8},{8,16},{16,24},{1,9},{9,17},{17,25},{2,10},{10,18},{18,26},{... | collective-permute-start | bytes 835592 | tf_op jit(solution)/shard_map/ppermute | solution.py:532
  20.6 12.7 %collective-permute-start.1 = (bf16[17,8,1024]{2,1,0:T(8,128)(2,1)S(1)}, bf16[17,8,1024]{2,1,0:T(8,128)(2,1)S(1)}, u32[]{:S(2)}, u32[]{:S(2)}) collective-permute-start(bf16[17,8,1024]{2,1,0:T(8,128)(2,1)S(1)} %get-tuple-element.38), channel_id=1, source_target_pairs={{8,0},{16,8},{24,16},{9,1},{17,9},{25,17},{10,2},{18,10},{26,18},{... | collective-permute-start | bytes 835592 | tf_op jit(solution)/shard_map/ppermute | solution.py:533
  30.9 20.6 %collective-permute-start.6 = (bf16[8,16,1024]{2,1,0:T(8,128)(2,1)S(1)}, bf16[8,16,1024]{2,1,0:T(8,128)(2,1)S(1)}, u32[]{:S(2)}, u32[]{:S(2)}) collective-permute-start(bf16[8,16,1024]{2,1,0:T(8,128)(2,1)S(1)} %get-tuple-element.51), channel_id=1, source_target_pairs={{0,5},{1,4},{2,7},{3,6},{4,1},{5,0},{6,3},{7,2},{8,13},{9,12},{10,... | collective-permute-start | bytes 786440 | tf_op jit(solution)/shard_map/ppermute | solution.py:523
  31.0 23.0 %collective-permute-start.10 = (bf16[8,16,1024]{2,1,0:T(8,128)(2,1)S(1)}, bf16[8,16,1024]{2,1,0:T(8,128)(2,1)S(1)}, u32[]{:S(2)}, u32[]{:S(2)}) collective-permute-start(bf16[8,16,1024]{2,1,0:T(8,128)(2,1)S(1)} %get-tuple-element.45.refs_0_), channel_id=1, source_target_pairs={{0,6},{1,7},{2,4},{3,5},{4,2},{5,3},{6,0},{7,1},{8,14},{9,15},{10,... | collective-permute-start | bytes 786440 | tf_op jit(solution)/shard_map/ppermute | solution.py:523
  51.4 9.4 %collective-permute-start.7 = (bf16[8,16,1024]{2,1,0:T(8,128)(2,1)}, bf16[8,16,1024]{2,1,0:T(8,128)(2,1)S(1)}, u32[]{:S(2)}, u32[]{:S(2)}) collective-permute-start(bf16[8,16,1024]{2,1,0:T(8,128)(2,1)} %gate.17), channel_id=1, source_target_pairs={{0,3},{1,2},{2,1},{3,0},{4,7},{5,6},{6,5},{7,4},{8,11},{9,10},{10,... | collective-permute-start | bytes 786440 | tf_op jit(solution)/shard_map/ppermute | solution.py:523
  51.5 14.1 %collective-permute-start.14 = (bf16[6,16,1024]{2,1,0:T(8,128)(2,1)}, bf16[6,16,1024]{2,1,0:T(8,128)(2,1)S(1)}, u32[]{:S(2)}, u32[]{:S(2)}) collective-permute-start(bf16[6,16,1024]{2,1,0:T(8,128)(2,1)} %gate.23), channel_id=1, source_target_pairs={{0,6},{1,7},{2,4},{3,5},{4,2},{5,3},{6,0},{7,1},{8,14},{9,15},{10,... | collective-permute-start | bytes 589832 | tf_op jit(solution)/shard_map/ppermute | solution.py:523
  54.0 25.0 %collective-permute-start.16 = (bf16[6,16,1024]{2,1,0:T(8,128)(2,1)}, bf16[6,16,1024]{2,1,0:T(8,128)(2,1)S(1)}, u32[]{:S(2)}, u32[]{:S(2)}) collective-permute-start(bf16[6,16,1024]{2,1,0:T(8,128)(2,1)} %gate.25), channel_id=1, source_target_pairs={{0,4},{1,5},{2,6},{3,7},{4,0},{5,1},{6,2},{7,3},{8,12},{9,13},{10,... | collective-permute-start | bytes 589832 | tf_op jit(solution)/shard_map/ppermute | solution.py:523
  57.6 21.4 %collective-permute-start.19 = (bf16[8,16,1024]{2,1,0:T(8,128)(2,1)}, bf16[8,16,1024]{2,1,0:T(8,128)(2,1)S(1)}, u32[]{:S(2)}, u32[]{:S(2)}) collective-permute-start(bf16[8,16,1024]{2,1,0:T(8,128)(2,1)} %gate.28), channel_id=1, source_target_pairs={{0,7},{1,6},{2,5},{3,4},{4,3},{5,2},{6,1},{7,0},{8,15},{9,14},{10,... | collective-permute-start | bytes 786440 | tf_op jit(solution)/shard_map/ppermute | solution.py:523
  58.3 22.2 %collective-permute-start.11 = (bf16[8,16,1024]{2,1,0:T(8,128)(2,1)}, bf16[8,16,1024]{2,1,0:T(8,128)(2,1)S(1)}, u32[]{:S(2)}, u32[]{:S(2)}) collective-permute-start(bf16[8,16,1024]{2,1,0:T(8,128)(2,1)} %gate.20), channel_id=1, source_target_pairs={{0,2},{1,3},{2,0},{3,1},{4,6},{5,7},{6,4},{7,5},{8,10},{9,11},{10,... | collective-permute-start | bytes 786440 | tf_op jit(solution)/shard_map/ppermute | solution.py:523
  60.8 47.8 %copy-start.3 = (bf16[8,16,1024]{2,1,0:T(8,128)(2,1)S(1)}, bf16[8,16,1024]{2,1,0:T(8,128)(2,1)}, u32[]{:S(2)}) copy-start(bf16[8,16,1024]{2,1,0:T(8,128)(2,1)} %get-tuple-element.47.refs_0_) | copy-start | bytes 786436
  60.8 26.2 %collective-permute-start.8 = (bf16[8,16,1024]{2,1,0:T(8,128)(2,1)}, bf16[8,16,1024]{2,1,0:T(8,128)(2,1)S(1)}, u32[]{:S(2)}, u32[]{:S(2)}) collective-permute-start(bf16[8,16,1024]{2,1,0:T(8,128)(2,1)} %gate.18), channel_id=1, source_target_pairs={{0,1},{1,0},{2,3},{3,2},{4,5},{5,4},{6,7},{7,6},{8,9},{9,8},{10,11... | collective-permute-start | bytes 786440 | tf_op jit(solution)/shard_map/ppermute | solution.py:523
  65.6 22.0 %collective-permute-start.15 = (bf16[2,16,1024]{2,1,0:T(8,128)(2,1)}, bf16[2,16,1024]{2,1,0:T(8,128)(2,1)S(1)}, u32[]{:S(2)}, u32[]{:S(2)}) collective-permute-start(bf16[2,16,1024]{2,1,0:T(8,128)(2,1)} %gate.24), channel_id=1, source_target_pairs={{0,4},{1,5},{2,6},{3,7},{4,0},{5,1},{6,2},{7,3},{8,12},{9,13},{10,... | collective-permute-start | bytes 196616 | tf_op jit(solution)/shard_map/ppermute | solution.py:523
  79.0 28.4 %collective-permute-start.13 = (bf16[8,16,1024]{2,1,0:T(8,128)(2,1)}, bf16[8,16,1024]{2,1,0:T(8,128)(2,1)S(1)}, u32[]{:S(2)}, u32[]{:S(2)}) collective-permute-start(bf16[8,16,1024]{2,1,0:T(8,128)(2,1)} %gate.22), channel_id=1, source_target_pairs={{0,3},{1,2},{2,1},{3,0},{4,7},{5,6},{6,5},{7,4},{8,11},{9,10},{10,... | collective-permute-start | bytes 786440 | tf_op jit(solution)/shard_map/ppermute | solution.py:523
  79.0 14.1 %collective-permute-start.17 = (bf16[6,16,1024]{2,1,0:T(8,128)(2,1)}, bf16[6,16,1024]{2,1,0:T(8,128)(2,1)S(1)}, u32[]{:S(2)}, u32[]{:S(2)}) collective-permute-start(bf16[6,16,1024]{2,1,0:T(8,128)(2,1)} %gate.26), channel_id=1, source_target_pairs={{0,7},{1,6},{2,5},{3,4},{4,3},{5,2},{6,1},{7,0},{8,15},{9,14},{10,... | collective-permute-start | bytes 589832 | tf_op jit(solution)/shard_map/ppermute | solution.py:523
  80.5 26.2 %collective-permute-start.20 = (bf16[6,16,1024]{2,1,0:T(8,128)(2,1)}, bf16[6,16,1024]{2,1,0:T(8,128)(2,1)}, u32[]{:S(2)}, u32[]{:S(2)}) collective-permute-start(bf16[6,16,1024]{2,1,0:T(8,128)(2,1)} %gate.29), channel_id=1, source_target_pairs={{0,5},{1,4},{2,7},{3,6},{4,1},{5,0},{6,3},{7,2},{8,13},{9,12},{10,... | collective-permute-start | bytes 589832 | tf_op jit(solution)/shard_map/ppermute | solution.py:523
  87.0 21.5 %collective-permute-start.12 = (bf16[8,16,1024]{2,1,0:T(8,128)(2,1)}, bf16[8,16,1024]{2,1,0:T(8,128)(2,1)S(1)}, u32[]{:S(2)}, u32[]{:S(2)}) collective-permute-start(bf16[8,16,1024]{2,1,0:T(8,128)(2,1)} %gate.21), channel_id=1, source_target_pairs={{0,2},{1,3},{2,0},{3,1},{4,6},{5,7},{6,4},{7,5},{8,10},{9,11},{10,... | collective-permute-start | bytes 786440 | tf_op jit(solution)/shard_map/ppermute | solution.py:523
  87.7 20.9 %collective-permute-start.9 = (bf16[8,16,1024]{2,1,0:T(8,128)(2,1)}, bf16[8,16,1024]{2,1,0:T(8,128)(2,1)S(1)}, u32[]{:S(2)}, u32[]{:S(2)}) collective-permute-start(bf16[8,16,1024]{2,1,0:T(8,128)(2,1)} %gate.19), channel_id=1, source_target_pairs={{0,1},{1,0},{2,3},{3,2},{4,5},{5,4},{6,7},{7,6},{8,9},{9,8},{10,11... | collective-permute-start | bytes 786440 | tf_op jit(solution)/shard_map/ppermute | solution.py:523
  93.1 19.1 %collective-permute-start.22 = (bf16[2,16,1024]{2,1,0:T(8,128)(2,1)}, bf16[2,16,1024]{2,1,0:T(8,128)(2,1)}, u32[]{:S(2)}, u32[]{:S(2)}) collective-permute-start(bf16[2,16,1024]{2,1,0:T(8,128)(2,1)} %gate.31), channel_id=1, source_target_pairs={{0,7},{1,6},{2,5},{3,4},{4,3},{5,2},{6,1},{7,0},{8,15},{9,14},{10,... | collective-permute-start | bytes 196616 | tf_op jit(solution)/shard_map/ppermute | solution.py:523
  106.7 5.5 %collective-permute-start.18 = (bf16[2,16,1024]{2,1,0:T(8,128)(2,1)}, bf16[2,16,1024]{2,1,0:T(8,128)(2,1)S(1)}, u32[]{:S(2)}, u32[]{:S(2)}) collective-permute-start(bf16[2,16,1024]{2,1,0:T(8,128)(2,1)} %gate.27), channel_id=1, source_target_pairs={{0,5},{1,4},{2,7},{3,6},{4,1},{5,0},{6,3},{7,2},{8,13},{9,12},{10,... | collective-permute-start | bytes 196616 | tf_op jit(solution)/shard_map/ppermute | solution.py:523
  107.4 6.3 %collective-permute-start.21 = (bf16[2,16,1024]{2,1,0:T(8,128)(2,1)}, bf16[2,16,1024]{2,1,0:T(8,128)(2,1)S(1)}, u32[]{:S(2)}, u32[]{:S(2)}) collective-permute-start(bf16[2,16,1024]{2,1,0:T(8,128)(2,1)} %gate.30), channel_id=1, source_target_pairs={{0,6},{1,7},{2,4},{3,5},{4,2},{5,3},{6,0},{7,1},{8,14},{9,15},{10,... | collective-permute-start | bytes 196616 | tf_op jit(solution)/shard_map/ppermute | solution.py:523
  (10 other events, 33.6 us)

commit v12 on v11

--- a/solution.py
+++ b/solution.py
@@ -196,17 +196,18 @@
     return jnp.concatenate([chosen, jnp.zeros((REACH, both.shape[1]), jnp.float32)], axis=0)
 
 
-def window_copies(ids, b, last, density, valid, cube, plane, sems):
+def window_copies(b, block, last, density, valid, cube, plane, sems):
     high = plane.shape[1]
-    here = pl.ds(pl.multiple_of(jnp.minimum(ids[b], last - 1) * (high // 2), high // 2), high)
+    here = pl.ds(pl.multiple_of(jnp.minimum(block, last - 1) * (high // 2), high // 2), high)
     return [
         pltpu.make_async_copy(density.at[:, here], cube.at[b], sems.at[2 * b]),
         pltpu.make_async_copy(valid.at[here], plane.at[b], sems.at[2 * b + 1]),
     ]
 
 
-def ready_kernel(ids, density, valid, row_taps, col_taps, after, col, row, cube, plane, sems):
-    copies = window_copies(ids, 0, ids[1], density, valid, cube, plane, sems)
+def ready_kernel(partner, me, density, valid, row_taps, col_taps, after, col, row, cube, plane, sems):
+    last = density.shape[1] * 2 // plane.shape[1] - 1
+    copies = window_copies(0, me[0] ^ partner, last, density, valid, cube, plane, sems)
     for copy in copies:
         copy.start()
     build_columns(listed(col_taps), col)
@@ -215,14 +216,14 @@
         copy.wait()
 
 
-def make_ready(ids, density, valid, row_taps, col_taps, after):
+def make_ready(me, partner, density, valid, row_taps, col_taps, after):
     slices, rows, cols = density.shape
     terms = row_taps.shape[0]
     high = LANES // terms
     vmem = pl.BlockSpec(memory_space=pltpu.VMEM)
     shapes = *matrix_shapes(terms, slices, high - HALO), (1, slices, high, cols)
     return pl.pallas_call(
-        ready_kernel,
+        functools.partial(ready_kernel, partner),
         name="ready",
         in_specs=[pl.BlockSpec(memory_space=pltpu.SMEM)] + [anywhere()] * 2 + [vmem] * 2 + [anywhere()],
         out_specs=[vmem] * 4,
@@ -230,26 +231,28 @@
         scratch_shapes=[pltpu.SemaphoreType.DMA((2,))],
         compiler_params=params(),
         cost_estimate=cost(1, 1),
-    )(jnp.stack([ids, jnp.full_like(ids, rows // (high - HALO) - 1)]), held(density), held(valid), row_taps, col_taps, after)
-
-
-def inner_kernel(pieces, loaded, ids, *refs):
-    count = len(pieces)
-    outs = sum(len(wanted) for wanted in pieces)
+    )(me, held(density), held(valid), row_taps, col_taps, after)
+
+
+def inner_kernel(wanted, loaded, end, me, *refs):
+    count = len(wanted)
+    pieces = [cut for _, cut in wanted]
+    blocks = [me[0] ^ k for k, _ in wanted]
+    outs = sum(len(cut) for cut in pieces)
     if loaded:
         (cube, plane, col, row, mean), tall = refs[:5], refs[-1]
         outs = list(refs[-1 - outs : -1])
     else:
         (density, valid, col, row, mean), (tall, cube, plane, sems) = refs[:5], refs[-4:]
         outs = list(refs[-4 - outs : -4])
-        copies = [window_copies(ids, b, ids[count], density, valid, cube, plane, sems) for b in range(count)]
+        copies = [window_copies(b, blocks[b], end, density, valid, cube, plane, sems) for b in range(count)]
         for copy in sum(copies, []):
             copy.start()
-    for b, wanted in enumerate(pieces):
+    for b, cut in enumerate(pieces):
         if not loaded:
             for copy in copies[b]:
                 copy.wait()
-        last = ids[b] == ids[count]
+        last = blocks[b] == end
         mask = inner_rows(plane[b], last)
         field = convolve(
             lambda s, b=b, last=last, mask=mask: mask * (inner_rows(cube[b, s], last) - mean[s : s + 1, :1]),
@@ -258,18 +261,18 @@
             tall,
             REACH,
         ).astype(jnp.bfloat16)
-        for _, start, stop in wanted:
+        for _, start, stop in cut:
             outs.pop(0)[...] = field[start:stop]
 
 
-def filter_inner(ids, pieces, density, valid, ready, mean, *after):
+def filter_inner(me, wanted, density, valid, ready, mean, *after):
     slices, rows, cols = density.shape
     col, row, cube, plane = ready
     high = plane.shape[1]
-    count = ids.shape[0]
+    count = len(wanted)
     loaded = not after
     vmem = pl.BlockSpec(memory_space=pltpu.VMEM)
-    shapes = [(stop - start, slices, cols) for wanted in pieces for _, start, stop in wanted]
+    shapes = [(stop - start, slices, cols) for _, cut in wanted for _, start, stop in cut]
     field = [resident(cube), resident(plane)] if loaded else [held(density), held(valid)]
     scratch = [pltpu.VMEM((GROUP * LANES, cols), jnp.bfloat16)]
     if not loaded:
@@ -279,7 +282,7 @@
             pltpu.SemaphoreType.DMA((2 * count,)),
         ]
     out = pl.pallas_call(
-        functools.partial(inner_kernel, pieces, loaded),
+        functools.partial(inner_kernel, wanted, loaded, rows // (high - HALO) - 1),
         name="inner",
         in_specs=[pl.BlockSpec(memory_space=pltpu.SMEM)]
         + [vmem if loaded else anywhere()] * 2
@@ -291,7 +294,7 @@
         compiler_params=params(),
         cost_estimate=cost(1, 1),
     )(
-        jnp.concatenate([ids, jnp.full((1,), rows // (high - HALO) - 1, ids.dtype)]),
+        me,
         *field,
         resident(col),
         resident(row),
@@ -299,12 +302,13 @@
         *after,
     )
     out = list(out)
-    return [[out.pop(0) for _ in wanted] for wanted in pieces]
-
-
-def band_kernel(pieces, ids, density, valid, above, below, col, row, mean, *refs):
+    return [[out.pop(0) for _ in cut] for _, cut in wanted]
+
+
+def band_kernel(wanted, me, density, valid, above, below, col, row, mean, *refs):
     (mask, tall, done, sems) = refs[-4:]
-    count = sum(len(wanted) for wanted in pieces)
+    pieces = [cut for _, cut in wanted]
+    count = sum(len(cut) for cut in pieces)
     outs = refs[-4 - count : -4]
     slices = mean.shape[0]
     rows, cols = valid.shape
@@ -339,8 +343,8 @@
                     ]
 
     def copies(b):
-        at = sum(len(wanted) for wanted in pieces[:b])
-        last = ids[b] == ids[len(pieces)]
+        at = sum(len(cut) for cut in pieces[:b])
+        last = (me[0] ^ wanted[b][0]) == rows // block - 1
         for p, (inner, start, stop) in enumerate(pieces[b]):
             here = jnp.where(last != (inner == 1), block - REACH, 0) + start
             yield pltpu.make_async_copy(done.at[b, pl.ds(here, stop - start)], outs[at + p], sems.at[at + p])
@@ -349,7 +353,8 @@
     def _():
         for j in range(PAIR):
             b = (step - steps) * PAIR + j
-            here = pl.ds(pl.multiple_of(ids[b] * block, block), high)
+            partner = sum(jnp.where(b == i, k, 0) for i, (k, _) in enumerate(wanted))
+            here = pl.ds(pl.multiple_of((me[0] ^ partner) * block, block), high)
             parts = []
             for g in range(slices // GROUP):
                 slab = tall[g * GROUP * terms : (g + 1) * GROUP * terms, here, :].reshape(GROUP * LANES, cols)
@@ -372,19 +377,19 @@
                 copy.wait()
 
 
-def filter_band(ids, pieces, density, valid, above, below, ready, mean, *after):
+def filter_band(me, wanted, density, valid, above, below, ready, mean, *after):
     slices, rows, cols = density.shape
     col, row = ready[:2]
     terms = col.shape[2] // LANES
     block = LANES // terms - HALO
-    count = len(pieces)
+    count = len(wanted)
 
     def whole(x):
         return pl.BlockSpec(x.shape, lambda i, at: (0,) * x.ndim, pipeline_mode=pl.Buffered(1))
 
-    shapes = [(stop - start, slices, cols) for wanted in pieces for _, start, stop in wanted]
+    shapes = [(stop - start, slices, cols) for _, cut in wanted for _, start, stop in cut]
     out = pl.pallas_call(
-        functools.partial(band_kernel, pieces),
+        functools.partial(band_kernel, wanted),
         name="band",
         grid_spec=pltpu.PrefetchScalarGridSpec(
             num_scalar_prefetch=1,
@@ -406,7 +411,7 @@
         compiler_params=params(),
         cost_estimate=cost(1, 1),
     )(
-        jnp.concatenate([ids, jnp.full((1,), rows // block - 1, ids.dtype)]),
+        me,
         held(density),
         held(valid),
         above,
@@ -417,10 +422,10 @@
         *after,
     )
     out = list(out)
-    return [[out.pop(0) for _ in wanted] for wanted in pieces]
-
-
-def project_kernel(count, place, weights, *refs):
+    return [[out.pop(0) for _ in cut] for _, cut in wanted]
+
+
+def project_kernel(count, me, weights, *refs):
     parts, (amp_out, like_out, token) = refs[:count], refs[-3:]
     zbins = weights.shape[0] // 2
     rows, _, cols = parts[0].shape
@@ -433,8 +438,38 @@
     token[...] = jnp.zeros_like(token)
 
 
-def project(place, weights, parts, rows, total, earlier):
+def weights_kernel(peers, me, amp_matrix, like_matrix, out):
+    slices = amp_matrix.shape[0] // peers
+    for n, matrix in enumerate((amp_matrix, like_matrix)):
+        rows = [matrix[pl.ds(pl.multiple_of((me[0] ^ k) * slices, slices), slices)] for k in range(peers)]
+        turned = jnp.concatenate(rows, axis=0).astype(jnp.float32).T
+        out[n * turned.shape[0] : (n + 1) * turned.shape[0]] = turned.astype(jnp.bfloat16)
+
+
+def arrange_weights(me, peers, amp_matrix, like_matrix):
+    slices, zbins = amp_matrix.shape
+    vmem = pl.BlockSpec(memory_space=pltpu.VMEM)
+    return pl.pallas_call(
+        functools.partial(weights_kernel, peers),
+        name="weights",
+        in_specs=[pl.BlockSpec(memory_space=pltpu.SMEM), vmem, vmem],
+        out_specs=vmem,
+        out_shape=pltpu.VMEM((2 * zbins, slices), jnp.bfloat16),
+        compiler_params=params(),
+        cost_estimate=cost(1, 1),
+    )(me, amp_matrix, like_matrix)
+
+
+def project(me, group, weights, parts, total, earlier):
+    inner, start, stop = group
+    rows = stop - start
     _, slices, cols = parts[0][0].shape
+    peers = len(parts)
+
+    def place(i, me):
+        upper = (me[0] == peers - 1) != (inner == 1)
+        return 0, i + jnp.where(upper, (total - REACH) // PAIR, 0) + start // PAIR
+
     zbins = weights.shape[0] // 2
     count = len(parts)
     shape = hbm((zbins, total * cols), jnp.bfloat16)
@@ -450,14 +485,14 @@
                 for _, start in parts
             ]
             + [anywhere()] * len(earlier),
-            out_specs=[pl.BlockSpec((zbins, PAIR * cols), lambda i, at: (0, i + at[0] // PAIR))] * 2
+            out_specs=[pl.BlockSpec((zbins, PAIR * cols), place)] * 2
             + [pl.BlockSpec((8, LANES), lambda i, at: (0, 0))],
         ),
         out_shape=[shape, shape, hbm((8, LANES), jnp.float32)],
         input_output_aliases={2 + count + i: i for i in range(len(earlier))},
         compiler_params=params(),
         cost_estimate=cost(1, 1),
-    )(place.reshape(1), weights, *[x for x, _ in parts], *earlier)
+    )(me, weights, *[x for x, _ in parts], *earlier)
 
 
 def gate_kernel(*refs):
@@ -495,20 +530,20 @@
     (6, INNER, None),
     (5, INNER, None),
     (7, INNER, 0),
-    (2, INNER, 1),
+    (2, INNER, 0),
     (4, HEAD, 1),
-    (3, INNER, 2),
+    (3, INNER, 1),
     (6, HEAD, 2),
-    (2, OUTER, 4),
+    (2, OUTER, 2),
     (5, HEAD, 3),
-    (1, INNER, 6),
+    (1, INNER, 4),
     (7, HEAD, 5),
     (3, OUTER, 6),
-    (1, OUTER, 10),
-    (4, TAIL, 7),
-    (6, TAIL, 9),
+    (1, OUTER, 7),
+    (4, TAIL, 9),
+    (6, TAIL, 10),
     (5, TAIL, 11),
-    (7, TAIL, 14),
+    (7, TAIL, 12),
 )
 
 
@@ -517,23 +552,20 @@
     peers = lax.axis_size("cuts")
     tiles = lax.axis_size("tile")
     block = rows // peers
-    me = lax.axis_index("cuts").astype(jnp.int32)
+    me = lax.axis_index("cuts").astype(jnp.int32).reshape(1)
 
     def swap(x, k):
         return lax.ppermute(x, "cuts", [(i, i ^ k) for i in range(peers)])
 
     own, first, last = masked_sums(density, valid)
     sums = [own] + [lax.ppermute(own, "tile", [(i, i ^ k) for i in range(tiles)]) for k in range(1, tiles)]
-    ready = make_ready(me ^ ORDER[0][0], density, valid, row_taps, col_taps, own)
+    ready = make_ready(me, ORDER[0][0], density, valid, row_taps, col_taps, own)
     mean, token = means(sums, slices, ready[0])
 
     made, arrived = {}, {}
 
     above = lax.ppermute(last, "tile", [(i, i + 1) for i in range(tiles - 1)])
     below = lax.ppermute(first, "tile", [(i + 1, i) for i in range(tiles - 1)])
-    def ids(wanted):
-        return jnp.stack([me ^ k for k, _ in wanted])
-
     def keep(wanted, got):
         for (k, cut), parts in zip(wanted, got):
             for piece, x in zip(cut, parts):
@@ -545,32 +577,29 @@
 
     after = ()
     for wanted in FIRST:
-        got = filter_inner(ids(wanted), [cut for _, cut in wanted], density, valid, ready, mean, *after)
+        got = filter_inner(me, wanted, density, valid, ready, mean, *after)
         keep(wanted, got)
         after = (resident(got[0][0]),)
     first_piece = ORDER[0][:2]
     send(*first_piece)
     got = filter_band(
-        ids(REST), [cut for _, cut in REST], density, valid, above, below, ready, mean, *after, resident(gate(token, arrived[first_piece], flops=BEFORE_BAND, space=pltpu.VMEM))
+        me, REST, density, valid, above, below, ready, mean, *after, resident(gate(token, arrived[first_piece], flops=BEFORE_BAND, space=pltpu.VMEM))
     )
     keep(REST, got)
     for piece in (INNER, OUTER):
         arrived[0, piece] = made[0, piece]
 
-    weights = jnp.concatenate([amp_matrix, like_matrix], axis=1).T.reshape(-1, peers, slices)
-    weights = weights[:, me ^ jnp.arange(peers)].reshape(-1, peers * slices)
+    weights = arrange_weights(me, peers, amp_matrix, like_matrix)
     result, tokens = [], []
 
     def finish(group):
-        inner, start, stop = group
-        place = jnp.where((me == peers - 1) != (inner == 1), block - REACH, 0) + start
         parts = []
         for k in range(peers):
             for piece in (group, INNER, OUTER):
-                if (k, piece) in arrived and piece[0] == inner:
-                    parts.append((arrived[k, piece], start - piece[1]))
+                if (k, piece) in arrived and piece[0] == group[0]:
+                    parts.append((arrived[k, piece], group[1] - piece[1]))
                     break
-        *result[:], token = project(place, weights, parts, stop - start, block, result)
+        *result[:], token = project(me, group, weights, parts, block, result)
         tokens.append(token)
 
     for at, (k, piece, wait) in enumerate(ORDER):

time: 117 us -> 112 us (0.957)
  waiting for transfers between devices: 9.58 us -> 39.2 us
  starting transfers between devices: 55.3 us -> 34.4 us
  local copies, waits for them, and re-layouts: 7.73 us -> 0.71 us
  Pallas kernels: 40.8 us -> 36.9 us
  other arithmetic: 1.58 us -> 0 us
    ppermute x18, waiting for transfers between devices: 9.03 us -> 34.3 us  [swap(): return lax.ppermute(x, 'cuts', [(i, i ^ k) for i in range(peers)])]
    ppermute x18, starting transfers between devices: 45.9 us -> 25.4 us  [swap(): return lax.ppermute(x, 'cuts', [(i, i ^ k) for i in range(peers)])]
    unnamed x22 -> x14, local copies, waits for them, and re-layouts: 4.67 us -> 0.71 us
    ppermute x1, waiting for transfers between devices: 0.23 us -> 3.87 us  [fast(): below = lax.ppermute(first, 'tile', [(i + 1, i) for i in range(tiles - 1)])]
    pallas_call x4 -> x5, Pallas kernels: 29.1 us -> 26.9 us  [the longest x1 16.1 us: filter_band(): pl.pallas_call(functools.partial(band_kernel, wanted), name='band', grid_...]
    gather x1 -> x0, local copies, waits for them, and re-layouts: 2.02 us -> none  [fast(): weights = weights[:, me ^ jnp.arange(peers)].reshape(-1, peers * slices)]
    pallas_call x3, Pallas kernels: 8.95 us -> 7.24 us  [project(): pl.pallas_call(functools.partial(project_kernel, count), name='project',...]
    concatenate x2 -> x0, other arithmetic: 1.49 us -> none  [the longest x1 1.41 us: fast(): jnp.concatenate([amp_matrix, like_matrix], axis=1)]
  transfers between devices with their start and end apart: 23 -> 23, of which waited for: 8 -> 8; matrix products, arithmetic and copies ran while one was open for 4% -> 0% of each run, Pallas kernels for 28% -> 27%
where the time goes in v12:
time: 112 us
  waiting for transfers between devices  39.2 us (35%)
  Pallas kernels  36.9 us (33%)
  starting transfers between devices  34.4 us (31%)
    ppermute x18, waiting for transfers between devices, swap(): return lax.ppermute(x, 'cuts', [(i, i ^ k) for i in range(peers)])  34.3 us
    ppermute x18, starting transfers between devices, swap(): return lax.ppermute(x, 'cuts', [(i, i ^ k) for i in range(peers)])  25.4 us
    pallas_call x1, Pallas kernels, filter_band(): pl.pallas_call(functools.partial(band_kernel, wanted), name='band', grid_...  16.1 us
    pallas_call x2, Pallas kernels, filter_inner(): pl.pallas_call(functools.partial(inner_kernel, wanted, loaded, rows // (h...  8.17 us
    pallas_call x3, Pallas kernels, project(): pl.pallas_call(functools.partial(project_kernel, count), name='project',...  7.24 us
    ppermute x3, starting transfers between devices, fast(): lax.ppermute(own, 'tile', [(i, i ^ k) for i in range(tiles)])  4.6 us
    ppermute x1, waiting for transfers between devices, fast(): below = lax.ppermute(first, 'tile', [(i + 1, i) for i in range(tiles - 1)])  3.87 us
    ppermute x1, starting transfers between devices, fast(): above = lax.ppermute(last, 'tile', [(i, i + 1) for i in range(tiles - 1)])  2.87 us
  transfers between devices with their start and end apart: 23, of which 8 were waited for; matrix products, arithmetic and copies ran while one was open for 0% of the time, Pallas kernels for 27%

profile of v12, /device:TPU:0, one launch (start us, length us, event | category | flops | bytes accessed | tf_op | source)
XLA Modules:
  0.0 111.9 jit_solution(432536005736953621)
XLA Ops:
  0.6 2.6 %sums.1 = (f32[24,128]{1,0:T(8,128)S(1)}, bf16[17,8,1024]{2,1,0:T(8,128)(2,1)S(1)}, bf16[17,8,1024]{2,1,0:T(8,128)(2,1)S(1)}) custom-call(bf16[16,128,1024]{2,1,0:T(8,128)(2,1)} %density.5, s32[128,1024]{1,0:T(8,128)} %valid.5), custom_call_target="tpu_custom_call" | custom-call | flops 1 | bytes 1 | tf_op jit(solution)/shard_map/sums/pallas_call | solution.py:154
  3.3 4.0 %collective-permute-start.4 = (f32[24,128]{1,0:T(8,128)S(1)}, f32[24,128]{1,0:T(8,128)S(1)}, u32[]{:S(2)}, u32[]{:S(2)}) collective-permute-start(f32[24,128]{1,0:T(8,128)S(1)} %get-tuple-element.39.after.refs_0_), channel_id=1, source_target_pairs={{0,24},{8,16},{16,8},{24,0},{1,25},{9,17},{17,9},{25,1},{2,26},{10... | collective-permute-start | bytes 36872 | tf_op jit(solution)/shard_map/ppermute | solution.py:561
  7.9 2.6 %ready.1 = (bf16[16,256,512]{2,1,0:T(8,128)(2,1)S(1)}, bf16[2,128,1024]{2,1,0:T(8,128)(2,1)S(1)}, bf16[1,16,32,1024]{3,2,1,0:T(8,128)(2,1)S(1)}, s32[1,32,1024]{2,1,0:T(8,128)S(1)}) custom-call(s32[1]{0:T(128)} %bitcast.me, bf16[16,128,1024]{2,1,0:T(8,128)(2,1)} %density.5, s32[128,1024]{1,0:T(8,128)} %valid.5, bf16[4,16,17]{2,1,0:T(8,128)(2,1)S(1)} %copy-done.4, ...), custom_call_target="tpu_custom_call" | custom-call | flops 1 | bytes 1 | tf_op jit(solution)/shard_map/ready/pallas_call | solution.py:225
  11.5 2.3 %inner.2.refs_5_ = bf16[8,16,1024]{2,1,0:T(8,128)(2,1)S(1)} custom-call(s32[1]{0:T(128)} %bitcast.me, bf16[1,16,32,1024]{3,2,1,0:T(8,128)(2,1)S(1)} %get-tuple-element.43.refs_0_, s32[1,32,1024]{2,1,0:T(8,128)S(1)} %get-tuple-element.44.refs_1_, bf16[16,256,512]{2,1,0:T(8,128)(2,1)S(1)} %get-tuple-element.40.refs_4_.refs_2_.col, ...), custom_call_target="tpu_custom_call" | custom-call | flops 1 | bytes 1 | tf_op jit(solution)/shard_map/inner/pallas_call | solution.py:284
  13.8 2.7 %collective-permute-start.5 = (bf16[8,16,1024]{2,1,0:T(8,128)(2,1)S(1)}, bf16[8,16,1024]{2,1,0:T(8,128)(2,1)S(1)}, u32[]{:S(2)}, u32[]{:S(2)}) collective-permute-start(bf16[8,16,1024]{2,1,0:T(8,128)(2,1)S(1)} %inner.2.refs_5_), channel_id=1, source_target_pairs={{0,4},{1,5},{2,6},{3,7},{4,0},{5,1},{6,2},{7,3},{8,12},{9,13},{10,... | collective-permute-start | bytes 786440 | tf_op jit(solution)/shard_map/ppermute | solution.py:558
  16.5 2.9 %collective-permute-start = (bf16[17,8,1024]{2,1,0:T(8,128)(2,1)S(1)}, bf16[17,8,1024]{2,1,0:T(8,128)(2,1)S(1)}, u32[]{:S(2)}, u32[]{:S(2)}) collective-permute-start(bf16[17,8,1024]{2,1,0:T(8,128)(2,1)S(1)} %get-tuple-element.37), channel_id=1, source_target_pairs={{0,8},{8,16},{16,24},{1,9},{9,17},{17,25},{2,10},{10,18},{18,26},{... | collective-permute-start | bytes 835592 | tf_op jit(solution)/shard_map/ppermute | solution.py:567
  19.3 1.5 %collective-permute-start.1 = (bf16[17,8,1024]{2,1,0:T(8,128)(2,1)S(1)}, bf16[17,8,1024]{2,1,0:T(8,128)(2,1)S(1)}, u32[]{:S(2)}, u32[]{:S(2)}) collective-permute-start(bf16[17,8,1024]{2,1,0:T(8,128)(2,1)S(1)} %get-tuple-element.38), channel_id=1, source_target_pairs={{8,0},{16,8},{24,16},{9,1},{17,9},{25,17},{10,2},{18,10},{26,18},{... | collective-permute-start | bytes 835592 | tf_op jit(solution)/shard_map/ppermute | solution.py:568
  20.8 5.9 %inner.3 = (bf16[8,16,1024]{2,1,0:T(8,128)(2,1)S(1)}, bf16[8,16,1024]{2,1,0:T(8,128)(2,1)S(1)}) custom-call(s32[1]{0:T(128)} %bitcast.me, bf16[16,128,1024]{2,1,0:T(8,128)(2,1)} %density.5, s32[128,1024]{1,0:T(8,128)} %valid.5, bf16[16,256,512]{2,1,0:T(8,128)(2,1)S(1)} %get-tuple-element.40.refs_4_.refs_2_.col, ...), custom_call_target="tpu_custom_call" | custom-call | flops 1 | bytes 1 | tf_op jit(solution)/shard_map/inner/pallas_call | solution.py:284
  26.7 1.4 %collective-permute-start.10 = (bf16[8,16,1024]{2,1,0:T(8,128)(2,1)S(1)}, bf16[8,16,1024]{2,1,0:T(8,128)(2,1)S(1)}, u32[]{:S(2)}, u32[]{:S(2)}) collective-permute-start(bf16[8,16,1024]{2,1,0:T(8,128)(2,1)S(1)} %get-tuple-element.45.refs_0_), channel_id=1, source_target_pairs={{0,6},{1,7},{2,4},{3,5},{4,2},{5,3},{6,0},{7,1},{8,14},{9,15},{10,... | collective-permute-start | bytes 786440 | tf_op jit(solution)/shard_map/ppermute | solution.py:558
  28.1 3.9 %collective-permute-done.1.below = bf16[17,8,1024]{2,1,0:T(8,128)(2,1)S(1)} collective-permute-done((bf16[17,8,1024]{2,1,0:T(8,128)(2,1)S(1)}, bf16[17,8,1024]{2,1,0:T(8,128)(2,1)S(1)}, u32[]{:S(2)}, u32[]{:S(2)}) %collective-permute-start.1) | collective-permute-done | bytes 278560 | tf_op jit(solution)/shard_map/ppermute | solution.py:568
  32.0 16.1 %band.1 = (bf16[6,16,1024]{2,1,0:T(8,128)(2,1)}, bf16[2,16,1024]{2,1,0:T(8,128)(2,1)}, bf16[8,16,1024]{2,1,0:T(8,128)(2,1)}, bf16[6,16,1024]{2,1,0:T(8,128)(2,1)...) custom-call(s32[1]{0:T(128)} %bitcast.me, ...), custom_call_target="tpu_custom_call" | custom-call | flops 1 | bytes 1 | tf_op jit(solution)/shard_map/band/pallas_call | solution.py:391
  48.5 1.6 %collective-permute-start.19 = (bf16[8,16,1024]{2,1,0:T(8,128)(2,1)}, bf16[8,16,1024]{2,1,0:T(8,128)(2,1)S(1)}, u32[]{:S(2)}, u32[]{:S(2)}) collective-permute-start(bf16[8,16,1024]{2,1,0:T(8,128)(2,1)} %gate.28), channel_id=1, source_target_pairs={{0,2},{1,3},{2,0},{3,1},{4,6},{5,7},{6,4},{7,5},{8,10},{9,11},{10,... | collective-permute-start | bytes 786440 | tf_op jit(solution)/shard_map/ppermute | solution.py:558
  50.2 3.5 %collective-permute-start.13 = (bf16[8,16,1024]{2,1,0:T(8,128)(2,1)}, bf16[8,16,1024]{2,1,0:T(8,128)(2,1)S(1)}, u32[]{:S(2)}, u32[]{:S(2)}) collective-permute-start(bf16[8,16,1024]{2,1,0:T(8,128)(2,1)} %gate.22), channel_id=1, source_target_pairs={{0,7},{1,6},{2,5},{3,4},{4,3},{5,2},{6,1},{7,0},{8,15},{9,14},{10,... | collective-permute-start | bytes 786440 | tf_op jit(solution)/shard_map/ppermute | solution.py:558
  53.6 2.3 %collective-permute-start.7 = (bf16[6,16,1024]{2,1,0:T(8,128)(2,1)}, bf16[6,16,1024]{2,1,0:T(8,128)(2,1)S(1)}, u32[]{:S(2)}, u32[]{:S(2)}) collective-permute-start(bf16[6,16,1024]{2,1,0:T(8,128)(2,1)} %gate.17), channel_id=1, source_target_pairs={{0,6},{1,7},{2,4},{3,5},{4,2},{5,3},{6,0},{7,1},{8,14},{9,15},{10,... | collective-permute-start | bytes 589832 | tf_op jit(solution)/shard_map/ppermute | solution.py:558
  55.9 4.8 %collective-permute-done.16.refs_1_.refs_4_ = bf16[6,16,1024]{2,1,0:T(8,128)(2,1)S(1)} collective-permute-done((bf16[6,16,1024]{2,1,0:T(8,128)(2,1)}, bf16[6,16,1024]{2,1,0:T(8,128)(2,1)S(1)}, u32[]{:S(2)}, u32[]{:S(2)}) %collective-permute-start.16) | collective-permute-done | bytes 196640 | tf_op jit(solution)/shard_map/ppermute | solution.py:558
  62.0 18.4 %collective-permute-done.19.refs_1_.refs_2_ = bf16[8,16,1024]{2,1,0:T(8,128)(2,1)S(1)} collective-permute-done((bf16[8,16,1024]{2,1,0:T(8,128)(2,1)}, bf16[8,16,1024]{2,1,0:T(8,128)(2,1)S(1)}, u32[]{:S(2)}, u32[]{:S(2)}) %collective-permute-start.19) | collective-permute-done | bytes 262176 | tf_op jit(solution)/shard_map/ppermute | solution.py:558
  80.5 5.0 %collective-permute-start.14 = (bf16[6,16,1024]{2,1,0:T(8,128)(2,1)}, bf16[6,16,1024]{2,1,0:T(8,128)(2,1)S(1)}, u32[]{:S(2)}, u32[]{:S(2)}) collective-permute-start(bf16[6,16,1024]{2,1,0:T(8,128)(2,1)} %gate.23), channel_id=1, source_target_pairs={{0,5},{1,4},{2,7},{3,6},{4,1},{5,0},{6,3},{7,2},{8,13},{9,12},{10,... | collective-permute-start | bytes 589832 | tf_op jit(solution)/shard_map/ppermute | solution.py:558
  86.3 6.6 %collective-permute-done.14.refs_1_.refs_5_ = bf16[6,16,1024]{2,1,0:T(8,128)(2,1)S(1)} collective-permute-done((bf16[6,16,1024]{2,1,0:T(8,128)(2,1)}, bf16[6,16,1024]{2,1,0:T(8,128)(2,1)S(1)}, u32[]{:S(2)}, u32[]{:S(2)}) %collective-permute-start.14) | collective-permute-done | bytes 196640 | tf_op jit(solution)/shard_map/ppermute | solution.py:558
  92.9 2.8 %collective-permute-start.18 = (bf16[2,16,1024]{2,1,0:T(8,128)(2,1)}, bf16[2,16,1024]{2,1,0:T(8,128)(2,1)S(1)}, u32[]{:S(2)}, u32[]{:S(2)}) collective-permute-start(bf16[2,16,1024]{2,1,0:T(8,128)(2,1)} %gate.27), channel_id=1, source_target_pairs={{0,5},{1,4},{2,7},{3,6},{4,1},{5,0},{6,3},{7,2},{8,13},{9,12},{10,... | collective-permute-start | bytes 196616 | tf_op jit(solution)/shard_map/ppermute | solution.py:558
  95.7 4.7 %collective-permute-start.22 = (bf16[2,16,1024]{2,1,0:T(8,128)(2,1)}, bf16[2,16,1024]{2,1,0:T(8,128)(2,1)S(1)}, u32[]{:S(2)}, u32[]{:S(2)}) collective-permute-start(bf16[2,16,1024]{2,1,0:T(8,128)(2,1)} %gate.31), channel_id=1, source_target_pairs={{0,7},{1,6},{2,5},{3,4},{4,3},{5,2},{6,1},{7,0},{8,15},{9,14},{10,... | collective-permute-start | bytes 196616 | tf_op jit(solution)/shard_map/ppermute | solution.py:558
  100.4 3.2 %project.3 = (bf16[128,16384]{1,0:T(8,128)(2,1)}, bf16[128,16384]{1,0:T(8,128)(2,1)}, f32[8,128]{1,0:T(8,128)}) custom-call(s32[1]{0:T(128)} %bitcast.me, bf16[256,128]{1,0:T(8,128)(2,1)S(1)} %weights.1, bf16[8,16,1024]{2,1,0:T(8,128)(2,1)S(1)} %copy-done.1, bf16[8,16,1024]{2,1,0:T(8,128)(2,1)S(1)} %collective-permute-done.20.refs_1_, ...), custom_call_target="tpu_custom_call" | custom-call | flops 1 | bytes 1 | tf_op jit(solution)/shard_map/project/pallas_call | solution.py:476
  104.5 2.7 %project.4 = (bf16[128,16384]{1,0:T(8,128)(2,1)}, bf16[128,16384]{1,0:T(8,128)(2,1)}, f32[8,128]{1,0:T(8,128)}) custom-call(s32[1]{0:T(128)} %bitcast.me, bf16[256,128]{1,0:T(8,128)(2,1)S(1)} %weights.1, bf16[8,16,1024]{2,1,0:T(8,128)(2,1)S(1)} %copy-done, ...), custom_call_target="tpu_custom_call", output_to_operand_aliasing={{0}: (10, {}), {1}: (11, {})} | custom-call | flops 1 | bytes 1 | tf_op jit(solution)/shard_map/project/pallas_call | solution.py:476
  107.3 3.3 %collective-permute-done.21.refs_6_ = bf16[2,16,1024]{2,1,0:T(8,128)(2,1)S(1)} collective-permute-done((bf16[2,16,1024]{2,1,0:T(8,128)(2,1)}, bf16[2,16,1024]{2,1,0:T(8,128)(2,1)S(1)}, u32[]{:S(2)}, u32[]{:S(2)}) %collective-permute-start.21) | collective-permute-done | bytes 65568 | tf_op jit(solution)/shard_map/ppermute | solution.py:558
  110.6 1.3 %project.5 = (bf16[128,16384]{1,0:T(8,128)(2,1)}, bf16[128,16384]{1,0:T(8,128)(2,1)}, f32[8,128]{1,0:T(8,128)}) custom-call(s32[1]{0:T(128)} %bitcast.me, bf16[256,128]{1,0:T(8,128)(2,1)S(1)} %weights.1, bf16[8,16,1024]{2,1,0:T(8,128)(2,1)S(1)} %copy-done, ...), custom_call_target="tpu_custom_call", output_to_operand_aliasing={{0}: (10, {}), {1}: (11, {})} | custom-call | flops 1 | bytes 1 | tf_op jit(solution)/shard_map/project/pallas_call | solution.py:476
  (62 shorter events, 5.3 us)
Async XLA Ops:
  3.3 7.2 %collective-permute-start.4 = (f32[24,128]{1,0:T(8,128)S(1)}, f32[24,128]{1,0:T(8,128)S(1)}, u32[]{:S(2)}, u32[]{:S(2)}) collective-permute-start(f32[24,128]{1,0:T(8,128)S(1)} %get-tuple-element.39.after.refs_0_), channel_id=1, source_target_pairs={{0,24},{8,16},{16,8},{24,0},{1,25},{9,17},{17,9},{25,1},{2,26},{10... | collective-permute-start | bytes 36872 | tf_op jit(solution)/shard_map/ppermute | solution.py:561
  7.2 3.7 %collective-permute-start.3 = (f32[24,128]{1,0:T(8,128)S(1)}, f32[24,128]{1,0:T(8,128)S(1)}, u32[]{:S(2)}, u32[]{:S(2)}) collective-permute-start(f32[24,128]{1,0:T(8,128)S(1)} %get-tuple-element.39.after.refs_0_), channel_id=1, source_target_pairs={{0,16},{8,24},{16,0},{24,8},{1,17},{9,25},{17,1},{25,9},{2,18},{10... | collective-permute-start | bytes 36872 | tf_op jit(solution)/shard_map/ppermute | solution.py:561
  7.7 3.7 %collective-permute-start.2 = (f32[24,128]{1,0:T(8,128)S(1)}, f32[24,128]{1,0:T(8,128)S(1)}, u32[]{:S(2)}, u32[]{:S(2)}) collective-permute-start(f32[24,128]{1,0:T(8,128)S(1)} %get-tuple-element.39.after.refs_0_), channel_id=1, source_target_pairs={{0,8},{8,0},{16,24},{24,16},{1,9},{9,1},{17,25},{25,17},{2,10},{10... | collective-permute-start | bytes 36872 | tf_op jit(solution)/shard_map/ppermute | solution.py:561
  13.8 14.3 %collective-permute-start.5 = (bf16[8,16,1024]{2,1,0:T(8,128)(2,1)S(1)}, bf16[8,16,1024]{2,1,0:T(8,128)(2,1)S(1)}, u32[]{:S(2)}, u32[]{:S(2)}) collective-permute-start(bf16[8,16,1024]{2,1,0:T(8,128)(2,1)S(1)} %inner.2.refs_5_), channel_id=1, source_target_pairs={{0,4},{1,5},{2,6},{3,7},{4,0},{5,1},{6,2},{7,3},{8,12},{9,13},{10,... | collective-permute-start | bytes 786440 | tf_op jit(solution)/shard_map/ppermute | solution.py:558
  16.5 11.7 %collective-permute-start = (bf16[17,8,1024]{2,1,0:T(8,128)(2,1)S(1)}, bf16[17,8,1024]{2,1,0:T(8,128)(2,1)S(1)}, u32[]{:S(2)}, u32[]{:S(2)}) collective-permute-start(bf16[17,8,1024]{2,1,0:T(8,128)(2,1)S(1)} %get-tuple-element.37), channel_id=1, source_target_pairs={{0,8},{8,16},{16,24},{1,9},{9,17},{17,25},{2,10},{10,18},{18,26},{... | collective-permute-start | bytes 835592 | tf_op jit(solution)/shard_map/ppermute | solution.py:567
  19.3 12.7 %collective-permute-start.1 = (bf16[17,8,1024]{2,1,0:T(8,128)(2,1)S(1)}, bf16[17,8,1024]{2,1,0:T(8,128)(2,1)S(1)}, u32[]{:S(2)}, u32[]{:S(2)}) collective-permute-start(bf16[17,8,1024]{2,1,0:T(8,128)(2,1)S(1)} %get-tuple-element.38), channel_id=1, source_target_pairs={{8,0},{16,8},{24,16},{9,1},{17,9},{25,17},{10,2},{18,10},{26,18},{... | collective-permute-start | bytes 835592 | tf_op jit(solution)/shard_map/ppermute | solution.py:568
  26.7 21.4 %collective-permute-start.10 = (bf16[8,16,1024]{2,1,0:T(8,128)(2,1)S(1)}, bf16[8,16,1024]{2,1,0:T(8,128)(2,1)S(1)}, u32[]{:S(2)}, u32[]{:S(2)}) collective-permute-start(bf16[8,16,1024]{2,1,0:T(8,128)(2,1)S(1)} %get-tuple-element.45.refs_0_), channel_id=1, source_target_pairs={{0,6},{1,7},{2,4},{3,5},{4,2},{5,3},{6,0},{7,1},{8,14},{9,15},{10,... | collective-permute-start | bytes 786440 | tf_op jit(solution)/shard_map/ppermute | solution.py:558
  28.1 25.5 %collective-permute-start.6 = (bf16[8,16,1024]{2,1,0:T(8,128)(2,1)S(1)}, bf16[8,16,1024]{2,1,0:T(8,128)(2,1)S(1)}, u32[]{:S(2)}, u32[]{:S(2)}) collective-permute-start(bf16[8,16,1024]{2,1,0:T(8,128)(2,1)S(1)} %get-tuple-element.50), channel_id=1, source_target_pairs={{0,5},{1,4},{2,7},{3,6},{4,1},{5,0},{6,3},{7,2},{8,13},{9,12},{10,... | collective-permute-start | bytes 786440 | tf_op jit(solution)/shard_map/ppermute | solution.py:558
  48.1 12.6 %collective-permute-start.16 = (bf16[6,16,1024]{2,1,0:T(8,128)(2,1)}, bf16[6,16,1024]{2,1,0:T(8,128)(2,1)S(1)}, u32[]{:S(2)}, u32[]{:S(2)}) collective-permute-start(bf16[6,16,1024]{2,1,0:T(8,128)(2,1)} %gate.25), channel_id=1, source_target_pairs={{0,4},{1,5},{2,6},{3,7},{4,0},{5,1},{6,2},{7,3},{8,12},{9,13},{10,... | collective-permute-start | bytes 589832 | tf_op jit(solution)/shard_map/ppermute | solution.py:558
  48.5 51.9 %copy-start.1 = (bf16[8,16,1024]{2,1,0:T(8,128)(2,1)S(1)}, bf16[8,16,1024]{2,1,0:T(8,128)(2,1)}, u32[]{:S(2)}) copy-start(bf16[8,16,1024]{2,1,0:T(8,128)(2,1)} %get-tuple-element.63.refs_0_) | copy-start | bytes 786436
  48.5 13.4 %collective-permute-start.11 = (bf16[8,16,1024]{2,1,0:T(8,128)(2,1)}, bf16[8,16,1024]{2,1,0:T(8,128)(2,1)S(1)}, u32[]{:S(2)}, u32[]{:S(2)}) collective-permute-start(bf16[8,16,1024]{2,1,0:T(8,128)(2,1)} %gate.20), channel_id=1, source_target_pairs={{0,3},{1,2},{2,1},{3,0},{4,7},{5,6},{6,5},{7,4},{8,11},{9,10},{10,... | collective-permute-start | bytes 786440 | tf_op jit(solution)/shard_map/ppermute | solution.py:558
  48.5 31.8 %collective-permute-start.19 = (bf16[8,16,1024]{2,1,0:T(8,128)(2,1)}, bf16[8,16,1024]{2,1,0:T(8,128)(2,1)S(1)}, u32[]{:S(2)}, u32[]{:S(2)}) collective-permute-start(bf16[8,16,1024]{2,1,0:T(8,128)(2,1)} %gate.28), channel_id=1, source_target_pairs={{0,2},{1,3},{2,0},{3,1},{4,6},{5,7},{6,4},{7,5},{8,10},{9,11},{10,... | collective-permute-start | bytes 786440 | tf_op jit(solution)/shard_map/ppermute | solution.py:558
  50.2 30.2 %collective-permute-start.13 = (bf16[8,16,1024]{2,1,0:T(8,128)(2,1)}, bf16[8,16,1024]{2,1,0:T(8,128)(2,1)S(1)}, u32[]{:S(2)}, u32[]{:S(2)}) collective-permute-start(bf16[8,16,1024]{2,1,0:T(8,128)(2,1)} %gate.22), channel_id=1, source_target_pairs={{0,7},{1,6},{2,5},{3,4},{4,3},{5,2},{6,1},{7,0},{8,15},{9,14},{10,... | collective-permute-start | bytes 786440 | tf_op jit(solution)/shard_map/ppermute | solution.py:558
  53.6 26.8 %collective-permute-start.7 = (bf16[6,16,1024]{2,1,0:T(8,128)(2,1)}, bf16[6,16,1024]{2,1,0:T(8,128)(2,1)S(1)}, u32[]{:S(2)}, u32[]{:S(2)}) collective-permute-start(bf16[6,16,1024]{2,1,0:T(8,128)(2,1)} %gate.17), channel_id=1, source_target_pairs={{0,6},{1,7},{2,4},{3,5},{4,2},{5,3},{6,0},{7,1},{8,14},{9,15},{10,... | collective-permute-start | bytes 589832 | tf_op jit(solution)/shard_map/ppermute | solution.py:558
  60.7 24.8 %collective-permute-start.17 = (bf16[6,16,1024]{2,1,0:T(8,128)(2,1)}, bf16[6,16,1024]{2,1,0:T(8,128)(2,1)S(1)}, u32[]{:S(2)}, u32[]{:S(2)}) collective-permute-start(bf16[6,16,1024]{2,1,0:T(8,128)(2,1)} %gate.26), channel_id=1, source_target_pairs={{0,7},{1,6},{2,5},{3,4},{4,3},{5,2},{6,1},{7,0},{8,15},{9,14},{10,... | collective-permute-start | bytes 589832 | tf_op jit(solution)/shard_map/ppermute | solution.py:558
  62.0 33.7 %collective-permute-start.12 = (bf16[8,16,1024]{2,1,0:T(8,128)(2,1)}, bf16[8,16,1024]{2,1,0:T(8,128)(2,1)S(1)}, u32[]{:S(2)}, u32[]{:S(2)}) collective-permute-start(bf16[8,16,1024]{2,1,0:T(8,128)(2,1)} %gate.21), channel_id=1, source_target_pairs={{0,3},{1,2},{2,1},{3,0},{4,7},{5,6},{6,5},{7,4},{8,11},{9,10},{10,... | collective-permute-start | bytes 786440 | tf_op jit(solution)/shard_map/ppermute | solution.py:558
  80.3 15.3 %collective-permute-start.20 = (bf16[8,16,1024]{2,1,0:T(8,128)(2,1)}, bf16[8,16,1024]{2,1,0:T(8,128)(2,1)S(1)}, u32[]{:S(2)}, u32[]{:S(2)}) collective-permute-start(bf16[8,16,1024]{2,1,0:T(8,128)(2,1)} %gate.29), channel_id=1, source_target_pairs={{0,1},{1,0},{2,3},{3,2},{4,5},{5,4},{6,7},{7,6},{8,9},{9,8},{10,11... | collective-permute-start | bytes 786440 | tf_op jit(solution)/shard_map/ppermute | solution.py:558
  80.4 23.9 %collective-permute-start.9 = (bf16[8,16,1024]{2,1,0:T(8,128)(2,1)}, bf16[8,16,1024]{2,1,0:T(8,128)(2,1)S(1)}, u32[]{:S(2)}, u32[]{:S(2)}) collective-permute-start(bf16[8,16,1024]{2,1,0:T(8,128)(2,1)} %gate.19), channel_id=1, source_target_pairs={{0,2},{1,3},{2,0},{3,1},{4,6},{5,7},{6,4},{7,5},{8,10},{9,11},{10,... | collective-permute-start | bytes 786440 | tf_op jit(solution)/shard_map/ppermute | solution.py:558
  80.5 12.5 %collective-permute-start.14 = (bf16[6,16,1024]{2,1,0:T(8,128)(2,1)}, bf16[6,16,1024]{2,1,0:T(8,128)(2,1)S(1)}, u32[]{:S(2)}, u32[]{:S(2)}) collective-permute-start(bf16[6,16,1024]{2,1,0:T(8,128)(2,1)} %gate.23), channel_id=1, source_target_pairs={{0,5},{1,4},{2,7},{3,6},{4,1},{5,0},{6,3},{7,2},{8,13},{9,12},{10,... | collective-permute-start | bytes 589832 | tf_op jit(solution)/shard_map/ppermute | solution.py:558
  85.5 19.0 %collective-permute-start.8 = (bf16[8,16,1024]{2,1,0:T(8,128)(2,1)}, bf16[8,16,1024]{2,1,0:T(8,128)(2,1)S(1)}, u32[]{:S(2)}, u32[]{:S(2)}) collective-permute-start(bf16[8,16,1024]{2,1,0:T(8,128)(2,1)} %gate.18), channel_id=1, source_target_pairs={{0,1},{1,0},{2,3},{3,2},{4,5},{5,4},{6,7},{7,6},{8,9},{9,8},{10,11... | collective-permute-start | bytes 786440 | tf_op jit(solution)/shard_map/ppermute | solution.py:558
  92.9 14.4 %collective-permute-start.18 = (bf16[2,16,1024]{2,1,0:T(8,128)(2,1)}, bf16[2,16,1024]{2,1,0:T(8,128)(2,1)S(1)}, u32[]{:S(2)}, u32[]{:S(2)}) collective-permute-start(bf16[2,16,1024]{2,1,0:T(8,128)(2,1)} %gate.27), channel_id=1, source_target_pairs={{0,5},{1,4},{2,7},{3,6},{4,1},{5,0},{6,3},{7,2},{8,13},{9,12},{10,... | collective-permute-start | bytes 196616 | tf_op jit(solution)/shard_map/ppermute | solution.py:558
  95.7 11.6 %collective-permute-start.15 = (bf16[2,16,1024]{2,1,0:T(8,128)(2,1)}, bf16[2,16,1024]{2,1,0:T(8,128)(2,1)S(1)}, u32[]{:S(2)}, u32[]{:S(2)}) collective-permute-start(bf16[2,16,1024]{2,1,0:T(8,128)(2,1)} %gate.24), channel_id=1, source_target_pairs={{0,4},{1,5},{2,6},{3,7},{4,0},{5,1},{6,2},{7,3},{8,12},{9,13},{10,... | collective-permute-start | bytes 196616 | tf_op jit(solution)/shard_map/ppermute | solution.py:558
  95.7 11.6 %collective-permute-start.22 = (bf16[2,16,1024]{2,1,0:T(8,128)(2,1)}, bf16[2,16,1024]{2,1,0:T(8,128)(2,1)S(1)}, u32[]{:S(2)}, u32[]{:S(2)}) collective-permute-start(bf16[2,16,1024]{2,1,0:T(8,128)(2,1)} %gate.31), channel_id=1, source_target_pairs={{0,7},{1,6},{2,5},{3,4},{4,3},{5,2},{6,1},{7,0},{8,15},{9,14},{10,... | collective-permute-start | bytes 196616 | tf_op jit(solution)/shard_map/ppermute | solution.py:558
  104.2 6.4 %collective-permute-start.21 = (bf16[2,16,1024]{2,1,0:T(8,128)(2,1)}, bf16[2,16,1024]{2,1,0:T(8,128)(2,1)S(1)}, u32[]{:S(2)}, u32[]{:S(2)}) collective-permute-start(bf16[2,16,1024]{2,1,0:T(8,128)(2,1)} %gate.30), channel_id=1, source_target_pairs={{0,6},{1,7},{2,4},{3,5},{4,2},{5,3},{6,0},{7,1},{8,14},{9,15},{10,... | collective-permute-start | bytes 196616 | tf_op jit(solution)/shard_map/ppermute | solution.py:558
  (6 other events, 142.3 us)

commit v13 on v12

--- a/solution.py
+++ b/solution.py
@@ -115,7 +115,7 @@
     return jnp.concatenate(parts, axis=1)
 
 
-def sums_kernel(density, valid, out, first, last, cube, plane, sems):
+def sums_kernel(density, valid, after, out, cube, plane, sems):
     slices, rows, cols = cube.shape
     step = rows // CHUNKS
 
@@ -142,21 +142,16 @@
         return 0
 
     lax.fori_loop(0, CHUNKS, body, 0)
-    first[:slices] = cube[:, :REACH]
-    first[slices] = plane[:REACH].astype(jnp.bfloat16)
-    last[:slices] = cube[:, rows - REACH :]
-    last[slices] = plane[rows - REACH :].astype(jnp.bfloat16)
-
-
-def masked_sums(density, valid):
+
+
+def masked_sums(density, valid, after):
     slices, rows, cols = density.shape
-    edge = pltpu.VMEM((slices + 1, REACH, cols), jnp.bfloat16)
     return pl.pallas_call(
         sums_kernel,
         name="sums",
-        in_specs=[anywhere()] * 2,
-        out_specs=[pl.BlockSpec(memory_space=pltpu.VMEM)] * 3,
-        out_shape=[pltpu.VMEM((slices + 8, LANES), jnp.float32), edge, edge],
+        in_specs=[anywhere()] * 3,
+        out_specs=pl.BlockSpec(memory_space=pltpu.VMEM),
+        out_shape=pltpu.VMEM((slices + 8, LANES), jnp.float32),
         scratch_shapes=[
             pltpu.VMEM(density.shape, jnp.bfloat16),
             pltpu.VMEM(valid.shape, jnp.int32),
@@ -164,16 +159,33 @@
         ],
         compiler_params=params(),
         cost_estimate=cost(1, 1),
-    )(held(density), held(valid))
+    )(held(density), held(valid), resident(after))
 
 
 def mean_kernel(*refs):
-    sums, (out, token) = refs[:4], refs[-2:]
+    sums, (out, token) = refs[:2], refs[-2:]
     slices = out.shape[0]
     token[...] = jnp.zeros_like(token)
-    total = sums[0][...] + sums[1][...] + sums[2][...] + sums[3][...]
+    total = sums[0][...] + sums[1][...]
     total = jnp.sum(total, axis=1, keepdims=True)
     out[...] = jnp.broadcast_to(total[:slices] / total[slices : slices + 1], out.shape)
+
+
+def add_kernel(one, two, out):
+    out[...] = one[...] + two[...]
+
+
+def add(one, two):
+    vmem = pl.BlockSpec(memory_space=pltpu.VMEM)
+    return pl.pallas_call(
+        add_kernel,
+        name="add",
+        in_specs=[vmem] * 2,
+        out_specs=vmem,
+        out_shape=pltpu.VMEM(one.shape, one.dtype),
+        compiler_params=params(),
+        cost_estimate=cost(1, 1),
+    )(one, two)
 
 
 def means(sums, slices, after):
@@ -205,57 +217,86 @@
     ]
 
 
-def ready_kernel(partner, me, density, valid, row_taps, col_taps, after, col, row, cube, plane, sems):
-    last = density.shape[1] * 2 // plane.shape[1] - 1
-    copies = window_copies(0, me[0] ^ partner, last, density, valid, cube, plane, sems)
+def ready_kernel(partner, me, density, valid, row_taps, col_taps, col, row, cube, plane, first, last, ends, masks, sems):
+    slices, rows, _ = density.shape
+    block = ends.shape[2]
+    copies = window_copies(0, me[0] ^ partner, rows // block - 1, density, valid, cube, plane, sems)
+    for n, start in enumerate((0, rows - block)):
+        copies.append(pltpu.make_async_copy(density.at[:, start : start + block], ends.at[n], sems.at[2 + 2 * n]))
+        copies.append(pltpu.make_async_copy(valid.at[start : start + block], masks.at[n], sems.at[3 + 2 * n]))
     for copy in copies:
         copy.start()
     build_columns(listed(col_taps), col)
     build_rows(listed(row_taps), row)
     for copy in copies:
         copy.wait()
-
-
-def make_ready(me, partner, density, valid, row_taps, col_taps, after):
+    first[:slices] = ends[0, :, :REACH]
+    first[slices] = masks[0, :REACH].astype(jnp.bfloat16)
+    last[:slices] = ends[1, :, block - REACH :]
+    last[slices] = masks[1, block - REACH :].astype(jnp.bfloat16)
+
+
+def make_ready(me, partner, density, valid, row_taps, col_taps):
     slices, rows, cols = density.shape
     terms = row_taps.shape[0]
     high = LANES // terms
+    block = high - HALO
     vmem = pl.BlockSpec(memory_space=pltpu.VMEM)
-    shapes = *matrix_shapes(terms, slices, high - HALO), (1, slices, high, cols)
+    edge = pltpu.VMEM((slices + 1, REACH, cols), jnp.bfloat16)
+    shapes = *matrix_shapes(terms, slices, block), (1, slices, high, cols)
     return pl.pallas_call(
         functools.partial(ready_kernel, partner),
         name="ready",
-        in_specs=[pl.BlockSpec(memory_space=pltpu.SMEM)] + [anywhere()] * 2 + [vmem] * 2 + [anywhere()],
-        out_specs=[vmem] * 4,
-        out_shape=[pltpu.VMEM(shape, jnp.bfloat16) for shape in shapes] + [pltpu.VMEM((1, high, cols), jnp.int32)],
-        scratch_shapes=[pltpu.SemaphoreType.DMA((2,))],
-        compiler_params=params(),
-        cost_estimate=cost(1, 1),
-    )(me, held(density), held(valid), row_taps, col_taps, after)
-
-
-def inner_kernel(wanted, loaded, end, me, *refs):
+        in_specs=[pl.BlockSpec(memory_space=pltpu.SMEM)] + [anywhere()] * 2 + [vmem] * 2,
+        out_specs=[vmem] * 6,
+        out_shape=[pltpu.VMEM(shape, jnp.bfloat16) for shape in shapes]
+        + [pltpu.VMEM((1, high, cols), jnp.int32), edge, edge],
+        scratch_shapes=[
+            pltpu.VMEM((2, slices, block, cols), jnp.bfloat16),
+            pltpu.VMEM((2, block, cols), jnp.int32),
+            pltpu.SemaphoreType.DMA((6,)),
+        ],
+        compiler_params=params(),
+        cost_estimate=cost(1, 1),
+    )(me, held(density), held(valid), row_taps, col_taps)
+
+
+def inner_kernel(wanted, loaded, own_mean, end, me, *refs):
     count = len(wanted)
-    pieces = [cut for _, cut in wanted]
     blocks = [me[0] ^ k for k, _ in wanted]
-    outs = sum(len(cut) for cut in pieces)
+    (first, second, col, row), refs = refs[:4], refs[4:]
+    mean = None if own_mean else refs[0]
+    results = sum(len(cut) for _, cut in wanted) + (1 if own_mean else 0)
     if loaded:
-        (cube, plane, col, row, mean), tall = refs[:5], refs[-1]
-        outs = list(refs[-1 - outs : -1])
+        cube, plane, tall = first, second, refs[-1]
+        outs = list(refs[-1 - results : -1])
     else:
-        (density, valid, col, row, mean), (tall, cube, plane, sems) = refs[:5], refs[-4:]
-        outs = list(refs[-4 - outs : -4])
-        copies = [window_copies(b, blocks[b], end, density, valid, cube, plane, sems) for b in range(count)]
+        tall, cube, plane, sems = refs[-4:]
+        outs = list(refs[-4 - results : -4])
+        copies = [window_copies(b, blocks[b], end, first, second, cube, plane, sems) for b in range(count)]
         for copy in sum(copies, []):
             copy.start()
-    for b, cut in enumerate(pieces):
+    for b, (_, cut) in enumerate(wanted):
         if not loaded:
             for copy in copies[b]:
                 copy.wait()
         last = blocks[b] == end
         mask = inner_rows(plane[b], last)
+        if own_mean:
+
+            def total(x):
+                x = x.reshape(x.shape[0] // 8, 8, x.shape[1]).sum(axis=0)
+                x = sum(x[:, c : c + LANES] for c in range(0, x.shape[1], LANES))
+                return jnp.sum(x, axis=0, keepdims=True)
+
+            sums = [total(mask * inner_rows(cube[b, s], last)) for s in range(cube.shape[1])]
+            sums = jnp.sum(jnp.concatenate(sums, axis=0), axis=1, keepdims=True)
+            centre = sums / jnp.sum(total(mask), axis=1, keepdims=True)
+            outs[-1][...] = jnp.broadcast_to(centre, outs[-1].shape)
+        else:
+            centre = mean[:, :1]
         field = convolve(
-            lambda s, b=b, last=last, mask=mask: mask * (inner_rows(cube[b, s], last) - mean[s : s + 1, :1]),
+            lambda s, b=b, last=last, mask=mask: mask * (inner_rows(cube[b, s], last) - centre[s : s + 1]),
             col,
             row,
             tall,
@@ -265,12 +306,12 @@
             outs.pop(0)[...] = field[start:stop]
 
 
-def filter_inner(me, wanted, density, valid, ready, mean, *after):
+def filter_inner(me, wanted, density, valid, ready, loaded, mean, *after):
     slices, rows, cols = density.shape
-    col, row, cube, plane = ready
+    col, row, cube, plane = ready[:4]
     high = plane.shape[1]
     count = len(wanted)
-    loaded = not after
+    own_mean = mean is None
     vmem = pl.BlockSpec(memory_space=pltpu.VMEM)
     shapes = [(stop - start, slices, cols) for _, cut in wanted for _, start, stop in cut]
     field = [resident(cube), resident(plane)] if loaded else [held(density), held(valid)]
@@ -281,28 +322,84 @@
             pltpu.VMEM((count, high, cols), jnp.int32),
             pltpu.SemaphoreType.DMA((2 * count,)),
         ]
+    means_in, means_out = ([], [pltpu.VMEM((slices, LANES), jnp.float32)]) if own_mean else ([mean], [])
     out = pl.pallas_call(
-        functools.partial(inner_kernel, wanted, loaded, rows // (high - HALO) - 1),
+        functools.partial(inner_kernel, wanted, loaded, own_mean, rows // (high - HALO) - 1),
         name="inner",
         in_specs=[pl.BlockSpec(memory_space=pltpu.SMEM)]
         + [vmem if loaded else anywhere()] * 2
-        + [vmem] * 3
+        + [vmem] * (2 + len(means_in))
         + [anywhere()] * len(after),
-        out_specs=[vmem] * len(shapes),
-        out_shape=[pltpu.VMEM(shape, jnp.bfloat16) for shape in shapes],
+        out_specs=[vmem] * (len(shapes) + len(means_out)),
+        out_shape=[pltpu.VMEM(shape, jnp.bfloat16) for shape in shapes] + means_out,
         scratch_shapes=scratch,
         compiler_params=params(),
         cost_estimate=cost(1, 1),
-    )(
-        me,
-        *field,
-        resident(col),
-        resident(row),
-        mean,
-        *after,
-    )
+    )(me, *field, resident(col), resident(row), *means_in, *after)
     out = list(out)
-    return [[out.pop(0) for _ in cut] for _, cut in wanted]
+    return [[out.pop(0) for _ in cut] for _, cut in wanted] + out
+
+
+def notes_kernel(mean, row_taps, col_taps, *refs):
+    terms, _, taps = row_taps.shape
+    count = len(refs) // 2
+    for centre, note in zip(refs[:count], refs[count:]):
+        note[...] = jnp.zeros_like(note)
+        note[:terms, :, :taps] = row_taps[...].astype(jnp.float32)
+        note[terms : 2 * terms, :, :taps] = col_taps[...].astype(jnp.float32)
+        note[2 * terms] = centre[...] - mean[...]
+
+
+def notes_of(mean, row_taps, col_taps, centres):
+    terms, slices, _ = row_taps.shape
+    vmem = pl.BlockSpec(memory_space=pltpu.VMEM)
+    return pl.pallas_call(
+        notes_kernel,
+        name="notes",
+        in_specs=[vmem] * (3 + len(centres)),
+        out_specs=[vmem] * len(centres),
+        out_shape=[hbm((2 * terms + 1, slices, LANES), jnp.float32)] * len(centres),
+        compiler_params=params(),
+        cost_estimate=cost(1, 1),
+    )(mean, row_taps, col_taps, *centres)
+
+
+def mend_kernel(end, me, valid, note, piece, out, col, row, tall, plane, sem):
+    terms = note.shape[0] // 2
+    high = plane.shape[0]
+    here = pl.ds(pl.multiple_of(jnp.minimum(me[0], end - 1) * (high // 2), high // 2), high)
+    copy = pltpu.make_async_copy(valid.at[here], plane, sem)
+    copy.start()
+    taps = [note[k, :, :TAPS].astype(jnp.bfloat16) for k in range(2 * terms)]
+    build_columns(taps[terms:], col)
+    build_rows(taps[:terms], row)
+    copy.wait()
+    mask = inner_rows(plane[...], me[0] == end)
+    field = convolve(lambda s: mask, col, row, tall, REACH)
+    shift = jnp.broadcast_to(note[2 * terms][:, :1], field.shape[1:])
+    out[...] = (piece[...].astype(jnp.float32) + shift[None] * field).astype(jnp.bfloat16)
+
+
+def mend(me, valid, note, piece):
+    rows, cols = valid.shape
+    terms, slices = note.shape[0] // 2, note.shape[1]
+    high = LANES // terms
+    vmem = pl.BlockSpec(memory_space=pltpu.VMEM)
+    return pl.pallas_call(
+        functools.partial(mend_kernel, rows // (high - HALO) - 1),
+        name="mend",
+        in_specs=[pl.BlockSpec(memory_space=pltpu.SMEM), anywhere(), vmem, vmem],
+        out_specs=vmem,
+        out_shape=pltpu.VMEM(piece.shape, jnp.bfloat16),
+        scratch_shapes=[pltpu.VMEM(shape, jnp.bfloat16) for shape in matrix_shapes(terms, slices, REACH)]
+        + [
+            pltpu.VMEM((GROUP * LANES, cols), jnp.bfloat16),
+            pltpu.VMEM((high, cols), jnp.int32),
+            pltpu.SemaphoreType.DMA,
+        ],
+        compiler_params=params(),
+        cost_estimate=cost(1, 1),
+    )(me, held(valid), note, piece)
 
 
 def band_kernel(wanted, me, density, valid, above, below, col, row, mean, *refs):
@@ -514,7 +611,7 @@
 
 INNER, OUTER = (1, 0, REACH), (0, 0, REACH)
 HEAD, TAIL = (0, 0, 6), (0, 6, REACH)
-FIRST = (((4, (INNER,)),), ((6, (INNER,)), (5, (INNER,))))
+EARLY = (4, 6)
 REST = (
     (5, (HEAD, TAIL)),
     (7, (INNER, HEAD, TAIL)),
@@ -545,6 +642,8 @@
     (5, TAIL, 11),
     (7, TAIL, 12),
 )
+NOTES, MENDED = 3, 14
+AFTER = 1
 
 
 def fast(density, valid, row_taps, col_taps, amp_matrix, like_matrix):
@@ -557,15 +656,8 @@
     def swap(x, k):
         return lax.ppermute(x, "cuts", [(i, i ^ k) for i in range(peers)])
 
-    own, first, last = masked_sums(density, valid)
-    sums = [own] + [lax.ppermute(own, "tile", [(i, i ^ k) for i in range(tiles)]) for k in range(1, tiles)]
-    ready = make_ready(me, ORDER[0][0], density, valid, row_taps, col_taps, own)
-    mean, token = means(sums, slices, ready[0])
-
     made, arrived = {}, {}
 
-    above = lax.ppermute(last, "tile", [(i, i + 1) for i in range(tiles - 1)])
-    below = lax.ppermute(first, "tile", [(i + 1, i) for i in range(tiles - 1)])
     def keep(wanted, got):
         for (k, cut), parts in zip(wanted, got):
             for piece, x in zip(cut, parts):
@@ -575,15 +667,32 @@
         x = made[k, piece]
         arrived[k, piece] = swap(gate(x, *before) if before else x, k)
 
-    after = ()
-    for wanted in FIRST:
-        got = filter_inner(me, wanted, density, valid, ready, mean, *after)
-        keep(wanted, got)
-        after = (resident(got[0][0]),)
+    ready = make_ready(me, EARLY[0], density, valid, row_taps, col_taps)
+    centres = []
+    for k in EARLY:
+        wanted = ((k, (INNER,)),)
+        got, centre = filter_inner(
+            me, wanted, density, valid, ready, not centres, None, *[resident(x) for x in centres]
+        )
+        keep(wanted, [got])
+        centres.append(centre)
+        send(k, INNER)
+    first, last = [gate(x, centres[0], space=pltpu.VMEM) for x in ready[4:]]
+    above = lax.ppermute(last, "tile", [(i, i + 1) for i in range(tiles - 1)])
+    below = lax.ppermute(first, "tile", [(i + 1, i) for i in range(tiles - 1)])
+    sums = [masked_sums(density, valid, centres[AFTER])]
+    for k in (1, 2):
+        if k == 2:
+            sums = [add(*sums)]
+        sums.append(lax.ppermute(sums[0], "tile", [(i, i ^ k) for i in range(tiles)]))
+    mean, token = means(sums, slices, centres[-1])
+    wanted = ((5, (INNER,)),)
+    got = filter_inner(me, wanted, density, valid, ready, False, mean)
+    keep(wanted, got)
     first_piece = ORDER[0][:2]
-    send(*first_piece)
     got = filter_band(
-        me, REST, density, valid, above, below, ready, mean, *after, resident(gate(token, arrived[first_piece], flops=BEFORE_BAND, space=pltpu.VMEM))
+        me, REST, density, valid, above, below, ready, mean, resident(made[5, INNER]),
+        resident(gate(token, arrived[first_piece], flops=BEFORE_BAND, space=pltpu.VMEM)),
     )
     keep(REST, got)
     for piece in (INNER, OUTER):
@@ -602,10 +711,18 @@
         *result[:], token = project(me, group, weights, parts, block, result)
         tokens.append(token)
 
+    notes = notes_of(mean, row_taps, col_taps, centres)
     for at, (k, piece, wait) in enumerate(ORDER):
+        if at == NOTES:
+            notes = [swap(gate(note, arrived[ORDER[0][:2]]), k) for k, note in zip(EARLY, notes)]
+        if at == MENDED:
+            for k_early, note in zip(EARLY, notes):
+                arrived[k_early, INNER] = mend(me, valid, note, arrived[k_early, INNER])
         if (k, piece) in arrived:
             continue
         before = [] if wait is None else [arrived[ORDER[wait][:2]]]
+        if at == MENDED:
+            before += [arrived[k_early, INNER] for k_early in EARLY]
         if at == len(ORDER) - 3:
             finish(INNER)
             before.append(tokens[0])

time: 112 us -> 130 us (1.16)
  Pallas kernels: 36.9 us -> 48.9 us
  starting transfers between devices: 34.4 us -> 37.1 us
  local copies, waits for them, and re-layouts: 0.71 us -> 2.14 us
    pallas_call x3 -> x8, Pallas kernels: 10.8 us -> 22.3 us  [the longest x3 10.1 us: filter_inner(): pl.pallas_call(functools.partial(inner_kernel, wanted, loaded, own_mean,...]
    ppermute x1, waiting for transfers between devices: 3.87 us -> 0.01 us  [fast(): below = lax.ppermute(first, 'tile', [(i + 1, i) for i in range(tiles - 1)])]
    ppermute x3 -> x2, waiting for transfers between devices: 0.96 us -> 3.57 us  [fast(): lax.ppermute(sums[0], 'tile', [(i, i ^ k) for i in range(tiles)])]
    ppermute x18 -> x20, waiting for transfers between devices: 34.3 us -> 36.5 us  [swap(): return lax.ppermute(x, 'cuts', [(i, i ^ k) for i in range(peers)])]
    ppermute x18 -> x20, starting transfers between devices: 25.4 us -> 27.1 us  [swap(): return lax.ppermute(x, 'cuts', [(i, i ^ k) for i in range(peers)])]
    unnamed x14 -> x18, local copies, waits for them, and re-layouts: 0.71 us -> 2.14 us
    ppermute x3 -> x2, starting transfers between devices: 4.6 us -> 5.4 us  [fast(): lax.ppermute(sums[0], 'tile', [(i, i ^ k) for i in range(tiles)])]
  transfers between devices with their start and end apart: 23 -> 24, of which waited for: 8 -> 7; matrix products, arithmetic and copies ran while one was open for 0% -> 0% of each run, Pallas kernels for 27% -> 32%
where the time goes in v13:
time: 130 us; the launch traced here: 129 us
  Pallas kernels  48.9 us (38%)
  waiting for transfers between devices  40.1 us (31%)
  starting transfers between devices  37.1 us (29%)
  local copies, waits for them, and re-layouts  2.14 us (2%)
    ppermute x20, waiting for transfers between devices, swap(): return lax.ppermute(x, 'cuts', [(i, i ^ k) for i in range(peers)])  36.5 us
    ppermute x20, starting transfers between devices, swap(): return lax.ppermute(x, 'cuts', [(i, i ^ k) for i in range(peers)])  27.1 us
    pallas_call x1, Pallas kernels, filter_band(): pl.pallas_call(functools.partial(band_kernel, wanted), name='band', grid_...  16.1 us
    pallas_call x3, Pallas kernels, filter_inner(): pl.pallas_call(functools.partial(inner_kernel, wanted, loaded, own_mean,...  10.1 us
    pallas_call x2, Pallas kernels, mend(): pl.pallas_call(functools.partial(mend_kernel, rows // (high - HALO) - 1),...  8.91 us
    pallas_call x3, Pallas kernels, project(): pl.pallas_call(functools.partial(project_kernel, count), name='project',...  7.29 us
    ppermute x2, starting transfers between devices, fast(): lax.ppermute(sums[0], 'tile', [(i, i ^ k) for i in range(tiles)])  5.4 us
    ppermute x2, waiting for transfers between devices, fast(): lax.ppermute(sums[0], 'tile', [(i, i ^ k) for i in range(tiles)])  3.57 us
  transfers between devices with their start and end apart: 24, of which 7 were waited for; matrix products, arithmetic and copies ran while one was open for 0% of the time, Pallas kernels for 32%

profile of v13, /device:TPU:0, one launch (start us, length us, event | category | flops | bytes accessed | tf_op | source)
XLA Modules:
  0.0 129.2 jit_solution(6012476164791258634)
XLA Ops:
  2.1 3.1 %ready.1 = (bf16[16,256,512]{2,1,0:T(8,128)(2,1)S(1)}, bf16[2,128,1024]{2,1,0:T(8,128)(2,1)S(1)}, bf16[1,16,32,1024]{3,2,1,0:T(8,128)(2,1)S(1)}, s32[1,32,1024]{...) custom-call(s32[1]{0:T(128)} %bitcast.me, bf16[16,128,1024]{2,1,0:T(8,128)(2,1)} %density.5, ...), custom_call_target="tpu_custom_call" | custom-call | flops 1 | bytes 1 | tf_op jit(solution)/shard_map/ready/pallas_call | solution.py:247
  5.1 2.6 %inner.3 = (bf16[8,16,1024]{2,1,0:T(8,128)(2,1)S(1)}, f32[16,128]{1,0:T(8,128)S(1)}) custom-call(s32[1]{0:T(128)} %bitcast.me, bf16[1,16,32,1024]{3,2,1,0:T(8,128)(2,1)S(1)} %get-tuple-element.41.refs_0_, s32[1,32,1024]{2,1,0:T(8,128)S(1)} %get-tuple-element.42.refs_1_, bf16[16,256,512]{2,1,0:T(8,128)(2,1)S(1)} %get-tuple-element.43.refs_2_.col, ...), custom_call_target="tpu_custom_call" | custom-call | flops 1 | bytes 1 | tf_op jit(solution)/shard_map/inner/pallas_call | solution.py:326
  7.8 4.1 %collective-permute-start.4 = (bf16[8,16,1024]{2,1,0:T(8,128)(2,1)S(1)}, bf16[8,16,1024]{2,1,0:T(8,128)(2,1)S(1)}, u32[]{:S(2)}, u32[]{:S(2)}) collective-permute-start(bf16[8,16,1024]{2,1,0:T(8,128)(2,1)S(1)} %get-tuple-element.50), channel_id=1, source_target_pairs={{0,4},{1,5},{2,6},{3,7},{4,0},{5,1},{6,2},{7,3},{8,12},{9,13},{10,... | collective-permute-start | bytes 786440 | tf_op jit(solution)/shard_map/ppermute | solution.py:657
  11.9 3.4 %collective-permute-start = (bf16[17,8,1024]{2,1,0:T(8,128)(2,1)S(1)}, bf16[17,8,1024]{2,1,0:T(8,128)(2,1)S(1)}, u32[]{:S(2)}, u32[]{:S(2)}) collective-permute-start(bf16[17,8,1024]{2,1,0:T(8,128)(2,1)S(1)} %gate.20), channel_id=1, source_target_pairs={{0,8},{8,16},{16,24},{1,9},{9,17},{17,25},{2,10},{10,18},{18,26},{... | collective-permute-start | bytes 835592 | tf_op jit(solution)/shard_map/ppermute | solution.py:681
  16.6 3.9 %inner.4 = (bf16[8,16,1024]{2,1,0:T(8,128)(2,1)S(1)}, f32[16,128]{1,0:T(8,128)S(1)}) custom-call(s32[1]{0:T(128)} %bitcast.me, bf16[16,128,1024]{2,1,0:T(8,128)(2,1)} %density.5, s32[128,1024]{1,0:T(8,128)} %valid.9, bf16[16,256,512]{2,1,0:T(8,128)(2,1)S(1)} %get-tuple-element.43.refs_2_.col, bf16[2,128,1024]{2,1,0:T(8,128)(2,1)S(1)} %get-tuple-element.44.refs_3_.row, ...), custom_call_target="tpu_custom_call" | custom-call | flops 1 | bytes 1 | tf_op jit(solution)/shard_map/inner/pallas_call | solution.py:326
  21.9 2.6 %sums.1.one = f32[24,128]{1,0:T(8,128)S(1)} custom-call(bf16[16,128,1024]{2,1,0:T(8,128)(2,1)} %density.5, s32[128,1024]{1,0:T(8,128)} %valid.9, f32[16,128]{1,0:T(8,128)S(1)} %get-tuple-element.47.after.refs_2_.refs_1_), custom_call_target="tpu_custom_call" | custom-call | flops 1 | bytes 1 | tf_op jit(solution)/shard_map/sums/pallas_call | solution.py:149
  24.4 2.7 %collective-permute-start.2 = (f32[24,128]{1,0:T(8,128)S(1)}, f32[24,128]{1,0:T(8,128)S(1)}, u32[]{:S(2)}, u32[]{:S(2)}) collective-permute-start(f32[24,128]{1,0:T(8,128)S(1)} %sums.1.one), channel_id=1, source_target_pairs={{0,8},{8,0},{16,24},{24,16},{1,9},{9,1},{17,25},{25,17},{2,10},{10... | collective-permute-start | bytes 36872 | tf_op jit(solution)/shard_map/ppermute | solution.py:687
  27.1 1.9 %collective-permute-done.2.two = f32[24,128]{1,0:T(8,128)S(1)} collective-permute-done((f32[24,128]{1,0:T(8,128)S(1)}, f32[24,128]{1,0:T(8,128)S(1)}, u32[]{:S(2)}, u32[]{:S(2)}) %collective-permute-start.2) | collective-permute-done | bytes 12320 | tf_op jit(solution)/shard_map/ppermute | solution.py:687
  29.0 2.7 %collective-permute-start.3 = (f32[24,128]{1,0:T(8,128)S(1)}, f32[24,128]{1,0:T(8,128)S(1)}, u32[]{:S(2)}, u32[]{:S(2)}) collective-permute-start(f32[24,128]{1,0:T(8,128)S(1)} %add.1.refs_0_), channel_id=1, source_target_pairs={{0,16},{8,24},{16,0},{24,8},{1,17},{9,25},{17,1},{25,9},{2,18},{10... | collective-permute-start | bytes 36872 | tf_op jit(solution)/shard_map/ppermute | solution.py:687
  31.7 1.7 %collective-permute-done.3.refs_1_ = f32[24,128]{1,0:T(8,128)S(1)} collective-permute-done((f32[24,128]{1,0:T(8,128)S(1)}, f32[24,128]{1,0:T(8,128)S(1)}, u32[]{:S(2)}, u32[]{:S(2)}) %collective-permute-start.3) | collective-permute-done | bytes 12320 | tf_op jit(solution)/shard_map/ppermute | solution.py:687
  33.5 3.6 %inner.5.refs_0_ = bf16[8,16,1024]{2,1,0:T(8,128)(2,1)S(1)} custom-call(s32[1]{0:T(128)} %bitcast.me, bf16[16,128,1024]{2,1,0:T(8,128)(2,1)} %density.5, s32[128,1024]{1,0:T(8,128)} %valid.9, bf16[16,256,512]{2,1,0:T(8,128)(2,1)S(1)} %get-tuple-element.43.refs_2_.col, bf16[2,128,1024]{2,1,0:T(8,128)(2,1)S(1)} %get-tuple-element.44.refs_3_.row, ...), custom_call_target="tpu_custom_call" | custom-call | flops 1 | bytes 1 | tf_op jit(solution)/shard_map/inner/pallas_call | solution.py:326
  37.3 16.1 %band.1 = (bf16[6,16,1024]{2,1,0:T(8,128)(2,1)}, bf16[2,16,1024]{2,1,0:T(8,128)(2,1)}, bf16[8,16,1024]{2,1,0:T(8,128)(2,1)}, bf16[6,16,1024]{2,1,0:T(8,128)(2,1)...) custom-call(s32[1]{0:T(128)} %bitcast.me, ...), custom_call_target="tpu_custom_call" | custom-call | flops 1 | bytes 1 | tf_op jit(solution)/shard_map/band/pallas_call | solution.py:488
  53.4 2.8 %collective-permute-start.10 = (bf16[8,16,1024]{2,1,0:T(8,128)(2,1)}, bf16[8,16,1024]{2,1,0:T(8,128)(2,1)S(1)}, u32[]{:S(2)}, u32[]{:S(2)}) collective-permute-start(bf16[8,16,1024]{2,1,0:T(8,128)(2,1)} %gate.26), channel_id=1, source_target_pairs={{0,3},{1,2},{2,1},{3,0},{4,7},{5,6},{6,5},{7,4},{8,11},{9,10},{10,... | collective-permute-start | bytes 786440 | tf_op jit(solution)/shard_map/ppermute | solution.py:657
  60.5 8.7 %collective-permute-done.17.refs_1_.refs_4_ = bf16[6,16,1024]{2,1,0:T(8,128)(2,1)S(1)} collective-permute-done((bf16[6,16,1024]{2,1,0:T(8,128)(2,1)}, bf16[6,16,1024]{2,1,0:T(8,128)(2,1)S(1)}, u32[]{:S(2)}, u32[]{:S(2)}) %collective-permute-start.17) | collective-permute-done | bytes 196640 | tf_op jit(solution)/shard_map/ppermute | solution.py:657
  69.2 18.6 %collective-permute-done.14.note = f32[9,16,128]{2,1,0:T(8,128)S(1)} collective-permute-done((f32[9,16,128]{2,1,0:T(8,128)}, f32[9,16,128]{2,1,0:T(8,128)S(1)}, u32[]{:S(2)}, u32[]{:S(2)}) %collective-permute-start.14) | collective-permute-done | bytes 73760 | tf_op jit(solution)/shard_map/ppermute | solution.py:657
  88.7 6.4 %collective-permute-done.15.note = f32[9,16,128]{2,1,0:T(8,128)S(1)} collective-permute-done((f32[9,16,128]{2,1,0:T(8,128)}, f32[9,16,128]{2,1,0:T(8,128)S(1)}, u32[]{:S(2)}, u32[]{:S(2)}) %collective-permute-start.15) | collective-permute-done | bytes 73760 | tf_op jit(solution)/shard_map/ppermute | solution.py:657
  95.1 2.7 %collective-permute-start.21 = (bf16[8,16,1024]{2,1,0:T(8,128)(2,1)}, bf16[8,16,1024]{2,1,0:T(8,128)(2,1)S(1)}, u32[]{:S(2)}, u32[]{:S(2)}) collective-permute-start(bf16[8,16,1024]{2,1,0:T(8,128)(2,1)} %gate.37), channel_id=1, source_target_pairs={{0,1},{1,0},{2,3},{3,2},{4,5},{5,4},{6,7},{7,6},{8,9},{9,8},{10,11... | collective-permute-start | bytes 786440 | tf_op jit(solution)/shard_map/ppermute | solution.py:657
  97.9 4.7 %collective-permute-start.8 = (bf16[8,16,1024]{2,1,0:T(8,128)(2,1)}, bf16[8,16,1024]{2,1,0:T(8,128)(2,1)S(1)}, u32[]{:S(2)}, u32[]{:S(2)}) collective-permute-start(bf16[8,16,1024]{2,1,0:T(8,128)(2,1)} %gate.25), channel_id=1, source_target_pairs={{0,2},{1,3},{2,0},{3,1},{4,6},{5,7},{6,4},{7,5},{8,10},{9,11},{10,... | collective-permute-start | bytes 786440 | tf_op jit(solution)/shard_map/ppermute | solution.py:657
  103.0 4.5 %mend.3.refs_3_.refs_6_ = bf16[8,16,1024]{2,1,0:T(8,128)(2,1)S(1)} custom-call(s32[1]{0:T(128)} %bitcast.me, s32[128,1024]{1,0:T(8,128)} %valid.9, f32[9,16,128]{2,1,0:T(8,128)S(1)} %collective-permute-done.15.note, bf16[8,16,1024]{2,1,0:T(8,128)(2,1)S(1)} %collective-permute-done.9.refs_1_.piece), custom_call_target="tpu_custom_call" | custom-call | flops 1 | bytes 1 | tf_op jit(solution)/shard_map/mend/pallas_call | solution.py:388
  107.5 4.5 %mend.2.refs_2_.refs_4_ = bf16[8,16,1024]{2,1,0:T(8,128)(2,1)S(1)} custom-call(s32[1]{0:T(128)} %bitcast.me, s32[128,1024]{1,0:T(8,128)} %valid.9, f32[9,16,128]{2,1,0:T(8,128)S(1)} %collective-permute-done.14.note, bf16[8,16,1024]{2,1,0:T(8,128)(2,1)S(1)} %collective-permute-done.4.refs_1_.piece), custom_call_target="tpu_custom_call" | custom-call | flops 1 | bytes 1 | tf_op jit(solution)/shard_map/mend/pallas_call | solution.py:388
  113.3 2.7 %collective-permute-start.19 = (bf16[2,16,1024]{2,1,0:T(8,128)(2,1)}, bf16[2,16,1024]{2,1,0:T(8,128)(2,1)S(1)}, u32[]{:S(2)}, u32[]{:S(2)}) collective-permute-start(bf16[2,16,1024]{2,1,0:T(8,128)(2,1)} %gate.35), channel_id=1, source_target_pairs={{0,5},{1,4},{2,7},{3,6},{4,1},{5,0},{6,3},{7,2},{8,13},{9,12},{10,... | collective-permute-start | bytes 196616 | tf_op jit(solution)/shard_map/ppermute | solution.py:657
  117.5 3.2 %project.3 = (bf16[128,16384]{1,0:T(8,128)(2,1)}, bf16[128,16384]{1,0:T(8,128)(2,1)}, f32[8,128]{1,0:T(8,128)}) custom-call(s32[1]{0:T(128)} %bitcast.me, bf16[256,128]{1,0:T(8,128)(2,1)S(1)} %weights.1, bf16[8,16,1024]{2,1,0:T(8,128)(2,1)S(1)} %copy-done.1, bf16[8,16,1024]{2,1,0:T(8,128)(2,1)S(1)} %collective-permute-done.21.refs_1_, ...), custom_call_target="tpu_custom_call" | custom-call | flops 1 | bytes 1 | tf_op jit(solution)/shard_map/project/pallas_call | solution.py:573
  121.3 2.3 %collective-permute-start.22 = (bf16[2,16,1024]{2,1,0:T(8,128)(2,1)}, bf16[2,16,1024]{2,1,0:T(8,128)(2,1)S(1)}, u32[]{:S(2)}, u32[]{:S(2)}) collective-permute-start(bf16[2,16,1024]{2,1,0:T(8,128)(2,1)} %gate.38), channel_id=1, source_target_pairs={{0,6},{1,7},{2,4},{3,5},{4,2},{5,3},{6,0},{7,1},{8,14},{9,15},{10,... | collective-permute-start | bytes 196616 | tf_op jit(solution)/shard_map/ppermute | solution.py:657
  123.6 2.8 %project.4 = (bf16[128,16384]{1,0:T(8,128)(2,1)}, bf16[128,16384]{1,0:T(8,128)(2,1)}, f32[8,128]{1,0:T(8,128)}) custom-call(s32[1]{0:T(128)} %bitcast.me, bf16[256,128]{1,0:T(8,128)(2,1)S(1)} %weights.1, bf16[8,16,1024]{2,1,0:T(8,128)(2,1)S(1)} %copy-done, ...), custom_call_target="tpu_custom_call", output_to_operand_aliasing={{0}: (10, {}), {1}: (11, {})} | custom-call | flops 1 | bytes 1 | tf_op jit(solution)/shard_map/project/pallas_call | solution.py:573
  (77 shorter events, 16.2 us)
Async XLA Ops:
  7.8 29.5 %collective-permute-start.4 = (bf16[8,16,1024]{2,1,0:T(8,128)(2,1)S(1)}, bf16[8,16,1024]{2,1,0:T(8,128)(2,1)S(1)}, u32[]{:S(2)}, u32[]{:S(2)}) collective-permute-start(bf16[8,16,1024]{2,1,0:T(8,128)(2,1)S(1)} %get-tuple-element.50), channel_id=1, source_target_pairs={{0,4},{1,5},{2,6},{3,7},{4,0},{5,1},{6,2},{7,3},{8,12},{9,13},{10,... | collective-permute-start | bytes 786440 | tf_op jit(solution)/shard_map/ppermute | solution.py:657
  11.9 25.4 %collective-permute-start = (bf16[17,8,1024]{2,1,0:T(8,128)(2,1)S(1)}, bf16[17,8,1024]{2,1,0:T(8,128)(2,1)S(1)}, u32[]{:S(2)}, u32[]{:S(2)}) collective-permute-start(bf16[17,8,1024]{2,1,0:T(8,128)(2,1)S(1)} %gate.20), channel_id=1, source_target_pairs={{0,8},{8,16},{16,24},{1,9},{9,17},{17,25},{2,10},{10,18},{18,26},{... | collective-permute-start | bytes 835592 | tf_op jit(solution)/shard_map/ppermute | solution.py:681
  15.3 22.0 %collective-permute-start.1 = (bf16[17,8,1024]{2,1,0:T(8,128)(2,1)S(1)}, bf16[17,8,1024]{2,1,0:T(8,128)(2,1)S(1)}, u32[]{:S(2)}, u32[]{:S(2)}) collective-permute-start(bf16[17,8,1024]{2,1,0:T(8,128)(2,1)S(1)} %gate.21), channel_id=1, source_target_pairs={{8,0},{16,8},{24,16},{9,1},{17,9},{25,17},{10,2},{18,10},{26,18},{... | collective-permute-start | bytes 835592 | tf_op jit(solution)/shard_map/ppermute | solution.py:682
  20.4 33.0 %collective-permute-start.9 = (bf16[8,16,1024]{2,1,0:T(8,128)(2,1)S(1)}, bf16[8,16,1024]{2,1,0:T(8,128)(2,1)S(1)}, u32[]{:S(2)}, u32[]{:S(2)}) collective-permute-start(bf16[8,16,1024]{2,1,0:T(8,128)(2,1)S(1)} %get-tuple-element.57), channel_id=1, source_target_pairs={{0,6},{1,7},{2,4},{3,5},{4,2},{5,3},{6,0},{7,1},{8,14},{9,15},{10,... | collective-permute-start | bytes 786440 | tf_op jit(solution)/shard_map/ppermute | solution.py:657
  24.4 4.6 %collective-permute-start.2 = (f32[24,128]{1,0:T(8,128)S(1)}, f32[24,128]{1,0:T(8,128)S(1)}, u32[]{:S(2)}, u32[]{:S(2)}) collective-permute-start(f32[24,128]{1,0:T(8,128)S(1)} %sums.1.one), channel_id=1, source_target_pairs={{0,8},{8,0},{16,24},{24,16},{1,9},{9,1},{17,25},{25,17},{2,10},{10... | collective-permute-start | bytes 36872 | tf_op jit(solution)/shard_map/ppermute | solution.py:687
  29.0 4.4 %collective-permute-start.3 = (f32[24,128]{1,0:T(8,128)S(1)}, f32[24,128]{1,0:T(8,128)S(1)}, u32[]{:S(2)}, u32[]{:S(2)}) collective-permute-start(f32[24,128]{1,0:T(8,128)S(1)} %add.1.refs_0_), channel_id=1, source_target_pairs={{0,16},{8,24},{16,0},{24,8},{1,17},{9,25},{17,1},{25,9},{2,18},{10... | collective-permute-start | bytes 36872 | tf_op jit(solution)/shard_map/ppermute | solution.py:687
  37.2 22.3 %collective-permute-start.5 = (bf16[8,16,1024]{2,1,0:T(8,128)(2,1)S(1)}, bf16[8,16,1024]{2,1,0:T(8,128)(2,1)S(1)}, u32[]{:S(2)}, u32[]{:S(2)}) collective-permute-start(bf16[8,16,1024]{2,1,0:T(8,128)(2,1)S(1)} %inner.5.refs_0_), channel_id=1, source_target_pairs={{0,5},{1,4},{2,7},{3,6},{4,1},{5,0},{6,3},{7,2},{8,13},{9,12},{10,... | collective-permute-start | bytes 786440 | tf_op jit(solution)/shard_map/ppermute | solution.py:657
  53.4 34.4 %collective-permute-start.10 = (bf16[8,16,1024]{2,1,0:T(8,128)(2,1)}, bf16[8,16,1024]{2,1,0:T(8,128)(2,1)S(1)}, u32[]{:S(2)}, u32[]{:S(2)}) collective-permute-start(bf16[8,16,1024]{2,1,0:T(8,128)(2,1)} %gate.26), channel_id=1, source_target_pairs={{0,3},{1,2},{2,1},{3,0},{4,7},{5,6},{6,5},{7,4},{8,11},{9,10},{10,... | collective-permute-start | bytes 786440 | tf_op jit(solution)/shard_map/ppermute | solution.py:657
  56.2 13.0 %collective-permute-start.17 = (bf16[6,16,1024]{2,1,0:T(8,128)(2,1)}, bf16[6,16,1024]{2,1,0:T(8,128)(2,1)S(1)}, u32[]{:S(2)}, u32[]{:S(2)}) collective-permute-start(bf16[6,16,1024]{2,1,0:T(8,128)(2,1)} %gate.33), channel_id=1, source_target_pairs={{0,4},{1,5},{2,6},{3,7},{4,0},{5,1},{6,2},{7,3},{8,12},{9,13},{10,... | collective-permute-start | bytes 589832 | tf_op jit(solution)/shard_map/ppermute | solution.py:657
  57.0 31.7 %collective-permute-start.20 = (bf16[8,16,1024]{2,1,0:T(8,128)(2,1)}, bf16[8,16,1024]{2,1,0:T(8,128)(2,1)S(1)}, u32[]{:S(2)}, u32[]{:S(2)}) collective-permute-start(bf16[8,16,1024]{2,1,0:T(8,128)(2,1)} %gate.36), channel_id=1, source_target_pairs={{0,2},{1,3},{2,0},{3,1},{4,6},{5,7},{6,4},{7,5},{8,10},{9,11},{10,... | collective-permute-start | bytes 786440 | tf_op jit(solution)/shard_map/ppermute | solution.py:657
  58.1 39.7 %collective-permute-start.12 = (bf16[8,16,1024]{2,1,0:T(8,128)(2,1)}, bf16[8,16,1024]{2,1,0:T(8,128)(2,1)S(1)}, u32[]{:S(2)}, u32[]{:S(2)}) collective-permute-start(bf16[8,16,1024]{2,1,0:T(8,128)(2,1)} %gate.28), channel_id=1, source_target_pairs={{0,7},{1,6},{2,5},{3,4},{4,3},{5,2},{6,1},{7,0},{8,15},{9,14},{10,... | collective-permute-start | bytes 786440 | tf_op jit(solution)/shard_map/ppermute | solution.py:657
  59.5 28.3 %collective-permute-start.14 = (f32[9,16,128]{2,1,0:T(8,128)}, f32[9,16,128]{2,1,0:T(8,128)S(1)}, u32[]{:S(2)}, u32[]{:S(2)}) collective-permute-start(f32[9,16,128]{2,1,0:T(8,128)} %gate.30), channel_id=1, source_target_pairs={{0,4},{1,5},{2,6},{3,7},{4,0},{5,1},{6,2},{7,3},{8,12},{9,13},{10,... | collective-permute-start | bytes 221192 | tf_op jit(solution)/shard_map/ppermute | solution.py:657
  69.2 33.4 %collective-permute-start.6 = (bf16[6,16,1024]{2,1,0:T(8,128)(2,1)}, bf16[6,16,1024]{2,1,0:T(8,128)(2,1)S(1)}, u32[]{:S(2)}, u32[]{:S(2)}) collective-permute-start(bf16[6,16,1024]{2,1,0:T(8,128)(2,1)} %gate.23), channel_id=1, source_target_pairs={{0,6},{1,7},{2,4},{3,5},{4,2},{5,3},{6,0},{7,1},{8,14},{9,15},{10,... | collective-permute-start | bytes 589832 | tf_op jit(solution)/shard_map/ppermute | solution.py:657
  87.8 15.0 %collective-permute-start.18 = (bf16[6,16,1024]{2,1,0:T(8,128)(2,1)}, bf16[6,16,1024]{2,1,0:T(8,128)(2,1)S(1)}, u32[]{:S(2)}, u32[]{:S(2)}) collective-permute-start(bf16[6,16,1024]{2,1,0:T(8,128)(2,1)} %gate.34), channel_id=1, source_target_pairs={{0,7},{1,6},{2,5},{3,4},{4,3},{5,2},{6,1},{7,0},{8,15},{9,14},{10,... | collective-permute-start | bytes 589832 | tf_op jit(solution)/shard_map/ppermute | solution.py:657
  87.8 7.3 %collective-permute-start.15 = (f32[9,16,128]{2,1,0:T(8,128)}, f32[9,16,128]{2,1,0:T(8,128)S(1)}, u32[]{:S(2)}, u32[]{:S(2)}) collective-permute-start(f32[9,16,128]{2,1,0:T(8,128)} %gate.31), channel_id=1, source_target_pairs={{0,6},{1,7},{2,4},{3,5},{4,2},{5,3},{6,0},{7,1},{8,14},{9,15},{10,... | collective-permute-start | bytes 221192 | tf_op jit(solution)/shard_map/ppermute | solution.py:657
  88.7 27.3 %collective-permute-start.11 = (bf16[8,16,1024]{2,1,0:T(8,128)(2,1)}, bf16[8,16,1024]{2,1,0:T(8,128)(2,1)S(1)}, u32[]{:S(2)}, u32[]{:S(2)}) collective-permute-start(bf16[8,16,1024]{2,1,0:T(8,128)(2,1)} %gate.27), channel_id=1, source_target_pairs={{0,3},{1,2},{2,1},{3,0},{4,7},{5,6},{6,5},{7,4},{8,11},{9,10},{10,... | collective-permute-start | bytes 786440 | tf_op jit(solution)/shard_map/ppermute | solution.py:657
  95.1 21.1 %collective-permute-start.21 = (bf16[8,16,1024]{2,1,0:T(8,128)(2,1)}, bf16[8,16,1024]{2,1,0:T(8,128)(2,1)S(1)}, u32[]{:S(2)}, u32[]{:S(2)}) collective-permute-start(bf16[8,16,1024]{2,1,0:T(8,128)(2,1)} %gate.37), channel_id=1, source_target_pairs={{0,1},{1,0},{2,3},{3,2},{4,5},{5,4},{6,7},{7,6},{8,9},{9,8},{10,11... | collective-permute-start | bytes 786440 | tf_op jit(solution)/shard_map/ppermute | solution.py:657
  97.9 23.5 %collective-permute-start.8 = (bf16[8,16,1024]{2,1,0:T(8,128)(2,1)}, bf16[8,16,1024]{2,1,0:T(8,128)(2,1)S(1)}, u32[]{:S(2)}, u32[]{:S(2)}) collective-permute-start(bf16[8,16,1024]{2,1,0:T(8,128)(2,1)} %gate.25), channel_id=1, source_target_pairs={{0,2},{1,3},{2,0},{3,1},{4,6},{5,7},{6,4},{7,5},{8,10},{9,11},{10,... | collective-permute-start | bytes 786440 | tf_op jit(solution)/shard_map/ppermute | solution.py:657
  102.6 10.7 %collective-permute-start.13 = (bf16[6,16,1024]{2,1,0:T(8,128)(2,1)}, bf16[6,16,1024]{2,1,0:T(8,128)(2,1)S(1)}, u32[]{:S(2)}, u32[]{:S(2)}) collective-permute-start(bf16[6,16,1024]{2,1,0:T(8,128)(2,1)} %gate.29), channel_id=1, source_target_pairs={{0,5},{1,4},{2,7},{3,6},{4,1},{5,0},{6,3},{7,2},{8,13},{9,12},{10,... | collective-permute-start | bytes 589832 | tf_op jit(solution)/shard_map/ppermute | solution.py:657
  102.8 20.8 %collective-permute-start.7 = (bf16[8,16,1024]{2,1,0:T(8,128)(2,1)}, bf16[8,16,1024]{2,1,0:T(8,128)(2,1)S(1)}, u32[]{:S(2)}, u32[]{:S(2)}) collective-permute-start(bf16[8,16,1024]{2,1,0:T(8,128)(2,1)} %gate.24), channel_id=1, source_target_pairs={{0,1},{1,0},{2,3},{3,2},{4,5},{5,4},{6,7},{7,6},{8,9},{9,8},{10,11... | collective-permute-start | bytes 786440 | tf_op jit(solution)/shard_map/ppermute | solution.py:657
  113.3 13.1 %collective-permute-start.19 = (bf16[2,16,1024]{2,1,0:T(8,128)(2,1)}, bf16[2,16,1024]{2,1,0:T(8,128)(2,1)S(1)}, u32[]{:S(2)}, u32[]{:S(2)}) collective-permute-start(bf16[2,16,1024]{2,1,0:T(8,128)(2,1)} %gate.35), channel_id=1, source_target_pairs={{0,5},{1,4},{2,7},{3,6},{4,1},{5,0},{6,3},{7,2},{8,13},{9,12},{10,... | collective-permute-start | bytes 196616 | tf_op jit(solution)/shard_map/ppermute | solution.py:657
  116.0 10.4 %collective-permute-start.16 = (bf16[2,16,1024]{2,1,0:T(8,128)(2,1)}, bf16[2,16,1024]{2,1,0:T(8,128)(2,1)S(1)}, u32[]{:S(2)}, u32[]{:S(2)}) collective-permute-start(bf16[2,16,1024]{2,1,0:T(8,128)(2,1)} %gate.32), channel_id=1, source_target_pairs={{0,4},{1,5},{2,6},{3,7},{4,0},{5,1},{6,2},{7,3},{8,12},{9,13},{10,... | collective-permute-start | bytes 196616 | tf_op jit(solution)/shard_map/ppermute | solution.py:657
  116.2 10.2 %collective-permute-start.23 = (bf16[2,16,1024]{2,1,0:T(8,128)(2,1)}, bf16[2,16,1024]{2,1,0:T(8,128)(2,1)S(1)}, u32[]{:S(2)}, u32[]{:S(2)}) collective-permute-start(bf16[2,16,1024]{2,1,0:T(8,128)(2,1)} %gate.39), channel_id=1, source_target_pairs={{0,7},{1,6},{2,5},{3,4},{4,3},{5,2},{6,1},{7,0},{8,15},{9,14},{10,... | collective-permute-start | bytes 196616 | tf_op jit(solution)/shard_map/ppermute | solution.py:657
  121.3 6.5 %collective-permute-start.22 = (bf16[2,16,1024]{2,1,0:T(8,128)(2,1)}, bf16[2,16,1024]{2,1,0:T(8,128)(2,1)S(1)}, u32[]{:S(2)}, u32[]{:S(2)}) collective-permute-start(bf16[2,16,1024]{2,1,0:T(8,128)(2,1)} %gate.38), channel_id=1, source_target_pairs={{0,6},{1,7},{2,4},{3,5},{4,2},{5,3},{6,0},{7,1},{8,14},{9,15},{10,... | collective-permute-start | bytes 196616 | tf_op jit(solution)/shard_map/ppermute | solution.py:657
  (9 other events, 218.2 us)

commit v14 on v13

--- a/solution.py
+++ b/solution.py
@@ -14,7 +14,7 @@
 PER = 4
 PAIR = 2
 CHUNKS = 8
-BEFORE_BAND = 2e9
+BEFORE_BAND = 1e9
 MIB = 1024 * 1024
 HALO = 2 * REACH
 
@@ -614,7 +614,7 @@
 EARLY = (4, 6)
 REST = (
     (5, (HEAD, TAIL)),
-    (7, (INNER, HEAD, TAIL)),
+    (7, (HEAD, TAIL)),
     (2, (INNER, OUTER)),
     (3, (INNER, OUTER)),
     (4, (HEAD, TAIL)),
@@ -626,14 +626,14 @@
     (4, INNER, None),
     (6, INNER, None),
     (5, INNER, None),
-    (7, INNER, 0),
+    (7, INNER, None),
     (2, INNER, 0),
     (4, HEAD, 1),
     (3, INNER, 1),
-    (6, HEAD, 2),
-    (2, OUTER, 2),
-    (5, HEAD, 3),
-    (1, INNER, 4),
+    (6, HEAD, (2, 3)),
+    (2, OUTER, 4),
+    (5, HEAD, 5),
+    (1, INNER, 6),
     (7, HEAD, 5),
     (3, OUTER, 6),
     (1, OUTER, 7),
@@ -642,7 +642,7 @@
     (5, TAIL, 11),
     (7, TAIL, 12),
 )
-NOTES, MENDED = 3, 14
+MENDED = 11
 AFTER = 1
 
 
@@ -686,13 +686,15 @@
             sums = [add(*sums)]
         sums.append(lax.ppermute(sums[0], "tile", [(i, i ^ k) for i in range(tiles)]))
     mean, token = means(sums, slices, centres[-1])
-    wanted = ((5, (INNER,)),)
-    got = filter_inner(me, wanted, density, valid, ready, False, mean)
+    notes = notes_of(mean, row_taps, col_taps, centres)
+    notes = [swap(note, k) for k, note in zip(EARLY, notes)]
+    wanted = ((5, (INNER,)), (7, (INNER,)))
+    token = gate(token, arrived[4, INNER], flops=BEFORE_BAND, space=pltpu.VMEM)
+    got = filter_inner(me, wanted, density, valid, ready, False, mean, above, below, resident(token))
     keep(wanted, got)
-    first_piece = ORDER[0][:2]
+    token = gate(token, *notes, space=pltpu.VMEM)
     got = filter_band(
-        me, REST, density, valid, above, below, ready, mean, resident(made[5, INNER]),
-        resident(gate(token, arrived[first_piece], flops=BEFORE_BAND, space=pltpu.VMEM)),
+        me, REST, density, valid, above, below, ready, mean, resident(made[5, INNER]), resident(token)
     )
     keep(REST, got)
     for piece in (INNER, OUTER):
@@ -711,16 +713,14 @@
         *result[:], token = project(me, group, weights, parts, block, result)
         tokens.append(token)
 
-    notes = notes_of(mean, row_taps, col_taps, centres)
     for at, (k, piece, wait) in enumerate(ORDER):
-        if at == NOTES:
-            notes = [swap(gate(note, arrived[ORDER[0][:2]]), k) for k, note in zip(EARLY, notes)]
         if at == MENDED:
             for k_early, note in zip(EARLY, notes):
                 arrived[k_early, INNER] = mend(me, valid, note, arrived[k_early, INNER])
         if (k, piece) in arrived:
             continue
-        before = [] if wait is None else [arrived[ORDER[wait][:2]]]
+        waits = wait if isinstance(wait, tuple) else () if wait is None else (wait,)
+        before = [arrived[ORDER[n][:2]] for n in waits]
         if at == MENDED:
             before += [arrived[k_early, INNER] for k_early in EARLY]
         if at == len(ORDER) - 3:

time: 130 us -> 129 us (level)
  waiting for transfers between devices: 40.1 us -> 26.8 us
  starting transfers between devices: 37.1 us -> 47.7 us
  Pallas kernels: 48.9 us -> 51.2 us
    ppermute x20, waiting for transfers between devices: 36.5 us -> 23.4 us  [swap(): return lax.ppermute(x, 'cuts', [(i, i ^ k) for i in range(peers)])]
    ppermute x20, starting transfers between devices: 27.1 us -> 37.2 us  [swap(): return lax.ppermute(x, 'cuts', [(i, i ^ k) for i in range(peers)])]
    pallas_call x3, Pallas kernels: 10.1 us -> 12.4 us  [filter_inner(): pl.pallas_call(functools.partial(inner_kernel, wanted, loaded, own_mean,...]
  transfers between devices with their start and end apart: 24 -> 24, of which waited for: 7 -> 8; matrix products, arithmetic and copies ran while one was open for 0% -> 0% of each run, Pallas kernels for 32% -> 34%
where the time goes in v14:
time: 129 us
  Pallas kernels  51.2 us (40%)
  starting transfers between devices  47.7 us (37%)
  waiting for transfers between devices  26.8 us (21%)
  local copies, waits for them, and re-layouts  2.13 us (2%)
    ppermute x20, starting transfers between devices, swap(): return lax.ppermute(x, 'cuts', [(i, i ^ k) for i in range(peers)])  37.2 us
    ppermute x20, waiting for transfers between devices, swap(): return lax.ppermute(x, 'cuts', [(i, i ^ k) for i in range(peers)])  23.4 us
    pallas_call x1, Pallas kernels, filter_band(): pl.pallas_call(functools.partial(band_kernel, wanted), name='band', grid_...  16.1 us
    pallas_call x3, Pallas kernels, filter_inner(): pl.pallas_call(functools.partial(inner_kernel, wanted, loaded, own_mean,...  12.4 us
    pallas_call x2, Pallas kernels, mend(): pl.pallas_call(functools.partial(mend_kernel, rows // (high - HALO) - 1),...  8.91 us
    pallas_call x3, Pallas kernels, project(): pl.pallas_call(functools.partial(project_kernel, count), name='project',...  7.28 us
    ppermute x2, starting transfers between devices, fast(): lax.ppermute(sums[0], 'tile', [(i, i ^ k) for i in range(tiles)])  5.62 us
    ppermute x1, starting transfers between devices, fast(): above = lax.ppermute(last, 'tile', [(i, i + 1) for i in range(tiles - 1)])  3.4 us
  transfers between devices with their start and end apart: 24, of which 8 were waited for; matrix products, arithmetic and copies ran while one was open for 0% of the time, Pallas kernels for 34%

profile of v14, /device:TPU:0, one launch (start us, length us, event | category | flops | bytes accessed | tf_op | source)
XLA Modules:
  0.0 128.7 jit_solution(8104820522638177103)
XLA Ops:
  2.1 3.1 %ready.1 = (bf16[16,256,512]{2,1,0:T(8,128)(2,1)S(1)}, bf16[2,128,1024]{2,1,0:T(8,128)(2,1)S(1)}, bf16[1,16,32,1024]{3,2,1,0:T(8,128)(2,1)S(1)}, s32[1,32,1024]{...) custom-call(s32[1]{0:T(128)} %bitcast.me, bf16[16,128,1024]{2,1,0:T(8,128)(2,1)} %density.5, ...), custom_call_target="tpu_custom_call" | custom-call | flops 1 | bytes 1 | tf_op jit(solution)/shard_map/ready/pallas_call | solution.py:247
  5.1 2.6 %inner.3 = (bf16[8,16,1024]{2,1,0:T(8,128)(2,1)S(1)}, f32[16,128]{1,0:T(8,128)S(1)}) custom-call(s32[1]{0:T(128)} %bitcast.me, bf16[1,16,32,1024]{3,2,1,0:T(8,128)(2,1)S(1)} %get-tuple-element.42.refs_0_, s32[1,32,1024]{2,1,0:T(8,128)S(1)} %get-tuple-element.43.refs_1_, bf16[16,256,512]{2,1,0:T(8,128)(2,1)S(1)} %get-tuple-element.44.refs_2_.col, ...), custom_call_target="tpu_custom_call" | custom-call | flops 1 | bytes 1 | tf_op jit(solution)/shard_map/inner/pallas_call | solution.py:326
  7.8 4.1 %collective-permute-start.4 = (bf16[8,16,1024]{2,1,0:T(8,128)(2,1)S(1)}, bf16[8,16,1024]{2,1,0:T(8,128)(2,1)S(1)}, u32[]{:S(2)}, u32[]{:S(2)}) collective-permute-start(bf16[8,16,1024]{2,1,0:T(8,128)(2,1)S(1)} %get-tuple-element.51), channel_id=1, source_target_pairs={{0,4},{1,5},{2,6},{3,7},{4,0},{5,1},{6,2},{7,3},{8,12},{9,13},{10,... | collective-permute-start | bytes 786440 | tf_op jit(solution)/shard_map/ppermute | solution.py:657
  11.9 3.4 %collective-permute-start = (bf16[17,8,1024]{2,1,0:T(8,128)(2,1)S(1)}, bf16[17,8,1024]{2,1,0:T(8,128)(2,1)S(1)}, u32[]{:S(2)}, u32[]{:S(2)}) collective-permute-start(bf16[17,8,1024]{2,1,0:T(8,128)(2,1)S(1)} %gate.18), channel_id=1, source_target_pairs={{0,8},{8,16},{16,24},{1,9},{9,17},{17,25},{2,10},{10,18},{18,26},{... | collective-permute-start | bytes 835592 | tf_op jit(solution)/shard_map/ppermute | solution.py:681
  16.7 3.9 %inner.4 = (bf16[8,16,1024]{2,1,0:T(8,128)(2,1)S(1)}, f32[16,128]{1,0:T(8,128)S(1)}) custom-call(s32[1]{0:T(128)} %bitcast.me, bf16[16,128,1024]{2,1,0:T(8,128)(2,1)} %density.5, s32[128,1024]{1,0:T(8,128)} %valid.9, bf16[16,256,512]{2,1,0:T(8,128)(2,1)S(1)} %get-tuple-element.44.refs_2_.col, bf16[2,128,1024]{2,1,0:T(8,128)(2,1)S(1)} %get-tuple-element.45.refs_3_.row, ...), custom_call_target="tpu_custom_call" | custom-call | flops 1 | bytes 1 | tf_op jit(solution)/shard_map/inner/pallas_call | solution.py:326
  22.1 2.6 %sums.1.one = f32[24,128]{1,0:T(8,128)S(1)} custom-call(bf16[16,128,1024]{2,1,0:T(8,128)(2,1)} %density.5, s32[128,1024]{1,0:T(8,128)} %valid.9, f32[16,128]{1,0:T(8,128)S(1)} %get-tuple-element.48.after.refs_2_.refs_1_), custom_call_target="tpu_custom_call" | custom-call | flops 1 | bytes 1 | tf_op jit(solution)/shard_map/sums/pallas_call | solution.py:149
  24.6 2.7 %collective-permute-start.2 = (f32[24,128]{1,0:T(8,128)S(1)}, f32[24,128]{1,0:T(8,128)S(1)}, u32[]{:S(2)}, u32[]{:S(2)}) collective-permute-start(f32[24,128]{1,0:T(8,128)S(1)} %sums.1.one), channel_id=1, source_target_pairs={{0,8},{8,0},{16,24},{24,16},{1,9},{9,1},{17,25},{25,17},{2,10},{10... | collective-permute-start | bytes 36872 | tf_op jit(solution)/shard_map/ppermute | solution.py:687
  29.0 2.9 %collective-permute-start.3 = (f32[24,128]{1,0:T(8,128)S(1)}, f32[24,128]{1,0:T(8,128)S(1)}, u32[]{:S(2)}, u32[]{:S(2)}) collective-permute-start(f32[24,128]{1,0:T(8,128)S(1)} %add.1.refs_0_), channel_id=1, source_target_pairs={{0,16},{8,24},{16,0},{24,8},{1,17},{9,25},{17,1},{25,9},{2,18},{10... | collective-permute-start | bytes 36872 | tf_op jit(solution)/shard_map/ppermute | solution.py:687
  37.5 6.0 %inner.5 = (bf16[8,16,1024]{2,1,0:T(8,128)(2,1)S(1)}, bf16[8,16,1024]{2,1,0:T(8,128)(2,1)S(1)}) custom-call(s32[1]{0:T(128)} %bitcast.me, bf16[16,128,1024]{2,1,0:T(8,128)(2,1)} %density.5, s32[128,1024]{1,0:T(8,128)} %valid.9, bf16[16,256,512]{2,1,0:T(8,128)(2,1)S(1)} %get-tuple-element.44.refs_2_.col, ...), custom_call_target="tpu_custom_call" | custom-call | flops 1 | bytes 1 | tf_op jit(solution)/shard_map/inner/pallas_call | solution.py:326
  45.1 16.1 %band.1 = (bf16[6,16,1024]{2,1,0:T(8,128)(2,1)}, bf16[2,16,1024]{2,1,0:T(8,128)(2,1)}, bf16[6,16,1024]{2,1,0:T(8,128)(2,1)}, bf16[2,16,1024]{2,1,0:T(8,128)(2,1)...) custom-call(s32[1]{0:T(128)} %bitcast.me, ...), custom_call_target="tpu_custom_call" | custom-call | flops 1 | bytes 1 | tf_op jit(solution)/shard_map/band/pallas_call | solution.py:488
  61.2 3.5 %collective-permute-start.16 = (bf16[6,16,1024]{2,1,0:T(8,128)(2,1)}, bf16[6,16,1024]{2,1,0:T(8,128)(2,1)S(1)}, u32[]{:S(2)}, u32[]{:S(2)}) collective-permute-start(bf16[6,16,1024]{2,1,0:T(8,128)(2,1)} %gate.28), channel_id=1, source_target_pairs={{0,4},{1,5},{2,6},{3,7},{4,0},{5,1},{6,2},{7,3},{8,12},{9,13},{10,... | collective-permute-start | bytes 589832 | tf_op jit(solution)/shard_map/ppermute | solution.py:657
  64.9 8.1 %collective-permute-done.7.refs_1_.refs_5_ = bf16[8,16,1024]{2,1,0:T(8,128)(2,1)S(1)} collective-permute-done((bf16[8,16,1024]{2,1,0:T(8,128)(2,1)S(1)}, bf16[8,16,1024]{2,1,0:T(8,128)(2,1)S(1)}, u32[]{:S(2)}, u32[]{:S(2)}) %collective-permute-start.7) | collective-permute-done | bytes 262176 | tf_op jit(solution)/shard_map/ppermute | solution.py:657
  73.0 2.6 %collective-permute-start.9 = (bf16[6,16,1024]{2,1,0:T(8,128)(2,1)}, bf16[6,16,1024]{2,1,0:T(8,128)(2,1)S(1)}, u32[]{:S(2)}, u32[]{:S(2)}) collective-permute-start(bf16[6,16,1024]{2,1,0:T(8,128)(2,1)} %gate.22), channel_id=1, source_target_pairs={{0,6},{1,7},{2,4},{3,5},{4,2},{5,3},{6,0},{7,1},{8,14},{9,15},{10,... | collective-permute-start | bytes 589832 | tf_op jit(solution)/shard_map/ppermute | solution.py:657
  75.6 1.9 %collective-permute-done.16.refs_1_.refs_4_ = bf16[6,16,1024]{2,1,0:T(8,128)(2,1)S(1)} collective-permute-done((bf16[6,16,1024]{2,1,0:T(8,128)(2,1)}, bf16[6,16,1024]{2,1,0:T(8,128)(2,1)S(1)}, u32[]{:S(2)}, u32[]{:S(2)}) %collective-permute-start.16) | collective-permute-done | bytes 196640 | tf_op jit(solution)/shard_map/ppermute | solution.py:657
  77.4 4.1 %collective-permute-done.14.refs_1_.refs_3_ = bf16[8,16,1024]{2,1,0:T(8,128)(2,1)S(1)} collective-permute-done((bf16[8,16,1024]{2,1,0:T(8,128)(2,1)}, bf16[8,16,1024]{2,1,0:T(8,128)(2,1)S(1)}, u32[]{:S(2)}, u32[]{:S(2)}) %collective-permute-start.14) | collective-permute-done | bytes 262176 | tf_op jit(solution)/shard_map/ppermute | solution.py:657
  81.6 4.2 %collective-permute-done.11.refs_1_.refs_2_ = bf16[8,16,1024]{2,1,0:T(8,128)(2,1)S(1)} collective-permute-done((bf16[8,16,1024]{2,1,0:T(8,128)(2,1)}, bf16[8,16,1024]{2,1,0:T(8,128)(2,1)S(1)}, u32[]{:S(2)}, u32[]{:S(2)}) %collective-permute-start.11) | collective-permute-done | bytes 262176 | tf_op jit(solution)/shard_map/ppermute | solution.py:657
  85.7 4.5 %mend.3.refs_3_.refs_6_ = bf16[8,16,1024]{2,1,0:T(8,128)(2,1)S(1)} custom-call(s32[1]{0:T(128)} %bitcast.me, s32[128,1024]{1,0:T(8,128)} %valid.9, f32[9,16,128]{2,1,0:T(8,128)S(1)} %collective-permute-done.6.refs_2_.note, bf16[8,16,1024]{2,1,0:T(8,128)(2,1)S(1)} %collective-permute-done.13.refs_1_.piece), custom_call_target="tpu_custom_call" | custom-call | flops 1 | bytes 1 | tf_op jit(solution)/shard_map/mend/pallas_call | solution.py:388
  90.2 4.5 %mend.2.refs_2_.refs_4_ = bf16[8,16,1024]{2,1,0:T(8,128)(2,1)S(1)} custom-call(s32[1]{0:T(128)} %bitcast.me, s32[128,1024]{1,0:T(8,128)} %valid.9, f32[9,16,128]{2,1,0:T(8,128)S(1)} %collective-permute-done.5.refs_1_.note, bf16[8,16,1024]{2,1,0:T(8,128)(2,1)S(1)} %collective-permute-done.4.refs_1_.piece), custom_call_target="tpu_custom_call" | custom-call | flops 1 | bytes 1 | tf_op jit(solution)/shard_map/mend/pallas_call | solution.py:388
  94.7 9.8 %collective-permute-start.19 = (bf16[6,16,1024]{2,1,0:T(8,128)(2,1)}, bf16[6,16,1024]{2,1,0:T(8,128)(2,1)S(1)}, u32[]{:S(2)}, u32[]{:S(2)}) collective-permute-start(bf16[6,16,1024]{2,1,0:T(8,128)(2,1)} %gate.31), channel_id=1, source_target_pairs={{0,7},{1,6},{2,5},{3,4},{4,3},{5,2},{6,1},{7,0},{8,15},{9,14},{10,... | collective-permute-start | bytes 589832 | tf_op jit(solution)/shard_map/ppermute | solution.py:657
  104.6 3.8 %collective-permute-done.19.refs_1_.refs_7_ = bf16[6,16,1024]{2,1,0:T(8,128)(2,1)S(1)} collective-permute-done((bf16[6,16,1024]{2,1,0:T(8,128)(2,1)}, bf16[6,16,1024]{2,1,0:T(8,128)(2,1)S(1)}, u32[]{:S(2)}, u32[]{:S(2)}) %collective-permute-start.19) | collective-permute-done | bytes 196640 | tf_op jit(solution)/shard_map/ppermute | solution.py:657
  108.4 7.4 %collective-permute-start.18 = (bf16[2,16,1024]{2,1,0:T(8,128)(2,1)}, bf16[2,16,1024]{2,1,0:T(8,128)(2,1)S(1)}, u32[]{:S(2)}, u32[]{:S(2)}) collective-permute-start(bf16[2,16,1024]{2,1,0:T(8,128)(2,1)} %gate.30), channel_id=1, source_target_pairs={{0,4},{1,5},{2,6},{3,7},{4,0},{5,1},{6,2},{7,3},{8,12},{9,13},{10,... | collective-permute-start | bytes 196616 | tf_op jit(solution)/shard_map/ppermute | solution.py:657
  117.0 3.2 %project.3 = (bf16[128,16384]{1,0:T(8,128)(2,1)}, bf16[128,16384]{1,0:T(8,128)(2,1)}, f32[8,128]{1,0:T(8,128)}) custom-call(s32[1]{0:T(128)} %bitcast.me, bf16[256,128]{1,0:T(8,128)(2,1)S(1)} %weights.1, bf16[8,16,1024]{2,1,0:T(8,128)(2,1)S(1)} %copy-done.1, bf16[8,16,1024]{2,1,0:T(8,128)(2,1)S(1)} %collective-permute-done.21.refs_1_, ...), custom_call_target="tpu_custom_call" | custom-call | flops 1 | bytes 1 | tf_op jit(solution)/shard_map/project/pallas_call | solution.py:573
  120.8 2.4 %collective-permute-start.22 = (bf16[2,16,1024]{2,1,0:T(8,128)(2,1)}, bf16[2,16,1024]{2,1,0:T(8,128)(2,1)S(1)}, u32[]{:S(2)}, u32[]{:S(2)}) collective-permute-start(bf16[2,16,1024]{2,1,0:T(8,128)(2,1)} %gate.34), channel_id=1, source_target_pairs={{0,6},{1,7},{2,4},{3,5},{4,2},{5,3},{6,0},{7,1},{8,14},{9,15},{10,... | collective-permute-start | bytes 196616 | tf_op jit(solution)/shard_map/ppermute | solution.py:657
  123.3 2.8 %project.4 = (bf16[128,16384]{1,0:T(8,128)(2,1)}, bf16[128,16384]{1,0:T(8,128)(2,1)}, f32[8,128]{1,0:T(8,128)}) custom-call(s32[1]{0:T(128)} %bitcast.me, bf16[256,128]{1,0:T(8,128)(2,1)S(1)} %weights.1, bf16[8,16,1024]{2,1,0:T(8,128)(2,1)S(1)} %copy-done, ...), custom_call_target="tpu_custom_call", output_to_operand_aliasing={{0}: (10, {}), {1}: (11, {})} | custom-call | flops 1 | bytes 1 | tf_op jit(solution)/shard_map/project/pallas_call | solution.py:573
  (75 shorter events, 18.0 us)
Async XLA Ops:
  7.8 28.3 %collective-permute-start.4 = (bf16[8,16,1024]{2,1,0:T(8,128)(2,1)S(1)}, bf16[8,16,1024]{2,1,0:T(8,128)(2,1)S(1)}, u32[]{:S(2)}, u32[]{:S(2)}) collective-permute-start(bf16[8,16,1024]{2,1,0:T(8,128)(2,1)S(1)} %get-tuple-element.51), channel_id=1, source_target_pairs={{0,4},{1,5},{2,6},{3,7},{4,0},{5,1},{6,2},{7,3},{8,12},{9,13},{10,... | collective-permute-start | bytes 786440 | tf_op jit(solution)/shard_map/ppermute | solution.py:657
  11.9 25.6 %collective-permute-start = (bf16[17,8,1024]{2,1,0:T(8,128)(2,1)S(1)}, bf16[17,8,1024]{2,1,0:T(8,128)(2,1)S(1)}, u32[]{:S(2)}, u32[]{:S(2)}) collective-permute-start(bf16[17,8,1024]{2,1,0:T(8,128)(2,1)S(1)} %gate.18), channel_id=1, source_target_pairs={{0,8},{8,16},{16,24},{1,9},{9,17},{17,25},{2,10},{10,18},{18,26},{... | collective-permute-start | bytes 835592 | tf_op jit(solution)/shard_map/ppermute | solution.py:681
  15.3 22.2 %collective-permute-start.1 = (bf16[17,8,1024]{2,1,0:T(8,128)(2,1)S(1)}, bf16[17,8,1024]{2,1,0:T(8,128)(2,1)S(1)}, u32[]{:S(2)}, u32[]{:S(2)}) collective-permute-start(bf16[17,8,1024]{2,1,0:T(8,128)(2,1)S(1)} %gate.19), channel_id=1, source_target_pairs={{8,0},{16,8},{24,16},{9,1},{17,9},{25,17},{10,2},{18,10},{26,18},{... | collective-permute-start | bytes 835592 | tf_op jit(solution)/shard_map/ppermute | solution.py:682
  20.6 40.6 %collective-permute-start.13 = (bf16[8,16,1024]{2,1,0:T(8,128)(2,1)S(1)}, bf16[8,16,1024]{2,1,0:T(8,128)(2,1)S(1)}, u32[]{:S(2)}, u32[]{:S(2)}) collective-permute-start(bf16[8,16,1024]{2,1,0:T(8,128)(2,1)S(1)} %get-tuple-element.63), channel_id=1, source_target_pairs={{0,6},{1,7},{2,4},{3,5},{4,2},{5,3},{6,0},{7,1},{8,14},{9,15},{10,... | collective-permute-start | bytes 786440 | tf_op jit(solution)/shard_map/ppermute | solution.py:657
  24.6 4.4 %collective-permute-start.2 = (f32[24,128]{1,0:T(8,128)S(1)}, f32[24,128]{1,0:T(8,128)S(1)}, u32[]{:S(2)}, u32[]{:S(2)}) collective-permute-start(f32[24,128]{1,0:T(8,128)S(1)} %sums.1.one), channel_id=1, source_target_pairs={{0,8},{8,0},{16,24},{24,16},{1,9},{9,1},{17,25},{25,17},{2,10},{10... | collective-permute-start | bytes 36872 | tf_op jit(solution)/shard_map/ppermute | solution.py:687
  29.0 4.6 %collective-permute-start.3 = (f32[24,128]{1,0:T(8,128)S(1)}, f32[24,128]{1,0:T(8,128)S(1)}, u32[]{:S(2)}, u32[]{:S(2)}) collective-permute-start(f32[24,128]{1,0:T(8,128)S(1)} %add.1.refs_0_), channel_id=1, source_target_pairs={{0,16},{8,24},{16,0},{24,8},{1,17},{9,25},{17,1},{25,9},{2,18},{10... | collective-permute-start | bytes 36872 | tf_op jit(solution)/shard_map/ppermute | solution.py:687
  34.4 10.7 %collective-permute-start.5 = (f32[9,16,128]{2,1,0:T(8,128)}, f32[9,16,128]{2,1,0:T(8,128)S(1)}, u32[]{:S(2)}, u32[]{:S(2)}) collective-permute-start(f32[9,16,128]{2,1,0:T(8,128)} %get-tuple-element.53), channel_id=1, source_target_pairs={{0,4},{1,5},{2,6},{3,7},{4,0},{5,1},{6,2},{7,3},{8,12},{9,13},{10,... | collective-permute-start | bytes 221192 | tf_op jit(solution)/shard_map/ppermute | solution.py:657
  36.1 9.0 %collective-permute-start.6 = (f32[9,16,128]{2,1,0:T(8,128)}, f32[9,16,128]{2,1,0:T(8,128)S(1)}, u32[]{:S(2)}, u32[]{:S(2)}) collective-permute-start(f32[9,16,128]{2,1,0:T(8,128)} %get-tuple-element.54), channel_id=1, source_target_pairs={{0,6},{1,7},{2,4},{3,5},{4,2},{5,3},{6,0},{7,1},{8,14},{9,15},{10,... | collective-permute-start | bytes 221192 | tf_op jit(solution)/shard_map/ppermute | solution.py:657
  43.4 21.4 %collective-permute-start.8 = (bf16[8,16,1024]{2,1,0:T(8,128)(2,1)S(1)}, bf16[8,16,1024]{2,1,0:T(8,128)(2,1)S(1)}, u32[]{:S(2)}, u32[]{:S(2)}) collective-permute-start(bf16[8,16,1024]{2,1,0:T(8,128)(2,1)S(1)} %get-tuple-element.58), channel_id=1, source_target_pairs={{0,7},{1,6},{2,5},{3,4},{4,3},{5,2},{6,1},{7,0},{8,15},{9,14},{10,... | collective-permute-start | bytes 786440 | tf_op jit(solution)/shard_map/ppermute | solution.py:657
  43.5 29.5 %collective-permute-start.7 = (bf16[8,16,1024]{2,1,0:T(8,128)(2,1)S(1)}, bf16[8,16,1024]{2,1,0:T(8,128)(2,1)S(1)}, u32[]{:S(2)}, u32[]{:S(2)}) collective-permute-start(bf16[8,16,1024]{2,1,0:T(8,128)(2,1)S(1)} %get-tuple-element.52.refs_0_), channel_id=1, source_target_pairs={{0,5},{1,4},{2,7},{3,6},{4,1},{5,0},{6,3},{7,2},{8,13},{9,12},{10,... | collective-permute-start | bytes 786440 | tf_op jit(solution)/shard_map/ppermute | solution.py:657
  61.2 16.2 %collective-permute-start.16 = (bf16[6,16,1024]{2,1,0:T(8,128)(2,1)}, bf16[6,16,1024]{2,1,0:T(8,128)(2,1)S(1)}, u32[]{:S(2)}, u32[]{:S(2)}) collective-permute-start(bf16[6,16,1024]{2,1,0:T(8,128)(2,1)} %gate.28), channel_id=1, source_target_pairs={{0,4},{1,5},{2,6},{3,7},{4,0},{5,1},{6,2},{7,3},{8,12},{9,13},{10,... | collective-permute-start | bytes 589832 | tf_op jit(solution)/shard_map/ppermute | solution.py:657
  64.8 16.8 %collective-permute-start.14 = (bf16[8,16,1024]{2,1,0:T(8,128)(2,1)}, bf16[8,16,1024]{2,1,0:T(8,128)(2,1)S(1)}, u32[]{:S(2)}, u32[]{:S(2)}) collective-permute-start(bf16[8,16,1024]{2,1,0:T(8,128)(2,1)} %gate.26), channel_id=1, source_target_pairs={{0,3},{1,2},{2,1},{3,0},{4,7},{5,6},{6,5},{7,4},{8,11},{9,10},{10,... | collective-permute-start | bytes 786440 | tf_op jit(solution)/shard_map/ppermute | solution.py:657
  64.8 20.9 %collective-permute-start.11 = (bf16[8,16,1024]{2,1,0:T(8,128)(2,1)}, bf16[8,16,1024]{2,1,0:T(8,128)(2,1)S(1)}, u32[]{:S(2)}, u32[]{:S(2)}) collective-permute-start(bf16[8,16,1024]{2,1,0:T(8,128)(2,1)} %gate.24), channel_id=1, source_target_pairs={{0,2},{1,3},{2,0},{3,1},{4,6},{5,7},{6,4},{7,5},{8,10},{9,11},{10,... | collective-permute-start | bytes 786440 | tf_op jit(solution)/shard_map/ppermute | solution.py:657
  73.0 21.6 %collective-permute-start.9 = (bf16[6,16,1024]{2,1,0:T(8,128)(2,1)}, bf16[6,16,1024]{2,1,0:T(8,128)(2,1)S(1)}, u32[]{:S(2)}, u32[]{:S(2)}) collective-permute-start(bf16[6,16,1024]{2,1,0:T(8,128)(2,1)} %gate.22), channel_id=1, source_target_pairs={{0,6},{1,7},{2,4},{3,5},{4,2},{5,3},{6,0},{7,1},{8,14},{9,15},{10,... | collective-permute-start | bytes 589832 | tf_op jit(solution)/shard_map/ppermute | solution.py:657
  77.4 27.0 %collective-permute-start.17 = (bf16[6,16,1024]{2,1,0:T(8,128)(2,1)}, bf16[6,16,1024]{2,1,0:T(8,128)(2,1)S(1)}, u32[]{:S(2)}, u32[]{:S(2)}) collective-permute-start(bf16[6,16,1024]{2,1,0:T(8,128)(2,1)} %gate.29), channel_id=1, source_target_pairs={{0,5},{1,4},{2,7},{3,6},{4,1},{5,0},{6,3},{7,2},{8,13},{9,12},{10,... | collective-permute-start | bytes 589832 | tf_op jit(solution)/shard_map/ppermute | solution.py:657
  81.6 34.3 %collective-permute-start.15 = (bf16[8,16,1024]{2,1,0:T(8,128)(2,1)}, bf16[8,16,1024]{2,1,0:T(8,128)(2,1)S(1)}, u32[]{:S(2)}, u32[]{:S(2)}) collective-permute-start(bf16[8,16,1024]{2,1,0:T(8,128)(2,1)} %gate.27), channel_id=1, source_target_pairs={{0,3},{1,2},{2,1},{3,0},{4,7},{5,6},{6,5},{7,4},{8,11},{9,10},{10,... | collective-permute-start | bytes 786440 | tf_op jit(solution)/shard_map/ppermute | solution.py:657
  81.6 34.3 %collective-permute-start.21 = (bf16[8,16,1024]{2,1,0:T(8,128)(2,1)}, bf16[8,16,1024]{2,1,0:T(8,128)(2,1)S(1)}, u32[]{:S(2)}, u32[]{:S(2)}) collective-permute-start(bf16[8,16,1024]{2,1,0:T(8,128)(2,1)} %gate.33), channel_id=1, source_target_pairs={{0,1},{1,0},{2,3},{3,2},{4,5},{5,4},{6,7},{7,6},{8,9},{9,8},{10,11... | collective-permute-start | bytes 786440 | tf_op jit(solution)/shard_map/ppermute | solution.py:657
  85.7 35.1 %collective-permute-start.12 = (bf16[8,16,1024]{2,1,0:T(8,128)(2,1)}, bf16[8,16,1024]{2,1,0:T(8,128)(2,1)S(1)}, u32[]{:S(2)}, u32[]{:S(2)}) collective-permute-start(bf16[8,16,1024]{2,1,0:T(8,128)(2,1)} %gate.25), channel_id=1, source_target_pairs={{0,2},{1,3},{2,0},{3,1},{4,6},{5,7},{6,4},{7,5},{8,10},{9,11},{10,... | collective-permute-start | bytes 786440 | tf_op jit(solution)/shard_map/ppermute | solution.py:657
  94.7 13.8 %collective-permute-start.19 = (bf16[6,16,1024]{2,1,0:T(8,128)(2,1)}, bf16[6,16,1024]{2,1,0:T(8,128)(2,1)S(1)}, u32[]{:S(2)}, u32[]{:S(2)}) collective-permute-start(bf16[6,16,1024]{2,1,0:T(8,128)(2,1)} %gate.31), channel_id=1, source_target_pairs={{0,7},{1,6},{2,5},{3,4},{4,3},{5,2},{6,1},{7,0},{8,15},{9,14},{10,... | collective-permute-start | bytes 589832 | tf_op jit(solution)/shard_map/ppermute | solution.py:657
  104.5 18.8 %collective-permute-start.10 = (bf16[8,16,1024]{2,1,0:T(8,128)(2,1)}, bf16[8,16,1024]{2,1,0:T(8,128)(2,1)S(1)}, u32[]{:S(2)}, u32[]{:S(2)}) collective-permute-start(bf16[8,16,1024]{2,1,0:T(8,128)(2,1)} %gate.23), channel_id=1, source_target_pairs={{0,1},{1,0},{2,3},{3,2},{4,5},{5,4},{6,7},{7,6},{8,9},{9,8},{10,11... | collective-permute-start | bytes 786440 | tf_op jit(solution)/shard_map/ppermute | solution.py:657
  108.4 17.6 %collective-permute-start.18 = (bf16[2,16,1024]{2,1,0:T(8,128)(2,1)}, bf16[2,16,1024]{2,1,0:T(8,128)(2,1)S(1)}, u32[]{:S(2)}, u32[]{:S(2)}) collective-permute-start(bf16[2,16,1024]{2,1,0:T(8,128)(2,1)} %gate.30), channel_id=1, source_target_pairs={{0,4},{1,5},{2,6},{3,7},{4,0},{5,1},{6,2},{7,3},{8,12},{9,13},{10,... | collective-permute-start | bytes 196616 | tf_op jit(solution)/shard_map/ppermute | solution.py:657
  115.8 10.2 %collective-permute-start.20 = (bf16[2,16,1024]{2,1,0:T(8,128)(2,1)}, bf16[2,16,1024]{2,1,0:T(8,128)(2,1)S(1)}, u32[]{:S(2)}, u32[]{:S(2)}) collective-permute-start(bf16[2,16,1024]{2,1,0:T(8,128)(2,1)} %gate.32), channel_id=1, source_target_pairs={{0,5},{1,4},{2,7},{3,6},{4,1},{5,0},{6,3},{7,2},{8,13},{9,12},{10,... | collective-permute-start | bytes 196616 | tf_op jit(solution)/shard_map/ppermute | solution.py:657
  115.8 10.2 %collective-permute-start.23 = (bf16[2,16,1024]{2,1,0:T(8,128)(2,1)}, bf16[2,16,1024]{2,1,0:T(8,128)(2,1)S(1)}, u32[]{:S(2)}, u32[]{:S(2)}) collective-permute-start(bf16[2,16,1024]{2,1,0:T(8,128)(2,1)} %gate.35), channel_id=1, source_target_pairs={{0,7},{1,6},{2,5},{3,4},{4,3},{5,2},{6,1},{7,0},{8,15},{9,14},{10,... | collective-permute-start | bytes 196616 | tf_op jit(solution)/shard_map/ppermute | solution.py:657
  120.8 6.5 %collective-permute-start.22 = (bf16[2,16,1024]{2,1,0:T(8,128)(2,1)}, bf16[2,16,1024]{2,1,0:T(8,128)(2,1)S(1)}, u32[]{:S(2)}, u32[]{:S(2)}) collective-permute-start(bf16[2,16,1024]{2,1,0:T(8,128)(2,1)} %gate.34), channel_id=1, source_target_pairs={{0,6},{1,7},{2,4},{3,5},{4,2},{5,3},{6,0},{7,1},{8,14},{9,15},{10,... | collective-permute-start | bytes 196616 | tf_op jit(solution)/shard_map/ppermute | solution.py:657
  (9 other events, 189.3 us)

commit v15 on v12

--- a/solution.py
+++ b/solution.py
@@ -540,10 +540,10 @@
     (7, HEAD, 5),
     (3, OUTER, 6),
     (1, OUTER, 7),
-    (4, TAIL, 9),
-    (6, TAIL, 10),
-    (5, TAIL, 11),
-    (7, TAIL, 12),
+    (4, TAIL, 7),
+    (6, TAIL, 9),
+    (5, TAIL, 10),
+    (7, TAIL, 11),
 )
 
 
@@ -606,10 +606,8 @@
         if (k, piece) in arrived:
             continue
         before = [] if wait is None else [arrived[ORDER[wait][:2]]]
-        if at == len(ORDER) - 3:
-            finish(INNER)
-            before.append(tokens[0])
         send(k, piece, *before)
+    finish(INNER)
     finish(HEAD)
     finish(TAIL)
     return tuple(result)

time: 112 us -> 114 us (1.018)
  starting transfers between devices: 34.4 us -> 35.6 us
    ppermute x18, starting transfers between devices: 25.4 us -> 26.6 us  [swap(): return lax.ppermute(x, 'cuts', [(i, i ^ k) for i in range(peers)])]
where the time goes in v15:
time: 114 us; the launch traced here: 113 us
  waiting for transfers between devices  39.8 us (35%)
  Pallas kernels  37 us (32%)
  starting transfers between devices  35.6 us (31%)
    ppermute x18, waiting for transfers between devices, swap(): return lax.ppermute(x, 'cuts', [(i, i ^ k) for i in range(peers)])  35 us
    ppermute x18, starting transfers between devices, swap(): return lax.ppermute(x, 'cuts', [(i, i ^ k) for i in range(peers)])  26.6 us
    pallas_call x1, Pallas kernels, filter_band(): pl.pallas_call(functools.partial(band_kernel, wanted), name='band', grid_...  16.1 us
    pallas_call x2, Pallas kernels, filter_inner(): pl.pallas_call(functools.partial(inner_kernel, wanted, loaded, rows // (h...  8.17 us
    pallas_call x3, Pallas kernels, project(): pl.pallas_call(functools.partial(project_kernel, count), name='project',...  7.29 us
    ppermute x3, starting transfers between devices, fast(): lax.ppermute(own, 'tile', [(i, i ^ k) for i in range(tiles)])  4.6 us
    ppermute x1, waiting for transfers between devices, fast(): below = lax.ppermute(first, 'tile', [(i + 1, i) for i in range(tiles - 1)])  3.87 us
    ppermute x1, starting transfers between devices, fast(): above = lax.ppermute(last, 'tile', [(i, i + 1) for i in range(tiles - 1)])  2.87 us
  transfers between devices with their start and end apart: 23, of which 8 were waited for; matrix products, arithmetic and copies ran while one was open for 0% of the time, Pallas kernels for 27%

profile of v15, /device:TPU:0, one launch (start us, length us, event | category | flops | bytes accessed | tf_op | source)
XLA Modules:
  0.0 113.2 jit_solution(7723939018308898225)
XLA Ops:
  0.6 2.6 %sums.1 = (f32[24,128]{1,0:T(8,128)S(1)}, bf16[17,8,1024]{2,1,0:T(8,128)(2,1)S(1)}, bf16[17,8,1024]{2,1,0:T(8,128)(2,1)S(1)}) custom-call(bf16[16,128,1024]{2,1,0:T(8,128)(2,1)} %density.5, s32[128,1024]{1,0:T(8,128)} %valid.5), custom_call_target="tpu_custom_call" | custom-call | flops 1 | bytes 1 | tf_op jit(solution)/shard_map/sums/pallas_call | solution.py:154
  3.3 4.0 %collective-permute-start.4 = (f32[24,128]{1,0:T(8,128)S(1)}, f32[24,128]{1,0:T(8,128)S(1)}, u32[]{:S(2)}, u32[]{:S(2)}) collective-permute-start(f32[24,128]{1,0:T(8,128)S(1)} %get-tuple-element.38.after.refs_0_), channel_id=1, source_target_pairs={{0,24},{8,16},{16,8},{24,0},{1,25},{9,17},{17,9},{25,1},{2,26},{10... | collective-permute-start | bytes 36872 | tf_op jit(solution)/shard_map/ppermute | solution.py:561
  7.9 2.6 %ready.1 = (bf16[16,256,512]{2,1,0:T(8,128)(2,1)S(1)}, bf16[2,128,1024]{2,1,0:T(8,128)(2,1)S(1)}, bf16[1,16,32,1024]{3,2,1,0:T(8,128)(2,1)S(1)}, s32[1,32,1024]{2,1,0:T(8,128)S(1)}) custom-call(s32[1]{0:T(128)} %bitcast.me, bf16[16,128,1024]{2,1,0:T(8,128)(2,1)} %density.5, s32[128,1024]{1,0:T(8,128)} %valid.5, bf16[4,16,17]{2,1,0:T(8,128)(2,1)S(1)} %copy-done.4, ...), custom_call_target="tpu_custom_call" | custom-call | flops 1 | bytes 1 | tf_op jit(solution)/shard_map/ready/pallas_call | solution.py:225
  11.5 2.3 %inner.2.refs_5_ = bf16[8,16,1024]{2,1,0:T(8,128)(2,1)S(1)} custom-call(s32[1]{0:T(128)} %bitcast.me, bf16[1,16,32,1024]{3,2,1,0:T(8,128)(2,1)S(1)} %get-tuple-element.42.refs_0_, s32[1,32,1024]{2,1,0:T(8,128)S(1)} %get-tuple-element.43.refs_1_, bf16[16,256,512]{2,1,0:T(8,128)(2,1)S(1)} %get-tuple-element.39.refs_4_.refs_2_.col, ...), custom_call_target="tpu_custom_call" | custom-call | flops 1 | bytes 1 | tf_op jit(solution)/shard_map/inner/pallas_call | solution.py:284
  13.8 2.7 %collective-permute-start.5 = (bf16[8,16,1024]{2,1,0:T(8,128)(2,1)S(1)}, bf16[8,16,1024]{2,1,0:T(8,128)(2,1)S(1)}, u32[]{:S(2)}, u32[]{:S(2)}) collective-permute-start(bf16[8,16,1024]{2,1,0:T(8,128)(2,1)S(1)} %inner.2.refs_5_), channel_id=1, source_target_pairs={{0,4},{1,5},{2,6},{3,7},{4,0},{5,1},{6,2},{7,3},{8,12},{9,13},{10,... | collective-permute-start | bytes 786440 | tf_op jit(solution)/shard_map/ppermute | solution.py:558
  16.5 2.9 %collective-permute-start = (bf16[17,8,1024]{2,1,0:T(8,128)(2,1)S(1)}, bf16[17,8,1024]{2,1,0:T(8,128)(2,1)S(1)}, u32[]{:S(2)}, u32[]{:S(2)}) collective-permute-start(bf16[17,8,1024]{2,1,0:T(8,128)(2,1)S(1)} %get-tuple-element.36), channel_id=1, source_target_pairs={{0,8},{8,16},{16,24},{1,9},{9,17},{17,25},{2,10},{10,18},{18,26},{... | collective-permute-start | bytes 835592 | tf_op jit(solution)/shard_map/ppermute | solution.py:567
  19.3 1.5 %collective-permute-start.1 = (bf16[17,8,1024]{2,1,0:T(8,128)(2,1)S(1)}, bf16[17,8,1024]{2,1,0:T(8,128)(2,1)S(1)}, u32[]{:S(2)}, u32[]{:S(2)}) collective-permute-start(bf16[17,8,1024]{2,1,0:T(8,128)(2,1)S(1)} %get-tuple-element.37), channel_id=1, source_target_pairs={{8,0},{16,8},{24,16},{9,1},{17,9},{25,17},{10,2},{18,10},{26,18},{... | collective-permute-start | bytes 835592 | tf_op jit(solution)/shard_map/ppermute | solution.py:568
  20.8 5.9 %inner.3 = (bf16[8,16,1024]{2,1,0:T(8,128)(2,1)S(1)}, bf16[8,16,1024]{2,1,0:T(8,128)(2,1)S(1)}) custom-call(s32[1]{0:T(128)} %bitcast.me, bf16[16,128,1024]{2,1,0:T(8,128)(2,1)} %density.5, s32[128,1024]{1,0:T(8,128)} %valid.5, bf16[16,256,512]{2,1,0:T(8,128)(2,1)S(1)} %get-tuple-element.39.refs_4_.refs_2_.col, ...), custom_call_target="tpu_custom_call" | custom-call | flops 1 | bytes 1 | tf_op jit(solution)/shard_map/inner/pallas_call | solution.py:284
  28.1 3.9 %collective-permute-done.1.below = bf16[17,8,1024]{2,1,0:T(8,128)(2,1)S(1)} collective-permute-done((bf16[17,8,1024]{2,1,0:T(8,128)(2,1)S(1)}, bf16[17,8,1024]{2,1,0:T(8,128)(2,1)S(1)}, u32[]{:S(2)}, u32[]{:S(2)}) %collective-permute-start.1) | collective-permute-done | bytes 278560 | tf_op jit(solution)/shard_map/ppermute | solution.py:568
  32.0 16.1 %band.1 = (bf16[6,16,1024]{2,1,0:T(8,128)(2,1)}, bf16[2,16,1024]{2,1,0:T(8,128)(2,1)}, bf16[8,16,1024]{2,1,0:T(8,128)(2,1)}, bf16[6,16,1024]{2,1,0:T(8,128)(2,1)...) custom-call(s32[1]{0:T(128)} %bitcast.me, ...), custom_call_target="tpu_custom_call" | custom-call | flops 1 | bytes 1 | tf_op jit(solution)/shard_map/band/pallas_call | solution.py:391
  48.6 1.6 %collective-permute-start.14 = (bf16[8,16,1024]{2,1,0:T(8,128)(2,1)}, bf16[8,16,1024]{2,1,0:T(8,128)(2,1)S(1)}, u32[]{:S(2)}, u32[]{:S(2)}) collective-permute-start(bf16[8,16,1024]{2,1,0:T(8,128)(2,1)} %gate.23), channel_id=1, source_target_pairs={{0,2},{1,3},{2,0},{3,1},{4,6},{5,7},{6,4},{7,5},{8,10},{9,11},{10,... | collective-permute-start | bytes 786440 | tf_op jit(solution)/shard_map/ppermute | solution.py:558
  50.1 2.9 %collective-permute-start.11 = (bf16[8,16,1024]{2,1,0:T(8,128)(2,1)}, bf16[8,16,1024]{2,1,0:T(8,128)(2,1)S(1)}, u32[]{:S(2)}, u32[]{:S(2)}) collective-permute-start(bf16[8,16,1024]{2,1,0:T(8,128)(2,1)} %gate.20), channel_id=1, source_target_pairs={{0,3},{1,2},{2,1},{3,0},{4,7},{5,6},{6,5},{7,4},{8,11},{9,10},{10,... | collective-permute-start | bytes 786440 | tf_op jit(solution)/shard_map/ppermute | solution.py:558
  53.0 1.9 %collective-permute-start.7 = (bf16[6,16,1024]{2,1,0:T(8,128)(2,1)}, bf16[6,16,1024]{2,1,0:T(8,128)(2,1)S(1)}, u32[]{:S(2)}, u32[]{:S(2)}) collective-permute-start(bf16[6,16,1024]{2,1,0:T(8,128)(2,1)} %gate.17), channel_id=1, source_target_pairs={{0,6},{1,7},{2,4},{3,5},{4,2},{5,3},{6,0},{7,1},{8,14},{9,15},{10,... | collective-permute-start | bytes 589832 | tf_op jit(solution)/shard_map/ppermute | solution.py:558
  54.9 8.6 %collective-permute-done.20.refs_1_.refs_4_ = bf16[6,16,1024]{2,1,0:T(8,128)(2,1)S(1)} collective-permute-done((bf16[6,16,1024]{2,1,0:T(8,128)(2,1)}, bf16[6,16,1024]{2,1,0:T(8,128)(2,1)S(1)}, u32[]{:S(2)}, u32[]{:S(2)}) %collective-permute-start.20) | collective-permute-done | bytes 196640 | tf_op jit(solution)/shard_map/ppermute | solution.py:558
  63.5 3.8 %collective-permute-done.14.refs_1_.refs_2_ = bf16[8,16,1024]{2,1,0:T(8,128)(2,1)S(1)} collective-permute-done((bf16[8,16,1024]{2,1,0:T(8,128)(2,1)}, bf16[8,16,1024]{2,1,0:T(8,128)(2,1)S(1)}, u32[]{:S(2)}, u32[]{:S(2)}) %collective-permute-start.14) | collective-permute-done | bytes 262176 | tf_op jit(solution)/shard_map/ppermute | solution.py:558
  67.3 10.9 %collective-permute-done.7.refs_1_.refs_6_ = bf16[6,16,1024]{2,1,0:T(8,128)(2,1)S(1)} collective-permute-done((bf16[6,16,1024]{2,1,0:T(8,128)(2,1)}, bf16[6,16,1024]{2,1,0:T(8,128)(2,1)S(1)}, u32[]{:S(2)}, u32[]{:S(2)}) %collective-permute-start.7) | collective-permute-done | bytes 196640 | tf_op jit(solution)/shard_map/ppermute | solution.py:558
  78.2 6.9 %collective-permute-start.9 = (bf16[8,16,1024]{2,1,0:T(8,128)(2,1)}, bf16[8,16,1024]{2,1,0:T(8,128)(2,1)S(1)}, u32[]{:S(2)}, u32[]{:S(2)}) collective-permute-start(bf16[8,16,1024]{2,1,0:T(8,128)(2,1)} %gate.19), channel_id=1, source_target_pairs={{0,2},{1,3},{2,0},{3,1},{4,6},{5,7},{6,4},{7,5},{8,10},{9,11},{10,... | collective-permute-start | bytes 786440 | tf_op jit(solution)/shard_map/ppermute | solution.py:558
  85.3 2.6 %collective-permute-start.12 = (bf16[8,16,1024]{2,1,0:T(8,128)(2,1)}, bf16[8,16,1024]{2,1,0:T(8,128)(2,1)S(1)}, u32[]{:S(2)}, u32[]{:S(2)}) collective-permute-start(bf16[8,16,1024]{2,1,0:T(8,128)(2,1)} %gate.21), channel_id=1, source_target_pairs={{0,3},{1,2},{2,1},{3,0},{4,7},{5,6},{6,5},{7,4},{8,11},{9,10},{10,... | collective-permute-start | bytes 786440 | tf_op jit(solution)/shard_map/ppermute | solution.py:558
  87.8 8.6 %collective-permute-done.18.refs_1_.refs_5_ = bf16[6,16,1024]{2,1,0:T(8,128)(2,1)S(1)} collective-permute-done((bf16[6,16,1024]{2,1,0:T(8,128)(2,1)}, bf16[6,16,1024]{2,1,0:T(8,128)(2,1)S(1)}, u32[]{:S(2)}, u32[]{:S(2)}) %collective-permute-start.18) | collective-permute-done | bytes 196640 | tf_op jit(solution)/shard_map/ppermute | solution.py:558
  96.9 3.3 %collective-permute-start.22 = (bf16[2,16,1024]{2,1,0:T(8,128)(2,1)}, bf16[2,16,1024]{2,1,0:T(8,128)(2,1)S(1)}, u32[]{:S(2)}, u32[]{:S(2)}) collective-permute-start(bf16[2,16,1024]{2,1,0:T(8,128)(2,1)} %gate.31), channel_id=1, source_target_pairs={{0,7},{1,6},{2,5},{3,4},{4,3},{5,2},{6,1},{7,0},{8,15},{9,14},{10,... | collective-permute-start | bytes 196616 | tf_op jit(solution)/shard_map/ppermute | solution.py:558
  100.2 2.5 %collective-permute-start.19 = (bf16[2,16,1024]{2,1,0:T(8,128)(2,1)}, bf16[2,16,1024]{2,1,0:T(8,128)(2,1)S(1)}, u32[]{:S(2)}, u32[]{:S(2)}) collective-permute-start(bf16[2,16,1024]{2,1,0:T(8,128)(2,1)} %gate.28), channel_id=1, source_target_pairs={{0,6},{1,7},{2,4},{3,5},{4,2},{5,3},{6,0},{7,1},{8,14},{9,15},{10,... | collective-permute-start | bytes 196616 | tf_op jit(solution)/shard_map/ppermute | solution.py:558
  102.8 3.2 %project.3 = (bf16[128,16384]{1,0:T(8,128)(2,1)}, bf16[128,16384]{1,0:T(8,128)(2,1)}, f32[8,128]{1,0:T(8,128)}) custom-call(s32[1]{0:T(128)} %bitcast.me, bf16[256,128]{1,0:T(8,128)(2,1)S(1)} %weights.1, bf16[8,16,1024]{2,1,0:T(8,128)(2,1)S(1)} %copy-done.1, bf16[8,16,1024]{2,1,0:T(8,128)(2,1)S(1)} %collective-permute-done.15.refs_1_, ...), custom_call_target="tpu_custom_call" | custom-call | flops 1 | bytes 1 | tf_op jit(solution)/shard_map/project/pallas_call | solution.py:476
  106.0 2.7 %project.4 = (bf16[128,16384]{1,0:T(8,128)(2,1)}, bf16[128,16384]{1,0:T(8,128)(2,1)}, f32[8,128]{1,0:T(8,128)}) custom-call(s32[1]{0:T(128)} %bitcast.me, bf16[256,128]{1,0:T(8,128)(2,1)S(1)} %weights.1, bf16[8,16,1024]{2,1,0:T(8,128)(2,1)S(1)} %copy-done, ...), custom_call_target="tpu_custom_call", output_to_operand_aliasing={{0}: (10, {}), {1}: (11, {})} | custom-call | flops 1 | bytes 1 | tf_op jit(solution)/shard_map/project/pallas_call | solution.py:476
  108.8 3.1 %collective-permute-done.16.refs_5_ = bf16[2,16,1024]{2,1,0:T(8,128)(2,1)S(1)} collective-permute-done((bf16[2,16,1024]{2,1,0:T(8,128)(2,1)}, bf16[2,16,1024]{2,1,0:T(8,128)(2,1)S(1)}, u32[]{:S(2)}, u32[]{:S(2)}) %collective-permute-start.16) | collective-permute-done | bytes 65568 | tf_op jit(solution)/shard_map/ppermute | solution.py:558
  (60 shorter events, 5.5 us)
Async XLA Ops:
  3.3 7.2 %collective-permute-start.4 = (f32[24,128]{1,0:T(8,128)S(1)}, f32[24,128]{1,0:T(8,128)S(1)}, u32[]{:S(2)}, u32[]{:S(2)}) collective-permute-start(f32[24,128]{1,0:T(8,128)S(1)} %get-tuple-element.38.after.refs_0_), channel_id=1, source_target_pairs={{0,24},{8,16},{16,8},{24,0},{1,25},{9,17},{17,9},{25,1},{2,26},{10... | collective-permute-start | bytes 36872 | tf_op jit(solution)/shard_map/ppermute | solution.py:561
  7.2 3.7 %collective-permute-start.3 = (f32[24,128]{1,0:T(8,128)S(1)}, f32[24,128]{1,0:T(8,128)S(1)}, u32[]{:S(2)}, u32[]{:S(2)}) collective-permute-start(f32[24,128]{1,0:T(8,128)S(1)} %get-tuple-element.38.after.refs_0_), channel_id=1, source_target_pairs={{0,16},{8,24},{16,0},{24,8},{1,17},{9,25},{17,1},{25,9},{2,18},{10... | collective-permute-start | bytes 36872 | tf_op jit(solution)/shard_map/ppermute | solution.py:561
  7.7 3.7 %collective-permute-start.2 = (f32[24,128]{1,0:T(8,128)S(1)}, f32[24,128]{1,0:T(8,128)S(1)}, u32[]{:S(2)}, u32[]{:S(2)}) collective-permute-start(f32[24,128]{1,0:T(8,128)S(1)} %get-tuple-element.38.after.refs_0_), channel_id=1, source_target_pairs={{0,8},{8,0},{16,24},{24,16},{1,9},{9,1},{17,25},{25,17},{2,10},{10... | collective-permute-start | bytes 36872 | tf_op jit(solution)/shard_map/ppermute | solution.py:561
  13.8 14.3 %collective-permute-start.5 = (bf16[8,16,1024]{2,1,0:T(8,128)(2,1)S(1)}, bf16[8,16,1024]{2,1,0:T(8,128)(2,1)S(1)}, u32[]{:S(2)}, u32[]{:S(2)}) collective-permute-start(bf16[8,16,1024]{2,1,0:T(8,128)(2,1)S(1)} %inner.2.refs_5_), channel_id=1, source_target_pairs={{0,4},{1,5},{2,6},{3,7},{4,0},{5,1},{6,2},{7,3},{8,12},{9,13},{10,... | collective-permute-start | bytes 786440 | tf_op jit(solution)/shard_map/ppermute | solution.py:558
  16.5 11.7 %collective-permute-start = (bf16[17,8,1024]{2,1,0:T(8,128)(2,1)S(1)}, bf16[17,8,1024]{2,1,0:T(8,128)(2,1)S(1)}, u32[]{:S(2)}, u32[]{:S(2)}) collective-permute-start(bf16[17,8,1024]{2,1,0:T(8,128)(2,1)S(1)} %get-tuple-element.36), channel_id=1, source_target_pairs={{0,8},{8,16},{16,24},{1,9},{9,17},{17,25},{2,10},{10,18},{18,26},{... | collective-permute-start | bytes 835592 | tf_op jit(solution)/shard_map/ppermute | solution.py:567
  19.3 12.7 %collective-permute-start.1 = (bf16[17,8,1024]{2,1,0:T(8,128)(2,1)S(1)}, bf16[17,8,1024]{2,1,0:T(8,128)(2,1)S(1)}, u32[]{:S(2)}, u32[]{:S(2)}) collective-permute-start(bf16[17,8,1024]{2,1,0:T(8,128)(2,1)S(1)} %get-tuple-element.37), channel_id=1, source_target_pairs={{8,0},{16,8},{24,16},{9,1},{17,9},{25,17},{10,2},{18,10},{26,18},{... | collective-permute-start | bytes 835592 | tf_op jit(solution)/shard_map/ppermute | solution.py:568
  26.7 21.4 %collective-permute-start.10 = (bf16[8,16,1024]{2,1,0:T(8,128)(2,1)S(1)}, bf16[8,16,1024]{2,1,0:T(8,128)(2,1)S(1)}, u32[]{:S(2)}, u32[]{:S(2)}) collective-permute-start(bf16[8,16,1024]{2,1,0:T(8,128)(2,1)S(1)} %get-tuple-element.44.refs_0_), channel_id=1, source_target_pairs={{0,6},{1,7},{2,4},{3,5},{4,2},{5,3},{6,0},{7,1},{8,14},{9,15},{10,... | collective-permute-start | bytes 786440 | tf_op jit(solution)/shard_map/ppermute | solution.py:558
  28.1 24.9 %collective-permute-start.6 = (bf16[8,16,1024]{2,1,0:T(8,128)(2,1)S(1)}, bf16[8,16,1024]{2,1,0:T(8,128)(2,1)S(1)}, u32[]{:S(2)}, u32[]{:S(2)}) collective-permute-start(bf16[8,16,1024]{2,1,0:T(8,128)(2,1)S(1)} %get-tuple-element.49), channel_id=1, source_target_pairs={{0,5},{1,4},{2,7},{3,6},{4,1},{5,0},{6,3},{7,2},{8,13},{9,12},{10,... | collective-permute-start | bytes 786440 | tf_op jit(solution)/shard_map/ppermute | solution.py:558
  48.2 15.3 %collective-permute-start.20 = (bf16[6,16,1024]{2,1,0:T(8,128)(2,1)}, bf16[6,16,1024]{2,1,0:T(8,128)(2,1)S(1)}, u32[]{:S(2)}, u32[]{:S(2)}) collective-permute-start(bf16[6,16,1024]{2,1,0:T(8,128)(2,1)} %gate.29), channel_id=1, source_target_pairs={{0,4},{1,5},{2,6},{3,7},{4,0},{5,1},{6,2},{7,3},{8,12},{9,13},{10,... | collective-permute-start | bytes 589832 | tf_op jit(solution)/shard_map/ppermute | solution.py:558
  48.6 54.2 %copy-start.1 = (bf16[8,16,1024]{2,1,0:T(8,128)(2,1)S(1)}, bf16[8,16,1024]{2,1,0:T(8,128)(2,1)}, u32[]{:S(2)}) copy-start(bf16[8,16,1024]{2,1,0:T(8,128)(2,1)} %get-tuple-element.63.refs_0_) | copy-start | bytes 786436
  48.6 18.7 %collective-permute-start.14 = (bf16[8,16,1024]{2,1,0:T(8,128)(2,1)}, bf16[8,16,1024]{2,1,0:T(8,128)(2,1)S(1)}, u32[]{:S(2)}, u32[]{:S(2)}) collective-permute-start(bf16[8,16,1024]{2,1,0:T(8,128)(2,1)} %gate.23), channel_id=1, source_target_pairs={{0,2},{1,3},{2,0},{3,1},{4,6},{5,7},{6,4},{7,5},{8,10},{9,11},{10,... | collective-permute-start | bytes 786440 | tf_op jit(solution)/shard_map/ppermute | solution.py:558
  50.1 35.0 %collective-permute-start.17 = (bf16[8,16,1024]{2,1,0:T(8,128)(2,1)}, bf16[8,16,1024]{2,1,0:T(8,128)(2,1)S(1)}, u32[]{:S(2)}, u32[]{:S(2)}) collective-permute-start(bf16[8,16,1024]{2,1,0:T(8,128)(2,1)} %gate.26), channel_id=1, source_target_pairs={{0,7},{1,6},{2,5},{3,4},{4,3},{5,2},{6,1},{7,0},{8,15},{9,14},{10,... | collective-permute-start | bytes 786440 | tf_op jit(solution)/shard_map/ppermute | solution.py:558
  50.1 35.0 %collective-permute-start.11 = (bf16[8,16,1024]{2,1,0:T(8,128)(2,1)}, bf16[8,16,1024]{2,1,0:T(8,128)(2,1)S(1)}, u32[]{:S(2)}, u32[]{:S(2)}) collective-permute-start(bf16[8,16,1024]{2,1,0:T(8,128)(2,1)} %gate.20), channel_id=1, source_target_pairs={{0,3},{1,2},{2,1},{3,0},{4,7},{5,6},{6,5},{7,4},{8,11},{9,10},{10,... | collective-permute-start | bytes 786440 | tf_op jit(solution)/shard_map/ppermute | solution.py:558
  53.0 25.2 %collective-permute-start.7 = (bf16[6,16,1024]{2,1,0:T(8,128)(2,1)}, bf16[6,16,1024]{2,1,0:T(8,128)(2,1)S(1)}, u32[]{:S(2)}, u32[]{:S(2)}) collective-permute-start(bf16[6,16,1024]{2,1,0:T(8,128)(2,1)} %gate.17), channel_id=1, source_target_pairs={{0,6},{1,7},{2,4},{3,5},{4,2},{5,3},{6,0},{7,1},{8,14},{9,15},{10,... | collective-permute-start | bytes 589832 | tf_op jit(solution)/shard_map/ppermute | solution.py:558
  63.5 21.7 %collective-permute-start.21 = (bf16[6,16,1024]{2,1,0:T(8,128)(2,1)}, bf16[6,16,1024]{2,1,0:T(8,128)(2,1)S(1)}, u32[]{:S(2)}, u32[]{:S(2)}) collective-permute-start(bf16[6,16,1024]{2,1,0:T(8,128)(2,1)} %gate.30), channel_id=1, source_target_pairs={{0,7},{1,6},{2,5},{3,4},{4,3},{5,2},{6,1},{7,0},{8,15},{9,14},{10,... | collective-permute-start | bytes 589832 | tf_op jit(solution)/shard_map/ppermute | solution.py:558
  67.3 29.6 %collective-permute-start.15 = (bf16[8,16,1024]{2,1,0:T(8,128)(2,1)}, bf16[8,16,1024]{2,1,0:T(8,128)(2,1)S(1)}, u32[]{:S(2)}, u32[]{:S(2)}) collective-permute-start(bf16[8,16,1024]{2,1,0:T(8,128)(2,1)} %gate.24), channel_id=1, source_target_pairs={{0,1},{1,0},{2,3},{3,2},{4,5},{5,4},{6,7},{7,6},{8,9},{9,8},{10,11... | collective-permute-start | bytes 786440 | tf_op jit(solution)/shard_map/ppermute | solution.py:558
  78.2 22.0 %collective-permute-start.9 = (bf16[8,16,1024]{2,1,0:T(8,128)(2,1)}, bf16[8,16,1024]{2,1,0:T(8,128)(2,1)S(1)}, u32[]{:S(2)}, u32[]{:S(2)}) collective-permute-start(bf16[8,16,1024]{2,1,0:T(8,128)(2,1)} %gate.19), channel_id=1, source_target_pairs={{0,2},{1,3},{2,0},{3,1},{4,6},{5,7},{6,4},{7,5},{8,10},{9,11},{10,... | collective-permute-start | bytes 786440 | tf_op jit(solution)/shard_map/ppermute | solution.py:558
  85.1 17.5 %collective-permute-start.8 = (bf16[8,16,1024]{2,1,0:T(8,128)(2,1)}, bf16[8,16,1024]{2,1,0:T(8,128)(2,1)S(1)}, u32[]{:S(2)}, u32[]{:S(2)}) collective-permute-start(bf16[8,16,1024]{2,1,0:T(8,128)(2,1)} %gate.18), channel_id=1, source_target_pairs={{0,1},{1,0},{2,3},{3,2},{4,5},{5,4},{6,7},{7,6},{8,9},{9,8},{10,11... | collective-permute-start | bytes 786440 | tf_op jit(solution)/shard_map/ppermute | solution.py:558
  85.2 11.3 %collective-permute-start.18 = (bf16[6,16,1024]{2,1,0:T(8,128)(2,1)}, bf16[6,16,1024]{2,1,0:T(8,128)(2,1)S(1)}, u32[]{:S(2)}, u32[]{:S(2)}) collective-permute-start(bf16[6,16,1024]{2,1,0:T(8,128)(2,1)} %gate.27), channel_id=1, source_target_pairs={{0,5},{1,4},{2,7},{3,6},{4,1},{5,0},{6,3},{7,2},{8,13},{9,12},{10,... | collective-permute-start | bytes 589832 | tf_op jit(solution)/shard_map/ppermute | solution.py:558
  85.3 20.8 %collective-permute-start.12 = (bf16[8,16,1024]{2,1,0:T(8,128)(2,1)}, bf16[8,16,1024]{2,1,0:T(8,128)(2,1)S(1)}, u32[]{:S(2)}, u32[]{:S(2)}) collective-permute-start(bf16[8,16,1024]{2,1,0:T(8,128)(2,1)} %gate.21), channel_id=1, source_target_pairs={{0,3},{1,2},{2,1},{3,0},{4,7},{5,6},{6,5},{7,4},{8,11},{9,10},{10,... | collective-permute-start | bytes 786440 | tf_op jit(solution)/shard_map/ppermute | solution.py:558
  96.4 12.3 %collective-permute-start.13 = (bf16[2,16,1024]{2,1,0:T(8,128)(2,1)}, bf16[2,16,1024]{2,1,0:T(8,128)(2,1)S(1)}, u32[]{:S(2)}, u32[]{:S(2)}) collective-permute-start(bf16[2,16,1024]{2,1,0:T(8,128)(2,1)} %gate.22), channel_id=1, source_target_pairs={{0,4},{1,5},{2,6},{3,7},{4,0},{5,1},{6,2},{7,3},{8,12},{9,13},{10,... | collective-permute-start | bytes 196616 | tf_op jit(solution)/shard_map/ppermute | solution.py:558
  96.9 11.9 %collective-permute-start.22 = (bf16[2,16,1024]{2,1,0:T(8,128)(2,1)}, bf16[2,16,1024]{2,1,0:T(8,128)(2,1)S(1)}, u32[]{:S(2)}, u32[]{:S(2)}) collective-permute-start(bf16[2,16,1024]{2,1,0:T(8,128)(2,1)} %gate.31), channel_id=1, source_target_pairs={{0,7},{1,6},{2,5},{3,4},{4,3},{5,2},{6,1},{7,0},{8,15},{9,14},{10,... | collective-permute-start | bytes 196616 | tf_op jit(solution)/shard_map/ppermute | solution.py:558
  100.2 8.6 %collective-permute-start.19 = (bf16[2,16,1024]{2,1,0:T(8,128)(2,1)}, bf16[2,16,1024]{2,1,0:T(8,128)(2,1)S(1)}, u32[]{:S(2)}, u32[]{:S(2)}) collective-permute-start(bf16[2,16,1024]{2,1,0:T(8,128)(2,1)} %gate.28), channel_id=1, source_target_pairs={{0,6},{1,7},{2,4},{3,5},{4,2},{5,3},{6,0},{7,1},{8,14},{9,15},{10,... | collective-permute-start | bytes 196616 | tf_op jit(solution)/shard_map/ppermute | solution.py:558
  102.7 9.2 %collective-permute-start.16 = (bf16[2,16,1024]{2,1,0:T(8,128)(2,1)}, bf16[2,16,1024]{2,1,0:T(8,128)(2,1)S(1)}, u32[]{:S(2)}, u32[]{:S(2)}) collective-permute-start(bf16[2,16,1024]{2,1,0:T(8,128)(2,1)} %gate.25), channel_id=1, source_target_pairs={{0,5},{1,4},{2,7},{3,6},{4,1},{5,0},{6,3},{7,2},{8,13},{9,12},{10,... | collective-permute-start | bytes 196616 | tf_op jit(solution)/shard_map/ppermute | solution.py:558
  (5 other events, 175.7 us)

commit v16 on v12

--- a/solution.py
+++ b/solution.py
@@ -97,19 +97,24 @@
     slices, _, wide = col.shape
     terms = wide // LANES
     high, cols = LANES // terms, tall.shape[1]
+    read = rows + HALO
+    if read < high:
+        for n in range(tall.shape[0] // high):
+            tall[n * high + read : (n + 1) * high] = jnp.zeros((high - read, cols), jnp.bfloat16)
     parts = []
     for g in range(slices // GROUP):
         for j in range(GROUP):
             s = g * GROUP + j
-            x = jnp.concatenate([field(s), jnp.zeros((high, LANES), jnp.float32)], axis=1)
-            x = pltpu.roll(x, REACH, 1).astype(jnp.bfloat16)
+            x = jnp.concatenate([field(s), jnp.zeros((read, LANES), jnp.float32)], axis=1)
+            x = pltpu.roll(x, REACH, 1)
             x = jnp.concatenate([x[:, c : c + 2 * LANES] for c in range(0, cols, LANES)], axis=0)
-            y = jnp.dot(x, col[s], preferred_element_type=jnp.float32).astype(jnp.bfloat16)
+            y = jnp.dot(x.astype(jnp.bfloat16), col[s], preferred_element_type=jnp.float32)
             for c in range(cols // LANES):
                 for k in range(terms):
-                    tall[(j * terms + k) * high : (j * terms + k + 1) * high, c * LANES : (c + 1) * LANES] = y[
-                        c * high : (c + 1) * high, k * LANES : (k + 1) * LANES
-                    ]
+                    at = (j * terms + k) * high
+                    tall[at : at + read, c * LANES : (c + 1) * LANES] = y[
+                        c * read : (c + 1) * read, k * LANES : (k + 1) * LANES
+                    ].astype(jnp.bfloat16)
         z = jnp.dot(row[g, : rows * GROUP], tall[...], preferred_element_type=jnp.float32)
         parts.append(z.reshape(rows, GROUP, cols))
     return jnp.concatenate(parts, axis=1)
@@ -192,8 +197,7 @@
 def inner_rows(both, last):
     both = both.astype(jnp.float32)
     rows = both.shape[0] - REACH
-    chosen = jnp.where(last, both[REACH:], both[:rows])
-    return jnp.concatenate([chosen, jnp.zeros((REACH, both.shape[1]), jnp.float32)], axis=0)
+    return jnp.where(last, both[REACH:], both[:rows])
 
 
 def window_copies(b, block, last, density, valid, cube, plane, sems):

time: 112 us -> 118 us (1.054)
  starting transfers between devices: 34.4 us -> 45.2 us
  waiting for transfers between devices: 39.2 us -> 35.1 us
  Pallas kernels: 36.9 us -> 35.7 us
    ppermute x18, starting transfers between devices: 25.4 us -> 36.3 us  [swap(): return lax.ppermute(x, 'cuts', [(i, i ^ k) for i in range(peers)])]
    ppermute x18, waiting for transfers between devices: 34.3 us -> 29.5 us  [swap(): return lax.ppermute(x, 'cuts', [(i, i ^ k) for i in range(peers)])]
  transfers between devices with their start and end apart: 23 -> 23, of which waited for: 8 -> 9; matrix products, arithmetic and copies ran while one was open for 0% -> 0% of each run, Pallas kernels for 27% -> 25%
where the time goes in v16:
time: 118 us
  starting transfers between devices  45.2 us (38%)
  Pallas kernels  35.7 us (30%)
  waiting for transfers between devices  35.1 us (30%)
    ppermute x18, starting transfers between devices, swap(): return lax.ppermute(x, 'cuts', [(i, i ^ k) for i in range(peers)])  36.3 us
    ppermute x18, waiting for transfers between devices, swap(): return lax.ppermute(x, 'cuts', [(i, i ^ k) for i in range(peers)])  29.5 us
    pallas_call x1, Pallas kernels, filter_band(): pl.pallas_call(functools.partial(band_kernel, wanted), name='band', grid_...  16.1 us
    pallas_call x3, Pallas kernels, project(): pl.pallas_call(functools.partial(project_kernel, count), name='project',...  7.26 us
    pallas_call x2, Pallas kernels, filter_inner(): pl.pallas_call(functools.partial(inner_kernel, wanted, loaded, rows // (h...  6.99 us
    ppermute x1, waiting for transfers between devices, fast(): below = lax.ppermute(first, 'tile', [(i + 1, i) for i in range(tiles - 1)])  4.69 us
    ppermute x3, starting transfers between devices, fast(): lax.ppermute(own, 'tile', [(i, i ^ k) for i in range(tiles)])  4.6 us
    ppermute x1, starting transfers between devices, fast(): above = lax.ppermute(last, 'tile', [(i, i + 1) for i in range(tiles - 1)])  2.87 us
  transfers between devices with their start and end apart: 23, of which 9 were waited for; matrix products, arithmetic and copies ran while one was open for 0% of the time, Pallas kernels for 25%

profile of v16, /device:TPU:0, one launch (start us, length us, event | category | flops | bytes accessed | tf_op | source)
XLA Modules:
  0.0 117.6 jit_solution(641864242294437281)
XLA Ops:
  0.6 2.6 %sums.1 = (f32[24,128]{1,0:T(8,128)S(1)}, bf16[17,8,1024]{2,1,0:T(8,128)(2,1)S(1)}, bf16[17,8,1024]{2,1,0:T(8,128)(2,1)S(1)}) custom-call(bf16[16,128,1024]{2,1,0:T(8,128)(2,1)} %density.5, s32[128,1024]{1,0:T(8,128)} %valid.5), custom_call_target="tpu_custom_call" | custom-call | flops 1 | bytes 1 | tf_op jit(solution)/shard_map/sums/pallas_call | solution.py:159
  3.3 4.0 %collective-permute-start.4 = (f32[24,128]{1,0:T(8,128)S(1)}, f32[24,128]{1,0:T(8,128)S(1)}, u32[]{:S(2)}, u32[]{:S(2)}) collective-permute-start(f32[24,128]{1,0:T(8,128)S(1)} %get-tuple-element.39.after.refs_0_), channel_id=1, source_target_pairs={{0,24},{8,16},{16,8},{24,0},{1,25},{9,17},{17,9},{25,1},{2,26},{10... | collective-permute-start | bytes 36872 | tf_op jit(solution)/shard_map/ppermute | solution.py:565
  7.9 2.6 %ready.1 = (bf16[16,256,512]{2,1,0:T(8,128)(2,1)S(1)}, bf16[2,128,1024]{2,1,0:T(8,128)(2,1)S(1)}, bf16[1,16,32,1024]{3,2,1,0:T(8,128)(2,1)S(1)}, s32[1,32,1024]{2,1,0:T(8,128)S(1)}) custom-call(s32[1]{0:T(128)} %bitcast.me, bf16[16,128,1024]{2,1,0:T(8,128)(2,1)} %density.5, s32[128,1024]{1,0:T(8,128)} %valid.5, bf16[4,16,17]{2,1,0:T(8,128)(2,1)S(1)} %copy-done.4, ...), custom_call_target="tpu_custom_call" | custom-call | flops 1 | bytes 1 | tf_op jit(solution)/shard_map/ready/pallas_call | solution.py:229
  11.5 1.9 %inner.2.refs_5_ = bf16[8,16,1024]{2,1,0:T(8,128)(2,1)S(1)} custom-call(s32[1]{0:T(128)} %bitcast.me, bf16[1,16,32,1024]{3,2,1,0:T(8,128)(2,1)S(1)} %get-tuple-element.43.refs_0_, s32[1,32,1024]{2,1,0:T(8,128)S(1)} %get-tuple-element.44.refs_1_, bf16[16,256,512]{2,1,0:T(8,128)(2,1)S(1)} %get-tuple-element.40.refs_4_.refs_2_.col, ...), custom_call_target="tpu_custom_call" | custom-call | flops 1 | bytes 1 | tf_op jit(solution)/shard_map/inner/pallas_call | solution.py:288
  13.4 2.7 %collective-permute-start.5 = (bf16[8,16,1024]{2,1,0:T(8,128)(2,1)S(1)}, bf16[8,16,1024]{2,1,0:T(8,128)(2,1)S(1)}, u32[]{:S(2)}, u32[]{:S(2)}) collective-permute-start(bf16[8,16,1024]{2,1,0:T(8,128)(2,1)S(1)} %inner.2.refs_5_), channel_id=1, source_target_pairs={{0,4},{1,5},{2,6},{3,7},{4,0},{5,1},{6,2},{7,3},{8,12},{9,13},{10,... | collective-permute-start | bytes 786440 | tf_op jit(solution)/shard_map/ppermute | solution.py:562
  16.1 2.9 %collective-permute-start = (bf16[17,8,1024]{2,1,0:T(8,128)(2,1)S(1)}, bf16[17,8,1024]{2,1,0:T(8,128)(2,1)S(1)}, u32[]{:S(2)}, u32[]{:S(2)}) collective-permute-start(bf16[17,8,1024]{2,1,0:T(8,128)(2,1)S(1)} %get-tuple-element.37), channel_id=1, source_target_pairs={{0,8},{8,16},{16,24},{1,9},{9,17},{17,25},{2,10},{10,18},{18,26},{... | collective-permute-start | bytes 835592 | tf_op jit(solution)/shard_map/ppermute | solution.py:571
  19.0 1.5 %collective-permute-start.1 = (bf16[17,8,1024]{2,1,0:T(8,128)(2,1)S(1)}, bf16[17,8,1024]{2,1,0:T(8,128)(2,1)S(1)}, u32[]{:S(2)}, u32[]{:S(2)}) collective-permute-start(bf16[17,8,1024]{2,1,0:T(8,128)(2,1)S(1)} %get-tuple-element.38), channel_id=1, source_target_pairs={{8,0},{16,8},{24,16},{9,1},{17,9},{25,17},{10,2},{18,10},{26,18},{... | collective-permute-start | bytes 835592 | tf_op jit(solution)/shard_map/ppermute | solution.py:572
  20.4 5.1 %inner.3 = (bf16[8,16,1024]{2,1,0:T(8,128)(2,1)S(1)}, bf16[8,16,1024]{2,1,0:T(8,128)(2,1)S(1)}) custom-call(s32[1]{0:T(128)} %bitcast.me, bf16[16,128,1024]{2,1,0:T(8,128)(2,1)} %density.5, s32[128,1024]{1,0:T(8,128)} %valid.5, bf16[16,256,512]{2,1,0:T(8,128)(2,1)S(1)} %get-tuple-element.40.refs_4_.refs_2_.col, ...), custom_call_target="tpu_custom_call" | custom-call | flops 1 | bytes 1 | tf_op jit(solution)/shard_map/inner/pallas_call | solution.py:288
  27.0 4.7 %collective-permute-done.1.below = bf16[17,8,1024]{2,1,0:T(8,128)(2,1)S(1)} collective-permute-done((bf16[17,8,1024]{2,1,0:T(8,128)(2,1)S(1)}, bf16[17,8,1024]{2,1,0:T(8,128)(2,1)S(1)}, u32[]{:S(2)}, u32[]{:S(2)}) %collective-permute-start.1) | collective-permute-done | bytes 278560 | tf_op jit(solution)/shard_map/ppermute | solution.py:572
  31.6 16.1 %band.1 = (bf16[6,16,1024]{2,1,0:T(8,128)(2,1)}, bf16[2,16,1024]{2,1,0:T(8,128)(2,1)}, bf16[8,16,1024]{2,1,0:T(8,128)(2,1)}, bf16[6,16,1024]{2,1,0:T(8,128)(2,1)...) custom-call(s32[1]{0:T(128)} %bitcast.me, ...), custom_call_target="tpu_custom_call" | custom-call | flops 1 | bytes 1 | tf_op jit(solution)/shard_map/band/pallas_call | solution.py:395
  48.2 9.4 %collective-permute-start.11 = (bf16[8,16,1024]{2,1,0:T(8,128)(2,1)}, bf16[8,16,1024]{2,1,0:T(8,128)(2,1)S(1)}, u32[]{:S(2)}, u32[]{:S(2)}) collective-permute-start(bf16[8,16,1024]{2,1,0:T(8,128)(2,1)} %gate.20), channel_id=1, source_target_pairs={{0,3},{1,2},{2,1},{3,0},{4,7},{5,6},{6,5},{7,4},{8,11},{9,10},{10,... | collective-permute-start | bytes 786440 | tf_op jit(solution)/shard_map/ppermute | solution.py:562
  59.3 2.5 %collective-permute-start.7 = (bf16[6,16,1024]{2,1,0:T(8,128)(2,1)}, bf16[6,16,1024]{2,1,0:T(8,128)(2,1)S(1)}, u32[]{:S(2)}, u32[]{:S(2)}) collective-permute-start(bf16[6,16,1024]{2,1,0:T(8,128)(2,1)} %gate.17), channel_id=1, source_target_pairs={{0,6},{1,7},{2,4},{3,5},{4,2},{5,3},{6,0},{7,1},{8,14},{9,15},{10,... | collective-permute-start | bytes 589832 | tf_op jit(solution)/shard_map/ppermute | solution.py:562
  61.9 2.5 %collective-permute-start.17 = (bf16[6,16,1024]{2,1,0:T(8,128)(2,1)}, bf16[6,16,1024]{2,1,0:T(8,128)(2,1)S(1)}, u32[]{:S(2)}, u32[]{:S(2)}) collective-permute-start(bf16[6,16,1024]{2,1,0:T(8,128)(2,1)} %gate.26), channel_id=1, source_target_pairs={{0,7},{1,6},{2,5},{3,4},{4,3},{5,2},{6,1},{7,0},{8,15},{9,14},{10,... | collective-permute-start | bytes 589832 | tf_op jit(solution)/shard_map/ppermute | solution.py:562
  64.4 2.1 %collective-permute-start.12 = (bf16[8,16,1024]{2,1,0:T(8,128)(2,1)}, bf16[8,16,1024]{2,1,0:T(8,128)(2,1)S(1)}, u32[]{:S(2)}, u32[]{:S(2)}) collective-permute-start(bf16[8,16,1024]{2,1,0:T(8,128)(2,1)} %gate.21), channel_id=1, source_target_pairs={{0,3},{1,2},{2,1},{3,0},{4,7},{5,6},{6,5},{7,4},{8,11},{9,10},{10,... | collective-permute-start | bytes 786440 | tf_op jit(solution)/shard_map/ppermute | solution.py:562
  66.5 4.8 %collective-permute-done.19.refs_1_.refs_2_ = bf16[8,16,1024]{2,1,0:T(8,128)(2,1)S(1)} collective-permute-done((bf16[8,16,1024]{2,1,0:T(8,128)(2,1)}, bf16[8,16,1024]{2,1,0:T(8,128)(2,1)S(1)}, u32[]{:S(2)}, u32[]{:S(2)}) %collective-permute-start.19) | collective-permute-done | bytes 262176 | tf_op jit(solution)/shard_map/ppermute | solution.py:562
  71.3 7.9 %collective-permute-done.13.refs_1_.refs_7_ = bf16[8,16,1024]{2,1,0:T(8,128)(2,1)S(1)} collective-permute-done((bf16[8,16,1024]{2,1,0:T(8,128)(2,1)}, bf16[8,16,1024]{2,1,0:T(8,128)(2,1)S(1)}, u32[]{:S(2)}, u32[]{:S(2)}) %collective-permute-start.13) | collective-permute-done | bytes 262176 | tf_op jit(solution)/shard_map/ppermute | solution.py:562
  79.2 5.7 %collective-permute-done.7.refs_1_.refs_6_ = bf16[6,16,1024]{2,1,0:T(8,128)(2,1)S(1)} collective-permute-done((bf16[6,16,1024]{2,1,0:T(8,128)(2,1)}, bf16[6,16,1024]{2,1,0:T(8,128)(2,1)S(1)}, u32[]{:S(2)}, u32[]{:S(2)}) %collective-permute-start.7) | collective-permute-done | bytes 196640 | tf_op jit(solution)/shard_map/ppermute | solution.py:562
  84.9 6.1 %collective-permute-start.14 = (bf16[6,16,1024]{2,1,0:T(8,128)(2,1)}, bf16[6,16,1024]{2,1,0:T(8,128)(2,1)S(1)}, u32[]{:S(2)}, u32[]{:S(2)}) collective-permute-start(bf16[6,16,1024]{2,1,0:T(8,128)(2,1)} %gate.23), channel_id=1, source_target_pairs={{0,5},{1,4},{2,7},{3,6},{4,1},{5,0},{6,3},{7,2},{8,13},{9,12},{10,... | collective-permute-start | bytes 589832 | tf_op jit(solution)/shard_map/ppermute | solution.py:562
  91.5 8.0 %collective-permute-done.14.refs_1_.refs_5_ = bf16[6,16,1024]{2,1,0:T(8,128)(2,1)S(1)} collective-permute-done((bf16[6,16,1024]{2,1,0:T(8,128)(2,1)}, bf16[6,16,1024]{2,1,0:T(8,128)(2,1)S(1)}, u32[]{:S(2)}, u32[]{:S(2)}) %collective-permute-start.14) | collective-permute-done | bytes 196640 | tf_op jit(solution)/shard_map/ppermute | solution.py:562
  99.5 3.0 %collective-permute-start.18 = (bf16[2,16,1024]{2,1,0:T(8,128)(2,1)}, bf16[2,16,1024]{2,1,0:T(8,128)(2,1)S(1)}, u32[]{:S(2)}, u32[]{:S(2)}) collective-permute-start(bf16[2,16,1024]{2,1,0:T(8,128)(2,1)} %gate.27), channel_id=1, source_target_pairs={{0,5},{1,4},{2,7},{3,6},{4,1},{5,0},{6,3},{7,2},{8,13},{9,12},{10,... | collective-permute-start | bytes 196616 | tf_op jit(solution)/shard_map/ppermute | solution.py:562
  103.1 2.8 %collective-permute-start.22 = (bf16[2,16,1024]{2,1,0:T(8,128)(2,1)}, bf16[2,16,1024]{2,1,0:T(8,128)(2,1)S(1)}, u32[]{:S(2)}, u32[]{:S(2)}) collective-permute-start(bf16[2,16,1024]{2,1,0:T(8,128)(2,1)} %gate.31), channel_id=1, source_target_pairs={{0,7},{1,6},{2,5},{3,4},{4,3},{5,2},{6,1},{7,0},{8,15},{9,14},{10,... | collective-permute-start | bytes 196616 | tf_op jit(solution)/shard_map/ppermute | solution.py:562
  105.9 3.2 %project.3 = (bf16[128,16384]{1,0:T(8,128)(2,1)}, bf16[128,16384]{1,0:T(8,128)(2,1)}, f32[8,128]{1,0:T(8,128)}) custom-call(s32[1]{0:T(128)} %bitcast.me, bf16[256,128]{1,0:T(8,128)(2,1)S(1)} %weights.1, bf16[8,16,1024]{2,1,0:T(8,128)(2,1)S(1)} %copy-done.1, bf16[8,16,1024]{2,1,0:T(8,128)(2,1)S(1)} %collective-permute-done.20.refs_1_, ...), custom_call_target="tpu_custom_call" | custom-call | flops 1 | bytes 1 | tf_op jit(solution)/shard_map/project/pallas_call | solution.py:480
  110.5 2.7 %project.4 = (bf16[128,16384]{1,0:T(8,128)(2,1)}, bf16[128,16384]{1,0:T(8,128)(2,1)}, f32[8,128]{1,0:T(8,128)}) custom-call(s32[1]{0:T(128)} %bitcast.me, bf16[256,128]{1,0:T(8,128)(2,1)S(1)} %weights.1, bf16[8,16,1024]{2,1,0:T(8,128)(2,1)S(1)} %copy-done, ...), custom_call_target="tpu_custom_call", output_to_operand_aliasing={{0}: (10, {}), {1}: (11, {})} | custom-call | flops 1 | bytes 1 | tf_op jit(solution)/shard_map/project/pallas_call | solution.py:480
  113.3 3.0 %collective-permute-done.21.refs_6_ = bf16[2,16,1024]{2,1,0:T(8,128)(2,1)S(1)} collective-permute-done((bf16[2,16,1024]{2,1,0:T(8,128)(2,1)}, bf16[2,16,1024]{2,1,0:T(8,128)(2,1)S(1)}, u32[]{:S(2)}, u32[]{:S(2)}) %collective-permute-start.21) | collective-permute-done | bytes 65568 | tf_op jit(solution)/shard_map/ppermute | solution.py:562
  (62 shorter events, 9.2 us)
Async XLA Ops:
  3.3 7.2 %collective-permute-start.4 = (f32[24,128]{1,0:T(8,128)S(1)}, f32[24,128]{1,0:T(8,128)S(1)}, u32[]{:S(2)}, u32[]{:S(2)}) collective-permute-start(f32[24,128]{1,0:T(8,128)S(1)} %get-tuple-element.39.after.refs_0_), channel_id=1, source_target_pairs={{0,24},{8,16},{16,8},{24,0},{1,25},{9,17},{17,9},{25,1},{2,26},{10... | collective-permute-start | bytes 36872 | tf_op jit(solution)/shard_map/ppermute | solution.py:565
  7.2 3.7 %collective-permute-start.3 = (f32[24,128]{1,0:T(8,128)S(1)}, f32[24,128]{1,0:T(8,128)S(1)}, u32[]{:S(2)}, u32[]{:S(2)}) collective-permute-start(f32[24,128]{1,0:T(8,128)S(1)} %get-tuple-element.39.after.refs_0_), channel_id=1, source_target_pairs={{0,16},{8,24},{16,0},{24,8},{1,17},{9,25},{17,1},{25,9},{2,18},{10... | collective-permute-start | bytes 36872 | tf_op jit(solution)/shard_map/ppermute | solution.py:565
  7.7 3.7 %collective-permute-start.2 = (f32[24,128]{1,0:T(8,128)S(1)}, f32[24,128]{1,0:T(8,128)S(1)}, u32[]{:S(2)}, u32[]{:S(2)}) collective-permute-start(f32[24,128]{1,0:T(8,128)S(1)} %get-tuple-element.39.after.refs_0_), channel_id=1, source_target_pairs={{0,8},{8,0},{16,24},{24,16},{1,9},{9,1},{17,25},{25,17},{2,10},{10... | collective-permute-start | bytes 36872 | tf_op jit(solution)/shard_map/ppermute | solution.py:565
  13.4 13.5 %collective-permute-start.5 = (bf16[8,16,1024]{2,1,0:T(8,128)(2,1)S(1)}, bf16[8,16,1024]{2,1,0:T(8,128)(2,1)S(1)}, u32[]{:S(2)}, u32[]{:S(2)}) collective-permute-start(bf16[8,16,1024]{2,1,0:T(8,128)(2,1)S(1)} %inner.2.refs_5_), channel_id=1, source_target_pairs={{0,4},{1,5},{2,6},{3,7},{4,0},{5,1},{6,2},{7,3},{8,12},{9,13},{10,... | collective-permute-start | bytes 786440 | tf_op jit(solution)/shard_map/ppermute | solution.py:562
  16.1 10.9 %collective-permute-start = (bf16[17,8,1024]{2,1,0:T(8,128)(2,1)S(1)}, bf16[17,8,1024]{2,1,0:T(8,128)(2,1)S(1)}, u32[]{:S(2)}, u32[]{:S(2)}) collective-permute-start(bf16[17,8,1024]{2,1,0:T(8,128)(2,1)S(1)} %get-tuple-element.37), channel_id=1, source_target_pairs={{0,8},{8,16},{16,24},{1,9},{9,17},{17,25},{2,10},{10,18},{18,26},{... | collective-permute-start | bytes 835592 | tf_op jit(solution)/shard_map/ppermute | solution.py:571
  19.0 12.7 %collective-permute-start.1 = (bf16[17,8,1024]{2,1,0:T(8,128)(2,1)S(1)}, bf16[17,8,1024]{2,1,0:T(8,128)(2,1)S(1)}, u32[]{:S(2)}, u32[]{:S(2)}) collective-permute-start(bf16[17,8,1024]{2,1,0:T(8,128)(2,1)S(1)} %get-tuple-element.38), channel_id=1, source_target_pairs={{8,0},{16,8},{24,16},{9,1},{17,9},{25,17},{10,2},{18,10},{26,18},{... | collective-permute-start | bytes 835592 | tf_op jit(solution)/shard_map/ppermute | solution.py:572
  25.5 22.2 %collective-permute-start.10 = (bf16[8,16,1024]{2,1,0:T(8,128)(2,1)S(1)}, bf16[8,16,1024]{2,1,0:T(8,128)(2,1)S(1)}, u32[]{:S(2)}, u32[]{:S(2)}) collective-permute-start(bf16[8,16,1024]{2,1,0:T(8,128)(2,1)S(1)} %get-tuple-element.45.refs_0_), channel_id=1, source_target_pairs={{0,6},{1,7},{2,4},{3,5},{4,2},{5,3},{6,0},{7,1},{8,14},{9,15},{10,... | collective-permute-start | bytes 786440 | tf_op jit(solution)/shard_map/ppermute | solution.py:562
  26.9 32.4 %collective-permute-start.6 = (bf16[8,16,1024]{2,1,0:T(8,128)(2,1)S(1)}, bf16[8,16,1024]{2,1,0:T(8,128)(2,1)S(1)}, u32[]{:S(2)}, u32[]{:S(2)}) collective-permute-start(bf16[8,16,1024]{2,1,0:T(8,128)(2,1)S(1)} %get-tuple-element.50), channel_id=1, source_target_pairs={{0,5},{1,4},{2,7},{3,6},{4,1},{5,0},{6,3},{7,2},{8,13},{9,12},{10,... | collective-permute-start | bytes 786440 | tf_op jit(solution)/shard_map/ppermute | solution.py:562
  47.8 14.1 %collective-permute-start.16 = (bf16[6,16,1024]{2,1,0:T(8,128)(2,1)}, bf16[6,16,1024]{2,1,0:T(8,128)(2,1)S(1)}, u32[]{:S(2)}, u32[]{:S(2)}) collective-permute-start(bf16[6,16,1024]{2,1,0:T(8,128)(2,1)} %gate.25), channel_id=1, source_target_pairs={{0,4},{1,5},{2,6},{3,7},{4,0},{5,1},{6,2},{7,3},{8,12},{9,13},{10,... | collective-permute-start | bytes 589832 | tf_op jit(solution)/shard_map/ppermute | solution.py:562
  48.2 57.7 %copy-start.1 = (bf16[8,16,1024]{2,1,0:T(8,128)(2,1)S(1)}, bf16[8,16,1024]{2,1,0:T(8,128)(2,1)}, u32[]{:S(2)}) copy-start(bf16[8,16,1024]{2,1,0:T(8,128)(2,1)} %get-tuple-element.63.refs_0_) | copy-start | bytes 786436
  48.2 16.2 %collective-permute-start.11 = (bf16[8,16,1024]{2,1,0:T(8,128)(2,1)}, bf16[8,16,1024]{2,1,0:T(8,128)(2,1)S(1)}, u32[]{:S(2)}, u32[]{:S(2)}) collective-permute-start(bf16[8,16,1024]{2,1,0:T(8,128)(2,1)} %gate.20), channel_id=1, source_target_pairs={{0,3},{1,2},{2,1},{3,0},{4,7},{5,6},{6,5},{7,4},{8,11},{9,10},{10,... | collective-permute-start | bytes 786440 | tf_op jit(solution)/shard_map/ppermute | solution.py:562
  57.6 13.7 %collective-permute-start.19 = (bf16[8,16,1024]{2,1,0:T(8,128)(2,1)}, bf16[8,16,1024]{2,1,0:T(8,128)(2,1)S(1)}, u32[]{:S(2)}, u32[]{:S(2)}) collective-permute-start(bf16[8,16,1024]{2,1,0:T(8,128)(2,1)} %gate.28), channel_id=1, source_target_pairs={{0,2},{1,3},{2,0},{3,1},{4,6},{5,7},{6,4},{7,5},{8,10},{9,11},{10,... | collective-permute-start | bytes 786440 | tf_op jit(solution)/shard_map/ppermute | solution.py:562
  58.3 20.9 %collective-permute-start.13 = (bf16[8,16,1024]{2,1,0:T(8,128)(2,1)}, bf16[8,16,1024]{2,1,0:T(8,128)(2,1)S(1)}, u32[]{:S(2)}, u32[]{:S(2)}) collective-permute-start(bf16[8,16,1024]{2,1,0:T(8,128)(2,1)} %gate.22), channel_id=1, source_target_pairs={{0,7},{1,6},{2,5},{3,4},{4,3},{5,2},{6,1},{7,0},{8,15},{9,14},{10,... | collective-permute-start | bytes 786440 | tf_op jit(solution)/shard_map/ppermute | solution.py:562
  59.3 25.6 %collective-permute-start.7 = (bf16[6,16,1024]{2,1,0:T(8,128)(2,1)}, bf16[6,16,1024]{2,1,0:T(8,128)(2,1)S(1)}, u32[]{:S(2)}, u32[]{:S(2)}) collective-permute-start(bf16[6,16,1024]{2,1,0:T(8,128)(2,1)} %gate.17), channel_id=1, source_target_pairs={{0,6},{1,7},{2,4},{3,5},{4,2},{5,3},{6,0},{7,1},{8,14},{9,15},{10,... | collective-permute-start | bytes 589832 | tf_op jit(solution)/shard_map/ppermute | solution.py:562
  61.9 29.2 %collective-permute-start.17 = (bf16[6,16,1024]{2,1,0:T(8,128)(2,1)}, bf16[6,16,1024]{2,1,0:T(8,128)(2,1)S(1)}, u32[]{:S(2)}, u32[]{:S(2)}) collective-permute-start(bf16[6,16,1024]{2,1,0:T(8,128)(2,1)} %gate.26), channel_id=1, source_target_pairs={{0,7},{1,6},{2,5},{3,4},{4,3},{5,2},{6,1},{7,0},{8,15},{9,14},{10,... | collective-permute-start | bytes 589832 | tf_op jit(solution)/shard_map/ppermute | solution.py:562
  64.4 38.2 %collective-permute-start.12 = (bf16[8,16,1024]{2,1,0:T(8,128)(2,1)}, bf16[8,16,1024]{2,1,0:T(8,128)(2,1)S(1)}, u32[]{:S(2)}, u32[]{:S(2)}) collective-permute-start(bf16[8,16,1024]{2,1,0:T(8,128)(2,1)} %gate.21), channel_id=1, source_target_pairs={{0,3},{1,2},{2,1},{3,0},{4,7},{5,6},{6,5},{7,4},{8,11},{9,10},{10,... | collective-permute-start | bytes 786440 | tf_op jit(solution)/shard_map/ppermute | solution.py:562
  71.3 31.8 %collective-permute-start.20 = (bf16[8,16,1024]{2,1,0:T(8,128)(2,1)}, bf16[8,16,1024]{2,1,0:T(8,128)(2,1)S(1)}, u32[]{:S(2)}, u32[]{:S(2)}) collective-permute-start(bf16[8,16,1024]{2,1,0:T(8,128)(2,1)} %gate.29), channel_id=1, source_target_pairs={{0,1},{1,0},{2,3},{3,2},{4,5},{5,4},{6,7},{7,6},{8,9},{9,8},{10,11... | collective-permute-start | bytes 786440 | tf_op jit(solution)/shard_map/ppermute | solution.py:562
  79.2 30.5 %collective-permute-start.9 = (bf16[8,16,1024]{2,1,0:T(8,128)(2,1)}, bf16[8,16,1024]{2,1,0:T(8,128)(2,1)S(1)}, u32[]{:S(2)}, u32[]{:S(2)}) collective-permute-start(bf16[8,16,1024]{2,1,0:T(8,128)(2,1)} %gate.19), channel_id=1, source_target_pairs={{0,2},{1,3},{2,0},{3,1},{4,6},{5,7},{6,4},{7,5},{8,10},{9,11},{10,... | collective-permute-start | bytes 786440 | tf_op jit(solution)/shard_map/ppermute | solution.py:562
  84.9 14.6 %collective-permute-start.14 = (bf16[6,16,1024]{2,1,0:T(8,128)(2,1)}, bf16[6,16,1024]{2,1,0:T(8,128)(2,1)S(1)}, u32[]{:S(2)}, u32[]{:S(2)}) collective-permute-start(bf16[6,16,1024]{2,1,0:T(8,128)(2,1)} %gate.23), channel_id=1, source_target_pairs={{0,5},{1,4},{2,7},{3,6},{4,1},{5,0},{6,3},{7,2},{8,13},{9,12},{10,... | collective-permute-start | bytes 589832 | tf_op jit(solution)/shard_map/ppermute | solution.py:562
  91.0 19.5 %collective-permute-start.8 = (bf16[8,16,1024]{2,1,0:T(8,128)(2,1)}, bf16[8,16,1024]{2,1,0:T(8,128)(2,1)S(1)}, u32[]{:S(2)}, u32[]{:S(2)}) collective-permute-start(bf16[8,16,1024]{2,1,0:T(8,128)(2,1)} %gate.18), channel_id=1, source_target_pairs={{0,1},{1,0},{2,3},{3,2},{4,5},{5,4},{6,7},{7,6},{8,9},{9,8},{10,11... | collective-permute-start | bytes 786440 | tf_op jit(solution)/shard_map/ppermute | solution.py:562
  99.5 13.7 %collective-permute-start.18 = (bf16[2,16,1024]{2,1,0:T(8,128)(2,1)}, bf16[2,16,1024]{2,1,0:T(8,128)(2,1)S(1)}, u32[]{:S(2)}, u32[]{:S(2)}) collective-permute-start(bf16[2,16,1024]{2,1,0:T(8,128)(2,1)} %gate.27), channel_id=1, source_target_pairs={{0,5},{1,4},{2,7},{3,6},{4,1},{5,0},{6,3},{7,2},{8,13},{9,12},{10,... | collective-permute-start | bytes 196616 | tf_op jit(solution)/shard_map/ppermute | solution.py:562
  102.5 10.7 %collective-permute-start.15 = (bf16[2,16,1024]{2,1,0:T(8,128)(2,1)}, bf16[2,16,1024]{2,1,0:T(8,128)(2,1)S(1)}, u32[]{:S(2)}, u32[]{:S(2)}) collective-permute-start(bf16[2,16,1024]{2,1,0:T(8,128)(2,1)} %gate.24), channel_id=1, source_target_pairs={{0,4},{1,5},{2,6},{3,7},{4,0},{5,1},{6,2},{7,3},{8,12},{9,13},{10,... | collective-permute-start | bytes 196616 | tf_op jit(solution)/shard_map/ppermute | solution.py:562
  103.1 10.2 %collective-permute-start.22 = (bf16[2,16,1024]{2,1,0:T(8,128)(2,1)}, bf16[2,16,1024]{2,1,0:T(8,128)(2,1)S(1)}, u32[]{:S(2)}, u32[]{:S(2)}) collective-permute-start(bf16[2,16,1024]{2,1,0:T(8,128)(2,1)} %gate.31), channel_id=1, source_target_pairs={{0,7},{1,6},{2,5},{3,4},{4,3},{5,2},{6,1},{7,0},{8,15},{9,14},{10,... | collective-permute-start | bytes 196616 | tf_op jit(solution)/shard_map/ppermute | solution.py:562
  109.7 6.5 %collective-permute-start.21 = (bf16[2,16,1024]{2,1,0:T(8,128)(2,1)}, bf16[2,16,1024]{2,1,0:T(8,128)(2,1)S(1)}, u32[]{:S(2)}, u32[]{:S(2)}) collective-permute-start(bf16[2,16,1024]{2,1,0:T(8,128)(2,1)} %gate.30), channel_id=1, source_target_pairs={{0,6},{1,7},{2,4},{3,5},{4,2},{5,3},{6,0},{7,1},{8,14},{9,15},{10,... | collective-permute-start | bytes 196616 | tf_op jit(solution)/shard_map/ppermute | solution.py:562
  (6 other events, 153.7 us)

commit v17 on v16

--- a/solution.py
+++ b/solution.py
@@ -93,11 +93,10 @@
     return (slices, 2 * LANES, terms * LANES), (slices // GROUP, rows * GROUP, GROUP * LANES)
 
 
-def convolve(field, col, row, tall, rows):
+def convolve(field, col, row, tall, rows, read):
     slices, _, wide = col.shape
     terms = wide // LANES
     high, cols = LANES // terms, tall.shape[1]
-    read = rows + HALO
     if read < high:
         for n in range(tall.shape[0] // high):
             tall[n * high + read : (n + 1) * high] = jnp.zeros((high - read, cols), jnp.bfloat16)
@@ -194,10 +193,13 @@
     )(*sums, resident(after))
 
 
-def inner_rows(both, last):
+def inner_rows(both, last, high):
     both = both.astype(jnp.float32)
     rows = both.shape[0] - REACH
-    return jnp.where(last, both[REACH:], both[:rows])
+    chosen = jnp.where(last, both[REACH:], both[:rows])
+    if high == rows:
+        return chosen
+    return jnp.concatenate([chosen, jnp.zeros((high - rows, both.shape[1]), jnp.float32)], axis=0)
 
 
 def window_copies(b, block, last, density, valid, cube, plane, sems):
@@ -252,18 +254,20 @@
         copies = [window_copies(b, blocks[b], end, density, valid, cube, plane, sems) for b in range(count)]
         for copy in sum(copies, []):
             copy.start()
+    high = REACH + HALO if loaded else plane.shape[1]
     for b, cut in enumerate(pieces):
         if not loaded:
             for copy in copies[b]:
                 copy.wait()
         last = blocks[b] == end
-        mask = inner_rows(plane[b], last)
+        mask = inner_rows(plane[b], last, high)
         field = convolve(
-            lambda s, b=b, last=last, mask=mask: mask * (inner_rows(cube[b, s], last) - mean[s : s + 1, :1]),
+            lambda s, b=b, last=last, mask=mask: mask * (inner_rows(cube[b, s], last, high) - mean[s : s + 1, :1]),
             col,
             row,
             tall,
             REACH,
+            high,
         ).astype(jnp.bfloat16)
         for _, start, stop in cut:
             outs.pop(0)[...] = field[start:stop]

time: 118 us -> 112 us (0.949)
  starting transfers between devices: 45.2 us -> 34.4 us
  waiting for transfers between devices: 35.1 us -> 39.2 us
    ppermute x18, starting transfers between devices: 36.3 us -> 25.4 us  [swap(): return lax.ppermute(x, 'cuts', [(i, i ^ k) for i in range(peers)])]
    ppermute x18, waiting for transfers between devices: 29.5 us -> 34.3 us  [swap(): return lax.ppermute(x, 'cuts', [(i, i ^ k) for i in range(peers)])]
  transfers between devices with their start and end apart: 23 -> 23, of which waited for: 9 -> 8; matrix products, arithmetic and copies ran while one was open for 0% -> 0% of each run, Pallas kernels for 25% -> 27%
where the time goes in v17:
time: 112 us
  waiting for transfers between devices  39.2 us (35%)
  Pallas kernels  36.5 us (33%)
  starting transfers between devices  34.4 us (31%)
    ppermute x18, waiting for transfers between devices, swap(): return lax.ppermute(x, 'cuts', [(i, i ^ k) for i in range(peers)])  34.3 us
    ppermute x18, starting transfers between devices, swap(): return lax.ppermute(x, 'cuts', [(i, i ^ k) for i in range(peers)])  25.4 us
    pallas_call x1, Pallas kernels, filter_band(): pl.pallas_call(functools.partial(band_kernel, wanted), name='band', grid_...  16.1 us
    pallas_call x2, Pallas kernels, filter_inner(): pl.pallas_call(functools.partial(inner_kernel, wanted, loaded, rows // (h...  7.81 us
    pallas_call x3, Pallas kernels, project(): pl.pallas_call(functools.partial(project_kernel, count), name='project',...  7.24 us
    ppermute x3, starting transfers between devices, fast(): lax.ppermute(own, 'tile', [(i, i ^ k) for i in range(tiles)])  4.6 us
    ppermute x1, waiting for transfers between devices, fast(): below = lax.ppermute(first, 'tile', [(i + 1, i) for i in range(tiles - 1)])  3.87 us
    ppermute x1, starting transfers between devices, fast(): above = lax.ppermute(last, 'tile', [(i, i + 1) for i in range(tiles - 1)])  2.87 us
  transfers between devices with their start and end apart: 23, of which 8 were waited for; matrix products, arithmetic and copies ran while one was open for 0% of the time, Pallas kernels for 27%

profile of v17, /device:TPU:0, one launch (start us, length us, event | category | flops | bytes accessed | tf_op | source)
XLA Modules:
  0.0 111.6 jit_solution(5047210255841910784)
XLA Ops:
  0.6 2.6 %sums.1 = (f32[24,128]{1,0:T(8,128)S(1)}, bf16[17,8,1024]{2,1,0:T(8,128)(2,1)S(1)}, bf16[17,8,1024]{2,1,0:T(8,128)(2,1)S(1)}) custom-call(bf16[16,128,1024]{2,1,0:T(8,128)(2,1)} %density.5, s32[128,1024]{1,0:T(8,128)} %valid.5), custom_call_target="tpu_custom_call" | custom-call | flops 1 | bytes 1 | tf_op jit(solution)/shard_map/sums/pallas_call | solution.py:158
  3.3 4.0 %collective-permute-start.4 = (f32[24,128]{1,0:T(8,128)S(1)}, f32[24,128]{1,0:T(8,128)S(1)}, u32[]{:S(2)}, u32[]{:S(2)}) collective-permute-start(f32[24,128]{1,0:T(8,128)S(1)} %get-tuple-element.39.after.refs_0_), channel_id=1, source_target_pairs={{0,24},{8,16},{16,8},{24,0},{1,25},{9,17},{17,9},{25,1},{2,26},{10... | collective-permute-start | bytes 36872 | tf_op jit(solution)/shard_map/ppermute | solution.py:569
  7.9 2.6 %ready.1 = (bf16[16,256,512]{2,1,0:T(8,128)(2,1)S(1)}, bf16[2,128,1024]{2,1,0:T(8,128)(2,1)S(1)}, bf16[1,16,32,1024]{3,2,1,0:T(8,128)(2,1)S(1)}, s32[1,32,1024]{2,1,0:T(8,128)S(1)}) custom-call(s32[1]{0:T(128)} %bitcast.me, bf16[16,128,1024]{2,1,0:T(8,128)(2,1)} %density.5, s32[128,1024]{1,0:T(8,128)} %valid.5, bf16[4,16,17]{2,1,0:T(8,128)(2,1)S(1)} %copy-done.4, ...), custom_call_target="tpu_custom_call" | custom-call | flops 1 | bytes 1 | tf_op jit(solution)/shard_map/ready/pallas_call | solution.py:231
  11.5 1.9 %inner.2.refs_5_ = bf16[8,16,1024]{2,1,0:T(8,128)(2,1)S(1)} custom-call(s32[1]{0:T(128)} %bitcast.me, bf16[1,16,32,1024]{3,2,1,0:T(8,128)(2,1)S(1)} %get-tuple-element.43.refs_0_, s32[1,32,1024]{2,1,0:T(8,128)S(1)} %get-tuple-element.44.refs_1_, bf16[16,256,512]{2,1,0:T(8,128)(2,1)S(1)} %get-tuple-element.40.refs_4_.refs_2_.col, ...), custom_call_target="tpu_custom_call" | custom-call | flops 1 | bytes 1 | tf_op jit(solution)/shard_map/inner/pallas_call | solution.py:292
  13.4 2.7 %collective-permute-start.5 = (bf16[8,16,1024]{2,1,0:T(8,128)(2,1)S(1)}, bf16[8,16,1024]{2,1,0:T(8,128)(2,1)S(1)}, u32[]{:S(2)}, u32[]{:S(2)}) collective-permute-start(bf16[8,16,1024]{2,1,0:T(8,128)(2,1)S(1)} %inner.2.refs_5_), channel_id=1, source_target_pairs={{0,4},{1,5},{2,6},{3,7},{4,0},{5,1},{6,2},{7,3},{8,12},{9,13},{10,... | collective-permute-start | bytes 786440 | tf_op jit(solution)/shard_map/ppermute | solution.py:566
  16.1 2.9 %collective-permute-start = (bf16[17,8,1024]{2,1,0:T(8,128)(2,1)S(1)}, bf16[17,8,1024]{2,1,0:T(8,128)(2,1)S(1)}, u32[]{:S(2)}, u32[]{:S(2)}) collective-permute-start(bf16[17,8,1024]{2,1,0:T(8,128)(2,1)S(1)} %get-tuple-element.37), channel_id=1, source_target_pairs={{0,8},{8,16},{16,24},{1,9},{9,17},{17,25},{2,10},{10,18},{18,26},{... | collective-permute-start | bytes 835592 | tf_op jit(solution)/shard_map/ppermute | solution.py:575
  19.0 1.5 %collective-permute-start.1 = (bf16[17,8,1024]{2,1,0:T(8,128)(2,1)S(1)}, bf16[17,8,1024]{2,1,0:T(8,128)(2,1)S(1)}, u32[]{:S(2)}, u32[]{:S(2)}) collective-permute-start(bf16[17,8,1024]{2,1,0:T(8,128)(2,1)S(1)} %get-tuple-element.38), channel_id=1, source_target_pairs={{8,0},{16,8},{24,16},{9,1},{17,9},{25,17},{10,2},{18,10},{26,18},{... | collective-permute-start | bytes 835592 | tf_op jit(solution)/shard_map/ppermute | solution.py:576
  20.4 5.9 %inner.3 = (bf16[8,16,1024]{2,1,0:T(8,128)(2,1)S(1)}, bf16[8,16,1024]{2,1,0:T(8,128)(2,1)S(1)}) custom-call(s32[1]{0:T(128)} %bitcast.me, bf16[16,128,1024]{2,1,0:T(8,128)(2,1)} %density.5, s32[128,1024]{1,0:T(8,128)} %valid.5, bf16[16,256,512]{2,1,0:T(8,128)(2,1)S(1)} %get-tuple-element.40.refs_4_.refs_2_.col, ...), custom_call_target="tpu_custom_call" | custom-call | flops 1 | bytes 1 | tf_op jit(solution)/shard_map/inner/pallas_call | solution.py:292
  26.3 1.4 %collective-permute-start.10 = (bf16[8,16,1024]{2,1,0:T(8,128)(2,1)S(1)}, bf16[8,16,1024]{2,1,0:T(8,128)(2,1)S(1)}, u32[]{:S(2)}, u32[]{:S(2)}) collective-permute-start(bf16[8,16,1024]{2,1,0:T(8,128)(2,1)S(1)} %get-tuple-element.45.refs_0_), channel_id=1, source_target_pairs={{0,6},{1,7},{2,4},{3,5},{4,2},{5,3},{6,0},{7,1},{8,14},{9,15},{10,... | collective-permute-start | bytes 786440 | tf_op jit(solution)/shard_map/ppermute | solution.py:566
  27.8 3.9 %collective-permute-done.1.below = bf16[17,8,1024]{2,1,0:T(8,128)(2,1)S(1)} collective-permute-done((bf16[17,8,1024]{2,1,0:T(8,128)(2,1)S(1)}, bf16[17,8,1024]{2,1,0:T(8,128)(2,1)S(1)}, u32[]{:S(2)}, u32[]{:S(2)}) %collective-permute-start.1) | collective-permute-done | bytes 278560 | tf_op jit(solution)/shard_map/ppermute | solution.py:576
  31.6 16.1 %band.1 = (bf16[6,16,1024]{2,1,0:T(8,128)(2,1)}, bf16[2,16,1024]{2,1,0:T(8,128)(2,1)}, bf16[8,16,1024]{2,1,0:T(8,128)(2,1)}, bf16[6,16,1024]{2,1,0:T(8,128)(2,1)...) custom-call(s32[1]{0:T(128)} %bitcast.me, ...), custom_call_target="tpu_custom_call" | custom-call | flops 1 | bytes 1 | tf_op jit(solution)/shard_map/band/pallas_call | solution.py:399
  48.2 1.6 %collective-permute-start.19 = (bf16[8,16,1024]{2,1,0:T(8,128)(2,1)}, bf16[8,16,1024]{2,1,0:T(8,128)(2,1)S(1)}, u32[]{:S(2)}, u32[]{:S(2)}) collective-permute-start(bf16[8,16,1024]{2,1,0:T(8,128)(2,1)} %gate.28), channel_id=1, source_target_pairs={{0,2},{1,3},{2,0},{3,1},{4,6},{5,7},{6,4},{7,5},{8,10},{9,11},{10,... | collective-permute-start | bytes 786440 | tf_op jit(solution)/shard_map/ppermute | solution.py:566
  49.8 3.5 %collective-permute-start.13 = (bf16[8,16,1024]{2,1,0:T(8,128)(2,1)}, bf16[8,16,1024]{2,1,0:T(8,128)(2,1)S(1)}, u32[]{:S(2)}, u32[]{:S(2)}) collective-permute-start(bf16[8,16,1024]{2,1,0:T(8,128)(2,1)} %gate.22), channel_id=1, source_target_pairs={{0,7},{1,6},{2,5},{3,4},{4,3},{5,2},{6,1},{7,0},{8,15},{9,14},{10,... | collective-permute-start | bytes 786440 | tf_op jit(solution)/shard_map/ppermute | solution.py:566
  53.3 2.3 %collective-permute-start.7 = (bf16[6,16,1024]{2,1,0:T(8,128)(2,1)}, bf16[6,16,1024]{2,1,0:T(8,128)(2,1)S(1)}, u32[]{:S(2)}, u32[]{:S(2)}) collective-permute-start(bf16[6,16,1024]{2,1,0:T(8,128)(2,1)} %gate.17), channel_id=1, source_target_pairs={{0,6},{1,7},{2,4},{3,5},{4,2},{5,3},{6,0},{7,1},{8,14},{9,15},{10,... | collective-permute-start | bytes 589832 | tf_op jit(solution)/shard_map/ppermute | solution.py:566
  55.6 4.8 %collective-permute-done.16.refs_1_.refs_4_ = bf16[6,16,1024]{2,1,0:T(8,128)(2,1)S(1)} collective-permute-done((bf16[6,16,1024]{2,1,0:T(8,128)(2,1)}, bf16[6,16,1024]{2,1,0:T(8,128)(2,1)S(1)}, u32[]{:S(2)}, u32[]{:S(2)}) %collective-permute-start.16) | collective-permute-done | bytes 196640 | tf_op jit(solution)/shard_map/ppermute | solution.py:566
  61.6 18.4 %collective-permute-done.19.refs_1_.refs_2_ = bf16[8,16,1024]{2,1,0:T(8,128)(2,1)S(1)} collective-permute-done((bf16[8,16,1024]{2,1,0:T(8,128)(2,1)}, bf16[8,16,1024]{2,1,0:T(8,128)(2,1)S(1)}, u32[]{:S(2)}, u32[]{:S(2)}) %collective-permute-start.19) | collective-permute-done | bytes 262176 | tf_op jit(solution)/shard_map/ppermute | solution.py:566
  80.1 5.0 %collective-permute-start.14 = (bf16[6,16,1024]{2,1,0:T(8,128)(2,1)}, bf16[6,16,1024]{2,1,0:T(8,128)(2,1)S(1)}, u32[]{:S(2)}, u32[]{:S(2)}) collective-permute-start(bf16[6,16,1024]{2,1,0:T(8,128)(2,1)} %gate.23), channel_id=1, source_target_pairs={{0,5},{1,4},{2,7},{3,6},{4,1},{5,0},{6,3},{7,2},{8,13},{9,12},{10,... | collective-permute-start | bytes 589832 | tf_op jit(solution)/shard_map/ppermute | solution.py:566
  86.0 6.6 %collective-permute-done.14.refs_1_.refs_5_ = bf16[6,16,1024]{2,1,0:T(8,128)(2,1)S(1)} collective-permute-done((bf16[6,16,1024]{2,1,0:T(8,128)(2,1)}, bf16[6,16,1024]{2,1,0:T(8,128)(2,1)S(1)}, u32[]{:S(2)}, u32[]{:S(2)}) %collective-permute-start.14) | collective-permute-done | bytes 196640 | tf_op jit(solution)/shard_map/ppermute | solution.py:566
  92.5 2.8 %collective-permute-start.18 = (bf16[2,16,1024]{2,1,0:T(8,128)(2,1)}, bf16[2,16,1024]{2,1,0:T(8,128)(2,1)S(1)}, u32[]{:S(2)}, u32[]{:S(2)}) collective-permute-start(bf16[2,16,1024]{2,1,0:T(8,128)(2,1)} %gate.27), channel_id=1, source_target_pairs={{0,5},{1,4},{2,7},{3,6},{4,1},{5,0},{6,3},{7,2},{8,13},{9,12},{10,... | collective-permute-start | bytes 196616 | tf_op jit(solution)/shard_map/ppermute | solution.py:566
  95.3 4.7 %collective-permute-start.22 = (bf16[2,16,1024]{2,1,0:T(8,128)(2,1)}, bf16[2,16,1024]{2,1,0:T(8,128)(2,1)S(1)}, u32[]{:S(2)}, u32[]{:S(2)}) collective-permute-start(bf16[2,16,1024]{2,1,0:T(8,128)(2,1)} %gate.31), channel_id=1, source_target_pairs={{0,7},{1,6},{2,5},{3,4},{4,3},{5,2},{6,1},{7,0},{8,15},{9,14},{10,... | collective-permute-start | bytes 196616 | tf_op jit(solution)/shard_map/ppermute | solution.py:566
  100.0 3.2 %project.3 = (bf16[128,16384]{1,0:T(8,128)(2,1)}, bf16[128,16384]{1,0:T(8,128)(2,1)}, f32[8,128]{1,0:T(8,128)}) custom-call(s32[1]{0:T(128)} %bitcast.me, bf16[256,128]{1,0:T(8,128)(2,1)S(1)} %weights.1, bf16[8,16,1024]{2,1,0:T(8,128)(2,1)S(1)} %copy-done.1, bf16[8,16,1024]{2,1,0:T(8,128)(2,1)S(1)} %collective-permute-done.20.refs_1_, ...), custom_call_target="tpu_custom_call" | custom-call | flops 1 | bytes 1 | tf_op jit(solution)/shard_map/project/pallas_call | solution.py:484
  104.2 2.7 %project.4 = (bf16[128,16384]{1,0:T(8,128)(2,1)}, bf16[128,16384]{1,0:T(8,128)(2,1)}, f32[8,128]{1,0:T(8,128)}) custom-call(s32[1]{0:T(128)} %bitcast.me, bf16[256,128]{1,0:T(8,128)(2,1)S(1)} %weights.1, bf16[8,16,1024]{2,1,0:T(8,128)(2,1)S(1)} %copy-done, ...), custom_call_target="tpu_custom_call", output_to_operand_aliasing={{0}: (10, {}), {1}: (11, {})} | custom-call | flops 1 | bytes 1 | tf_op jit(solution)/shard_map/project/pallas_call | solution.py:484
  106.9 3.3 %collective-permute-done.21.refs_6_ = bf16[2,16,1024]{2,1,0:T(8,128)(2,1)S(1)} collective-permute-done((bf16[2,16,1024]{2,1,0:T(8,128)(2,1)}, bf16[2,16,1024]{2,1,0:T(8,128)(2,1)S(1)}, u32[]{:S(2)}, u32[]{:S(2)}) %collective-permute-start.21) | collective-permute-done | bytes 65568 | tf_op jit(solution)/shard_map/ppermute | solution.py:566
  110.2 1.3 %project.5 = (bf16[128,16384]{1,0:T(8,128)(2,1)}, bf16[128,16384]{1,0:T(8,128)(2,1)}, f32[8,128]{1,0:T(8,128)}) custom-call(s32[1]{0:T(128)} %bitcast.me, bf16[256,128]{1,0:T(8,128)(2,1)S(1)} %weights.1, bf16[8,16,1024]{2,1,0:T(8,128)(2,1)S(1)} %copy-done, ...), custom_call_target="tpu_custom_call", output_to_operand_aliasing={{0}: (10, {}), {1}: (11, {})} | custom-call | flops 1 | bytes 1 | tf_op jit(solution)/shard_map/project/pallas_call | solution.py:484
  (62 shorter events, 5.3 us)
Async XLA Ops:
  3.3 7.2 %collective-permute-start.4 = (f32[24,128]{1,0:T(8,128)S(1)}, f32[24,128]{1,0:T(8,128)S(1)}, u32[]{:S(2)}, u32[]{:S(2)}) collective-permute-start(f32[24,128]{1,0:T(8,128)S(1)} %get-tuple-element.39.after.refs_0_), channel_id=1, source_target_pairs={{0,24},{8,16},{16,8},{24,0},{1,25},{9,17},{17,9},{25,1},{2,26},{10... | collective-permute-start | bytes 36872 | tf_op jit(solution)/shard_map/ppermute | solution.py:569
  7.2 3.7 %collective-permute-start.3 = (f32[24,128]{1,0:T(8,128)S(1)}, f32[24,128]{1,0:T(8,128)S(1)}, u32[]{:S(2)}, u32[]{:S(2)}) collective-permute-start(f32[24,128]{1,0:T(8,128)S(1)} %get-tuple-element.39.after.refs_0_), channel_id=1, source_target_pairs={{0,16},{8,24},{16,0},{24,8},{1,17},{9,25},{17,1},{25,9},{2,18},{10... | collective-permute-start | bytes 36872 | tf_op jit(solution)/shard_map/ppermute | solution.py:569
  7.7 3.7 %collective-permute-start.2 = (f32[24,128]{1,0:T(8,128)S(1)}, f32[24,128]{1,0:T(8,128)S(1)}, u32[]{:S(2)}, u32[]{:S(2)}) collective-permute-start(f32[24,128]{1,0:T(8,128)S(1)} %get-tuple-element.39.after.refs_0_), channel_id=1, source_target_pairs={{0,8},{8,0},{16,24},{24,16},{1,9},{9,1},{17,25},{25,17},{2,10},{10... | collective-permute-start | bytes 36872 | tf_op jit(solution)/shard_map/ppermute | solution.py:569
  13.4 14.3 %collective-permute-start.5 = (bf16[8,16,1024]{2,1,0:T(8,128)(2,1)S(1)}, bf16[8,16,1024]{2,1,0:T(8,128)(2,1)S(1)}, u32[]{:S(2)}, u32[]{:S(2)}) collective-permute-start(bf16[8,16,1024]{2,1,0:T(8,128)(2,1)S(1)} %inner.2.refs_5_), channel_id=1, source_target_pairs={{0,4},{1,5},{2,6},{3,7},{4,0},{5,1},{6,2},{7,3},{8,12},{9,13},{10,... | collective-permute-start | bytes 786440 | tf_op jit(solution)/shard_map/ppermute | solution.py:566
  16.1 11.7 %collective-permute-start = (bf16[17,8,1024]{2,1,0:T(8,128)(2,1)S(1)}, bf16[17,8,1024]{2,1,0:T(8,128)(2,1)S(1)}, u32[]{:S(2)}, u32[]{:S(2)}) collective-permute-start(bf16[17,8,1024]{2,1,0:T(8,128)(2,1)S(1)} %get-tuple-element.37), channel_id=1, source_target_pairs={{0,8},{8,16},{16,24},{1,9},{9,17},{17,25},{2,10},{10,18},{18,26},{... | collective-permute-start | bytes 835592 | tf_op jit(solution)/shard_map/ppermute | solution.py:575
  19.0 12.7 %collective-permute-start.1 = (bf16[17,8,1024]{2,1,0:T(8,128)(2,1)S(1)}, bf16[17,8,1024]{2,1,0:T(8,128)(2,1)S(1)}, u32[]{:S(2)}, u32[]{:S(2)}) collective-permute-start(bf16[17,8,1024]{2,1,0:T(8,128)(2,1)S(1)} %get-tuple-element.38), channel_id=1, source_target_pairs={{8,0},{16,8},{24,16},{9,1},{17,9},{25,17},{10,2},{18,10},{26,18},{... | collective-permute-start | bytes 835592 | tf_op jit(solution)/shard_map/ppermute | solution.py:576
  26.3 21.4 %collective-permute-start.10 = (bf16[8,16,1024]{2,1,0:T(8,128)(2,1)S(1)}, bf16[8,16,1024]{2,1,0:T(8,128)(2,1)S(1)}, u32[]{:S(2)}, u32[]{:S(2)}) collective-permute-start(bf16[8,16,1024]{2,1,0:T(8,128)(2,1)S(1)} %get-tuple-element.45.refs_0_), channel_id=1, source_target_pairs={{0,6},{1,7},{2,4},{3,5},{4,2},{5,3},{6,0},{7,1},{8,14},{9,15},{10,... | collective-permute-start | bytes 786440 | tf_op jit(solution)/shard_map/ppermute | solution.py:566
  27.8 25.5 %collective-permute-start.6 = (bf16[8,16,1024]{2,1,0:T(8,128)(2,1)S(1)}, bf16[8,16,1024]{2,1,0:T(8,128)(2,1)S(1)}, u32[]{:S(2)}, u32[]{:S(2)}) collective-permute-start(bf16[8,16,1024]{2,1,0:T(8,128)(2,1)S(1)} %get-tuple-element.50), channel_id=1, source_target_pairs={{0,5},{1,4},{2,7},{3,6},{4,1},{5,0},{6,3},{7,2},{8,13},{9,12},{10,... | collective-permute-start | bytes 786440 | tf_op jit(solution)/shard_map/ppermute | solution.py:566
  47.8 12.6 %collective-permute-start.16 = (bf16[6,16,1024]{2,1,0:T(8,128)(2,1)}, bf16[6,16,1024]{2,1,0:T(8,128)(2,1)S(1)}, u32[]{:S(2)}, u32[]{:S(2)}) collective-permute-start(bf16[6,16,1024]{2,1,0:T(8,128)(2,1)} %gate.25), channel_id=1, source_target_pairs={{0,4},{1,5},{2,6},{3,7},{4,0},{5,1},{6,2},{7,3},{8,12},{9,13},{10,... | collective-permute-start | bytes 589832 | tf_op jit(solution)/shard_map/ppermute | solution.py:566
  48.2 51.9 %copy-start.1 = (bf16[8,16,1024]{2,1,0:T(8,128)(2,1)S(1)}, bf16[8,16,1024]{2,1,0:T(8,128)(2,1)}, u32[]{:S(2)}) copy-start(bf16[8,16,1024]{2,1,0:T(8,128)(2,1)} %get-tuple-element.63.refs_0_) | copy-start | bytes 786436
  48.2 13.4 %collective-permute-start.11 = (bf16[8,16,1024]{2,1,0:T(8,128)(2,1)}, bf16[8,16,1024]{2,1,0:T(8,128)(2,1)S(1)}, u32[]{:S(2)}, u32[]{:S(2)}) collective-permute-start(bf16[8,16,1024]{2,1,0:T(8,128)(2,1)} %gate.20), channel_id=1, source_target_pairs={{0,3},{1,2},{2,1},{3,0},{4,7},{5,6},{6,5},{7,4},{8,11},{9,10},{10,... | collective-permute-start | bytes 786440 | tf_op jit(solution)/shard_map/ppermute | solution.py:566
  48.2 31.8 %collective-permute-start.19 = (bf16[8,16,1024]{2,1,0:T(8,128)(2,1)}, bf16[8,16,1024]{2,1,0:T(8,128)(2,1)S(1)}, u32[]{:S(2)}, u32[]{:S(2)}) collective-permute-start(bf16[8,16,1024]{2,1,0:T(8,128)(2,1)} %gate.28), channel_id=1, source_target_pairs={{0,2},{1,3},{2,0},{3,1},{4,6},{5,7},{6,4},{7,5},{8,10},{9,11},{10,... | collective-permute-start | bytes 786440 | tf_op jit(solution)/shard_map/ppermute | solution.py:566
  49.8 30.2 %collective-permute-start.13 = (bf16[8,16,1024]{2,1,0:T(8,128)(2,1)}, bf16[8,16,1024]{2,1,0:T(8,128)(2,1)S(1)}, u32[]{:S(2)}, u32[]{:S(2)}) collective-permute-start(bf16[8,16,1024]{2,1,0:T(8,128)(2,1)} %gate.22), channel_id=1, source_target_pairs={{0,7},{1,6},{2,5},{3,4},{4,3},{5,2},{6,1},{7,0},{8,15},{9,14},{10,... | collective-permute-start | bytes 786440 | tf_op jit(solution)/shard_map/ppermute | solution.py:566
  53.3 26.8 %collective-permute-start.7 = (bf16[6,16,1024]{2,1,0:T(8,128)(2,1)}, bf16[6,16,1024]{2,1,0:T(8,128)(2,1)S(1)}, u32[]{:S(2)}, u32[]{:S(2)}) collective-permute-start(bf16[6,16,1024]{2,1,0:T(8,128)(2,1)} %gate.17), channel_id=1, source_target_pairs={{0,6},{1,7},{2,4},{3,5},{4,2},{5,3},{6,0},{7,1},{8,14},{9,15},{10,... | collective-permute-start | bytes 589832 | tf_op jit(solution)/shard_map/ppermute | solution.py:566
  60.3 24.8 %collective-permute-start.17 = (bf16[6,16,1024]{2,1,0:T(8,128)(2,1)}, bf16[6,16,1024]{2,1,0:T(8,128)(2,1)S(1)}, u32[]{:S(2)}, u32[]{:S(2)}) collective-permute-start(bf16[6,16,1024]{2,1,0:T(8,128)(2,1)} %gate.26), channel_id=1, source_target_pairs={{0,7},{1,6},{2,5},{3,4},{4,3},{5,2},{6,1},{7,0},{8,15},{9,14},{10,... | collective-permute-start | bytes 589832 | tf_op jit(solution)/shard_map/ppermute | solution.py:566
  61.6 33.7 %collective-permute-start.12 = (bf16[8,16,1024]{2,1,0:T(8,128)(2,1)}, bf16[8,16,1024]{2,1,0:T(8,128)(2,1)S(1)}, u32[]{:S(2)}, u32[]{:S(2)}) collective-permute-start(bf16[8,16,1024]{2,1,0:T(8,128)(2,1)} %gate.21), channel_id=1, source_target_pairs={{0,3},{1,2},{2,1},{3,0},{4,7},{5,6},{6,5},{7,4},{8,11},{9,10},{10,... | collective-permute-start | bytes 786440 | tf_op jit(solution)/shard_map/ppermute | solution.py:566
  80.0 15.4 %collective-permute-start.20 = (bf16[8,16,1024]{2,1,0:T(8,128)(2,1)}, bf16[8,16,1024]{2,1,0:T(8,128)(2,1)S(1)}, u32[]{:S(2)}, u32[]{:S(2)}) collective-permute-start(bf16[8,16,1024]{2,1,0:T(8,128)(2,1)} %gate.29), channel_id=1, source_target_pairs={{0,1},{1,0},{2,3},{3,2},{4,5},{5,4},{6,7},{7,6},{8,9},{9,8},{10,11... | collective-permute-start | bytes 786440 | tf_op jit(solution)/shard_map/ppermute | solution.py:566
  80.0 23.9 %collective-permute-start.9 = (bf16[8,16,1024]{2,1,0:T(8,128)(2,1)}, bf16[8,16,1024]{2,1,0:T(8,128)(2,1)S(1)}, u32[]{:S(2)}, u32[]{:S(2)}) collective-permute-start(bf16[8,16,1024]{2,1,0:T(8,128)(2,1)} %gate.19), channel_id=1, source_target_pairs={{0,2},{1,3},{2,0},{3,1},{4,6},{5,7},{6,4},{7,5},{8,10},{9,11},{10,... | collective-permute-start | bytes 786440 | tf_op jit(solution)/shard_map/ppermute | solution.py:566
  80.1 12.5 %collective-permute-start.14 = (bf16[6,16,1024]{2,1,0:T(8,128)(2,1)}, bf16[6,16,1024]{2,1,0:T(8,128)(2,1)S(1)}, u32[]{:S(2)}, u32[]{:S(2)}) collective-permute-start(bf16[6,16,1024]{2,1,0:T(8,128)(2,1)} %gate.23), channel_id=1, source_target_pairs={{0,5},{1,4},{2,7},{3,6},{4,1},{5,0},{6,3},{7,2},{8,13},{9,12},{10,... | collective-permute-start | bytes 589832 | tf_op jit(solution)/shard_map/ppermute | solution.py:566
  85.1 19.0 %collective-permute-start.8 = (bf16[8,16,1024]{2,1,0:T(8,128)(2,1)}, bf16[8,16,1024]{2,1,0:T(8,128)(2,1)S(1)}, u32[]{:S(2)}, u32[]{:S(2)}) collective-permute-start(bf16[8,16,1024]{2,1,0:T(8,128)(2,1)} %gate.18), channel_id=1, source_target_pairs={{0,1},{1,0},{2,3},{3,2},{4,5},{5,4},{6,7},{7,6},{8,9},{9,8},{10,11... | collective-permute-start | bytes 786440 | tf_op jit(solution)/shard_map/ppermute | solution.py:566
  92.5 14.4 %collective-permute-start.18 = (bf16[2,16,1024]{2,1,0:T(8,128)(2,1)}, bf16[2,16,1024]{2,1,0:T(8,128)(2,1)S(1)}, u32[]{:S(2)}, u32[]{:S(2)}) collective-permute-start(bf16[2,16,1024]{2,1,0:T(8,128)(2,1)} %gate.27), channel_id=1, source_target_pairs={{0,5},{1,4},{2,7},{3,6},{4,1},{5,0},{6,3},{7,2},{8,13},{9,12},{10,... | collective-permute-start | bytes 196616 | tf_op jit(solution)/shard_map/ppermute | solution.py:566
  95.3 11.6 %collective-permute-start.15 = (bf16[2,16,1024]{2,1,0:T(8,128)(2,1)}, bf16[2,16,1024]{2,1,0:T(8,128)(2,1)S(1)}, u32[]{:S(2)}, u32[]{:S(2)}) collective-permute-start(bf16[2,16,1024]{2,1,0:T(8,128)(2,1)} %gate.24), channel_id=1, source_target_pairs={{0,4},{1,5},{2,6},{3,7},{4,0},{5,1},{6,2},{7,3},{8,12},{9,13},{10,... | collective-permute-start | bytes 196616 | tf_op jit(solution)/shard_map/ppermute | solution.py:566
  95.3 11.6 %collective-permute-start.22 = (bf16[2,16,1024]{2,1,0:T(8,128)(2,1)}, bf16[2,16,1024]{2,1,0:T(8,128)(2,1)S(1)}, u32[]{:S(2)}, u32[]{:S(2)}) collective-permute-start(bf16[2,16,1024]{2,1,0:T(8,128)(2,1)} %gate.31), channel_id=1, source_target_pairs={{0,7},{1,6},{2,5},{3,4},{4,3},{5,2},{6,1},{7,0},{8,15},{9,14},{10,... | collective-permute-start | bytes 196616 | tf_op jit(solution)/shard_map/ppermute | solution.py:566
  103.9 6.4 %collective-permute-start.21 = (bf16[2,16,1024]{2,1,0:T(8,128)(2,1)}, bf16[2,16,1024]{2,1,0:T(8,128)(2,1)S(1)}, u32[]{:S(2)}, u32[]{:S(2)}) collective-permute-start(bf16[2,16,1024]{2,1,0:T(8,128)(2,1)} %gate.30), channel_id=1, source_target_pairs={{0,6},{1,7},{2,4},{3,5},{4,2},{5,3},{6,0},{7,1},{8,14},{9,15},{10,... | collective-permute-start | bytes 196616 | tf_op jit(solution)/shard_map/ppermute | solution.py:566
  (6 other events, 142.3 us)
